TPU v7x, 512 devices: a whole 4x4x16 slice. The times are simulated.
512 devices in a mesh: dp: 32 (over y, x, core), feat: 16 (over z).
Axes of the slice: x: 4, y: 4, z: 16, core: 2. Of those that a mesh axis runs over, the one named last changes fastest.
Arguments:
- edge_feats: bfloat16 [65536, 768], P('dp', 'feat'), may hold values from -6 to 6
- edge_dst: int32 [65536], P('dp'), may hold values from 0 to 16383, as said below
- self_feats: bfloat16 [16384, 768], P('dp', 'feat'), may hold values from -6 to 6
- neigh_one: bfloat16 [768, 1024], P('feat'), may hold values from -0.21875 to 0.21875
- self_one: bfloat16 [768, 1024], P('feat'), may hold values from -0.21875 to 0.21875
- bias_one: float32 [1024], P('feat'), may hold values from -3 to 3
- tile_index: int32 [128, 2], P('dp'), may hold values from 0 to 3
- tile_values: bfloat16 [128, 128, 128], P('dp'), may hold values from -0.5 to 0.5
- seed_live: int32 [16384], P('dp'), may hold values 0 or 1
- neigh_two: bfloat16 [1024, 1024], P('feat'), may hold values from -0.1875 to 0.1875
- self_two: bfloat16 [1024, 1024], P('feat'), may hold values from -0.1875 to 0.1875
- bias_two: float32 [1024], P('feat'), may hold values from -3 to 3
- cotangent: bfloat16 [16384, 1024], P('dp', 'feat'), may hold values from -0.046875 to 0.046875
Outputs:
- second_out: bfloat16 [16384, 1024], P('dp', 'feat')
- grad_neigh: float32 [1024, 1024], P('feat')
- grad_self: float32 [1024, 1024], P('feat')
Inputs may be any that keep to these rules, and one draw needn't show every extreme that they name: `edge_dst`: the owner of target vertex v is v // 512. Among the 2048 edges of one index of dp at most 128 have targets of one owner; in every draw each index of dp has some owner with exactly 128, and some owner receives exactly 128 from every index of dp.
All inputs are finite; a program needn't handle non-finite values. No bound on the sum of `seed_live` on one device may be relied on, other than what follows from the above.
Results may differ from a plain program's by a relative error of at most 0.0053.
Values may be sent and summed in bfloat16 or wider, within the bound.
No kernel may reach another device: no remote copies, remote signals or barrier semaphores. Data moves between devices by JAX's collectives and lax.ppermute only.
A program may use at most 128 MiB of HBM per device.

v0:
```python
import jax
import jax.numpy as jnp
from jax import lax
from jax.sharding import PartitionSpec as P


def body(
    edge_feats,
    edge_dst,
    self_feats,
    neigh_one,
    self_one,
    bias_one,
    tile_index,
    tile_values,
    seed_live,
    neigh_two,
    self_two,
    bias_two,
    cotangent,
):
    groups = lax.axis_size("dp")
    edge_rows = edge_feats.shape[0]
    feat_cols = edge_feats.shape[1]
    tgt_rows = self_feats.shape[0]
    hidden_cols = bias_one.shape[0]
    bucket_cap = 2 * edge_rows // groups
    owner_ids = edge_dst // tgt_rows
    local_ids = edge_dst - owner_ids * tgt_rows
    owner_hot = (owner_ids[:, None] == jnp.arange(groups, dtype=jnp.int32)[None, :]).astype(
        jnp.int32
    )
    bucket_rank = jnp.sum((jnp.cumsum(owner_hot, axis=0) - owner_hot) * owner_hot, axis=1)
    slot_pos = owner_ids * bucket_cap + bucket_rank
    send_rows = (
        jnp.zeros((groups * bucket_cap, feat_cols), jnp.bfloat16).at[slot_pos].set(edge_feats)
    )
    send_rows = send_rows.reshape(groups, bucket_cap, feat_cols)
    slot_local = jnp.full((groups * bucket_cap,), tgt_rows, jnp.int32).at[slot_pos].set(local_ids)
    slot_local = slot_local.reshape(groups, bucket_cap)
    recv_rows, recv_ids = (
        lax.all_to_all(send_rows, "dp", split_axis=0, concat_axis=0, tiled=True),
        lax.all_to_all(slot_local, "dp", split_axis=0, concat_axis=0, tiled=True),
    )
    flat_ids = recv_ids.reshape(-1)
    summed = jax.ops.segment_sum(
        recv_rows.reshape(groups * bucket_cap, feat_cols).astype(jnp.float32),
        flat_ids,
        num_segments=tgt_rows + 1,
    )[:tgt_rows]
    degree = jax.ops.segment_sum(
        jnp.ones(flat_ids.shape, jnp.float32), flat_ids, num_segments=tgt_rows + 1
    )[:tgt_rows]
    neigh_mean = (summed / jnp.maximum(degree, 1.0)[:, None]).astype(jnp.bfloat16)
    first_part = jnp.dot(neigh_mean, neigh_one, preferred_element_type=jnp.float32)
    first_part = first_part + jnp.dot(self_feats, self_one, preferred_element_type=jnp.float32)
    first = lax.psum_scatter(first_part, "feat", scatter_dimension=1, tiled=True)
    hidden = jax.nn.relu(first + bias_one).astype(jnp.bfloat16)
    tile_count = tgt_rows // 128
    tile_iota = jnp.arange(tile_count, dtype=jnp.int32)
    hidden_tiles = hidden.reshape(tile_count, 128, hidden_cols)
    source_pick = (tile_index[:, 1:2] == tile_iota[None, :]).astype(jnp.bfloat16)
    sources = jnp.einsum(
        "kn,nrc->krc", source_pick, hidden_tiles, preferred_element_type=jnp.float32
    ).astype(jnp.bfloat16)
    tile_terms = jnp.einsum(
        "kij,kjc->kic", tile_values, sources, preferred_element_type=jnp.float32
    )
    output_pick = (tile_index[:, 0:1] == tile_iota[None, :]).astype(jnp.float32)
    aggregated = jnp.einsum("kn,kic->nic", output_pick, tile_terms, precision=lax.Precision.HIGHEST)
    aggregated = aggregated.reshape(tgt_rows, hidden_cols).astype(jnp.bfloat16)
    second_part = jnp.dot(aggregated, neigh_two, preferred_element_type=jnp.float32)
    second_part = second_part + jnp.dot(hidden, self_two, preferred_element_type=jnp.float32)
    second = lax.psum_scatter(second_part, "feat", scatter_dimension=1, tiled=True)
    live_mask = seed_live.astype(jnp.float32)[:, None]
    second_out = ((second + bias_two) * live_mask).astype(jnp.bfloat16)
    masked_grad = cotangent * seed_live[:, None].astype(jnp.bfloat16)
    full_grad = lax.all_gather(masked_grad, "feat", axis=1, tiled=True)
    local_neigh = lax.dot_general(
        aggregated, full_grad, (((0,), (0,)), ((), ())), preferred_element_type=jnp.float32
    )
    local_self = lax.dot_general(
        hidden, full_grad, (((0,), (0,)), ((), ())), preferred_element_type=jnp.float32
    )
    grad_neigh, grad_self = lax.psum((local_neigh, local_self), "dp")
    return (second_out, grad_neigh, grad_self)


def solution(mesh):
    in_specs = (
        P("dp", "feat"),
        P("dp"),
        P("dp", "feat"),
        P("feat", None),
        P("feat", None),
        P("feat"),
        P("dp", None),
        P("dp", None, None),
        P("dp"),
        P("feat", None),
        P("feat", None),
        P("feat"),
        P("dp", "feat"),
    )
    out_specs = (P("dp", "feat"), P("feat", None), P("feat", None))
    return jax.shard_map(body, mesh=mesh, in_specs=in_specs, out_specs=out_specs, check_vma=False)
```

profile of v0, /device:TPU:1, one launch (start us, length us, event | category | flops | bytes accessed | tf_op | source)
XLA Modules:
  0.0 478.2 jit_solution(4493061894201755145)
XLA Ops:
  7.2 0.8 add_select_fusion
  8.0 9.1 %reduce-window.6 = s32[32,16,128]{2,1,0:T(8,128)S(1)} reduce-window(s32[32,16,128]{2,1,0:T(8,128)S(1)} %fusion.6, s32[]{:T(128)} %constant.18.clone.1), window={size=1x1x128 pad=0_0x0_0x127_0}, to_apply=%region_0.1 | reduce-window | flops 8323072 | bytes 524292 | tf_op jit(solution)/shard_map/reduce-window
  17.9 8.6 %scatter_custom_fusion = s32[4096]{0:T(1024)} fusion(s32[2048]{0:T(1024)S(1)} %get-tuple-element.6, s32[2048]{0:T(1024)S(1)} %get-tuple-element.5, s32[]{:T(128)} %constant.13.clone.1), kind=kCustom, calls=%fused_computation.44 | custom fusion | bytes 16388 | tf_op jit(solution)/shard_map/scatter | solution.py:39
  26.6 10.4 %all-to-all-start = ((s32[32,1,128]{2,1,0:T(1,128)}), s32[32,1,128]{2,1,0:T(1,128)S(1)}, u32[]{:S(2)}, u32[]{:S(2)}) async-start(s32[32,1,128]{2,1,0:T(1,128)} %bitcast.8), calls=%async_computation | async-start | bytes 32768 | tf_op jit(solution)/shard_map/all_to_all | solution.py:43
  37.2 6.1 %scatter_custom_fusion.1 = bf16[4096,48]{1,0:T(8,128)(2,1)S(1)} fusion(s32[2048]{0:T(1024)S(1)} %get-tuple-element.6, bf16[2048,48]{1,0:T(8,128)(2,1)S(1)} %copy.34, bf16[]{:T(256)} %constant.37.clone.1), kind=kCustom, calls=%fused_computation.9 | custom fusion | bytes 393218 | tf_op jit(solution)/shard_map/scatter | solution.py:36
  43.3 1.1 copy.35
  44.4 7.6 %all-to-all-start.1 = ((bf16[32,128,48]{1,2,0:T(8,128)(2,1)}), bf16[32,128,48]{1,2,0:T(8,128)(2,1)S(1)}, u32[]{:S(2)}, u32[]{:S(2)}) async-start(bf16[32,128,48]{1,2,0:T(8,128)(2,1)} %copy.35), calls=%async_computation.1 | async-start | bytes 786432 | tf_op jit(solution)/shard_map/all_to_all | solution.py:42
  52.1 28.8 %scatter_custom_fusion.3 = f32[513]{0:T(1024)S(1)} fusion(s32[4096]{0:T(1024)S(1)} %bitcast.66, f32[4096]{0:T(1024)S(1)} %broadcast.35, f32[]{:T(128)} %constant.12.clone.1), kind=kCustom, calls=%fused_computation.48 | custom fusion | flops 4096 | bytes 2056 | tf_op jit(solution)/shard_map/scatter-add | solution.py:51
  81.2 22.4 %scatter_custom_fusion.2 = f32[513,48]{1,0:T(8,128)S(1)} fusion(s32[4096]{0:T(1024)S(1)} %bitcast.67, f32[4096,48]{1,0:T(8,128)S(1)} %bitcast.60, f32[]{:T(128)} %constant.12.clone.1), kind=kCustom, calls=%fused_computation.20 | custom fusion | flops 196608 | bytes 98500 | tf_op jit(solution)/shard_map/scatter-add | solution.py:46
  103.7 0.6 fusion.9
  104.2 1.8 convolution_add_fusion
  106.2 0.6 copy-done.9
  106.9 0.6 broadcast_multiply_fusion
  107.7 70.4 %reduce-scatter.3.cloned.1.call-done = f32[512,64]{0,1:T(8,128)} async-done(((f32[512,1024]{0,1:T(8,128)}), f32[512,64]{0,1:T(8,128)}) %reduce-scatter.3.cloned.1.call-update) | async-done | bytes 131088 | tf_op jit(solution)/shard_map/reduce_scatter | solution.py:57
  178.1 1.0 maximum_convert_fusion
  180.3 1.8 convolution_add_fusion.1
  182.3 67.7 %all-gather.2.cloned.1.call-done = bf16[512,1024]{0,1:T(8,128)(2,1)} async-done(((bf16[512,64]{0,1:T(8,128)(2,1)}), bf16[512,1024]{0,1:T(8,128)(2,1)}) %all-gather.2.cloned.1.call-update) | async-done | bytes 1048592 | tf_op jit(solution)/shard_map/all_gather | solution.py:78
  250.0 2.4 fusion.13
  252.4 2.4 fusion.34
  254.7 67.4 %reduce-scatter.5.cloned.1.call-done = f32[512,64]{0,1:T(8,128)} async-done(((f32[512,1024]{0,1:T(8,128)}), f32[512,64]{0,1:T(8,128)}) %reduce-scatter.5.cloned.1.call-update) | async-done | bytes 131088 | tf_op jit(solution)/shard_map/reduce_scatter | solution.py:74
  322.1 1.6 multiply_convert_fusion
  323.7 144.6 %all-reduce.3.cloned.1.call-done = (f32[64,1024]{1,0:T(8,128)}, f32[64,1024]{1,0:T(8,128)}) async-done(((f32[64,1024]{1,0:T(8,128)}, f32[64,1024]{1,0:T(8,128)}), (f32[64,1024]{1,0:T(8,128)}, f32[64,1024]{1,0:T(8,128)})) %all-reduce.3.cloned.1.call-update) | async-done | bytes 524304 | tf_op jit(solution)/shard_map/psum | solution.py:85
  468.3 1.7 copy.60
  470.0 1.7 copy.61
  (53 shorter events, 3.2 us)
Async XLA Ops:
  7.2 172.7 %copy-start = (bf16[64,1024]{1,0:T(8,128)(2,1)S(1)}, bf16[64,1024]{1,0:T(8,128)(2,1)}, u32[]{:S(2)}) copy-start(bf16[64,1024]{1,0:T(8,128)(2,1)} %param.22) | copy-start | bytes 393220
  7.2 10.7 %copy-start.8 = (s32[2048]{0:T(1024)S(1)}, s32[2048]{0:T(1024)}, u32[]{:S(2)}) copy-start(s32[2048]{0:T(1024)} %param.14) | copy-start | bytes 24580
  7.2 29.7 %copy-start.1 = (bf16[2048,48]{0,1:T(8,128)(2,1)S(1)}, bf16[2048,48]{0,1:T(8,128)(2,1)}, u32[]{:S(2)}) copy-start(bf16[2048,48]{0,1:T(8,128)(2,1)} %param.13) | copy-start | bytes 589828
  26.6 17.8 %all-to-all-start = ((s32[32,1,128]{2,1,0:T(1,128)}), s32[32,1,128]{2,1,0:T(1,128)S(1)}, u32[]{:S(2)}, u32[]{:S(2)}) async-start(s32[32,1,128]{2,1,0:T(1,128)} %bitcast.8), calls=%async_computation | async-start | bytes 32768 | tf_op jit(solution)/shard_map/all_to_all | solution.py:43
  44.4 59.3 %copy-start.4 = (bf16[48,1024]{1,0:T(8,128)(2,1)S(1)}, bf16[48,1024]{1,0:T(8,128)(2,1)}, u32[]{:S(2)}) copy-start(bf16[48,1024]{1,0:T(8,128)(2,1)} %param.16) | copy-start | bytes 294916
  44.4 36.5 %all-to-all-start.1 = ((bf16[32,128,48]{1,2,0:T(8,128)(2,1)}), bf16[32,128,48]{1,2,0:T(8,128)(2,1)S(1)}, u32[]{:S(2)}, u32[]{:S(2)}) async-start(bf16[32,128,48]{1,2,0:T(8,128)(2,1)} %copy.35), calls=%async_computation.1 | async-start | bytes 786432 | tf_op jit(solution)/shard_map/all_to_all | solution.py:42
  52.0 126.1 %reduce-scatter.3.cloned.1.call-start = ((), (), s32[]{:S(2)}) async-start(), calls=%async_computation.4 | async-start | bytes 2228224 | tf_op jit(solution)/shard_map/reduce_scatter | solution.py:57
  80.9 23.4 %copy-start.5 = (bf16[48,1024]{1,0:T(8,128)(2,1)S(1)}, bf16[48,1024]{1,0:T(8,128)(2,1)}, u32[]{:S(2)}) copy-start(bf16[48,1024]{1,0:T(8,128)(2,1)} %param.17) | copy-start | bytes 294916
  80.9 23.4 %copy-start.7 = (bf16[512,48]{0,1:T(8,128)(2,1)S(1)}, bf16[512,48]{0,1:T(8,128)(2,1)}, u32[]{:S(2)}) copy-start(bf16[512,48]{0,1:T(8,128)(2,1)} %param.15) | copy-start | bytes 147460
  106.1 0.7 copy-start.9
  106.1 0.9 copy-start.6
  106.1 1.6 copy-start.10
  106.1 72.0 %copy-start.11 = (f32[64]{0:T(128)S(1)}, f32[64]{0:T(128)}, u32[]{:S(2)}) copy-start(f32[64]{0:T(128)} %param.18) | copy-start | bytes 772
  106.1 73.2 %copy-start.3 = (bf16[4,128,128]{2,1,0:T(8,128)(2,1)S(1)}, bf16[4,128,128]{2,1,0:T(8,128)(2,1)}, u32[]{:S(2)}) copy-start(bf16[4,128,128]{2,1,0:T(8,128)(2,1)} %param.20) | copy-start | bytes 393220
  106.1 74.2 %copy-start.2 = (bf16[64,1024]{1,0:T(8,128)(2,1)S(1)}, bf16[64,1024]{1,0:T(8,128)(2,1)}, u32[]{:S(2)}) copy-start(bf16[64,1024]{1,0:T(8,128)(2,1)} %param.23) | copy-start | bytes 393220
  106.1 143.8 %all-gather.2.cloned.1.call-start = ((), (), s32[]{:S(2)}) async-start(), calls=%async_computation.6 | async-start | bytes 1114112 | tf_op jit(solution)/shard_map/all_gather | solution.py:78
  107.6 214.5 %reduce-scatter.5.cloned.1.call-start = ((), (), s32[]{:S(2)}) async-start(), calls=%async_computation.5 | async-start | bytes 2228224 | tf_op jit(solution)/shard_map/reduce_scatter | solution.py:74
  182.2 139.9 %copy-start.12 = (f32[64]{0:T(128)S(1)}, f32[64]{0:T(128)}, u32[]{:S(2)}) copy-start(f32[64]{0:T(128)} %param.24) | copy-start | bytes 772
  182.2 286.1 %all-reduce.3.cloned.1.call-start = ((), (), s32[]{:S(2)}) async-start(), calls=%async_computation.7 | async-start | bytes 1048576 | tf_op jit(solution)/shard_map/psum | solution.py:85
Sparse Core Ops, SparseCore 0:
  106.2 71.7 reduce-scatter.2
  180.7 69.2 all-gather.1
  252.8 69.2 reduce-scatter.4
  325.8 142.5 all-reduce.2
where the time goes:
time: 479 us; the launch traced here: 478 us
  waiting for transfers between devices  350 us (73%)
  other arithmetic  64.7 us (14%)
  local copies, waits for them, and re-layouts  20.9 us (4%)
  starting transfers between devices  18.2 us (4%)
  between operations  14.1 us (3%)
  matrix products  10.2 us (2%)
    psum x1, waiting for transfers between devices, body(): grad_neigh, grad_self = lax.psum((local_neigh, local_self), 'dp')  145 us
    reduce_scatter x1, waiting for transfers between devices, body(): lax.psum_scatter(first_part, 'feat', scatter_dimension=1, tiled=True)  70.4 us
    all_gather x1, waiting for transfers between devices, body(): full_grad = lax.all_gather(masked_grad, 'feat', axis=1, tiled=True)  67.7 us
    reduce_scatter x1, waiting for transfers between devices, body(): lax.psum_scatter(second_part, 'feat', scatter_dimension=1, tiled=True)  67.4 us
    scatter-add x1, other arithmetic, body(): jax.ops.segment_sum(jnp.ones(flat_ids.shape, jnp.float32), flat_ids, num_...  28.8 us
    scatter-add x1, other arithmetic, body(): jax.ops.segment_sum(recv_rows.reshape(groups * bucket_cap, feat_cols).ast...  22.4 us
    all_to_all x1, starting transfers between devices, body(): lax.all_to_all(slot_local, 'dp', split_axis=0, concat_axis=0, tiled=True)  10.4 us
  transfers between devices with their start and end apart: 6, of which 4 were waited for; matrix products, arithmetic and copies ran while one was open for 10% of the time, Pallas kernels for 0%

commit v1 on v0

v1 whole, which is shorter than its diff:
```python
import functools

import jax
import jax.numpy as jnp
from jax import lax
from jax.experimental import pallas as pl
from jax.experimental.pallas import tpu as pltpu
from jax.sharding import PartitionSpec as P

BF = jnp.bfloat16
F32 = jnp.float32
NT = (((1,), (1,)), ((), ()))
TN = (((0,), (0,)), ((), ()))
ROWS = 64
GROUP = 4
VMEM_LIMIT = 48 * 1024 * 1024


def call(kernel, out_shape, n_in, scratch=(), smem=(), flops=0, nbytes=0):
    in_specs = [
        pl.BlockSpec(memory_space=pltpu.SMEM if i in smem else pltpu.VMEM) for i in range(n_in)
    ]
    out_specs = jax.tree.map(lambda _: pl.BlockSpec(memory_space=pltpu.VMEM), out_shape)
    return pl.pallas_call(
        kernel,
        out_shape=out_shape,
        in_specs=in_specs,
        out_specs=out_specs,
        scratch_shapes=list(scratch),
        compiler_params=pltpu.CompilerParams(vmem_limit_bytes=VMEM_LIMIT),
        cost_estimate=pl.CostEstimate(flops=flops, bytes_accessed=nbytes, transcendentals=0),
    )


def pack_kernel(groups, tgt_rows, feats_ref, dst_ref, send_ref, masked):
    cols, edges = feats_ref.shape
    cap = send_ref.shape[2]
    dst = jnp.concatenate([dst_ref[i : i + 1, :] for i in range(dst_ref.shape[0])], axis=1)
    owner = dst // tgt_rows
    local = dst - owner * tgt_rows
    half = tgt_rows // 2
    code = jnp.where(local < half, local - half, local - (half - 1)).astype(F32)
    owner_hot = lax.broadcasted_iota(jnp.int32, (groups, edges), 0) == owner
    owner_hot = owner_hot.astype(F32)
    step = 256
    before = (
        lax.broadcasted_iota(jnp.int32, (step, step), 0)
        < lax.broadcasted_iota(jnp.int32, (step, step), 1)
    ).astype(BF)
    seen = jnp.zeros((groups, 1), F32)
    ranks = []
    for i in range(edges // step):
        part = owner_hot[:, i * step : (i + 1) * step]
        prior = jnp.dot(part.astype(BF), before, preferred_element_type=F32) + seen
        ranks.append(jnp.sum(prior * part, axis=0, keepdims=True))
        seen = seen + jnp.sum(part, axis=1, keepdims=True)
    rank = jnp.concatenate(ranks, axis=1).astype(jnp.int32)
    rank_hot = (lax.broadcasted_iota(jnp.int32, (cap, edges), 0) == rank).astype(F32).astype(BF)
    extra_row = lax.broadcasted_iota(jnp.int32, (ROWS - cols, edges), 0)
    extra = jnp.where(extra_row == 0, code, jnp.where(extra_row == 1, 1.0, 0.0)).astype(BF)
    hot = owner_hot.astype(BF)
    some = masked.shape[0] // ROWS
    for g in range(groups // some):
        for j in range(some):
            o = g * some + j
            live = hot[o : o + 1, :]
            masked[j * ROWS : j * ROWS + cols, :] = feats_ref[...] * live
            masked[j * ROWS + cols : (j + 1) * ROWS, :] = extra * live
        out = lax.dot_general(masked[...], rank_hot, NT, preferred_element_type=F32).astype(BF)
        for j in range(some):
            send_ref[g * some + j] = out[j * ROWS : (j + 1) * ROWS, :]


def mean_kernel(recv_ref, self_ref, out_ref):
    groups, rows, cap = recv_ref.shape
    cols, targets = self_ref.shape
    tiles = out_ref.shape[0]
    half = targets // 2
    vertex = lax.broadcasted_iota(jnp.int32, (targets, 1), 0)
    vertex = jnp.where(vertex < half, vertex - half, vertex - (half - 1)).astype(F32)
    acc = jnp.zeros((rows, targets), F32)
    some = 8
    for g in range(groups // some):
        part = jnp.concatenate([recv_ref[g * some + j] for j in range(some)], axis=1)
        code = part[cols : cols + 1, :].astype(F32)
        hot = (vertex == code).astype(F32).astype(BF)
        acc = acc + lax.dot_general(part, hot, NT, preferred_element_type=F32)
    degree = jnp.maximum(acc[cols + 1 : cols + 2, :], 1.0)
    mean = (acc[:cols, :] / degree).astype(BF)
    width = targets // tiles
    for t in range(tiles):
        out_ref[t, :cols, :] = mean[:, t * width : (t + 1) * width]
        out_ref[t, cols:, :] = self_ref[:, t * width : (t + 1) * width]


def hidden_kernel(parts_ref, bias_ref, index_ref, values_ref, live_ref, out_ref, left_ref, acc):
    n, cols, width = parts_ref.shape
    tiles = out_ref.shape[0]
    bias = bias_ref[...]
    for t in range(tiles):
        total = parts_ref[t].astype(F32)
        for k in range(1, n // tiles):
            total = total + parts_ref[k * tiles + t].astype(F32)
        out_ref[t, cols:, :] = jnp.maximum(total + bias, 0.0).astype(BF)
    acc[...] = jnp.zeros_like(acc)
    for k in range(values_ref.shape[0]):
        source = out_ref[index_ref[k, 1], cols:, :]
        target = index_ref[k, 0]
        acc[target] += lax.dot_general(source, values_ref[k], NT, preferred_element_type=F32)
    for t in range(tiles):
        out_ref[t, :cols, :] = acc[t].astype(BF)
        live = live_ref[t : t + 1, :].astype(BF)
        left_ref[:, t * width : (t + 1) * width] = out_ref[t] * live


def grad_kernel(left_ref, cot_ref, out_ref):
    pieces, piece_rows, piece_cols = out_ref.shape
    quarters = left_ref.shape[0] // piece_rows
    for c in range(pieces // quarters):
        cot = cot_ref[c * piece_cols : (c + 1) * piece_cols, :]
        block = lax.dot_general(left_ref[...], cot, NT, preferred_element_type=F32).astype(BF)
        for q in range(quarters):
            out_ref[c * quarters + q] = block[q * piece_rows : (q + 1) * piece_rows, :]


def body(
    edge_feats,
    edge_dst,
    self_feats,
    neigh_one,
    self_one,
    bias_one,
    tile_index,
    tile_values,
    seed_live,
    neigh_two,
    self_two,
    bias_two,
    cotangent,
):
    groups = lax.axis_size("dp")
    n_feat = lax.axis_size("feat")
    edges, cols = edge_feats.shape
    targets = self_feats.shape[0]
    hid = bias_one.shape[0]
    full = neigh_one.shape[1]
    cap = 2 * edges // groups
    tiles = targets // 128
    near = [[GROUP * i + j for j in range(GROUP)] for i in range(n_feat // GROUP)]

    with jax.named_scope("weights"):
        first_w = lax.all_gather(
            jnp.concatenate([neigh_one, self_one], axis=0),
            "feat", axis=0, tiled=True, axis_index_groups=near,
        )
        second_w = lax.all_gather(
            jnp.concatenate([neigh_two, self_two], axis=0),
            "feat", axis=0, tiled=True, axis_index_groups=near,
        )
    with jax.named_scope("cotangent"):
        full_cot = lax.all_gather(cotangent.T, "feat", axis=0, tiled=True)

    with jax.named_scope("edges"):
        send = call(
            functools.partial(pack_kernel, groups, targets),
            jax.ShapeDtypeStruct((groups, ROWS, cap), BF),
            2,
            scratch=[pltpu.VMEM((8 * ROWS, edges), BF)],
            flops=2 * groups * ROWS * edges * cap,
            nbytes=8 << 20,
        )(edge_feats.T, edge_dst.reshape(-1, 128))
        recv = lax.all_to_all(send, "dp", split_axis=0, concat_axis=0, tiled=True)
        acts = call(
            mean_kernel,
            jax.ShapeDtypeStruct((tiles, 2 * cols, 128), BF),
            2,
            flops=2 * groups * ROWS * cap * targets,
            nbytes=8 << 20,
        )(recv, self_feats.T)

    with jax.named_scope("first"):
        acts = lax.all_to_all(
            acts, "feat", split_axis=0, concat_axis=0, tiled=True, axis_index_groups=near
        )
        first = lax.dot_general(
            first_w, acts.reshape(-1, 128), TN, preferred_element_type=F32
        ).astype(BF)
        first = lax.all_to_all(
            first.reshape(n_feat, hid, 128), "feat", split_axis=0, concat_axis=0, tiled=True
        )
        pair, left = call(
            hidden_kernel,
            (
                jax.ShapeDtypeStruct((tiles, 2 * hid, 128), BF),
                jax.ShapeDtypeStruct((2 * hid, targets), BF),
            ),
            5,
            scratch=[pltpu.VMEM((tiles, hid, 128), F32)],
            smem=(2,),
            flops=2 * 4 * hid * 128 * 128,
            nbytes=4 << 20,
        )(
            first,
            bias_one.reshape(hid, 1),
            tile_index,
            tile_values,
            seed_live.reshape(tiles, 128).astype(F32),
        )

    with jax.named_scope("grads"):
        piece_rows = 2 * hid * full // 128 // groups
        terms = call(
            grad_kernel,
            jax.ShapeDtypeStruct((groups, piece_rows, 128), BF),
            2,
            flops=2 * 2 * hid * targets * full,
            nbytes=2 << 20,
        )(left, full_cot)
        terms = lax.all_to_all(terms, "dp", split_axis=0, concat_axis=0, tiled=True)
        mine = jnp.sum(terms.astype(F32), axis=0, keepdims=True)
        grads = lax.all_gather(mine, "dp", axis=0, tiled=True)
        grads = grads.reshape(full // 128, 2 * hid // piece_rows, piece_rows, 128)
        grads = grads.transpose(1, 2, 0, 3).reshape(2, hid, full)

    with jax.named_scope("second"):
        pair = lax.all_to_all(
            pair, "feat", split_axis=0, concat_axis=0, tiled=True, axis_index_groups=near
        )
        second = lax.dot_general(
            second_w, pair.reshape(-1, 128), TN, preferred_element_type=F32
        ).astype(BF)
        second = lax.all_to_all(
            second.reshape(n_feat, hid, 128), "feat", split_axis=0, concat_axis=0, tiled=True
        )
        second = jnp.sum(second.reshape(n_feat // tiles, tiles, hid, 128).astype(F32), axis=0)
        second = second + bias_two[None, :, None]
        second = second * seed_live.reshape(tiles, 1, 128).astype(F32)
        second_out = second.astype(BF).transpose(0, 2, 1).reshape(targets, hid)
    return (second_out, grads[0], grads[1])


def solution(mesh):
    in_specs = (
        P("dp", "feat"),
        P("dp"),
        P("dp", "feat"),
        P("feat", None),
        P("feat", None),
        P("feat"),
        P("dp", None),
        P("dp", None, None),
        P("dp"),
        P("feat", None),
        P("feat", None),
        P("feat"),
        P("dp", "feat"),
    )
    out_specs = (P("dp", "feat"), P("feat", None), P("feat", None))
    return jax.shard_map(body, mesh=mesh, in_specs=in_specs, out_specs=out_specs, check_vma=False)
```

time: 479 us -> 178 us (0.37)
  waiting for transfers between devices: 350 us -> 42.4 us
  other arithmetic: 64.7 us -> 1.53 us
  blocking collectives: 0 us -> 46.3 us
  starting transfers between devices: 18.2 us -> 54.7 us
  local copies, waits for them, and re-layouts: 20.9 us -> 6.95 us
  Pallas kernels: 0 us -> 8.01 us
  matrix products: 10.2 us -> 3.54 us
    psum x1 -> x0, waiting for transfers between devices: 145 us -> none  [body(): grad_neigh, grad_self = lax.psum((local_neigh, local_self), 'dp')]
    reduce_scatter x2 -> x0, waiting for transfers between devices: 138 us -> none  [the longest x1 70.4 us: body(): lax.psum_scatter(first_part, 'feat', scatter_dimension=1, tiled=True)]
    scatter-add x2 -> x0, other arithmetic: 51.2 us -> none  [the longest x1 28.8 us: body(): jax.ops.segment_sum(jnp.ones(flat_ids.shape, jnp.float32), flat_ids, num_...]
    all_gather x1 -> x2, waiting for transfers between devices: 67.7 us -> 18.3 us  [the longest x1 18.3 us: body(): lax.all_gather(jnp.concatenate([neigh_two, self_two], axis=0), 'feat', ax...]
    all_gather x0 -> x2, blocking collectives: none -> 46.3 us  [the longest x1 25.3 us: body(): grads = lax.all_gather(mine, 'dp', axis=0, tiled=True)]
    all_to_all x2 -> x6, starting transfers between devices: 18 us -> 54.6 us  [the longest x1 13.2 us: body(): lax.all_to_all(first.reshape(n_feat, hid, 128), 'feat', split_axis=0, con...]
    all_to_all x2 -> x6, waiting for transfers between devices: 0.01 us -> 23.4 us  [the longest x1 11 us: body(): lax.all_to_all(first.reshape(n_feat, hid, 128), 'feat', split_axis=0, con...]
    scatter x2 -> x0, local copies, waits for them, and re-layouts: 14.7 us -> none  [the longest x1 8.62 us: body(): jnp.full((groups * bucket_cap,), tgt_rows, jnp.int32).at[slot_pos]]
  transfers between devices with their start and end apart: 6 -> 8, of which waited for: 4 -> 4; matrix products, arithmetic and copies ran while one was open for 10% -> 3% of each run, Pallas kernels for 0% -> 5%
where the time goes in v1:
time: 178 us
  starting transfers between devices  54.7 us (31%)
  blocking collectives  46.3 us (26%)
  waiting for transfers between devices  42.4 us (24%)
  between operations  14.2 us (8%)
  Pallas kernels  8.01 us (4%)
  local copies, waits for them, and re-layouts  6.95 us (4%)
  matrix products  3.54 us (2%)
    all_gather x1, blocking collectives, body(): grads = lax.all_gather(mine, 'dp', axis=0, tiled=True)  25.3 us
    all_gather x1, blocking collectives, body(): lax.all_gather(jnp.concatenate([neigh_one, self_one], axis=0), 'feat', ax...  20.9 us
    all_gather x1, waiting for transfers between devices, body(): lax.all_gather(jnp.concatenate([neigh_two, self_two], axis=0), 'feat', ax...  18.3 us
    all_to_all x1, starting transfers between devices, body(): lax.all_to_all(first.reshape(n_feat, hid, 128), 'feat', split_axis=0, con...  13.2 us
    all_to_all x1, waiting for transfers between devices, body(): lax.all_to_all(first.reshape(n_feat, hid, 128), 'feat', split_axis=0, con...  11 us
    all_to_all x1, starting transfers between devices, body(): recv = lax.all_to_all(send, 'dp', split_axis=0, concat_axis=0, tiled=True)  10.6 us
    all_to_all x1, starting transfers between devices, body(): lax.all_to_all(second.reshape(n_feat, hid, 128), 'feat', split_axis=0, co...  10.2 us
    all_to_all x1, waiting for transfers between devices, body(): recv = lax.all_to_all(send, 'dp', split_axis=0, concat_axis=0, tiled=True)  9.91 us
  transfers between devices with their start and end apart: 8, of which 4 were waited for; matrix products, arithmetic and copies ran while one was open for 3% of the time, Pallas kernels for 5%

profile of v1, /device:TPU:1, one launch (start us, length us, event | category | flops | bytes accessed | tf_op | source)
XLA Modules:
  0.0 177.5 jit_solution(2979074699919098705)
XLA Ops:
  7.9 0.9 copy-done.2
  8.8 3.3 %edges.2 = bf16[32,64,128]{2,1,0:T(8,128)(2,1)} custom-call(bf16[48,2048]{1,0:T(8,128)(2,1)S(1)} %bitcast.34, s32[16,128]{1,0:T(8,128)S(1)} %bitcast.36), custom_call_target="tpu_custom_call" | custom-call | flops 1073741824 | bytes 8388608 | tf_op jit(solution)/shard_map/edges/pallas_call | solution.py:164
  12.2 10.6 %all-to-all-start = ((bf16[32,64,128]{2,1,0:T(8,128)(2,1)}), bf16[32,64,128]{2,1,0:T(8,128)(2,1)S(1)}, u32[]{:S(2)}, u32[]{:S(2)}) async-start(bf16[32,64,128]{2,1,0:T(8,128)(2,1)} %edges.2), calls=%async_computation | async-start | bytes 1048576 | tf_op jit(solution)/shard_map/edges/all_to_all | solution.py:172
  22.8 0.7 pad_maximum_fusion
  23.6 0.9 copy-done.7
  24.5 9.9 %all-to-all-done.recv_ref = bf16[32,64,128]{2,1,0:T(8,128)(2,1)S(1)} async-done(((bf16[32,64,128]{2,1,0:T(8,128)(2,1)}), bf16[32,64,128]{2,1,0:T(8,128)(2,1)S(1)}, u32[]{:S(2)}, u32[]{:S(2)}) %all-to-all-start) | async-done | bytes 524320 | tf_op jit(solution)/shard_map/edges/all_to_all | solution.py:172
  34.4 2.0 %edges.3 = bf16[4,96,128]{2,1,0:T(8,128)(2,1)} custom-call(bf16[32,64,128]{2,1,0:T(8,128)(2,1)S(1)} %all-to-all-done.recv_ref, bf16[48,512]{1,0:T(8,128)(2,1)S(1)} %bitcast.35), custom_call_target="tpu_custom_call" | custom-call | flops 268435456 | bytes 8388608 | tf_op jit(solution)/shard_map/edges/pallas_call | solution.py:173
  36.4 3.7 %all-to-all-start.1 = ((bf16[4,96,128]{2,1,0:T(8,128)(2,1)}), bf16[4,96,128]{2,1,0:T(8,128)(2,1)S(1)}, u32[]{:S(2)}, u32[]{:S(2)}) async-start(bf16[4,96,128]{2,1,0:T(8,128)(2,1)} %edges.3), calls=%async_computation.1 | async-start | bytes 196608 | tf_op jit(solution)/shard_map/first/all_to_all | solution.py:182
  40.1 20.9 %all_gather.13 = bf16[384,1024]{1,0:T(8,128)(2,1)S(1)} all-gather(bf16[96,1024]{1,0:T(8,128)(2,1)S(1)} %pad_maximum_fusion.1), channel_id=1, replica_groups={{0,1,2,3},{4,5,6,7},{8,9,10,11},{12,13,14,15},{16,17,18,19},{20,21,22,2..., dimensions={0}, use_global_device_ids=true | all-gather | bytes 983040 | tf_op jit(solution)/shard_map/weights/all_gather | solution.py:152
  61.0 1.1 convolution_convert_fusion.1
  62.1 13.2 %all-to-all-start.2 = ((bf16[16,64,128]{2,1,0:T(8,128)(2,1)}), bf16[16,64,128]{2,1,0:T(8,128)(2,1)S(1)}, u32[]{:S(2)}, u32[]{:S(2)}) async-start(bf16[16,64,128]{2,1,0:T(8,128)(2,1)} %bitcast.4), calls=%async_computation.2 | async-start | bytes 524288 | tf_op jit(solution)/shard_map/first/all_to_all | solution.py:188
  77.4 11.0 %all-to-all-done.2.parts_ref = bf16[16,64,128]{2,1,0:T(8,128)(2,1)S(1)} async-done(((bf16[16,64,128]{2,1,0:T(8,128)(2,1)}), bf16[16,64,128]{2,1,0:T(8,128)(2,1)S(1)}, u32[]{:S(2)}, u32[]{:S(2)}) %all-to-all-start.2) | async-done | bytes 262176 | tf_op jit(solution)/shard_map/first/all_to_all | solution.py:188
  88.4 1.5 first.1
  89.9 8.3 %all-to-all-start.3 = ((bf16[4,128,128]{2,1,0:T(8,128)(2,1)}), bf16[4,128,128]{2,1,0:T(8,128)(2,1)S(1)}, u32[]{:S(2)}, u32[]{:S(2)}) async-start(bf16[4,128,128]{2,1,0:T(8,128)(2,1)} %get-tuple-element.5), calls=%async_computation.3 | async-start | bytes 262144 | tf_op jit(solution)/shard_map/second/all_to_all | solution.py:226
  98.2 1.2 copy-done
  99.5 1.1 grads.1
  100.6 2.4 %all-to-all-done.3 = bf16[4,128,128]{2,1,0:T(8,128)(2,1)S(1)} async-done(((bf16[4,128,128]{2,1,0:T(8,128)(2,1)}), bf16[4,128,128]{2,1,0:T(8,128)(2,1)S(1)}, u32[]{:S(2)}, u32[]{:S(2)}) %all-to-all-start.3) | async-done | bytes 131104 | tf_op jit(solution)/shard_map/second/all_to_all | solution.py:226
  103.0 8.7 %all-to-all-start.5 = ((bf16[32,32,128]{2,1,0:T(8,128)(2,1)}), bf16[32,32,128]{2,1,0:T(8,128)(2,1)S(1)}, u32[]{:S(2)}, u32[]{:S(2)}) async-start(bf16[32,32,128]{2,1,0:T(8,128)(2,1)} %grads.1), calls=%async_computation.5 | async-start | bytes 524288 | tf_op jit(solution)/shard_map/grads/all_to_all | solution.py:219
  111.7 18.3 %all-gather.4.cloned.1.call-done = bf16[512,1024]{1,0:T(8,128)(2,1)} async-done(((bf16[128,1024]{1,0:T(8,128)(2,1)}), bf16[512,1024]{1,0:T(8,128)(2,1)}) %all-gather.4.cloned.1.call-update) | async-done | bytes 1048592 | tf_op jit(solution)/shard_map/weights/all_gather | solution.py:156
  130.0 2.4 %convolution_convert_fusion = bf16[1024,128]{1,0:T(8,128)(2,1)} fusion(bf16[512,1024]{1,0:T(8,128)(2,1)} %all-gather.4.cloned.1.call-done, bf16[512,128]{1,0:T(8,128)(2,1)S(1)} %bitcast.41), kind=kOutput, calls=%fused_computation | convolution fusion | flops 134348800 | bytes 1441792 | tf_op jit(solution)/shard_map/second/dot_general | solution.py:229
  132.5 10.2 %all-to-all-start.4 = ((bf16[16,64,128]{2,1,0:T(8,128)(2,1)}), bf16[16,64,128]{2,1,0:T(8,128)(2,1)S(1)}, u32[]{:S(2)}, u32[]{:S(2)}) async-start(bf16[16,64,128]{2,1,0:T(8,128)(2,1)} %bitcast.8), calls=%async_computation.4 | async-start | bytes 524288 | tf_op jit(solution)/shard_map/second/all_to_all | solution.py:232
  142.7 25.3 %all-gather = f32[1024,128]{1,0:T(8,128)S(1)} all-gather(f32[32,128]{1,0:T(8,128)S(1)} %convert_reduce_fusion.1), channel_id=2, replica_groups=mesh['dp'=32,'feat'=16] {'dp'}, dimensions={0}, use_global_device_ids=true | all-gather | bytes 540672 | tf_op jit(solution)/shard_map/grads/all_gather | solution.py:221
  168.4 0.9 copy_bitcast_fusion
  170.0 0.7 copy_bitcast_fusion.2
  (40 shorter events, 3.9 us)
Async XLA Ops:
  7.2 91.1 %all-gather.6.cloned.1.call-start = ((), (), s32[]{:S(2)}) async-start(), calls=%async_computation.7 | async-start | bytes 1114112 | tf_op jit(solution)/shard_map/cotangent/all_gather | solution.py:161
  7.2 0.7 copy-start.4
  7.9 0.9 copy-start.2
  12.2 10.6 %copy-start.5 = (bf16[64,1024]{1,0:T(8,128)(2,1)S(1)}, bf16[64,1024]{1,0:T(8,128)(2,1)}, u32[]{:S(2)}) copy-start(bf16[64,1024]{1,0:T(8,128)(2,1)} %param.23) | copy-start | bytes 393220
  12.2 10.6 %copy-start.6 = (bf16[64,1024]{1,0:T(8,128)(2,1)S(1)}, bf16[64,1024]{1,0:T(8,128)(2,1)}, u32[]{:S(2)}) copy-start(bf16[64,1024]{1,0:T(8,128)(2,1)} %param.22) | copy-start | bytes 393220
  12.2 22.2 %all-to-all-start = ((bf16[32,64,128]{2,1,0:T(8,128)(2,1)}), bf16[32,64,128]{2,1,0:T(8,128)(2,1)S(1)}, u32[]{:S(2)}, u32[]{:S(2)}) async-start(bf16[32,64,128]{2,1,0:T(8,128)(2,1)} %edges.2), calls=%async_computation | async-start | bytes 1048576 | tf_op jit(solution)/shard_map/edges/all_to_all | solution.py:172
  22.7 107.3 %all-gather.4.cloned.1.call-start = ((), (), s32[]{:S(2)}) async-start(), calls=%async_computation.6 | async-start | bytes 1310720 | tf_op jit(solution)/shard_map/weights/all_gather | solution.py:156
  23.5 0.9 copy-start.7
  23.5 0.9 copy-start.8
  24.5 9.9 %copy-start.3 = (bf16[512,48]{0,1:T(8,128)(2,1)S(1)}, bf16[512,48]{0,1:T(8,128)(2,1)}, u32[]{:S(2)}) copy-start(bf16[512,48]{0,1:T(8,128)(2,1)} %param.15) | copy-start | bytes 147460
  36.4 24.6 %all-to-all-start.1 = ((bf16[4,96,128]{2,1,0:T(8,128)(2,1)}), bf16[4,96,128]{2,1,0:T(8,128)(2,1)S(1)}, u32[]{:S(2)}, u32[]{:S(2)}) async-start(bf16[4,96,128]{2,1,0:T(8,128)(2,1)} %edges.3), calls=%async_computation.1 | async-start | bytes 196608 | tf_op jit(solution)/shard_map/first/all_to_all | solution.py:182
  62.1 26.3 %copy-start.1 = (bf16[4,128,128]{2,1,0:T(8,128)(2,1)S(1)}, bf16[4,128,128]{2,1,0:T(8,128)(2,1)}, u32[]{:S(2)}) copy-start(bf16[4,128,128]{2,1,0:T(8,128)(2,1)} %values_ref.1) | copy-start | bytes 393220
  62.1 26.3 %all-to-all-start.2 = ((bf16[16,64,128]{2,1,0:T(8,128)(2,1)}), bf16[16,64,128]{2,1,0:T(8,128)(2,1)S(1)}, u32[]{:S(2)}, u32[]{:S(2)}) async-start(bf16[16,64,128]{2,1,0:T(8,128)(2,1)} %bitcast.4), calls=%async_computation.2 | async-start | bytes 524288 | tf_op jit(solution)/shard_map/first/all_to_all | solution.py:188
  75.3 0.7 copy-start.11
  76.0 0.7 copy-start.10
  76.7 0.7 copy-start.9
  89.9 13.1 %all-to-all-start.3 = ((bf16[4,128,128]{2,1,0:T(8,128)(2,1)}), bf16[4,128,128]{2,1,0:T(8,128)(2,1)S(1)}, u32[]{:S(2)}, u32[]{:S(2)}) async-start(bf16[4,128,128]{2,1,0:T(8,128)(2,1)} %get-tuple-element.5), calls=%async_computation.3 | async-start | bytes 262144 | tf_op jit(solution)/shard_map/second/all_to_all | solution.py:226
  98.2 1.2 copy-start
  103.0 29.5 %all-to-all-start.5 = ((bf16[32,32,128]{2,1,0:T(8,128)(2,1)}), bf16[32,32,128]{2,1,0:T(8,128)(2,1)S(1)}, u32[]{:S(2)}, u32[]{:S(2)}) async-start(bf16[32,32,128]{2,1,0:T(8,128)(2,1)} %grads.1), calls=%async_computation.5 | async-start | bytes 524288 | tf_op jit(solution)/shard_map/grads/all_to_all | solution.py:219
  132.5 36.8 %all-to-all-start.4 = ((bf16[16,64,128]{2,1,0:T(8,128)(2,1)}), bf16[16,64,128]{2,1,0:T(8,128)(2,1)S(1)}, u32[]{:S(2)}, u32[]{:S(2)}) async-start(bf16[16,64,128]{2,1,0:T(8,128)(2,1)} %bitcast.8), calls=%async_computation.4 | async-start | bytes 524288 | tf_op jit(solution)/shard_map/second/all_to_all | solution.py:232
  169.3 0.7 copy-start.12
Sparse Core Ops, SparseCore 0:
  10.1 69.3 all-gather.5
  82.1 47.8 all-gather.3

commit v2 on v1

--- a/solution.py
+++ b/solution.py
@@ -93,34 +93,74 @@
         out_ref[t, cols:, :] = self_ref[:, t * width : (t + 1) * width]
 
 
-def hidden_kernel(parts_ref, bias_ref, index_ref, values_ref, live_ref, out_ref, left_ref, acc):
+def hidden_kernel(parts_ref, bias_ref, out_ref):
     n, cols, width = parts_ref.shape
-    tiles = out_ref.shape[0]
+    copies, tiles = out_ref.shape[:2]
     bias = bias_ref[...]
     for t in range(tiles):
         total = parts_ref[t].astype(F32)
         for k in range(1, n // tiles):
             total = total + parts_ref[k * tiles + t].astype(F32)
-        out_ref[t, cols:, :] = jnp.maximum(total + bias, 0.0).astype(BF)
+        hidden = jnp.maximum(total + bias, 0.0).astype(BF)
+        for c in range(copies):
+            out_ref[c, t] = hidden
+
+
+def aggregate_kernel(mine_ref, hid_ref, index_ref, values_ref, live_ref, own_ref, left_ref, hidden, acc):
+    group, tiles, cols, width = hid_ref.shape
+    wide = group * cols
+    for t in range(tiles):
+        for j in range(group):
+            hidden[t, j * cols : (j + 1) * cols, :] = hid_ref[j, t]
     acc[...] = jnp.zeros_like(acc)
     for k in range(values_ref.shape[0]):
-        source = out_ref[index_ref[k, 1], cols:, :]
+        source = hidden[index_ref[k, 1]]
         target = index_ref[k, 0]
         acc[target] += lax.dot_general(source, values_ref[k], NT, preferred_element_type=F32)
     for t in range(tiles):
-        out_ref[t, :cols, :] = acc[t].astype(BF)
         live = live_ref[t : t + 1, :].astype(BF)
-        left_ref[:, t * width : (t + 1) * width] = out_ref[t] * live
+        at = slice(t * width, (t + 1) * width)
+        left_ref[:wide, at] = acc[t].astype(BF) * live
+        left_ref[wide:, at] = hidden[t] * live
+    mine = mine_ref[0]
+    agg = acc[mine].astype(BF)
+    hid = hidden[mine]
+    for j in range(group):
+        own_ref[j, :cols, :] = agg[j * cols : (j + 1) * cols, :]
+        own_ref[j, cols:, :] = hid[j * cols : (j + 1) * cols, :]
 
 
 def grad_kernel(left_ref, cot_ref, out_ref):
-    pieces, piece_rows, piece_cols = out_ref.shape
-    quarters = left_ref.shape[0] // piece_rows
-    for c in range(pieces // quarters):
-        cot = cot_ref[c * piece_cols : (c + 1) * piece_cols, :]
-        block = lax.dot_general(left_ref[...], cot, NT, preferred_element_type=F32).astype(BF)
-        for q in range(quarters):
-            out_ref[c * quarters + q] = block[q * piece_rows : (q + 1) * piece_rows, :]
+    group = 4
+    rows, width = left_ref.shape[0], 128
+    block = lax.dot_general(left_ref[...], cot_ref[...], NT, preferred_element_type=F32)
+    wide = rows // 2
+    cols = wide // group
+    at = 0
+    for w in range(2):
+        for r in range(0, cols, 8):
+            for c in range(0, cot_ref.shape[0], width):
+                rows_of = [
+                    block[w * wide + j * cols + r : w * wide + j * cols + r + 8, c : c + width]
+                    for j in range(group)
+                ]
+                out_ref[at] = jnp.concatenate(rows_of, axis=0).astype(BF)
+                at += 1
+
+
+def place_kernel(pieces_ref, neigh_ref, self_ref):
+    half = 64
+    at = 0
+    for out_ref in (neigh_ref, self_ref):
+        for r in range(0, out_ref.shape[0], 8):
+            for c in range(2):
+                parts = [pieces_ref[at, h] for h in range(4)]
+                for e in range(2):
+                    for p in range(2):
+                        pair = [parts[2 * p + i][:, e * half : (e + 1) * half] for i in range(2)]
+                        to = (8 * c + 4 * e + 2 * p) * half
+                        out_ref[r : r + 8, to : to + 2 * half] = jnp.concatenate(pair, axis=1)
+                at += 1
 
 
 def body(
@@ -146,19 +186,23 @@
     full = neigh_one.shape[1]
     cap = 2 * edges // groups
     tiles = targets // 128
-    near = [[GROUP * i + j for j in range(GROUP)] for i in range(n_feat // GROUP)]
+    blocks = n_feat // GROUP
+    near = [[GROUP * i + j for j in range(GROUP)] for i in range(blocks)]
+    far = [[i + GROUP * j for j in range(blocks)] for i in range(GROUP)]
+
+    def swap(x, axis, among=None):
+        return lax.all_to_all(
+            x, axis, split_axis=0, concat_axis=0, tiled=True, axis_index_groups=among
+        )
+
+    def spread(x, n, axis, among=None):
+        return swap(jnp.broadcast_to(x[None], (n,) + x.shape), axis, among)
 
     with jax.named_scope("weights"):
-        first_w = lax.all_gather(
-            jnp.concatenate([neigh_one, self_one], axis=0),
-            "feat", axis=0, tiled=True, axis_index_groups=near,
-        )
-        second_w = lax.all_gather(
-            jnp.concatenate([neigh_two, self_two], axis=0),
-            "feat", axis=0, tiled=True, axis_index_groups=near,
-        )
+        first_w = spread(jnp.concatenate([neigh_one, self_one], axis=0), GROUP, "feat", near)
+        second_w = spread(jnp.concatenate([neigh_two, self_two], axis=0), GROUP, "feat", near)
     with jax.named_scope("cotangent"):
-        full_cot = lax.all_gather(cotangent.T, "feat", axis=0, tiled=True)
+        cot = spread(cotangent.T, blocks, "feat", far).reshape(blocks * hid, targets)
 
     with jax.named_scope("edges"):
         send = call(
@@ -169,7 +213,7 @@
             flops=2 * groups * ROWS * edges * cap,
             nbytes=8 << 20,
         )(edge_feats.T, edge_dst.reshape(-1, 128))
-        recv = lax.all_to_all(send, "dp", split_axis=0, concat_axis=0, tiled=True)
+        recv = swap(send, "dp")
         acts = call(
             mean_kernel,
             jax.ShapeDtypeStruct((tiles, 2 * cols, 128), BF),
@@ -179,64 +223,64 @@
         )(recv, self_feats.T)
 
     with jax.named_scope("first"):
-        acts = lax.all_to_all(
-            acts, "feat", split_axis=0, concat_axis=0, tiled=True, axis_index_groups=near
-        )
+        acts = swap(acts, "feat", near)
         first = lax.dot_general(
-            first_w, acts.reshape(-1, 128), TN, preferred_element_type=F32
+            first_w.reshape(-1, full), acts.reshape(-1, 128), TN, preferred_element_type=F32
         ).astype(BF)
-        first = lax.all_to_all(
-            first.reshape(n_feat, hid, 128), "feat", split_axis=0, concat_axis=0, tiled=True
-        )
-        pair, left = call(
+        first = swap(first.reshape(n_feat, hid, 128), "feat")
+        hidden = call(
             hidden_kernel,
+            jax.ShapeDtypeStruct((GROUP, tiles, hid, 128), BF),
+            2,
+            nbytes=1 << 20,
+        )(first, bias_one.reshape(hid, 1))
+        hidden = swap(hidden, "feat", near)
+        live = seed_live.reshape(tiles, 128).astype(F32)
+        own, left = call(
+            aggregate_kernel,
             (
-                jax.ShapeDtypeStruct((tiles, 2 * hid, 128), BF),
-                jax.ShapeDtypeStruct((2 * hid, targets), BF),
+                jax.ShapeDtypeStruct((GROUP, 2 * hid, 128), BF),
+                jax.ShapeDtypeStruct((2 * GROUP * hid, targets), BF),
             ),
             5,
-            scratch=[pltpu.VMEM((tiles, hid, 128), F32)],
-            smem=(2,),
-            flops=2 * 4 * hid * 128 * 128,
+            scratch=[
+                pltpu.VMEM((tiles, GROUP * hid, 128), BF),
+                pltpu.VMEM((tiles, GROUP * hid, 128), F32),
+            ],
+            smem=(0, 2),
+            flops=2 * 4 * GROUP * hid * 128 * 128,
             nbytes=4 << 20,
-        )(
-            first,
-            bias_one.reshape(hid, 1),
-            tile_index,
-            tile_values,
-            seed_live.reshape(tiles, 128).astype(F32),
-        )
+        )((lax.axis_index("feat") % GROUP).reshape(1), hidden, tile_index, tile_values, live)
 
     with jax.named_scope("grads"):
-        piece_rows = 2 * hid * full // 128 // groups
         terms = call(
             grad_kernel,
-            jax.ShapeDtypeStruct((groups, piece_rows, 128), BF),
+            jax.ShapeDtypeStruct((groups, GROUP * 8, 128), BF),
             2,
             flops=2 * 2 * hid * targets * full,
             nbytes=2 << 20,
-        )(left, full_cot)
-        terms = lax.all_to_all(terms, "dp", split_axis=0, concat_axis=0, tiled=True)
-        mine = jnp.sum(terms.astype(F32), axis=0, keepdims=True)
-        grads = lax.all_gather(mine, "dp", axis=0, tiled=True)
-        grads = grads.reshape(full // 128, 2 * hid // piece_rows, piece_rows, 128)
-        grads = grads.transpose(1, 2, 0, 3).reshape(2, hid, full)
+        )(left, cot)
+        terms = swap(terms, "dp")
+        mine = jnp.sum(terms.astype(F32), axis=0).reshape(GROUP, 8, 128)
+        mine = swap(mine, "feat", near)
+        pieces = spread(mine, groups, "dp")
+        grad_neigh, grad_self = call(
+            place_kernel,
+            (jax.ShapeDtypeStruct((hid, full), F32), jax.ShapeDtypeStruct((hid, full), F32)),
+            1,
+            nbytes=1 << 20,
+        )(pieces)
 
     with jax.named_scope("second"):
-        pair = lax.all_to_all(
-            pair, "feat", split_axis=0, concat_axis=0, tiled=True, axis_index_groups=near
-        )
         second = lax.dot_general(
-            second_w, pair.reshape(-1, 128), TN, preferred_element_type=F32
+            second_w.reshape(-1, full), own.reshape(-1, 128), TN, preferred_element_type=F32
         ).astype(BF)
-        second = lax.all_to_all(
-            second.reshape(n_feat, hid, 128), "feat", split_axis=0, concat_axis=0, tiled=True
-        )
-        second = jnp.sum(second.reshape(n_feat // tiles, tiles, hid, 128).astype(F32), axis=0)
+        second = swap(second.reshape(n_feat, hid, 128), "feat")
+        second = jnp.sum(second.reshape(blocks, tiles, hid, 128).astype(F32), axis=0)
         second = second + bias_two[None, :, None]
-        second = second * seed_live.reshape(tiles, 1, 128).astype(F32)
+        second = second * live[:, None, :]
         second_out = second.astype(BF).transpose(0, 2, 1).reshape(targets, hid)
-    return (second_out, grads[0], grads[1])
+    return (second_out, grad_neigh, grad_self)
 
 
 def solution(mesh):

time: 178 us -> 222 us (1.25); the launches traced: 178 us -> 217 us
  waiting for transfers between devices: 42.4 us -> 85.6 us
  blocking collectives: 46.3 us -> 63.4 us
  between operations: 14.2 us -> 0.8 us
  starting transfers between devices: 54.7 us -> 49.8 us
    all_to_all x0 -> x4, blocking collectives: none -> 63.4 us  [swap(): lax.all_to_all(x, axis, split_axis=0, concat_axis=0, tiled=True, axis_ind...]
    all_to_all x6 -> x7, waiting for transfers between devices: 23.4 us -> 85.6 us  [swap(): lax.all_to_all(x, axis, split_axis=0, concat_axis=0, tiled=True, axis_ind...]
    all_gather x2 -> x0, blocking collectives: 46.3 us -> none  [the longest x1 25.3 us: body(): grads = lax.all_gather(mine, 'dp', axis=0, tiled=True)]
    all_gather x2 -> x0, waiting for transfers between devices: 18.3 us -> none  [the longest x1 18.3 us: body(): lax.all_gather(jnp.concatenate([neigh_two, self_two], axis=0), 'feat', ax...]
    all_to_all x6 -> x7, starting transfers between devices: 54.6 us -> 49.8 us  [swap(): lax.all_to_all(x, axis, split_axis=0, concat_axis=0, tiled=True, axis_ind...]
    broadcast_in_dim x0 -> x4, local copies, waits for them, and re-layouts: none -> 2.8 us  [spread(): return swap(jnp.broadcast_to(x[None], (n,) + x.shape), axis, among)]
  transfers between devices with their start and end apart: 8 -> 7, of which waited for: 4 -> 7; matrix products, arithmetic and copies ran while one was open for 3% -> 1% of each run, Pallas kernels for 5% -> 1%
where the time goes in v2:
time: 222 us; the launch traced here: 217 us
  waiting for transfers between devices  85.6 us (39%)
  blocking collectives  63.4 us (29%)
  starting transfers between devices  49.8 us (22%)
  Pallas kernels  7.49 us (3%)
  local copies, waits for them, and re-layouts  7.43 us (3%)
  matrix products  2.26 us (1%)
    all_to_all x7, waiting for transfers between devices, swap(): lax.all_to_all(x, axis, split_axis=0, concat_axis=0, tiled=True, axis_ind...  85.6 us
    all_to_all x4, blocking collectives, swap(): lax.all_to_all(x, axis, split_axis=0, concat_axis=0, tiled=True, axis_ind...  63.4 us
    all_to_all x7, starting transfers between devices, swap(): lax.all_to_all(x, axis, split_axis=0, concat_axis=0, tiled=True, axis_ind...  49.8 us
  transfers between devices with their start and end apart: 7, of which 7 were waited for; matrix products, arithmetic and copies ran while one was open for 1% of the time, Pallas kernels for 1%

profile of v2, /device:TPU:1, one launch (start us, length us, event | category | flops | bytes accessed | tf_op | source)
XLA Modules:
  0.0 217.5 jit_solution(3529078019601878202)
XLA Ops:
  2.3 2.5 %edges.2 = bf16[32,64,128]{2,1,0:T(8,128)(2,1)S(1)} custom-call(bf16[48,2048]{1,0:T(8,128)(2,1)S(1)} %bitcast.33, s32[16,128]{1,0:T(8,128)S(1)} %bitcast.35), custom_call_target="tpu_custom_call" | custom-call | flops 1073741824 | bytes 8388608 | tf_op jit(solution)/shard_map/edges/pallas_call | solution.py:208
  4.8 21.3 %all_to_all.55.recv_ref = bf16[32,64,128]{2,1,0:T(8,128)(2,1)S(1)} all-to-all(bf16[32,64,128]{2,1,0:T(8,128)(2,1)S(1)} %edges.2), channel_id=1, replica_groups=mesh['dp'=32,'feat'=16] {'dp'}, dimensions={0} | all-to-all | bytes 1048576 | tf_op jit(solution)/shard_map/edges/all_to_all | solution.py:194
  26.1 2.0 edges.3
  28.2 4.5 %all-to-all-start.3 = ((bf16[4,96,128]{2,1,0:T(8,128)(2,1)}), bf16[4,96,128]{2,1,0:T(8,128)(2,1)S(1)}, u32[]{:S(2)}, u32[]{:S(2)}) async-start(bf16[4,96,128]{2,1,0:T(8,128)(2,1)} %edges.3), calls=%async_computation.3 | async-start | bytes 196608 | tf_op jit(solution)/shard_map/first/all_to_all | solution.py:194
  32.7 4.7 %all-to-all-done.3 = bf16[4,96,128]{2,1,0:T(8,128)(2,1)S(1)} async-done(((bf16[4,96,128]{2,1,0:T(8,128)(2,1)}), bf16[4,96,128]{2,1,0:T(8,128)(2,1)S(1)}, u32[]{:S(2)}, u32[]{:S(2)}) %all-to-all-start.3) | async-done | bytes 98336 | tf_op jit(solution)/shard_map/first/all_to_all | solution.py:194
  37.4 22.0 %all_to_all.56 = bf16[4,96,1024]{2,1,0:T(8,128)(2,1)S(1)} all-to-all(bf16[4,96,1024]{2,1,0:T(8,128)(2,1)S(1)} %broadcast_in_dim.9), channel_id=1, replica_groups={{0,1,2,3},{4,5,6,7},{8,9,10,11},{12,13,14,15},{16,17,18,19},{20,21,22,2..., dimensions={0} | all-to-all | bytes 1572864 | tf_op jit(solution)/shard_map/weights/all_to_all | solution.py:194
  59.4 1.1 fusion
  60.5 12.7 %all-to-all-start.4 = ((bf16[16,64,128]{2,1,0:T(8,128)(2,1)}), bf16[16,64,128]{2,1,0:T(8,128)(2,1)S(1)}, u32[]{:S(2)}, u32[]{:S(2)}) async-start(bf16[16,64,128]{2,1,0:T(8,128)(2,1)} %bitcast.5), calls=%async_computation.4 | async-start | bytes 524288 | tf_op jit(solution)/shard_map/first/all_to_all | solution.py:194
  74.0 12.0 %all-to-all-done.4.parts_ref = bf16[16,64,128]{2,1,0:T(8,128)(2,1)S(1)} async-done(((bf16[16,64,128]{2,1,0:T(8,128)(2,1)}), bf16[16,64,128]{2,1,0:T(8,128)(2,1)S(1)}, u32[]{:S(2)}, u32[]{:S(2)}) %all-to-all-start.4) | async-done | bytes 262176 | tf_op jit(solution)/shard_map/first/all_to_all | solution.py:194
  86.1 13.3 %all_to_all.57.hid_ref = bf16[4,4,64,128]{3,2,1,0:T(8,128)(2,1)S(1)} all-to-all(bf16[4,4,64,128]{3,2,1,0:T(8,128)(2,1)S(1)} %first.2), channel_id=1, replica_groups={{0,1,2,3},{4,5,6,7},{8,9,10,11},{12,13,14,15},{16,17,18,19},{20,21,22,2..., dimensions={0} | all-to-all | bytes 524288 | tf_op jit(solution)/shard_map/first/all_to_all | solution.py:194
  100.1 6.3 %all-to-all-start.7 = ((bf16[4,64,512]{2,1,0:T(8,128)(2,1)}), bf16[4,64,512]{2,1,0:T(8,128)(2,1)S(1)}, u32[]{:S(2)}, u32[]{:S(2)}) async-start(bf16[4,64,512]{2,1,0:T(8,128)(2,1)} %broadcast_in_dim.10), calls=%async_computation.7 | async-start | bytes 524288 | tf_op jit(solution)/shard_map/cotangent/all_to_all | solution.py:194
  108.8 10.8 %all-to-all-done.7 = bf16[4,64,512]{2,1,0:T(8,128)(2,1)S(1)} async-done(((bf16[4,64,512]{2,1,0:T(8,128)(2,1)}), bf16[4,64,512]{2,1,0:T(8,128)(2,1)S(1)}, u32[]{:S(2)}, u32[]{:S(2)}) %all-to-all-start.7) | async-done | bytes 262176 | tf_op jit(solution)/shard_map/cotangent/all_to_all | solution.py:194
  119.6 1.0 grads.2
  120.6 13.3 %all-to-all-start.8 = ((bf16[32,32,128]{2,1,0:T(8,128)(2,1)}), bf16[32,32,128]{2,1,0:T(8,128)(2,1)S(1)}, u32[]{:S(2)}, u32[]{:S(2)}) async-start(bf16[32,32,128]{2,1,0:T(8,128)(2,1)} %grads.2), calls=%async_computation.8 | async-start | bytes 524288 | tf_op jit(solution)/shard_map/grads/all_to_all | solution.py:194
  134.2 8.7 %all-to-all-done.8 = bf16[32,32,128]{2,1,0:T(8,128)(2,1)S(1)} async-done(((bf16[32,32,128]{2,1,0:T(8,128)(2,1)}), bf16[32,32,128]{2,1,0:T(8,128)(2,1)S(1)}, u32[]{:S(2)}, u32[]{:S(2)}) %all-to-all-start.8) | async-done | bytes 262176 | tf_op jit(solution)/shard_map/grads/all_to_all | solution.py:194
  142.9 1.1 broadcast_in_dim.8
  144.0 3.5 %all-to-all-start = ((bf16[4,128,1024]{1,2,0:T(8,128)(2,1)}), bf16[4,128,1024]{1,2,0:T(8,128)(2,1)S(1)}, u32[]{:S(2)}, u32[]{:S(2)}) async-start(bf16[4,128,1024]{1,2,0:T(8,128)(2,1)} %broadcast_in_dim.8), calls=%async_computation | async-start | bytes 2097152 | tf_op jit(solution)/shard_map/weights/all_to_all | solution.py:194
  147.6 25.5 %all-to-all-done = bf16[4,128,1024]{1,2,0:T(8,128)(2,1)S(1)} async-done(((bf16[4,128,1024]{1,2,0:T(8,128)(2,1)}), bf16[4,128,1024]{1,2,0:T(8,128)(2,1)S(1)}, u32[]{:S(2)}, u32[]{:S(2)}) %all-to-all-start) | async-done | bytes 1048608 | tf_op jit(solution)/shard_map/weights/all_to_all | solution.py:194
  173.1 6.8 %all_to_all.58 = f32[4,8,128]{2,1,0:T(8,128)S(1)} all-to-all(f32[4,8,128]{2,1,0:T(8,128)S(1)} %bitcast.38), channel_id=1, replica_groups={{0,1,2,3},{4,5,6,7},{8,9,10,11},{12,13,14,15},{16,17,18,19},{20,21,22,2..., dimensions={0} | all-to-all | bytes 32768 | tf_op jit(solution)/shard_map/grads/all_to_all | solution.py:194
  180.8 5.9 %all-to-all-start.10 = ((f32[32,4,8,128]{3,2,1,0:T(8,128)}), f32[32,4,8,128]{3,2,1,0:T(8,128)S(1)}, u32[]{:S(2)}, u32[]{:S(2)}) async-start(f32[32,4,8,128]{3,2,1,0:T(8,128)} %broadcast_in_dim.11), calls=%async_computation.10 | async-start | bytes 1048576 | tf_op jit(solution)/shard_map/grads/all_to_all | solution.py:194
  186.7 1.1 fusion.1
  187.8 10.5 %all-to-all-done.10.pieces_ref = f32[32,4,8,128]{3,2,1,0:T(8,128)S(1)} async-done(((f32[32,4,8,128]{3,2,1,0:T(8,128)}), f32[32,4,8,128]{3,2,1,0:T(8,128)S(1)}, u32[]{:S(2)}, u32[]{:S(2)}) %all-to-all-start.10) | async-done | bytes 524320 | tf_op jit(solution)/shard_map/grads/all_to_all | solution.py:194
  198.4 3.5 %all-to-all-start.6 = ((bf16[16,64,128]{2,1,0:T(8,128)(2,1)}), bf16[16,64,128]{2,1,0:T(8,128)(2,1)S(1)}, u32[]{:S(2)}, u32[]{:S(2)}) async-start(bf16[16,64,128]{2,1,0:T(8,128)(2,1)} %bitcast.9), calls=%async_computation.6 | async-start | bytes 524288 | tf_op jit(solution)/shard_map/second/all_to_all | solution.py:194
  202.8 13.3 %all-to-all-done.6 = bf16[16,64,128]{2,1,0:T(8,128)(2,1)S(1)} async-done(((bf16[16,64,128]{2,1,0:T(8,128)(2,1)}), bf16[16,64,128]{2,1,0:T(8,128)(2,1)S(1)}, u32[]{:S(2)}, u32[]{:S(2)}) %all-to-all-start.6) | async-done | bytes 262176 | tf_op jit(solution)/shard_map/second/all_to_all | solution.py:194
  (41 shorter events, 9.0 us)
Async XLA Ops:
  0.6 0.9 copy-start.1
  1.6 0.7 copy-start.3
  4.8 21.3 %copy-start.2 = (bf16[512,48]{0,1:T(8,128)(2,1)S(1)}, bf16[512,48]{0,1:T(8,128)(2,1)}, u32[]{:S(2)}) copy-start(bf16[512,48]{0,1:T(8,128)(2,1)} %param.15) | copy-start | bytes 147460
  28.2 4.5 %copy-start.6 = (bf16[48,1024]{1,0:T(8,128)(2,1)S(1)}, bf16[48,1024]{1,0:T(8,128)(2,1)}, u32[]{:S(2)}) copy-start(bf16[48,1024]{1,0:T(8,128)(2,1)} %param.17) | copy-start | bytes 294916
  28.2 4.5 %copy-start.7 = (bf16[48,1024]{1,0:T(8,128)(2,1)S(1)}, bf16[48,1024]{1,0:T(8,128)(2,1)}, u32[]{:S(2)}) copy-start(bf16[48,1024]{1,0:T(8,128)(2,1)} %param.16) | copy-start | bytes 294916
  28.2 9.2 %all-to-all-start.3 = ((bf16[4,96,128]{2,1,0:T(8,128)(2,1)}), bf16[4,96,128]{2,1,0:T(8,128)(2,1)S(1)}, u32[]{:S(2)}, u32[]{:S(2)}) async-start(bf16[4,96,128]{2,1,0:T(8,128)(2,1)} %edges.3), calls=%async_computation.3 | async-start | bytes 196608 | tf_op jit(solution)/shard_map/first/all_to_all | solution.py:194
  60.5 25.5 %all-to-all-start.4 = ((bf16[16,64,128]{2,1,0:T(8,128)(2,1)}), bf16[16,64,128]{2,1,0:T(8,128)(2,1)S(1)}, u32[]{:S(2)}, u32[]{:S(2)}) async-start(bf16[16,64,128]{2,1,0:T(8,128)(2,1)} %bitcast.5), calls=%async_computation.4 | async-start | bytes 524288 | tf_op jit(solution)/shard_map/first/all_to_all | solution.py:194
  73.2 0.7 copy-start.11
  86.1 13.3 %copy-start.8 = (bf16[512,64]{0,1:T(8,128)(2,1)S(1)}, bf16[512,64]{0,1:T(8,128)(2,1)}, u32[]{:S(2)}) copy-start(bf16[512,64]{0,1:T(8,128)(2,1)} %param.25) | copy-start | bytes 196612
  100.1 7.7 %copy-start = (bf16[4,128,128]{2,1,0:T(8,128)(2,1)S(1)}, bf16[4,128,128]{2,1,0:T(8,128)(2,1)}, u32[]{:S(2)}) copy-start(bf16[4,128,128]{2,1,0:T(8,128)(2,1)} %values_ref.1) | copy-start | bytes 393220
  100.1 19.5 %all-to-all-start.7 = ((bf16[4,64,512]{2,1,0:T(8,128)(2,1)}), bf16[4,64,512]{2,1,0:T(8,128)(2,1)S(1)}, u32[]{:S(2)}, u32[]{:S(2)}) async-start(bf16[4,64,512]{2,1,0:T(8,128)(2,1)} %broadcast_in_dim.10), calls=%async_computation.7 | async-start | bytes 524288 | tf_op jit(solution)/shard_map/cotangent/all_to_all | solution.py:194
  106.4 0.7 copy-start.10
  107.2 0.7 copy-start.9
  120.6 13.3 %copy-start.4 = (bf16[64,1024]{1,0:T(8,128)(2,1)S(1)}, bf16[64,1024]{1,0:T(8,128)(2,1)}, u32[]{:S(2)}) copy-start(bf16[64,1024]{1,0:T(8,128)(2,1)} %param.23) | copy-start | bytes 393220
  120.6 13.4 %copy-start.5 = (bf16[64,1024]{1,0:T(8,128)(2,1)S(1)}, bf16[64,1024]{1,0:T(8,128)(2,1)}, u32[]{:S(2)}) copy-start(bf16[64,1024]{1,0:T(8,128)(2,1)} %param.22) | copy-start | bytes 393220
  120.6 22.2 %all-to-all-start.8 = ((bf16[32,32,128]{2,1,0:T(8,128)(2,1)}), bf16[32,32,128]{2,1,0:T(8,128)(2,1)S(1)}, u32[]{:S(2)}, u32[]{:S(2)}) async-start(bf16[32,32,128]{2,1,0:T(8,128)(2,1)} %grads.2), calls=%async_computation.8 | async-start | bytes 524288 | tf_op jit(solution)/shard_map/grads/all_to_all | solution.py:194
  144.0 29.1 %all-to-all-start = ((bf16[4,128,1024]{1,2,0:T(8,128)(2,1)}), bf16[4,128,1024]{1,2,0:T(8,128)(2,1)S(1)}, u32[]{:S(2)}, u32[]{:S(2)}) async-start(bf16[4,128,1024]{1,2,0:T(8,128)(2,1)} %broadcast_in_dim.8), calls=%async_computation | async-start | bytes 2097152 | tf_op jit(solution)/shard_map/weights/all_to_all | solution.py:194
  180.8 17.6 %all-to-all-start.10 = ((f32[32,4,8,128]{3,2,1,0:T(8,128)}), f32[32,4,8,128]{3,2,1,0:T(8,128)S(1)}, u32[]{:S(2)}, u32[]{:S(2)}) async-start(f32[32,4,8,128]{3,2,1,0:T(8,128)} %broadcast_in_dim.11), calls=%async_computation.10 | async-start | bytes 1048576 | tf_op jit(solution)/shard_map/grads/all_to_all | solution.py:194
  198.4 17.7 %all-to-all-start.6 = ((bf16[16,64,128]{2,1,0:T(8,128)(2,1)}), bf16[16,64,128]{2,1,0:T(8,128)(2,1)S(1)}, u32[]{:S(2)}, u32[]{:S(2)}) async-start(bf16[16,64,128]{2,1,0:T(8,128)(2,1)} %bitcast.9), calls=%async_computation.6 | async-start | bytes 524288 | tf_op jit(solution)/shard_map/second/all_to_all | solution.py:194
  216.1 0.7 copy-start.12

commit v3 on v2

v3 whole, which is shorter than its diff:
```python
import functools

import jax
import jax.numpy as jnp
from jax import lax
from jax.experimental import pallas as pl
from jax.experimental.pallas import tpu as pltpu
from jax.sharding import PartitionSpec as P

BF = jnp.bfloat16
F32 = jnp.float32
NT = (((1,), (1,)), ((), ()))
TN = (((0,), (0,)), ((), ()))
ROWS = 64
GROUP = 4
VMEM_LIMIT = 48 * 1024 * 1024


def call(kernel, out_shape, n_in, scratch=(), smem=(), late=(), flops=0, nbytes=0):
    spaces = {i: pltpu.SMEM for i in smem} | {i: pl.ANY for i in late}
    in_specs = [pl.BlockSpec(memory_space=spaces.get(i, pltpu.VMEM)) for i in range(n_in)]
    out_specs = jax.tree.map(lambda _: pl.BlockSpec(memory_space=pltpu.VMEM), out_shape)
    return pl.pallas_call(
        kernel,
        out_shape=out_shape,
        in_specs=in_specs,
        out_specs=out_specs,
        scratch_shapes=list(scratch),
        compiler_params=pltpu.CompilerParams(vmem_limit_bytes=VMEM_LIMIT),
        cost_estimate=pl.CostEstimate(flops=flops, bytes_accessed=nbytes, transcendentals=0),
    )


def pack_kernel(groups, tgt_rows, feats_ref, dst_ref, send_ref, masked):
    cols, edges = feats_ref.shape
    cap = send_ref.shape[2]
    dst = jnp.concatenate([dst_ref[i : i + 1, :] for i in range(dst_ref.shape[0])], axis=1)
    owner = dst // tgt_rows
    local = dst - owner * tgt_rows
    half = tgt_rows // 2
    code = jnp.where(local < half, local - half, local - (half - 1)).astype(F32)
    owner_hot = lax.broadcasted_iota(jnp.int32, (groups, edges), 0) == owner
    owner_hot = owner_hot.astype(F32)
    step = 256
    before = (
        lax.broadcasted_iota(jnp.int32, (step, step), 0)
        < lax.broadcasted_iota(jnp.int32, (step, step), 1)
    ).astype(BF)
    seen = jnp.zeros((groups, 1), F32)
    ranks = []
    for i in range(edges // step):
        part = owner_hot[:, i * step : (i + 1) * step]
        prior = jnp.dot(part.astype(BF), before, preferred_element_type=F32) + seen
        ranks.append(jnp.sum(prior * part, axis=0, keepdims=True))
        seen = seen + jnp.sum(part, axis=1, keepdims=True)
    rank = jnp.concatenate(ranks, axis=1).astype(jnp.int32)
    rank_hot = (lax.broadcasted_iota(jnp.int32, (cap, edges), 0) == rank).astype(F32).astype(BF)
    extra_row = lax.broadcasted_iota(jnp.int32, (ROWS - cols, edges), 0)
    extra = jnp.where(extra_row == 0, code, jnp.where(extra_row == 1, 1.0, 0.0)).astype(BF)
    hot = owner_hot.astype(BF)
    some = masked.shape[0] // ROWS
    for g in range(groups // some):
        for j in range(some):
            o = g * some + j
            live = hot[o : o + 1, :]
            masked[j * ROWS : j * ROWS + cols, :] = feats_ref[...] * live
            masked[j * ROWS + cols : (j + 1) * ROWS, :] = extra * live
        out = lax.dot_general(masked[...], rank_hot, NT, preferred_element_type=F32).astype(BF)
        for j in range(some):
            send_ref[g * some + j] = out[j * ROWS : (j + 1) * ROWS, :]


def column_sets(weight, group):
    half = 64
    n = weight.shape[1] // half
    sets = []
    for j in range(group):
        blocks = [weight[:, b * half : (b + 1) * half] for b in range(j, n, group)]
        sets.append(jnp.concatenate(blocks, axis=1))
    return sets


def first_pieces_kernel(mine_ref, neigh_ref, own_ref, self_ref, cot_ref, late_ref, out_ref, cot_out_ref):
    del late_ref
    mine = mine_ref[0]
    rows = neigh_ref.shape[0]
    group, _, width = out_ref.shape
    both = zip(column_sets(neigh_ref[...], group), column_sets(own_ref[...], group))
    for j, (neigh, own) in enumerate(both):
        to = jnp.bitwise_xor(mine, j)
        out_ref[to, :rows, :] = neigh
        out_ref[to, rows : 2 * rows, :] = own
        out_ref[to, 2 * rows : 3 * rows, :] = self_ref[:, :width]
        out_ref[to, 3 * rows :, :] = self_ref[:, width:]
    cot_out_ref[...] = cot_ref[...]


def second_pieces_kernel(mine_ref, neigh_ref, own_ref, late_ref, out_ref):
    del late_ref
    mine = mine_ref[0]
    rows = neigh_ref.shape[0]
    both = zip(column_sets(neigh_ref[...], out_ref.shape[0]), column_sets(own_ref[...], out_ref.shape[0]))
    for j, (neigh, own) in enumerate(both):
        to = jnp.bitwise_xor(mine, j)
        out_ref[to, :rows, :] = neigh
        out_ref[to, rows:, :] = own


def mean_kernel(cols, recv_ref, cot_ref, far_ref, late1_ref, late2_ref, late3_ref, out_ref, cots_ref):
    del late1_ref, late2_ref, late3_ref
    groups, rows, cap = recv_ref.shape
    targets = out_ref.shape[2]
    half = targets // 2
    vertex = lax.broadcasted_iota(jnp.int32, (targets, 1), 0)
    vertex = jnp.where(vertex < half, vertex - half, vertex - (half - 1)).astype(F32)
    acc = jnp.zeros((rows, targets), F32)
    some = 8
    for g in range(groups // some):
        part = jnp.concatenate([recv_ref[g * some + j] for j in range(some)], axis=1)
        code = part[cols : cols + 1, :].astype(F32)
        hot = (vertex == code).astype(F32).astype(BF)
        acc = acc + lax.dot_general(part, hot, NT, preferred_element_type=F32)
    degree = jnp.maximum(acc[cols + 1 : cols + 2, :], 1.0)
    mean = (acc[:cols, :] / degree).astype(BF)
    for j in range(out_ref.shape[0]):
        out_ref[j] = mean
    cots_ref[0] = cot_ref[...]
    cots_ref[1] = far_ref[...]


def first_kernel(mine_ref, mean_ref, p0_ref, p1_ref, p2_ref, p3_ref, out_ref, weight, acts):
    mine = mine_ref[0]
    group, rows, targets = mean_ref.shape
    width = targets // 2
    for k, piece in enumerate((p0_ref, p1_ref, p2_ref, p3_ref)):
        at = slice(2 * rows * k, 2 * rows * (k + 1))
        mid = 2 * rows * k + rows
        weight[at, :] = piece[: 2 * rows, :]
        acts[2 * rows * k : mid, :] = mean_ref[jnp.bitwise_xor(mine, k)]
        acts[mid : mid + rows, :width] = piece[2 * rows : 3 * rows, :]
        acts[mid : mid + rows, width:] = piece[3 * rows :, :]
    total = lax.dot_general(weight[...], acts[...], TN, preferred_element_type=F32)
    n, cols, _ = out_ref.shape
    for z in range(n):
        out_ref[z] = total[z * cols : (z + 1) * cols, :].astype(BF)


def hidden_kernel(parts_ref, bias_ref, late_ref, out_ref):
    del late_ref
    total = parts_ref[0].astype(F32)
    for k in range(1, parts_ref.shape[0]):
        total = total + parts_ref[k].astype(F32)
    hidden = jnp.maximum(total + bias_ref[...], 0.0).astype(BF)
    for c in range(out_ref.shape[0]):
        out_ref[c] = hidden


def grad_kernel(
    place_ref, index_ref, hid_ref, values_ref, live_ref, near_ref, far_ref, agg_ref, out_ref, left, cot, acc
):
    group, cols, targets = hid_ref.shape
    width = values_ref.shape[1]
    wide = group * cols
    across = place_ref[0]
    for k, ref in enumerate((near_ref, near_ref, far_ref, far_ref)):
        cot[jnp.bitwise_xor(across, k)] = ref[k % 2]
    acc[...] = jnp.zeros_like(acc)
    for k in range(values_ref.shape[0]):
        source = index_ref[k, 1]
        at = pl.ds(pl.multiple_of(source * width, width), width)
        rows = jnp.concatenate([hid_ref[j, :, at] for j in range(group)], axis=0)
        target = index_ref[k, 0]
        acc[target] += lax.dot_general(rows, values_ref[k], NT, preferred_element_type=F32)
    live = live_ref[...].astype(BF)
    for t in range(targets // width):
        at = slice(t * width, (t + 1) * width)
        tile = acc[t].astype(BF)
        agg_ref[:, at] = tile
        left[:wide, at] = tile * live[:, at]
    for j in range(group):
        left[wide + j * cols : wide + (j + 1) * cols, :] = hid_ref[j] * live
    right = jnp.concatenate([cot[j] for j in range(group)], axis=0)
    block = lax.dot_general(left[...], right, NT, preferred_element_type=F32)
    at = 0
    for w in range(2):
        for r in range(0, cols, 8):
            for c in range(0, right.shape[0], 128):
                rows_of = [
                    block[w * wide + j * cols + r : w * wide + j * cols + r + 8, c : c + 128]
                    for j in range(group)
                ]
                out_ref[at] = jnp.concatenate(rows_of, axis=0).astype(BF)
                at += 1


def second_kernel(mine_ref, agg_ref, hid_ref, p0_ref, p1_ref, p2_ref, p3_ref, out_ref, weight, acts):
    mine = mine_ref[0]
    group, rows, targets = hid_ref.shape
    for k, piece in enumerate((p0_ref, p1_ref, p2_ref, p3_ref)):
        weight[jnp.bitwise_xor(mine, k)] = piece[...]
    for j in range(group):
        acts[2 * rows * j : 2 * rows * j + rows, :] = agg_ref[j * rows : (j + 1) * rows, :]
        acts[2 * rows * j + rows : 2 * rows * (j + 1), :] = hid_ref[j]
    both = jnp.concatenate([weight[j] for j in range(group)], axis=0)
    total = lax.dot_general(both, acts[...], TN, preferred_element_type=F32)
    n, cols, _ = out_ref.shape
    for z in range(n):
        out_ref[z] = total[z * cols : (z + 1) * cols, :].astype(BF)


def sum_kernel(mine_ref, terms_ref, out_ref):
    mine = mine_ref[0]
    total = terms_ref[0].astype(F32)
    for d in range(1, terms_ref.shape[0]):
        total = total + terms_ref[d].astype(F32)
    rows = out_ref.shape[1]
    for j in range(out_ref.shape[0]):
        out_ref[jnp.bitwise_xor(mine, j)] = total[j * rows : (j + 1) * rows, :]


def copies_kernel(p0_ref, p1_ref, p2_ref, p3_ref, late_ref, out_ref):
    del late_ref
    whole = jnp.concatenate([p0_ref[...], p1_ref[...], p2_ref[...], p3_ref[...]], axis=0)
    for d in range(out_ref.shape[0]):
        out_ref[d] = whole


def place_kernel(mine_ref, pieces_ref, neigh_ref, self_ref):
    mine = mine_ref[0]
    half = 64
    at = 0
    for out_ref in (neigh_ref, self_ref):
        for r in range(0, out_ref.shape[0], 8):
            for c in range(2):
                parts = [
                    pieces_ref[at, pl.ds(pl.multiple_of(jnp.bitwise_xor(mine, h) * 8, 8), 8), :]
                    for h in range(4)
                ]
                for e in range(2):
                    for p in range(2):
                        pair = [parts[2 * p + i][:, e * half : (e + 1) * half] for i in range(2)]
                        to = (8 * c + 4 * e + 2 * p) * half
                        out_ref[r : r + 8, to : to + 2 * half] = jnp.concatenate(pair, axis=1)
                at += 1


def out_kernel(parts_ref, bias_ref, live_ref, out_ref):
    total = parts_ref[0].astype(F32)
    for k in range(1, parts_ref.shape[0]):
        total = total + parts_ref[k].astype(F32)
    out_ref[...] = ((total + bias_ref[...]) * live_ref[...]).astype(BF)


def body(
    edge_feats,
    edge_dst,
    self_feats,
    neigh_one,
    self_one,
    bias_one,
    tile_index,
    tile_values,
    seed_live,
    neigh_two,
    self_two,
    bias_two,
    cotangent,
):
    groups = lax.axis_size("dp")
    n_feat = lax.axis_size("feat")
    edges, cols = edge_feats.shape
    targets = self_feats.shape[0]
    hid = bias_one.shape[0]
    full = neigh_one.shape[1]
    cap = 2 * edges // groups
    blocks = n_feat // GROUP
    wide = full // GROUP
    near = [[GROUP * i + j for j in range(GROUP)] for i in range(blocks)]
    far = [[i + GROUP * j for j in range(blocks)] for i in range(GROUP)]
    z = lax.axis_index("feat")
    mine = (z % GROUP).reshape(1)
    across = (z // GROUP).reshape(1)
    live = seed_live.reshape(1, targets).astype(F32)

    def swap(x, axis, among=None):
        return lax.all_to_all(
            x, axis, split_axis=0, concat_axis=0, tiled=True, axis_index_groups=among
        )

    def trade(x, k):
        return lax.ppermute(x, "feat", [(i, i ^ k) for i in range(n_feat)])

    def shape(*dims, dtype=BF):
        return jax.ShapeDtypeStruct(dims, dtype)

    with jax.named_scope("edges"):
        send = call(
            functools.partial(pack_kernel, groups, targets),
            shape(groups, ROWS, cap),
            2,
            scratch=[pltpu.VMEM((8 * ROWS, edges), BF)],
            flops=2 * groups * ROWS * edges * cap,
            nbytes=8 << 20,
        )(edge_feats.T, edge_dst.reshape(-1, 128))
        recv = swap(send, "dp")
    with jax.named_scope("pieces"):
        pieces, cot = call(
            first_pieces_kernel,
            (shape(GROUP, 4 * cols, wide), shape(hid, targets)),
            6,
            smem=(0,),
            late=(5,),
            nbytes=2 << 20,
        )(mine, neigh_one, self_one, self_feats.T, cotangent.T, send)
        got = [trade(pieces[k], k) for k in range(1, GROUP)]
        cot_far = trade(cot, GROUP)
    with jax.named_scope("mean"):
        mean, cots = call(
            functools.partial(mean_kernel, cols),
            (shape(GROUP, cols, targets), shape(2, hid, targets)),
            6,
            late=(3, 4, 5),
            flops=2 * groups * ROWS * cap * targets,
            nbytes=8 << 20,
        )(recv, cot, cot_far, *got)
        cots_far = trade(cots, 2 * GROUP)
        mean = swap(mean, "feat", near)
    with jax.named_scope("first"):
        first = call(
            first_kernel,
            shape(blocks, hid, targets),
            6,
            scratch=[pltpu.VMEM((8 * cols, wide), BF), pltpu.VMEM((8 * cols, targets), BF)],
            smem=(0,),
            flops=2 * 8 * cols * wide * targets,
            nbytes=2 << 20,
        )(mine, mean, pieces[0], *got)
        first = swap(first, "feat", far)
        hidden = call(
            hidden_kernel, shape(GROUP, hid, targets), 3, late=(2,), nbytes=1 << 20
        )(first, bias_one.reshape(hid, 1), cots_far)
        hidden = swap(hidden, "feat", near)
    with jax.named_scope("grads"):
        agg, terms = call(
            grad_kernel,
            (shape(wide, targets), shape(groups, GROUP * 8, 128)),
            7,
            scratch=[
                pltpu.VMEM((2 * wide, targets), BF),
                pltpu.VMEM((blocks, hid, targets), BF),
                pltpu.VMEM((targets // 128, wide, 128), F32),
            ],
            smem=(0, 1),
            flops=2 * 2 * wide * targets * wide,
            nbytes=4 << 20,
        )(across, tile_index, hidden, tile_values, live, cots, cots_far)
        terms = swap(terms, "dp")
        mine_sum = call(
            sum_kernel, shape(GROUP, 8, 128, dtype=F32), 2, smem=(0,), nbytes=1 << 20
        )(mine, terms)
        sums = [mine_sum[0]] + [trade(mine_sum[k], k) for k in range(1, GROUP)]
    with jax.named_scope("second"):
        pieces = call(
            second_pieces_kernel,
            shape(GROUP, 2 * hid, wide),
            4,
            smem=(0,),
            late=(3,),
            nbytes=1 << 20,
        )(mine, neigh_two, self_two, agg)
        got = [trade(pieces[k], k) for k in range(1, GROUP)]
        second = call(
            second_kernel,
            shape(blocks, hid, targets),
            7,
            scratch=[pltpu.VMEM((GROUP, 2 * hid, wide), BF), pltpu.VMEM((2 * wide, targets), BF)],
            smem=(0,),
            flops=2 * 2 * wide * wide * targets,
            nbytes=2 << 20,
        )(mine, agg, hidden, pieces[0], *got)
        second = swap(second, "feat", far)
        second_out = call(out_kernel, shape(hid, targets), 3, nbytes=1 << 20)(
            second, bias_two.reshape(hid, 1), live
        ).T
    with jax.named_scope("place"):
        spread = call(
            copies_kernel, shape(groups, GROUP * 8, 128, dtype=F32), 5, late=(4,), nbytes=1 << 20
        )(*sums, second)
        spread = swap(spread, "dp")
        grad_neigh, grad_self = call(
            place_kernel,
            (shape(hid, full, dtype=F32), shape(hid, full, dtype=F32)),
            2,
            smem=(0,),
            nbytes=1 << 20,
        )(mine, spread)
    return (second_out, grad_neigh, grad_self)


def solution(mesh):
    in_specs = (
        P("dp", "feat"),
        P("dp"),
        P("dp", "feat"),
        P("feat", None),
        P("feat", None),
        P("feat"),
        P("dp", None),
        P("dp", None, None),
        P("dp"),
        P("feat", None),
        P("feat", None),
        P("feat"),
        P("dp", "feat"),
    )
    out_specs = (P("dp", "feat"), P("feat", None), P("feat", None))
    return jax.shard_map(body, mesh=mesh, in_specs=in_specs, out_specs=out_specs, check_vma=False)
```

time: 222 us -> 178 us (0.80); the launches traced: 217 us -> 177 us
  blocking collectives: 63.4 us -> 11.9 us
  starting transfers between devices: 49.8 us -> 100 us
  waiting for transfers between devices: 85.6 us -> 48.6 us
  Pallas kernels: 7.49 us -> 12.2 us
  local copies, waits for them, and re-layouts: 7.43 us -> 3.22 us
  matrix products: 2.26 us -> 0 us
    all_to_all x7 -> x6, waiting for transfers between devices: 85.6 us -> 19.9 us  [swap(): lax.all_to_all(x, axis, split_axis=0, concat_axis=0, tiled=True, axis_ind...]
    all_to_all x4 -> x1, blocking collectives: 63.4 us -> 11.9 us  [swap(): lax.all_to_all(x, axis, split_axis=0, concat_axis=0, tiled=True, axis_ind...]
    ppermute x0 -> x11, starting transfers between devices: none -> 48.1 us  [trade(): return lax.ppermute(x, 'feat', [(i, i ^ k) for i in range(n_feat)])]
    ppermute x0 -> x11, waiting for transfers between devices: none -> 28.8 us  [trade(): return lax.ppermute(x, 'feat', [(i, i ^ k) for i in range(n_feat)])]
    pallas_call x6 -> x12, Pallas kernels: 7.49 us -> 12.2 us  [the longest x1 3.31 us: body(): call(functools.partial(pack_kernel, groups, targets), shape(groups, ROWS,...]
    broadcast_in_dim x4 -> x0, local copies, waits for them, and re-layouts: 2.8 us -> none  [spread(): return swap(jnp.broadcast_to(x[None], (n,) + x.shape), axis, among)]
    all_to_all x7 -> x6, starting transfers between devices: 49.8 us -> 52 us  [swap(): lax.all_to_all(x, axis, split_axis=0, concat_axis=0, tiled=True, axis_ind...]
    dot_general x2 -> x0, matrix products: 2.26 us -> none  [the longest x1 1.13 us: body(): lax.dot_general(second_w.reshape(-1, full), own.reshape(-1, 128), TN, pre...]
  transfers between devices with their start and end apart: 7 -> 17, of which waited for: 7 -> 7; matrix products, arithmetic and copies ran while one was open for 1% -> 0% of each run, Pallas kernels for 1% -> 1%
where the time goes in v3:
time: 178 us; the launch traced here: 177 us
  starting transfers between devices  100 us (56%)
  waiting for transfers between devices  48.6 us (27%)
  Pallas kernels  12.2 us (7%)
  blocking collectives  11.9 us (7%)
  local copies, waits for them, and re-layouts  3.22 us (2%)
    all_to_all x6, starting transfers between devices, swap(): lax.all_to_all(x, axis, split_axis=0, concat_axis=0, tiled=True, axis_ind...  52 us
    ppermute x11, starting transfers between devices, trade(): return lax.ppermute(x, 'feat', [(i, i ^ k) for i in range(n_feat)])  48.1 us
    ppermute x11, waiting for transfers between devices, trade(): return lax.ppermute(x, 'feat', [(i, i ^ k) for i in range(n_feat)])  28.8 us
    all_to_all x6, waiting for transfers between devices, swap(): lax.all_to_all(x, axis, split_axis=0, concat_axis=0, tiled=True, axis_ind...  19.9 us
    all_to_all x1, blocking collectives, swap(): lax.all_to_all(x, axis, split_axis=0, concat_axis=0, tiled=True, axis_ind...  11.9 us
  transfers between devices with their start and end apart: 17, of which 7 were waited for; matrix products, arithmetic and copies ran while one was open for 0% of the time, Pallas kernels for 1%

profile of v3, /device:TPU:1, one launch (start us, length us, event | category | flops | bytes accessed | tf_op | source)
XLA Modules:
  0.0 177.1 jit_solution(16139542305246976912)
XLA Ops:
  2.3 3.3 %edges.1.late_ref = bf16[32,64,128]{2,1,0:T(8,128)(2,1)} custom-call(bf16[48,2048]{1,0:T(8,128)(2,1)S(1)} %bitcast.38, s32[16,128]{1,0:T(8,128)S(1)} %bitcast.39), custom_call_target="tpu_custom_call" | custom-call | flops 1073741824 | bytes 8388608 | tf_op jit(solution)/shard_map/edges/pallas_call | solution.py:297
  5.6 10.6 %all-to-all-start = ((bf16[32,64,128]{2,1,0:T(8,128)(2,1)}), bf16[32,64,128]{2,1,0:T(8,128)(2,1)S(1)}, u32[]{:S(2)}, u32[]{:S(2)}) async-start(bf16[32,64,128]{2,1,0:T(8,128)(2,1)} %edges.1.late_ref), calls=%async_computation | async-start | bytes 1048576 | tf_op jit(solution)/shard_map/edges/all_to_all | solution.py:286
  16.4 1.9 %collective-permute-start.1 = (bf16[192,256]{1,0:T(8,128)(2,1)S(1)}, bf16[192,256]{1,0:T(8,128)(2,1)S(1)}, u32[]{:S(2)}, u32[]{:S(2)}) collective-permute-start(bf16[192,256]{1,0:T(8,128)(2,1)S(1)} %get-tuple-element.22), channel_id=1, source_target_pairs={{0,1},{1,0},{2,3},{3,2},{4,5},{5,4},{6,7},{7,6},{8,9},{9,8},{10,11... | collective-permute-start | bytes 294920 | tf_op jit(solution)/shard_map/pieces/ppermute | solution.py:291
  18.3 4.7 %collective-permute-start.2 = (bf16[192,256]{1,0:T(8,128)(2,1)S(1)}, bf16[192,256]{1,0:T(8,128)(2,1)S(1)}, u32[]{:S(2)}, u32[]{:S(2)}) collective-permute-start(bf16[192,256]{1,0:T(8,128)(2,1)S(1)} %get-tuple-element.21), channel_id=1, source_target_pairs={{0,2},{1,3},{2,0},{3,1},{4,6},{5,7},{6,4},{7,5},{8,10},{9,11},{10,... | collective-permute-start | bytes 294920 | tf_op jit(solution)/shard_map/pieces/ppermute | solution.py:291
  23.0 2.7 %collective-permute-start.3 = (bf16[192,256]{1,0:T(8,128)(2,1)S(1)}, bf16[192,256]{1,0:T(8,128)(2,1)S(1)}, u32[]{:S(2)}, u32[]{:S(2)}) collective-permute-start(bf16[192,256]{1,0:T(8,128)(2,1)S(1)} %get-tuple-element.20), channel_id=1, source_target_pairs={{0,3},{1,2},{2,1},{3,0},{4,7},{5,6},{6,5},{7,4},{8,11},{9,10},{10,... | collective-permute-start | bytes 294920 | tf_op jit(solution)/shard_map/pieces/ppermute | solution.py:291
  25.7 8.1 %collective-permute-start = (bf16[64,512]{1,0:T(8,128)(2,1)S(1)}, bf16[64,512]{1,0:T(8,128)(2,1)S(1)}, u32[]{:S(2)}, u32[]{:S(2)}) collective-permute-start(bf16[64,512]{1,0:T(8,128)(2,1)S(1)} %get-tuple-element.11.cot_ref), channel_id=1, source_target_pairs={{0,4},{1,5},{2,6},{3,7},{4,0},{5,1},{6,2},{7,3},{8,12},{9,13},{10,... | collective-permute-start | bytes 196616 | tf_op jit(solution)/shard_map/pieces/ppermute | solution.py:291
  33.8 3.2 %collective-permute-done.far_ref = bf16[64,512]{1,0:T(8,128)(2,1)S(1)} collective-permute-done((bf16[64,512]{1,0:T(8,128)(2,1)S(1)}, bf16[64,512]{1,0:T(8,128)(2,1)S(1)}, u32[]{:S(2)}, u32[]{:S(2)}) %collective-permute-start) | collective-permute-done | bytes 65568 | tf_op jit(solution)/shard_map/pieces/ppermute | solution.py:291
  38.4 11.9 %all_to_all.35.mean_ref = bf16[4,48,512]{2,1,0:T(8,128)(2,1)S(1)} all-to-all(bf16[4,48,512]{2,1,0:T(8,128)(2,1)S(1)} %get-tuple-element.13), channel_id=1, replica_groups={{0,1,2,3},{4,5,6,7},{8,9,10,11},{12,13,14,15},{16,17,18,19},{20,21,22,2..., dimensions={0} | all-to-all | bytes 393216 | tf_op jit(solution)/shard_map/mean/all_to_all | solution.py:286
  51.4 11.4 %all-to-all-start.2 = ((bf16[4,64,512]{2,1,0:T(8,128)(2,1)}), bf16[4,64,512]{2,1,0:T(8,128)(2,1)S(1)}, u32[]{:S(2)}, u32[]{:S(2)}) async-start(bf16[4,64,512]{2,1,0:T(8,128)(2,1)} %first.2), calls=%async_computation.2 | async-start | bytes 524288 | tf_op jit(solution)/shard_map/first/all_to_all | solution.py:286
  62.8 12.2 %collective-permute-start.4 = (bf16[2,64,512]{2,1,0:T(8,128)(2,1)S(1)}, bf16[2,64,512]{2,1,0:T(8,128)(2,1)S(1)}, u32[]{:S(2)}, u32[]{:S(2)}) collective-permute-start(bf16[2,64,512]{2,1,0:T(8,128)(2,1)S(1)} %get-tuple-element.14.near_ref), channel_id=1, source_target_pairs={{0,8},{1,9},{2,10},{3,11},{4,12},{5,13},{6,14},{7,15},{8,0},{9,1},... | collective-permute-start | bytes 393224 | tf_op jit(solution)/shard_map/mean/ppermute | solution.py:291
  75.1 18.6 %collective-permute-done.4.late_ref.far_ref = bf16[2,64,512]{2,1,0:T(8,128)(2,1)S(1)} collective-permute-done((bf16[2,64,512]{2,1,0:T(8,128)(2,1)S(1)}, bf16[2,64,512]{2,1,0:T(8,128)(2,1)S(1)}, u32[]{:S(2)}, u32[]{:S(2)}) %collective-permute-start.4) | collective-permute-done | bytes 131104 | tf_op jit(solution)/shard_map/mean/ppermute | solution.py:291
  94.6 5.7 %all-to-all-start.3 = ((bf16[4,64,512]{2,1,0:T(8,128)(2,1)}), bf16[4,64,512]{2,1,0:T(8,128)(2,1)S(1)}, u32[]{:S(2)}, u32[]{:S(2)}) async-start(bf16[4,64,512]{2,1,0:T(8,128)(2,1)} %first.3), calls=%async_computation.3 | async-start | bytes 524288 | tf_op jit(solution)/shard_map/first/all_to_all | solution.py:286
  100.9 6.9 %all-to-all-done.3.hid_ref = bf16[4,64,512]{2,1,0:T(8,128)(2,1)S(1)} async-done(((bf16[4,64,512]{2,1,0:T(8,128)(2,1)}), bf16[4,64,512]{2,1,0:T(8,128)(2,1)S(1)}, u32[]{:S(2)}, u32[]{:S(2)}) %all-to-all-start.3) | async-done | bytes 262176 | tf_op jit(solution)/shard_map/first/all_to_all | solution.py:286
  109.6 9.5 %all-to-all-start.5 = ((bf16[32,32,128]{2,1,0:T(8,128)(2,1)}), bf16[32,32,128]{2,1,0:T(8,128)(2,1)S(1)}, u32[]{:S(2)}, u32[]{:S(2)}) async-start(bf16[32,32,128]{2,1,0:T(8,128)(2,1)} %get-tuple-element.16), calls=%async_computation.5 | async-start | bytes 524288 | tf_op jit(solution)/shard_map/grads/all_to_all | solution.py:286
  121.3 3.3 %collective-permute-start.6 = (bf16[128,256]{1,0:T(8,128)(2,1)S(1)}, bf16[128,256]{1,0:T(8,128)(2,1)S(1)}, u32[]{:S(2)}, u32[]{:S(2)}) collective-permute-start(bf16[128,256]{1,0:T(8,128)(2,1)S(1)} %get-tuple-element.24), channel_id=1, source_target_pairs={{0,2},{1,3},{2,0},{3,1},{4,6},{5,7},{6,4},{7,5},{8,10},{9,11},{10,... | collective-permute-start | bytes 196616 | tf_op jit(solution)/shard_map/second/ppermute | solution.py:291
  124.6 4.0 %collective-permute-start.7 = (bf16[128,256]{1,0:T(8,128)(2,1)S(1)}, bf16[128,256]{1,0:T(8,128)(2,1)S(1)}, u32[]{:S(2)}, u32[]{:S(2)}) collective-permute-start(bf16[128,256]{1,0:T(8,128)(2,1)S(1)} %get-tuple-element.23), channel_id=1, source_target_pairs={{0,3},{1,2},{2,1},{3,0},{4,7},{5,6},{6,5},{7,4},{8,11},{9,10},{10,... | collective-permute-start | bytes 196616 | tf_op jit(solution)/shard_map/second/ppermute | solution.py:291
  128.7 2.8 %collective-permute-done.7.p3_ref = bf16[128,256]{1,0:T(8,128)(2,1)S(1)} collective-permute-done((bf16[128,256]{1,0:T(8,128)(2,1)S(1)}, bf16[128,256]{1,0:T(8,128)(2,1)S(1)}, u32[]{:S(2)}, u32[]{:S(2)}) %collective-permute-start.7) | collective-permute-done | bytes 65568 | tf_op jit(solution)/shard_map/second/ppermute | solution.py:291
  132.6 3.8 %all-to-all-start.4 = ((bf16[4,64,512]{2,1,0:T(8,128)(2,1)}), bf16[4,64,512]{2,1,0:T(8,128)(2,1)S(1)}, u32[]{:S(2)}, u32[]{:S(2)}) async-start(bf16[4,64,512]{2,1,0:T(8,128)(2,1)} %second.4), calls=%async_computation.4 | async-start | bytes 524288 | tf_op jit(solution)/shard_map/second/all_to_all | solution.py:286
  138.3 4.2 %collective-permute-start.9 = (f32[8,128]{1,0:T(8,128)S(1)}, f32[8,128]{1,0:T(8,128)S(1)}, u32[]{:S(2)}, u32[]{:S(2)}) collective-permute-start(f32[8,128]{1,0:T(8,128)S(1)} %get-tuple-element.28), channel_id=1, source_target_pairs={{0,2},{1,3},{2,0},{3,1},{4,6},{5,7},{6,4},{7,5},{8,10},{9,11},{10,... | collective-permute-start | bytes 12296 | tf_op jit(solution)/shard_map/grads/ppermute | solution.py:291
  142.5 3.2 %collective-permute-start.10 = (f32[8,128]{1,0:T(8,128)S(1)}, f32[8,128]{1,0:T(8,128)S(1)}, u32[]{:S(2)}, u32[]{:S(2)}) collective-permute-start(f32[8,128]{1,0:T(8,128)S(1)} %get-tuple-element.27), channel_id=1, source_target_pairs={{0,3},{1,2},{2,1},{3,0},{4,7},{5,6},{6,5},{7,4},{8,11},{9,10},{10,... | collective-permute-start | bytes 12296 | tf_op jit(solution)/shard_map/grads/ppermute | solution.py:291
  145.7 4.0 %collective-permute-done.10.p3_ref = f32[8,128]{1,0:T(8,128)S(1)} collective-permute-done((f32[8,128]{1,0:T(8,128)S(1)}, f32[8,128]{1,0:T(8,128)S(1)}, u32[]{:S(2)}, u32[]{:S(2)}) %collective-permute-start.10) | collective-permute-done | bytes 4128 | tf_op jit(solution)/shard_map/grads/ppermute | solution.py:291
  149.8 2.9 %all-to-all-done.4.parts_ref.late_ref = bf16[4,64,512]{2,1,0:T(8,128)(2,1)S(1)} async-done(((bf16[4,64,512]{2,1,0:T(8,128)(2,1)}), bf16[4,64,512]{2,1,0:T(8,128)(2,1)S(1)}, u32[]{:S(2)}, u32[]{:S(2)}) %all-to-all-start.4) | async-done | bytes 262176 | tf_op jit(solution)/shard_map/second/all_to_all | solution.py:286
  153.5 11.1 %all-to-all-start.6 = ((f32[32,32,128]{2,1,0:T(8,128)}), f32[32,32,128]{2,1,0:T(8,128)S(1)}, u32[]{:S(2)}, u32[]{:S(2)}) async-start(f32[32,32,128]{2,1,0:T(8,128)} %place.2), calls=%async_computation.6 | async-start | bytes 1048576 | tf_op jit(solution)/shard_map/place/all_to_all | solution.py:286
  166.1 10.1 %all-to-all-done.6.pieces_ref = f32[32,32,128]{2,1,0:T(8,128)S(1)} async-done(((f32[32,32,128]{2,1,0:T(8,128)}), f32[32,32,128]{2,1,0:T(8,128)S(1)}, u32[]{:S(2)}, u32[]{:S(2)}) %all-to-all-start.6) | async-done | bytes 524320 | tf_op jit(solution)/shard_map/place/all_to_all | solution.py:286
  (56 shorter events, 16.0 us)
Async XLA Ops:
  5.6 10.6 %copy-start.3 = (bf16[48,1024]{1,0:T(8,128)(2,1)S(1)}, bf16[48,1024]{1,0:T(8,128)(2,1)}, u32[]{:S(2)}) copy-start(bf16[48,1024]{1,0:T(8,128)(2,1)} %neigh_ref.2) | copy-start | bytes 294916
  5.6 10.6 %copy-start.4 = (bf16[48,1024]{1,0:T(8,128)(2,1)S(1)}, bf16[48,1024]{1,0:T(8,128)(2,1)}, u32[]{:S(2)}) copy-start(bf16[48,1024]{1,0:T(8,128)(2,1)} %own_ref.2) | copy-start | bytes 294916
  5.6 10.6 %copy-start.5 = (bf16[512,64]{0,1:T(8,128)(2,1)S(1)}, bf16[512,64]{0,1:T(8,128)(2,1)}, u32[]{:S(2)}) copy-start(bf16[512,64]{0,1:T(8,128)(2,1)} %param.25) | copy-start | bytes 196612
  5.6 10.6 %copy-start.6 = (bf16[512,48]{0,1:T(8,128)(2,1)S(1)}, bf16[512,48]{0,1:T(8,128)(2,1)}, u32[]{:S(2)}) copy-start(bf16[512,48]{0,1:T(8,128)(2,1)} %param.15) | copy-start | bytes 147460
  5.6 31.4 %all-to-all-start = ((bf16[32,64,128]{2,1,0:T(8,128)(2,1)}), bf16[32,64,128]{2,1,0:T(8,128)(2,1)S(1)}, u32[]{:S(2)}, u32[]{:S(2)}) async-start(bf16[32,64,128]{2,1,0:T(8,128)(2,1)} %edges.1.late_ref), calls=%async_computation | async-start | bytes 1048576 | tf_op jit(solution)/shard_map/edges/all_to_all | solution.py:286
  16.4 20.6 %collective-permute-start.1 = (bf16[192,256]{1,0:T(8,128)(2,1)S(1)}, bf16[192,256]{1,0:T(8,128)(2,1)S(1)}, u32[]{:S(2)}, u32[]{:S(2)}) collective-permute-start(bf16[192,256]{1,0:T(8,128)(2,1)S(1)} %get-tuple-element.22), channel_id=1, source_target_pairs={{0,1},{1,0},{2,3},{3,2},{4,5},{5,4},{6,7},{7,6},{8,9},{9,8},{10,11... | collective-permute-start | bytes 294920 | tf_op jit(solution)/shard_map/pieces/ppermute | solution.py:291
  18.3 18.7 %collective-permute-start.2 = (bf16[192,256]{1,0:T(8,128)(2,1)S(1)}, bf16[192,256]{1,0:T(8,128)(2,1)S(1)}, u32[]{:S(2)}, u32[]{:S(2)}) collective-permute-start(bf16[192,256]{1,0:T(8,128)(2,1)S(1)} %get-tuple-element.21), channel_id=1, source_target_pairs={{0,2},{1,3},{2,0},{3,1},{4,6},{5,7},{6,4},{7,5},{8,10},{9,11},{10,... | collective-permute-start | bytes 294920 | tf_op jit(solution)/shard_map/pieces/ppermute | solution.py:291
  23.0 14.0 %collective-permute-start.3 = (bf16[192,256]{1,0:T(8,128)(2,1)S(1)}, bf16[192,256]{1,0:T(8,128)(2,1)S(1)}, u32[]{:S(2)}, u32[]{:S(2)}) collective-permute-start(bf16[192,256]{1,0:T(8,128)(2,1)S(1)} %get-tuple-element.20), channel_id=1, source_target_pairs={{0,3},{1,2},{2,1},{3,0},{4,7},{5,6},{6,5},{7,4},{8,11},{9,10},{10,... | collective-permute-start | bytes 294920 | tf_op jit(solution)/shard_map/pieces/ppermute | solution.py:291
  25.7 11.3 %collective-permute-start = (bf16[64,512]{1,0:T(8,128)(2,1)S(1)}, bf16[64,512]{1,0:T(8,128)(2,1)S(1)}, u32[]{:S(2)}, u32[]{:S(2)}) collective-permute-start(bf16[64,512]{1,0:T(8,128)(2,1)S(1)} %get-tuple-element.11.cot_ref), channel_id=1, source_target_pairs={{0,4},{1,5},{2,6},{3,7},{4,0},{5,1},{6,2},{7,3},{8,12},{9,13},{10,... | collective-permute-start | bytes 196616 | tf_op jit(solution)/shard_map/pieces/ppermute | solution.py:291
  51.4 42.4 %all-to-all-start.2 = ((bf16[4,64,512]{2,1,0:T(8,128)(2,1)}), bf16[4,64,512]{2,1,0:T(8,128)(2,1)S(1)}, u32[]{:S(2)}, u32[]{:S(2)}) async-start(bf16[4,64,512]{2,1,0:T(8,128)(2,1)} %first.2), calls=%async_computation.2 | async-start | bytes 524288 | tf_op jit(solution)/shard_map/first/all_to_all | solution.py:286
  62.8 12.2 %copy-start.11 = (f32[64]{0:T(128)S(1)}, f32[64]{0:T(128)}, u32[]{:S(2)}) copy-start(f32[64]{0:T(128)} %param.18) | copy-start | bytes 772
  62.8 30.9 %collective-permute-start.4 = (bf16[2,64,512]{2,1,0:T(8,128)(2,1)S(1)}, bf16[2,64,512]{2,1,0:T(8,128)(2,1)S(1)}, u32[]{:S(2)}, u32[]{:S(2)}) collective-permute-start(bf16[2,64,512]{2,1,0:T(8,128)(2,1)S(1)} %get-tuple-element.14.near_ref), channel_id=1, source_target_pairs={{0,8},{1,9},{2,10},{3,11},{4,12},{5,13},{6,14},{7,15},{8,0},{9,1},... | collective-permute-start | bytes 393224 | tf_op jit(solution)/shard_map/mean/ppermute | solution.py:291
  94.6 13.3 %copy-start = (bf16[4,128,128]{2,1,0:T(8,128)(2,1)S(1)}, bf16[4,128,128]{2,1,0:T(8,128)(2,1)}, u32[]{:S(2)}) copy-start(bf16[4,128,128]{2,1,0:T(8,128)(2,1)} %values_ref.1) | copy-start | bytes 393220
  94.6 13.3 %all-to-all-start.3 = ((bf16[4,64,512]{2,1,0:T(8,128)(2,1)}), bf16[4,64,512]{2,1,0:T(8,128)(2,1)S(1)}, u32[]{:S(2)}, u32[]{:S(2)}) async-start(bf16[4,64,512]{2,1,0:T(8,128)(2,1)} %first.3), calls=%async_computation.3 | async-start | bytes 524288 | tf_op jit(solution)/shard_map/first/all_to_all | solution.py:286
  109.6 9.6 %copy-start.2 = (bf16[64,1024]{1,0:T(8,128)(2,1)S(1)}, bf16[64,1024]{1,0:T(8,128)(2,1)}, u32[]{:S(2)}) copy-start(bf16[64,1024]{1,0:T(8,128)(2,1)} %own_ref.3) | copy-start | bytes 393220
  109.6 22.9 %all-to-all-start.5 = ((bf16[32,32,128]{2,1,0:T(8,128)(2,1)}), bf16[32,32,128]{2,1,0:T(8,128)(2,1)S(1)}, u32[]{:S(2)}, u32[]{:S(2)}) async-start(bf16[32,32,128]{2,1,0:T(8,128)(2,1)} %get-tuple-element.16), calls=%async_computation.5 | async-start | bytes 524288 | tf_op jit(solution)/shard_map/grads/all_to_all | solution.py:286
  119.4 9.3 %collective-permute-start.5 = (bf16[128,256]{1,0:T(8,128)(2,1)S(1)}, bf16[128,256]{1,0:T(8,128)(2,1)S(1)}, u32[]{:S(2)}, u32[]{:S(2)}) collective-permute-start(bf16[128,256]{1,0:T(8,128)(2,1)S(1)} %get-tuple-element.25), channel_id=1, source_target_pairs={{0,1},{1,0},{2,3},{3,2},{4,5},{5,4},{6,7},{7,6},{8,9},{9,8},{10,11... | collective-permute-start | bytes 196616 | tf_op jit(solution)/shard_map/second/ppermute | solution.py:291
  121.3 7.4 %collective-permute-start.6 = (bf16[128,256]{1,0:T(8,128)(2,1)S(1)}, bf16[128,256]{1,0:T(8,128)(2,1)S(1)}, u32[]{:S(2)}, u32[]{:S(2)}) collective-permute-start(bf16[128,256]{1,0:T(8,128)(2,1)S(1)} %get-tuple-element.24), channel_id=1, source_target_pairs={{0,2},{1,3},{2,0},{3,1},{4,6},{5,7},{6,4},{7,5},{8,10},{9,11},{10,... | collective-permute-start | bytes 196616 | tf_op jit(solution)/shard_map/second/ppermute | solution.py:291
  124.6 6.9 %collective-permute-start.7 = (bf16[128,256]{1,0:T(8,128)(2,1)S(1)}, bf16[128,256]{1,0:T(8,128)(2,1)S(1)}, u32[]{:S(2)}, u32[]{:S(2)}) collective-permute-start(bf16[128,256]{1,0:T(8,128)(2,1)S(1)} %get-tuple-element.23), channel_id=1, source_target_pairs={{0,3},{1,2},{2,1},{3,0},{4,7},{5,6},{6,5},{7,4},{8,11},{9,10},{10,... | collective-permute-start | bytes 196616 | tf_op jit(solution)/shard_map/second/ppermute | solution.py:291
  132.6 20.1 %all-to-all-start.4 = ((bf16[4,64,512]{2,1,0:T(8,128)(2,1)}), bf16[4,64,512]{2,1,0:T(8,128)(2,1)S(1)}, u32[]{:S(2)}, u32[]{:S(2)}) async-start(bf16[4,64,512]{2,1,0:T(8,128)(2,1)} %second.4), calls=%async_computation.4 | async-start | bytes 524288 | tf_op jit(solution)/shard_map/second/all_to_all | solution.py:286
  136.4 9.3 %collective-permute-start.8 = (f32[8,128]{1,0:T(8,128)S(1)}, f32[8,128]{1,0:T(8,128)S(1)}, u32[]{:S(2)}, u32[]{:S(2)}) collective-permute-start(f32[8,128]{1,0:T(8,128)S(1)} %get-tuple-element.29), channel_id=1, source_target_pairs={{0,1},{1,0},{2,3},{3,2},{4,5},{5,4},{6,7},{7,6},{8,9},{9,8},{10,11... | collective-permute-start | bytes 12296 | tf_op jit(solution)/shard_map/grads/ppermute | solution.py:291
  138.3 7.4 %collective-permute-start.9 = (f32[8,128]{1,0:T(8,128)S(1)}, f32[8,128]{1,0:T(8,128)S(1)}, u32[]{:S(2)}, u32[]{:S(2)}) collective-permute-start(f32[8,128]{1,0:T(8,128)S(1)} %get-tuple-element.28), channel_id=1, source_target_pairs={{0,2},{1,3},{2,0},{3,1},{4,6},{5,7},{6,4},{7,5},{8,10},{9,11},{10,... | collective-permute-start | bytes 12296 | tf_op jit(solution)/shard_map/grads/ppermute | solution.py:291
  142.5 7.2 %collective-permute-start.10 = (f32[8,128]{1,0:T(8,128)S(1)}, f32[8,128]{1,0:T(8,128)S(1)}, u32[]{:S(2)}, u32[]{:S(2)}) collective-permute-start(f32[8,128]{1,0:T(8,128)S(1)} %get-tuple-element.27), channel_id=1, source_target_pairs={{0,3},{1,2},{2,1},{3,0},{4,7},{5,6},{6,5},{7,4},{8,11},{9,10},{10,... | collective-permute-start | bytes 12296 | tf_op jit(solution)/shard_map/grads/ppermute | solution.py:291
  153.5 22.6 %all-to-all-start.6 = ((f32[32,32,128]{2,1,0:T(8,128)}), f32[32,32,128]{2,1,0:T(8,128)S(1)}, u32[]{:S(2)}, u32[]{:S(2)}) async-start(f32[32,32,128]{2,1,0:T(8,128)} %place.2), calls=%async_computation.6 | async-start | bytes 1048576 | tf_op jit(solution)/shard_map/place/all_to_all | solution.py:286
  (6 other events, 18.2 us)

commit v4 on v3

--- a/solution.py
+++ b/solution.py
@@ -80,7 +80,7 @@
     return sets
 
 
-def first_pieces_kernel(mine_ref, neigh_ref, own_ref, self_ref, cot_ref, late_ref, out_ref, cot_out_ref):
+def first_pieces_kernel(mine_ref, neigh_ref, own_ref, self_ref, late_ref, out_ref):
     del late_ref
     mine = mine_ref[0]
     rows = neigh_ref.shape[0]
@@ -92,7 +92,6 @@
         out_ref[to, rows : 2 * rows, :] = own
         out_ref[to, 2 * rows : 3 * rows, :] = self_ref[:, :width]
         out_ref[to, 3 * rows :, :] = self_ref[:, width:]
-    cot_out_ref[...] = cot_ref[...]
 
 
 def second_pieces_kernel(mine_ref, neigh_ref, own_ref, late_ref, out_ref):
@@ -106,7 +105,7 @@
         out_ref[to, rows:, :] = own
 
 
-def mean_kernel(cols, recv_ref, cot_ref, far_ref, late1_ref, late2_ref, late3_ref, out_ref, cots_ref):
+def mean_kernel(cols, recv_ref, late1_ref, late2_ref, late3_ref, out_ref):
     del late1_ref, late2_ref, late3_ref
     groups, rows, cap = recv_ref.shape
     targets = out_ref.shape[2]
@@ -124,11 +123,11 @@
     mean = (acc[:cols, :] / degree).astype(BF)
     for j in range(out_ref.shape[0]):
         out_ref[j] = mean
-    cots_ref[0] = cot_ref[...]
-    cots_ref[1] = far_ref[...]
-
-
-def first_kernel(mine_ref, mean_ref, p0_ref, p1_ref, p2_ref, p3_ref, out_ref, weight, acts):
+
+
+def first_kernel(
+    mine_ref, mean_ref, p0_ref, p1_ref, p2_ref, p3_ref, cot_ref, out_ref, weight, acts
+):
     mine = mine_ref[0]
     group, rows, targets = mean_ref.shape
     width = targets // 2
@@ -140,30 +139,27 @@
         acts[mid : mid + rows, :width] = piece[2 * rows : 3 * rows, :]
         acts[mid : mid + rows, width:] = piece[3 * rows :, :]
     total = lax.dot_general(weight[...], acts[...], TN, preferred_element_type=F32)
-    n, cols, _ = out_ref.shape
-    for z in range(n):
-        out_ref[z] = total[z * cols : (z + 1) * cols, :].astype(BF)
-
-
-def hidden_kernel(parts_ref, bias_ref, late_ref, out_ref):
-    del late_ref
-    total = parts_ref[0].astype(F32)
+    cols = cot_ref.shape[0]
+    for z in range(out_ref.shape[0]):
+        out_ref[z, :cols, :] = total[z * cols : (z + 1) * cols, :].astype(BF)
+        out_ref[z, cols:, :] = cot_ref[...]
+
+
+def hidden_kernel(parts_ref, bias_ref, late1_ref, late2_ref, late3_ref, out_ref):
+    del late1_ref, late2_ref, late3_ref
+    cols = bias_ref.shape[0]
+    total = parts_ref[0, :cols, :].astype(F32)
     for k in range(1, parts_ref.shape[0]):
-        total = total + parts_ref[k].astype(F32)
+        total = total + parts_ref[k, :cols, :].astype(F32)
     hidden = jnp.maximum(total + bias_ref[...], 0.0).astype(BF)
     for c in range(out_ref.shape[0]):
         out_ref[c] = hidden
 
 
-def grad_kernel(
-    place_ref, index_ref, hid_ref, values_ref, live_ref, near_ref, far_ref, agg_ref, out_ref, left, cot, acc
-):
+def grad_kernel(index_ref, hid_ref, values_ref, live_ref, parts_ref, agg_ref, out_ref, left, acc):
     group, cols, targets = hid_ref.shape
     width = values_ref.shape[1]
     wide = group * cols
-    across = place_ref[0]
-    for k, ref in enumerate((near_ref, near_ref, far_ref, far_ref)):
-        cot[jnp.bitwise_xor(across, k)] = ref[k % 2]
     acc[...] = jnp.zeros_like(acc)
     for k in range(values_ref.shape[0]):
         source = index_ref[k, 1]
@@ -179,7 +175,7 @@
         left[:wide, at] = tile * live[:, at]
     for j in range(group):
         left[wide + j * cols : wide + (j + 1) * cols, :] = hid_ref[j] * live
-    right = jnp.concatenate([cot[j] for j in range(group)], axis=0)
+    right = jnp.concatenate([parts_ref[j, cols:, :] for j in range(parts_ref.shape[0])], axis=0)
     block = lax.dot_general(left[...], right, NT, preferred_element_type=F32)
     at = 0
     for w in range(2):
@@ -279,7 +275,6 @@
     far = [[i + GROUP * j for j in range(blocks)] for i in range(GROUP)]
     z = lax.axis_index("feat")
     mine = (z % GROUP).reshape(1)
-    across = (z // GROUP).reshape(1)
     live = seed_live.reshape(1, targets).astype(F32)
 
     def swap(x, axis, among=None):
@@ -304,71 +299,70 @@
         )(edge_feats.T, edge_dst.reshape(-1, 128))
         recv = swap(send, "dp")
     with jax.named_scope("pieces"):
-        pieces, cot = call(
+        pieces = call(
             first_pieces_kernel,
-            (shape(GROUP, 4 * cols, wide), shape(hid, targets)),
-            6,
-            smem=(0,),
-            late=(5,),
+            shape(GROUP, 4 * cols, wide),
+            5,
+            smem=(0,),
+            late=(4,),
             nbytes=2 << 20,
-        )(mine, neigh_one, self_one, self_feats.T, cotangent.T, send)
+        )(mine, neigh_one, self_one, self_feats.T, send)
         got = [trade(pieces[k], k) for k in range(1, GROUP)]
-        cot_far = trade(cot, GROUP)
     with jax.named_scope("mean"):
-        mean, cots = call(
+        mean = call(
             functools.partial(mean_kernel, cols),
-            (shape(GROUP, cols, targets), shape(2, hid, targets)),
-            6,
-            late=(3, 4, 5),
+            shape(GROUP, cols, targets),
+            4,
+            late=(1, 2, 3),
             flops=2 * groups * ROWS * cap * targets,
             nbytes=8 << 20,
-        )(recv, cot, cot_far, *got)
-        cots_far = trade(cots, 2 * GROUP)
+        )(recv, *got)
         mean = swap(mean, "feat", near)
     with jax.named_scope("first"):
         first = call(
             first_kernel,
-            shape(blocks, hid, targets),
-            6,
+            shape(blocks, 2 * hid, targets),
+            7,
             scratch=[pltpu.VMEM((8 * cols, wide), BF), pltpu.VMEM((8 * cols, targets), BF)],
             smem=(0,),
             flops=2 * 8 * cols * wide * targets,
             nbytes=2 << 20,
-        )(mine, mean, pieces[0], *got)
-        first = swap(first, "feat", far)
+        )(mine, mean, pieces[0], *got, cotangent.T)
+        parts = swap(first, "feat", far)
+    with jax.named_scope("pieces"):
+        pieces = call(
+            second_pieces_kernel,
+            shape(GROUP, 2 * hid, wide),
+            4,
+            smem=(0,),
+            late=(3,),
+            nbytes=1 << 20,
+        )(mine, neigh_two, self_two, first)
+        got = [trade(pieces[k], k) for k in range(1, GROUP)]
+    with jax.named_scope("hidden"):
         hidden = call(
-            hidden_kernel, shape(GROUP, hid, targets), 3, late=(2,), nbytes=1 << 20
-        )(first, bias_one.reshape(hid, 1), cots_far)
+            hidden_kernel, shape(GROUP, hid, targets), 5, late=(2, 3, 4), nbytes=1 << 20
+        )(parts, bias_one.reshape(hid, 1), *got)
         hidden = swap(hidden, "feat", near)
     with jax.named_scope("grads"):
         agg, terms = call(
             grad_kernel,
             (shape(wide, targets), shape(groups, GROUP * 8, 128)),
-            7,
+            5,
             scratch=[
                 pltpu.VMEM((2 * wide, targets), BF),
-                pltpu.VMEM((blocks, hid, targets), BF),
                 pltpu.VMEM((targets // 128, wide, 128), F32),
             ],
-            smem=(0, 1),
+            smem=(0,),
             flops=2 * 2 * wide * targets * wide,
             nbytes=4 << 20,
-        )(across, tile_index, hidden, tile_values, live, cots, cots_far)
+        )(tile_index, hidden, tile_values, live, parts)
         terms = swap(terms, "dp")
         mine_sum = call(
             sum_kernel, shape(GROUP, 8, 128, dtype=F32), 2, smem=(0,), nbytes=1 << 20
         )(mine, terms)
         sums = [mine_sum[0]] + [trade(mine_sum[k], k) for k in range(1, GROUP)]
     with jax.named_scope("second"):
-        pieces = call(
-            second_pieces_kernel,
-            shape(GROUP, 2 * hid, wide),
-            4,
-            smem=(0,),
-            late=(3,),
-            nbytes=1 << 20,
-        )(mine, neigh_two, self_two, agg)
-        got = [trade(pieces[k], k) for k in range(1, GROUP)]
         second = call(
             second_kernel,
             shape(blocks, hid, targets),

time: 178 us -> 166 us (0.933)
  starting transfers between devices: 100 us -> 88.7 us
  blocking collectives: 11.9 us -> 9.68 us
    ppermute x11 -> x9, starting transfers between devices: 48.1 us -> 27.8 us  [trade(): return lax.ppermute(x, 'feat', [(i, i ^ k) for i in range(n_feat)])]
    all_to_all x6, starting transfers between devices: 52 us -> 60.9 us  [swap(): lax.all_to_all(x, axis, split_axis=0, concat_axis=0, tiled=True, axis_ind...]
    all_to_all x6, waiting for transfers between devices: 19.9 us -> 24.9 us  [swap(): lax.all_to_all(x, axis, split_axis=0, concat_axis=0, tiled=True, axis_ind...]
    ppermute x11 -> x9, waiting for transfers between devices: 28.8 us -> 25.3 us  [trade(): return lax.ppermute(x, 'feat', [(i, i ^ k) for i in range(n_feat)])]
    all_to_all x1, blocking collectives: 11.9 us -> 9.68 us  [swap(): lax.all_to_all(x, axis, split_axis=0, concat_axis=0, tiled=True, axis_ind...]
  transfers between devices with their start and end apart: 17 -> 15, of which waited for: 7 -> 9; matrix products, arithmetic and copies ran while one was open for 0% -> 0% of each run, Pallas kernels for 1% -> 1%
where the time goes in v4:
time: 166 us; the launch traced here: 165 us
  starting transfers between devices  88.7 us (53%)
  waiting for transfers between devices  50.3 us (30%)
  Pallas kernels  12.3 us (7%)
  blocking collectives  9.68 us (6%)
  local copies, waits for them, and re-layouts  3.32 us (2%)
    all_to_all x6, starting transfers between devices, swap(): lax.all_to_all(x, axis, split_axis=0, concat_axis=0, tiled=True, axis_ind...  60.9 us
    ppermute x9, starting transfers between devices, trade(): return lax.ppermute(x, 'feat', [(i, i ^ k) for i in range(n_feat)])  27.8 us
    ppermute x9, waiting for transfers between devices, trade(): return lax.ppermute(x, 'feat', [(i, i ^ k) for i in range(n_feat)])  25.3 us
    all_to_all x6, waiting for transfers between devices, swap(): lax.all_to_all(x, axis, split_axis=0, concat_axis=0, tiled=True, axis_ind...  24.9 us
    all_to_all x1, blocking collectives, swap(): lax.all_to_all(x, axis, split_axis=0, concat_axis=0, tiled=True, axis_ind...  9.68 us
    pallas_call x1, Pallas kernels, body(): call(functools.partial(pack_kernel, groups, targets), shape(groups, ROWS,...  3.33 us
  transfers between devices with their start and end apart: 15, of which 9 were waited for; matrix products, arithmetic and copies ran while one was open for 0% of the time, Pallas kernels for 1%

profile of v4, /device:TPU:1, one launch (start us, length us, event | category | flops | bytes accessed | tf_op | source)
XLA Modules:
  0.0 165.2 jit_solution(438728987920514865)
XLA Ops:
  2.3 3.3 %edges.1.late_ref = bf16[32,64,128]{2,1,0:T(8,128)(2,1)} custom-call(bf16[48,2048]{1,0:T(8,128)(2,1)S(1)} %bitcast.37, s32[16,128]{1,0:T(8,128)S(1)} %bitcast.38), custom_call_target="tpu_custom_call" | custom-call | flops 1073741824 | bytes 8388608 | tf_op jit(solution)/shard_map/edges/pallas_call | solution.py:292
  5.6 10.6 %all-to-all-start = ((bf16[32,64,128]{2,1,0:T(8,128)(2,1)}), bf16[32,64,128]{2,1,0:T(8,128)(2,1)S(1)}, u32[]{:S(2)}, u32[]{:S(2)}) async-start(bf16[32,64,128]{2,1,0:T(8,128)(2,1)} %edges.1.late_ref), calls=%async_computation | async-start | bytes 1048576 | tf_op jit(solution)/shard_map/edges/all_to_all | solution.py:281
  18.3 4.7 %collective-permute-start.1 = (bf16[192,256]{1,0:T(8,128)(2,1)S(1)}, bf16[192,256]{1,0:T(8,128)(2,1)S(1)}, u32[]{:S(2)}, u32[]{:S(2)}) collective-permute-start(bf16[192,256]{1,0:T(8,128)(2,1)S(1)} %get-tuple-element.13), channel_id=1, source_target_pairs={{0,2},{1,3},{2,0},{3,1},{4,6},{5,7},{6,4},{7,5},{8,10},{9,11},{10,... | collective-permute-start | bytes 294920 | tf_op jit(solution)/shard_map/pieces/ppermute | solution.py:286
  23.0 2.7 %collective-permute-start.2 = (bf16[192,256]{1,0:T(8,128)(2,1)S(1)}, bf16[192,256]{1,0:T(8,128)(2,1)S(1)}, u32[]{:S(2)}, u32[]{:S(2)}) collective-permute-start(bf16[192,256]{1,0:T(8,128)(2,1)S(1)} %get-tuple-element.12), channel_id=1, source_target_pairs={{0,3},{1,2},{2,1},{3,0},{4,7},{5,6},{6,5},{7,4},{8,11},{9,10},{10,... | collective-permute-start | bytes 294920 | tf_op jit(solution)/shard_map/pieces/ppermute | solution.py:286
  25.7 2.1 %collective-permute-done.1.late2_ref.p2_ref = bf16[192,256]{1,0:T(8,128)(2,1)S(1)} collective-permute-done((bf16[192,256]{1,0:T(8,128)(2,1)S(1)}, bf16[192,256]{1,0:T(8,128)(2,1)S(1)}, u32[]{:S(2)}, u32[]{:S(2)}) %collective-permute-start.1) | collective-permute-done | bytes 98336 | tf_op jit(solution)/shard_map/pieces/ppermute | solution.py:286
  27.8 2.5 %collective-permute-done.2.late3_ref.p3_ref = bf16[192,256]{1,0:T(8,128)(2,1)S(1)} collective-permute-done((bf16[192,256]{1,0:T(8,128)(2,1)S(1)}, bf16[192,256]{1,0:T(8,128)(2,1)S(1)}, u32[]{:S(2)}, u32[]{:S(2)}) %collective-permute-start.2) | collective-permute-done | bytes 98336 | tf_op jit(solution)/shard_map/pieces/ppermute | solution.py:286
  31.7 9.7 %all_to_all.35.mean_ref = bf16[4,48,512]{2,1,0:T(8,128)(2,1)S(1)} all-to-all(bf16[4,48,512]{2,1,0:T(8,128)(2,1)S(1)} %mean.1), channel_id=1, replica_groups={{0,1,2,3},{4,5,6,7},{8,9,10,11},{12,13,14,15},{16,17,18,19},{20,21,22,2..., dimensions={0} | all-to-all | bytes 393216 | tf_op jit(solution)/shard_map/mean/all_to_all | solution.py:281
  42.5 13.2 %all-to-all-start.2 = ((bf16[4,128,512]{2,1,0:T(8,128)(2,1)}), bf16[4,128,512]{2,1,0:T(8,128)(2,1)S(1)}, u32[]{:S(2)}, u32[]{:S(2)}) async-start(bf16[4,128,512]{2,1,0:T(8,128)(2,1)} %first.1.late_ref), calls=%async_computation.2 | async-start | bytes 1048576 | tf_op jit(solution)/shard_map/first/all_to_all | solution.py:281
  55.8 2.5 %collective-permute-start.3 = (bf16[128,256]{1,0:T(8,128)(2,1)S(1)}, bf16[128,256]{1,0:T(8,128)(2,1)S(1)}, u32[]{:S(2)}, u32[]{:S(2)}) collective-permute-start(bf16[128,256]{1,0:T(8,128)(2,1)S(1)} %get-tuple-element.18), channel_id=1, source_target_pairs={{0,1},{1,0},{2,3},{3,2},{4,5},{5,4},{6,7},{7,6},{8,9},{9,8},{10,11... | collective-permute-start | bytes 196616 | tf_op jit(solution)/shard_map/pieces/ppermute | solution.py:286
  58.4 4.4 %collective-permute-start.4 = (bf16[128,256]{1,0:T(8,128)(2,1)S(1)}, bf16[128,256]{1,0:T(8,128)(2,1)S(1)}, u32[]{:S(2)}, u32[]{:S(2)}) collective-permute-start(bf16[128,256]{1,0:T(8,128)(2,1)S(1)} %get-tuple-element.17), channel_id=1, source_target_pairs={{0,2},{1,3},{2,0},{3,1},{4,6},{5,7},{6,4},{7,5},{8,10},{9,11},{10,... | collective-permute-start | bytes 196616 | tf_op jit(solution)/shard_map/pieces/ppermute | solution.py:286
  62.8 2.3 %collective-permute-start.5 = (bf16[128,256]{1,0:T(8,128)(2,1)S(1)}, bf16[128,256]{1,0:T(8,128)(2,1)S(1)}, u32[]{:S(2)}, u32[]{:S(2)}) collective-permute-start(bf16[128,256]{1,0:T(8,128)(2,1)S(1)} %get-tuple-element.16), channel_id=1, source_target_pairs={{0,3},{1,2},{2,1},{3,0},{4,7},{5,6},{6,5},{7,4},{8,11},{9,10},{10,... | collective-permute-start | bytes 196616 | tf_op jit(solution)/shard_map/pieces/ppermute | solution.py:286
  65.3 13.7 %collective-permute-done.3.late1_ref.p1_ref = bf16[128,256]{1,0:T(8,128)(2,1)S(1)} collective-permute-done((bf16[128,256]{1,0:T(8,128)(2,1)S(1)}, bf16[128,256]{1,0:T(8,128)(2,1)S(1)}, u32[]{:S(2)}, u32[]{:S(2)}) %collective-permute-start.3) | collective-permute-done | bytes 65568 | tf_op jit(solution)/shard_map/pieces/ppermute | solution.py:286
  78.9 3.0 %collective-permute-done.5.late3_ref.p3_ref = bf16[128,256]{1,0:T(8,128)(2,1)S(1)} collective-permute-done((bf16[128,256]{1,0:T(8,128)(2,1)S(1)}, bf16[128,256]{1,0:T(8,128)(2,1)S(1)}, u32[]{:S(2)}, u32[]{:S(2)}) %collective-permute-start.5) | collective-permute-done | bytes 65568 | tf_op jit(solution)/shard_map/pieces/ppermute | solution.py:286
  82.8 9.2 %all-to-all-start.3 = ((bf16[4,64,512]{2,1,0:T(8,128)(2,1)}), bf16[4,64,512]{2,1,0:T(8,128)(2,1)S(1)}, u32[]{:S(2)}, u32[]{:S(2)}) async-start(bf16[4,64,512]{2,1,0:T(8,128)(2,1)} %hidden.1), calls=%async_computation.3 | async-start | bytes 524288 | tf_op jit(solution)/shard_map/hidden/all_to_all | solution.py:281
  92.8 4.9 %all-to-all-done.3.hid_ref = bf16[4,64,512]{2,1,0:T(8,128)(2,1)S(1)} async-done(((bf16[4,64,512]{2,1,0:T(8,128)(2,1)}), bf16[4,64,512]{2,1,0:T(8,128)(2,1)S(1)}, u32[]{:S(2)}, u32[]{:S(2)}) %all-to-all-start.3) | async-done | bytes 262176 | tf_op jit(solution)/shard_map/hidden/all_to_all | solution.py:281
  99.4 12.2 %all-to-all-start.5 = ((bf16[32,32,128]{2,1,0:T(8,128)(2,1)}), bf16[32,32,128]{2,1,0:T(8,128)(2,1)S(1)}, u32[]{:S(2)}, u32[]{:S(2)}) async-start(bf16[32,32,128]{2,1,0:T(8,128)(2,1)} %get-tuple-element.8), calls=%async_computation.5 | async-start | bytes 524288 | tf_op jit(solution)/shard_map/grads/all_to_all | solution.py:281
  112.7 7.8 %all-to-all-done.5.terms_ref = bf16[32,32,128]{2,1,0:T(8,128)(2,1)S(1)} async-done(((bf16[32,32,128]{2,1,0:T(8,128)(2,1)}), bf16[32,32,128]{2,1,0:T(8,128)(2,1)S(1)}, u32[]{:S(2)}, u32[]{:S(2)}) %all-to-all-start.5) | async-done | bytes 262176 | tf_op jit(solution)/shard_map/grads/all_to_all | solution.py:281
  120.6 7.2 %all-to-all-start.4 = ((bf16[4,64,512]{2,1,0:T(8,128)(2,1)}), bf16[4,64,512]{2,1,0:T(8,128)(2,1)S(1)}, u32[]{:S(2)}, u32[]{:S(2)}) async-start(bf16[4,64,512]{2,1,0:T(8,128)(2,1)} %second.2), calls=%async_computation.4 | async-start | bytes 524288 | tf_op jit(solution)/shard_map/second/all_to_all | solution.py:281
  129.8 3.3 %collective-permute-start.7 = (f32[8,128]{1,0:T(8,128)S(1)}, f32[8,128]{1,0:T(8,128)S(1)}, u32[]{:S(2)}, u32[]{:S(2)}) collective-permute-start(f32[8,128]{1,0:T(8,128)S(1)} %get-tuple-element.20), channel_id=1, source_target_pairs={{0,2},{1,3},{2,0},{3,1},{4,6},{5,7},{6,4},{7,5},{8,10},{9,11},{10,... | collective-permute-start | bytes 12296 | tf_op jit(solution)/shard_map/grads/ppermute | solution.py:286
  133.1 4.0 %collective-permute-start.8 = (f32[8,128]{1,0:T(8,128)S(1)}, f32[8,128]{1,0:T(8,128)S(1)}, u32[]{:S(2)}, u32[]{:S(2)}) collective-permute-start(f32[8,128]{1,0:T(8,128)S(1)} %get-tuple-element.19), channel_id=1, source_target_pairs={{0,3},{1,2},{2,1},{3,0},{4,7},{5,6},{6,5},{7,4},{8,11},{9,10},{10,... | collective-permute-start | bytes 12296 | tf_op jit(solution)/shard_map/grads/ppermute | solution.py:286
  137.2 4.0 %collective-permute-done.8.p3_ref = f32[8,128]{1,0:T(8,128)S(1)} collective-permute-done((f32[8,128]{1,0:T(8,128)S(1)}, f32[8,128]{1,0:T(8,128)S(1)}, u32[]{:S(2)}, u32[]{:S(2)}) %collective-permute-start.8) | collective-permute-done | bytes 4128 | tf_op jit(solution)/shard_map/grads/ppermute | solution.py:286
  141.2 2.0 %all-to-all-done.4.parts_ref.late_ref = bf16[4,64,512]{2,1,0:T(8,128)(2,1)S(1)} async-done(((bf16[4,64,512]{2,1,0:T(8,128)(2,1)}), bf16[4,64,512]{2,1,0:T(8,128)(2,1)S(1)}, u32[]{:S(2)}, u32[]{:S(2)}) %all-to-all-start.4) | async-done | bytes 262176 | tf_op jit(solution)/shard_map/second/all_to_all | solution.py:281
  144.1 8.5 %all-to-all-start.6 = ((f32[32,32,128]{2,1,0:T(8,128)}), f32[32,32,128]{2,1,0:T(8,128)S(1)}, u32[]{:S(2)}, u32[]{:S(2)}) async-start(f32[32,32,128]{2,1,0:T(8,128)} %place.2), calls=%async_computation.6 | async-start | bytes 1048576 | tf_op jit(solution)/shard_map/place/all_to_all | solution.py:281
  154.1 10.2 %all-to-all-done.6.pieces_ref = f32[32,32,128]{2,1,0:T(8,128)S(1)} async-done(((f32[32,32,128]{2,1,0:T(8,128)}), f32[32,32,128]{2,1,0:T(8,128)S(1)}, u32[]{:S(2)}, u32[]{:S(2)}) %all-to-all-start.6) | async-done | bytes 524320 | tf_op jit(solution)/shard_map/place/all_to_all | solution.py:281
  (52 shorter events, 16.1 us)
Async XLA Ops:
  5.6 10.6 %copy-start.3 = (bf16[48,1024]{1,0:T(8,128)(2,1)S(1)}, bf16[48,1024]{1,0:T(8,128)(2,1)}, u32[]{:S(2)}) copy-start(bf16[48,1024]{1,0:T(8,128)(2,1)} %neigh_ref.2) | copy-start | bytes 294916
  5.6 10.6 %copy-start.4 = (bf16[48,1024]{1,0:T(8,128)(2,1)S(1)}, bf16[48,1024]{1,0:T(8,128)(2,1)}, u32[]{:S(2)}) copy-start(bf16[48,1024]{1,0:T(8,128)(2,1)} %own_ref.2) | copy-start | bytes 294916
  5.6 10.6 %copy-start.6 = (bf16[512,48]{0,1:T(8,128)(2,1)S(1)}, bf16[512,48]{0,1:T(8,128)(2,1)}, u32[]{:S(2)}) copy-start(bf16[512,48]{0,1:T(8,128)(2,1)} %param.15) | copy-start | bytes 147460
  5.6 24.7 %all-to-all-start = ((bf16[32,64,128]{2,1,0:T(8,128)(2,1)}), bf16[32,64,128]{2,1,0:T(8,128)(2,1)S(1)}, u32[]{:S(2)}, u32[]{:S(2)}) async-start(bf16[32,64,128]{2,1,0:T(8,128)(2,1)} %edges.1.late_ref), calls=%async_computation | async-start | bytes 1048576 | tf_op jit(solution)/shard_map/edges/all_to_all | solution.py:281
  16.4 9.3 %collective-permute-start = (bf16[192,256]{1,0:T(8,128)(2,1)S(1)}, bf16[192,256]{1,0:T(8,128)(2,1)S(1)}, u32[]{:S(2)}, u32[]{:S(2)}) collective-permute-start(bf16[192,256]{1,0:T(8,128)(2,1)S(1)} %get-tuple-element.14), channel_id=1, source_target_pairs={{0,1},{1,0},{2,3},{3,2},{4,5},{5,4},{6,7},{7,6},{8,9},{9,8},{10,11... | collective-permute-start | bytes 294920 | tf_op jit(solution)/shard_map/pieces/ppermute | solution.py:286
  18.3 9.5 %collective-permute-start.1 = (bf16[192,256]{1,0:T(8,128)(2,1)S(1)}, bf16[192,256]{1,0:T(8,128)(2,1)S(1)}, u32[]{:S(2)}, u32[]{:S(2)}) collective-permute-start(bf16[192,256]{1,0:T(8,128)(2,1)S(1)} %get-tuple-element.13), channel_id=1, source_target_pairs={{0,2},{1,3},{2,0},{3,1},{4,6},{5,7},{6,4},{7,5},{8,10},{9,11},{10,... | collective-permute-start | bytes 294920 | tf_op jit(solution)/shard_map/pieces/ppermute | solution.py:286
  23.0 7.3 %collective-permute-start.2 = (bf16[192,256]{1,0:T(8,128)(2,1)S(1)}, bf16[192,256]{1,0:T(8,128)(2,1)S(1)}, u32[]{:S(2)}, u32[]{:S(2)}) collective-permute-start(bf16[192,256]{1,0:T(8,128)(2,1)S(1)} %get-tuple-element.12), channel_id=1, source_target_pairs={{0,3},{1,2},{2,1},{3,0},{4,7},{5,6},{6,5},{7,4},{8,11},{9,10},{10,... | collective-permute-start | bytes 294920 | tf_op jit(solution)/shard_map/pieces/ppermute | solution.py:286
  31.7 9.7 %copy-start.5 = (bf16[512,64]{0,1:T(8,128)(2,1)S(1)}, bf16[512,64]{0,1:T(8,128)(2,1)}, u32[]{:S(2)}) copy-start(bf16[512,64]{0,1:T(8,128)(2,1)} %param.25) | copy-start | bytes 196612
  42.5 13.2 %copy-start.1 = (bf16[64,1024]{1,0:T(8,128)(2,1)S(1)}, bf16[64,1024]{1,0:T(8,128)(2,1)}, u32[]{:S(2)}) copy-start(bf16[64,1024]{1,0:T(8,128)(2,1)} %neigh_ref.3) | copy-start | bytes 393220
  42.5 13.2 %copy-start.2 = (bf16[64,1024]{1,0:T(8,128)(2,1)S(1)}, bf16[64,1024]{1,0:T(8,128)(2,1)}, u32[]{:S(2)}) copy-start(bf16[64,1024]{1,0:T(8,128)(2,1)} %own_ref.3) | copy-start | bytes 393220
  42.5 39.5 %all-to-all-start.2 = ((bf16[4,128,512]{2,1,0:T(8,128)(2,1)}), bf16[4,128,512]{2,1,0:T(8,128)(2,1)S(1)}, u32[]{:S(2)}, u32[]{:S(2)}) async-start(bf16[4,128,512]{2,1,0:T(8,128)(2,1)} %first.1.late_ref), calls=%async_computation.2 | async-start | bytes 1048576 | tf_op jit(solution)/shard_map/first/all_to_all | solution.py:281
  55.8 23.1 %collective-permute-start.3 = (bf16[128,256]{1,0:T(8,128)(2,1)S(1)}, bf16[128,256]{1,0:T(8,128)(2,1)S(1)}, u32[]{:S(2)}, u32[]{:S(2)}) collective-permute-start(bf16[128,256]{1,0:T(8,128)(2,1)S(1)} %get-tuple-element.18), channel_id=1, source_target_pairs={{0,1},{1,0},{2,3},{3,2},{4,5},{5,4},{6,7},{7,6},{8,9},{9,8},{10,11... | collective-permute-start | bytes 196616 | tf_op jit(solution)/shard_map/pieces/ppermute | solution.py:286
  58.4 20.6 %collective-permute-start.4 = (bf16[128,256]{1,0:T(8,128)(2,1)S(1)}, bf16[128,256]{1,0:T(8,128)(2,1)S(1)}, u32[]{:S(2)}, u32[]{:S(2)}) collective-permute-start(bf16[128,256]{1,0:T(8,128)(2,1)S(1)} %get-tuple-element.17), channel_id=1, source_target_pairs={{0,2},{1,3},{2,0},{3,1},{4,6},{5,7},{6,4},{7,5},{8,10},{9,11},{10,... | collective-permute-start | bytes 196616 | tf_op jit(solution)/shard_map/pieces/ppermute | solution.py:286
  62.8 2.3 %copy-start.11 = (f32[64]{0:T(128)S(1)}, f32[64]{0:T(128)}, u32[]{:S(2)}) copy-start(f32[64]{0:T(128)} %param.18) | copy-start | bytes 772
  62.8 19.1 %collective-permute-start.5 = (bf16[128,256]{1,0:T(8,128)(2,1)S(1)}, bf16[128,256]{1,0:T(8,128)(2,1)S(1)}, u32[]{:S(2)}, u32[]{:S(2)}) collective-permute-start(bf16[128,256]{1,0:T(8,128)(2,1)S(1)} %get-tuple-element.16), channel_id=1, source_target_pairs={{0,3},{1,2},{2,1},{3,0},{4,7},{5,6},{6,5},{7,4},{8,11},{9,10},{10,... | collective-permute-start | bytes 196616 | tf_op jit(solution)/shard_map/pieces/ppermute | solution.py:286
  82.8 9.2 %copy-start.9 = (s32[512]{0:T(512)S(1)}, s32[512]{0:T(512)}, u32[]{:S(2)}) copy-start(s32[512]{0:T(512)} %param.21) | copy-start | bytes 6148
  82.8 14.9 %copy-start = (bf16[4,128,128]{2,1,0:T(8,128)(2,1)S(1)}, bf16[4,128,128]{2,1,0:T(8,128)(2,1)}, u32[]{:S(2)}) copy-start(bf16[4,128,128]{2,1,0:T(8,128)(2,1)} %values_ref.1) | copy-start | bytes 393220
  82.8 14.9 %all-to-all-start.3 = ((bf16[4,64,512]{2,1,0:T(8,128)(2,1)}), bf16[4,64,512]{2,1,0:T(8,128)(2,1)S(1)}, u32[]{:S(2)}, u32[]{:S(2)}) async-start(bf16[4,64,512]{2,1,0:T(8,128)(2,1)} %hidden.1), calls=%async_computation.3 | async-start | bytes 524288 | tf_op jit(solution)/shard_map/hidden/all_to_all | solution.py:281
  99.4 21.1 %all-to-all-start.5 = ((bf16[32,32,128]{2,1,0:T(8,128)(2,1)}), bf16[32,32,128]{2,1,0:T(8,128)(2,1)S(1)}, u32[]{:S(2)}, u32[]{:S(2)}) async-start(bf16[32,32,128]{2,1,0:T(8,128)(2,1)} %get-tuple-element.8), calls=%async_computation.5 | async-start | bytes 524288 | tf_op jit(solution)/shard_map/grads/all_to_all | solution.py:281
  120.6 22.6 %all-to-all-start.4 = ((bf16[4,64,512]{2,1,0:T(8,128)(2,1)}), bf16[4,64,512]{2,1,0:T(8,128)(2,1)S(1)}, u32[]{:S(2)}, u32[]{:S(2)}) async-start(bf16[4,64,512]{2,1,0:T(8,128)(2,1)} %second.2), calls=%async_computation.4 | async-start | bytes 524288 | tf_op jit(solution)/shard_map/second/all_to_all | solution.py:281
  127.9 9.3 %collective-permute-start.6 = (f32[8,128]{1,0:T(8,128)S(1)}, f32[8,128]{1,0:T(8,128)S(1)}, u32[]{:S(2)}, u32[]{:S(2)}) collective-permute-start(f32[8,128]{1,0:T(8,128)S(1)} %get-tuple-element.21), channel_id=1, source_target_pairs={{0,1},{1,0},{2,3},{3,2},{4,5},{5,4},{6,7},{7,6},{8,9},{9,8},{10,11... | collective-permute-start | bytes 12296 | tf_op jit(solution)/shard_map/grads/ppermute | solution.py:286
  129.8 7.4 %collective-permute-start.7 = (f32[8,128]{1,0:T(8,128)S(1)}, f32[8,128]{1,0:T(8,128)S(1)}, u32[]{:S(2)}, u32[]{:S(2)}) collective-permute-start(f32[8,128]{1,0:T(8,128)S(1)} %get-tuple-element.20), channel_id=1, source_target_pairs={{0,2},{1,3},{2,0},{3,1},{4,6},{5,7},{6,4},{7,5},{8,10},{9,11},{10,... | collective-permute-start | bytes 12296 | tf_op jit(solution)/shard_map/grads/ppermute | solution.py:286
  133.1 8.1 %collective-permute-start.8 = (f32[8,128]{1,0:T(8,128)S(1)}, f32[8,128]{1,0:T(8,128)S(1)}, u32[]{:S(2)}, u32[]{:S(2)}) collective-permute-start(f32[8,128]{1,0:T(8,128)S(1)} %get-tuple-element.19), channel_id=1, source_target_pairs={{0,3},{1,2},{2,1},{3,0},{4,7},{5,6},{6,5},{7,4},{8,11},{9,10},{10,... | collective-permute-start | bytes 12296 | tf_op jit(solution)/shard_map/grads/ppermute | solution.py:286
  144.1 20.2 %all-to-all-start.6 = ((f32[32,32,128]{2,1,0:T(8,128)}), f32[32,32,128]{2,1,0:T(8,128)S(1)}, u32[]{:S(2)}, u32[]{:S(2)}) async-start(f32[32,32,128]{2,1,0:T(8,128)} %place.2), calls=%async_computation.6 | async-start | bytes 1048576 | tf_op jit(solution)/shard_map/place/all_to_all | solution.py:281
  (4 other events, 3.0 us)

commit v5 on v4

--- a/solution.py
+++ b/solution.py
@@ -126,7 +126,7 @@
 
 
 def first_kernel(
-    mine_ref, mean_ref, p0_ref, p1_ref, p2_ref, p3_ref, cot_ref, out_ref, weight, acts
+    mine_ref, mean_ref, p0_ref, p1_ref, p2_ref, p3_ref, out_ref, weight, acts
 ):
     mine = mine_ref[0]
     group, rows, targets = mean_ref.shape
@@ -139,24 +139,22 @@
         acts[mid : mid + rows, :width] = piece[2 * rows : 3 * rows, :]
         acts[mid : mid + rows, width:] = piece[3 * rows :, :]
     total = lax.dot_general(weight[...], acts[...], TN, preferred_element_type=F32)
-    cols = cot_ref.shape[0]
+    cols = out_ref.shape[1]
     for z in range(out_ref.shape[0]):
-        out_ref[z, :cols, :] = total[z * cols : (z + 1) * cols, :].astype(BF)
-        out_ref[z, cols:, :] = cot_ref[...]
+        out_ref[z] = total[z * cols : (z + 1) * cols, :].astype(BF)
 
 
 def hidden_kernel(parts_ref, bias_ref, late1_ref, late2_ref, late3_ref, out_ref):
     del late1_ref, late2_ref, late3_ref
-    cols = bias_ref.shape[0]
-    total = parts_ref[0, :cols, :].astype(F32)
+    total = parts_ref[0].astype(F32)
     for k in range(1, parts_ref.shape[0]):
-        total = total + parts_ref[k, :cols, :].astype(F32)
+        total = total + parts_ref[k].astype(F32)
     hidden = jnp.maximum(total + bias_ref[...], 0.0).astype(BF)
     for c in range(out_ref.shape[0]):
         out_ref[c] = hidden
 
 
-def grad_kernel(index_ref, hid_ref, values_ref, live_ref, parts_ref, agg_ref, out_ref, left, acc):
+def grad_kernel(index_ref, hid_ref, values_ref, live_ref, cot_ref, agg_ref, out_ref, left, acc):
     group, cols, targets = hid_ref.shape
     width = values_ref.shape[1]
     wide = group * cols
@@ -175,12 +173,11 @@
         left[:wide, at] = tile * live[:, at]
     for j in range(group):
         left[wide + j * cols : wide + (j + 1) * cols, :] = hid_ref[j] * live
-    right = jnp.concatenate([parts_ref[j, cols:, :] for j in range(parts_ref.shape[0])], axis=0)
-    block = lax.dot_general(left[...], right, NT, preferred_element_type=F32)
+    block = lax.dot_general(left[...], cot_ref[...], NT, preferred_element_type=F32)
     at = 0
     for w in range(2):
         for r in range(0, cols, 8):
-            for c in range(0, right.shape[0], 128):
+            for c in range(0, cot_ref.shape[0], 128):
                 rows_of = [
                     block[w * wide + j * cols + r : w * wide + j * cols + r + 8, c : c + 128]
                     for j in range(group)
@@ -288,6 +285,8 @@
     def shape(*dims, dtype=BF):
         return jax.ShapeDtypeStruct(dims, dtype)
 
+    with jax.named_scope("cotangent"):
+        cot = lax.all_gather(cotangent.T, "feat", axis=0, tiled=True, axis_index_groups=far)
     with jax.named_scope("edges"):
         send = call(
             functools.partial(pack_kernel, groups, targets),
@@ -321,13 +320,13 @@
     with jax.named_scope("first"):
         first = call(
             first_kernel,
-            shape(blocks, 2 * hid, targets),
-            7,
+            shape(blocks, hid, targets),
+            6,
             scratch=[pltpu.VMEM((8 * cols, wide), BF), pltpu.VMEM((8 * cols, targets), BF)],
             smem=(0,),
             flops=2 * 8 * cols * wide * targets,
             nbytes=2 << 20,
-        )(mine, mean, pieces[0], *got, cotangent.T)
+        )(mine, mean, pieces[0], *got)
         parts = swap(first, "feat", far)
     with jax.named_scope("pieces"):
         pieces = call(
@@ -356,7 +355,7 @@
             smem=(0,),
             flops=2 * 2 * wide * targets * wide,
             nbytes=4 << 20,
-        )(tile_index, hidden, tile_values, live, parts)
+        )(tile_index, hidden, tile_values, live, cot)
         terms = swap(terms, "dp")
         mine_sum = call(
             sum_kernel, shape(GROUP, 8, 128, dtype=F32), 2, smem=(0,), nbytes=1 << 20

time: 166 us -> 168 us (1.012)
  blocking collectives: 9.68 us -> 28.6 us
  waiting for transfers between devices: 50.3 us -> 33.1 us
    all_gather x0 -> x1, blocking collectives: none -> 19.1 us  [body(): lax.all_gather(cotangent.T, 'feat', axis=0, tiled=True, axis_index_groups...]
    ppermute x9, waiting for transfers between devices: 25.3 us -> 15.1 us  [trade(): return lax.ppermute(x, 'feat', [(i, i ^ k) for i in range(n_feat)])]
    all_to_all x6, waiting for transfers between devices: 24.9 us -> 17.9 us  [swap(): lax.all_to_all(x, axis, split_axis=0, concat_axis=0, tiled=True, axis_ind...]
    ppermute x9, starting transfers between devices: 27.8 us -> 30.1 us  [trade(): return lax.ppermute(x, 'feat', [(i, i ^ k) for i in range(n_feat)])]
    all_to_all x6, starting transfers between devices: 60.9 us -> 58.6 us  [swap(): lax.all_to_all(x, axis, split_axis=0, concat_axis=0, tiled=True, axis_ind...]
where the time goes in v5:
time: 168 us; the launch traced here: 167 us
  starting transfers between devices  88.7 us (53%)
  waiting for transfers between devices  33.1 us (20%)
  blocking collectives  28.6 us (17%)
  Pallas kernels  12.2 us (7%)
  local copies, waits for them, and re-layouts  3.23 us (2%)
    all_to_all x6, starting transfers between devices, swap(): lax.all_to_all(x, axis, split_axis=0, concat_axis=0, tiled=True, axis_ind...  58.6 us
    ppermute x9, starting transfers between devices, trade(): return lax.ppermute(x, 'feat', [(i, i ^ k) for i in range(n_feat)])  30.1 us
    all_gather x1, blocking collectives, body(): lax.all_gather(cotangent.T, 'feat', axis=0, tiled=True, axis_index_groups...  19.1 us
    all_to_all x6, waiting for transfers between devices, swap(): lax.all_to_all(x, axis, split_axis=0, concat_axis=0, tiled=True, axis_ind...  17.9 us
    ppermute x9, waiting for transfers between devices, trade(): return lax.ppermute(x, 'feat', [(i, i ^ k) for i in range(n_feat)])  15.1 us
    all_to_all x1, blocking collectives, swap(): lax.all_to_all(x, axis, split_axis=0, concat_axis=0, tiled=True, axis_ind...  9.55 us
  transfers between devices with their start and end apart: 15, of which 9 were waited for; matrix products, arithmetic and copies ran while one was open for 0% of the time, Pallas kernels for 1%

profile of v5, /device:TPU:1, one launch (start us, length us, event | category | flops | bytes accessed | tf_op | source)
XLA Modules:
  0.0 166.7 jit_solution(7586667192625516217)
XLA Ops:
  2.3 3.3 %edges.1.late_ref = bf16[32,64,128]{2,1,0:T(8,128)(2,1)} custom-call(bf16[48,2048]{1,0:T(8,128)(2,1)S(1)} %bitcast.36, s32[16,128]{1,0:T(8,128)S(1)} %bitcast.37), custom_call_target="tpu_custom_call" | custom-call | flops 1073741824 | bytes 8388608 | tf_op jit(solution)/shard_map/edges/pallas_call | solution.py:291
  5.6 10.6 %all-to-all-start = ((bf16[32,64,128]{2,1,0:T(8,128)(2,1)}), bf16[32,64,128]{2,1,0:T(8,128)(2,1)S(1)}, u32[]{:S(2)}, u32[]{:S(2)}) async-start(bf16[32,64,128]{2,1,0:T(8,128)(2,1)} %edges.1.late_ref), calls=%async_computation | async-start | bytes 1048576 | tf_op jit(solution)/shard_map/edges/all_to_all | solution.py:278
  16.4 1.9 %collective-permute-start = (bf16[192,256]{1,0:T(8,128)(2,1)S(1)}, bf16[192,256]{1,0:T(8,128)(2,1)S(1)}, u32[]{:S(2)}, u32[]{:S(2)}) collective-permute-start(bf16[192,256]{1,0:T(8,128)(2,1)S(1)} %get-tuple-element.14), channel_id=1, source_target_pairs={{0,1},{1,0},{2,3},{3,2},{4,5},{5,4},{6,7},{7,6},{8,9},{9,8},{10,11... | collective-permute-start | bytes 294920 | tf_op jit(solution)/shard_map/pieces/ppermute | solution.py:283
  18.3 4.7 %collective-permute-start.1 = (bf16[192,256]{1,0:T(8,128)(2,1)S(1)}, bf16[192,256]{1,0:T(8,128)(2,1)S(1)}, u32[]{:S(2)}, u32[]{:S(2)}) collective-permute-start(bf16[192,256]{1,0:T(8,128)(2,1)S(1)} %get-tuple-element.13), channel_id=1, source_target_pairs={{0,2},{1,3},{2,0},{3,1},{4,6},{5,7},{6,4},{7,5},{8,10},{9,11},{10,... | collective-permute-start | bytes 294920 | tf_op jit(solution)/shard_map/pieces/ppermute | solution.py:283
  23.0 2.7 %collective-permute-start.2 = (bf16[192,256]{1,0:T(8,128)(2,1)S(1)}, bf16[192,256]{1,0:T(8,128)(2,1)S(1)}, u32[]{:S(2)}, u32[]{:S(2)}) collective-permute-start(bf16[192,256]{1,0:T(8,128)(2,1)S(1)} %get-tuple-element.12), channel_id=1, source_target_pairs={{0,3},{1,2},{2,1},{3,0},{4,7},{5,6},{6,5},{7,4},{8,11},{9,10},{10,... | collective-permute-start | bytes 294920 | tf_op jit(solution)/shard_map/pieces/ppermute | solution.py:283
  25.7 2.1 %collective-permute-done.1.late2_ref.p2_ref = bf16[192,256]{1,0:T(8,128)(2,1)S(1)} collective-permute-done((bf16[192,256]{1,0:T(8,128)(2,1)S(1)}, bf16[192,256]{1,0:T(8,128)(2,1)S(1)}, u32[]{:S(2)}, u32[]{:S(2)}) %collective-permute-start.1) | collective-permute-done | bytes 98336 | tf_op jit(solution)/shard_map/pieces/ppermute | solution.py:283
  27.8 2.5 %collective-permute-done.2.late3_ref.p3_ref = bf16[192,256]{1,0:T(8,128)(2,1)S(1)} collective-permute-done((bf16[192,256]{1,0:T(8,128)(2,1)S(1)}, bf16[192,256]{1,0:T(8,128)(2,1)S(1)}, u32[]{:S(2)}, u32[]{:S(2)}) %collective-permute-start.2) | collective-permute-done | bytes 98336 | tf_op jit(solution)/shard_map/pieces/ppermute | solution.py:283
  31.7 9.5 %all_to_all.35.mean_ref = bf16[4,48,512]{2,1,0:T(8,128)(2,1)S(1)} all-to-all(bf16[4,48,512]{2,1,0:T(8,128)(2,1)S(1)} %mean.1), channel_id=1, replica_groups={{0,1,2,3},{4,5,6,7},{8,9,10,11},{12,13,14,15},{16,17,18,19},{20,21,22,2..., dimensions={0} | all-to-all | bytes 393216 | tf_op jit(solution)/shard_map/mean/all_to_all | solution.py:278
  42.2 13.2 %all-to-all-start.2 = ((bf16[4,64,512]{2,1,0:T(8,128)(2,1)}), bf16[4,64,512]{2,1,0:T(8,128)(2,1)S(1)}, u32[]{:S(2)}, u32[]{:S(2)}) async-start(bf16[4,64,512]{2,1,0:T(8,128)(2,1)} %first.1.late_ref), calls=%async_computation.2 | async-start | bytes 524288 | tf_op jit(solution)/shard_map/first/all_to_all | solution.py:278
  55.6 2.5 %collective-permute-start.3 = (bf16[128,256]{1,0:T(8,128)(2,1)S(1)}, bf16[128,256]{1,0:T(8,128)(2,1)S(1)}, u32[]{:S(2)}, u32[]{:S(2)}) collective-permute-start(bf16[128,256]{1,0:T(8,128)(2,1)S(1)} %get-tuple-element.18), channel_id=1, source_target_pairs={{0,1},{1,0},{2,3},{3,2},{4,5},{5,4},{6,7},{7,6},{8,9},{9,8},{10,11... | collective-permute-start | bytes 196616 | tf_op jit(solution)/shard_map/pieces/ppermute | solution.py:283
  58.1 4.4 %collective-permute-start.4 = (bf16[128,256]{1,0:T(8,128)(2,1)S(1)}, bf16[128,256]{1,0:T(8,128)(2,1)S(1)}, u32[]{:S(2)}, u32[]{:S(2)}) collective-permute-start(bf16[128,256]{1,0:T(8,128)(2,1)S(1)} %get-tuple-element.17), channel_id=1, source_target_pairs={{0,2},{1,3},{2,0},{3,1},{4,6},{5,7},{6,4},{7,5},{8,10},{9,11},{10,... | collective-permute-start | bytes 196616 | tf_op jit(solution)/shard_map/pieces/ppermute | solution.py:283
  62.6 2.3 %collective-permute-start.5 = (bf16[128,256]{1,0:T(8,128)(2,1)S(1)}, bf16[128,256]{1,0:T(8,128)(2,1)S(1)}, u32[]{:S(2)}, u32[]{:S(2)}) collective-permute-start(bf16[128,256]{1,0:T(8,128)(2,1)S(1)} %get-tuple-element.16), channel_id=1, source_target_pairs={{0,3},{1,2},{2,1},{3,0},{4,7},{5,6},{6,5},{7,4},{8,11},{9,10},{10,... | collective-permute-start | bytes 196616 | tf_op jit(solution)/shard_map/pieces/ppermute | solution.py:283
  67.7 4.5 %collective-permute-done.5.late3_ref.p3_ref = bf16[128,256]{1,0:T(8,128)(2,1)S(1)} collective-permute-done((bf16[128,256]{1,0:T(8,128)(2,1)S(1)}, bf16[128,256]{1,0:T(8,128)(2,1)S(1)}, u32[]{:S(2)}, u32[]{:S(2)}) %collective-permute-start.5) | collective-permute-done | bytes 65568 | tf_op jit(solution)/shard_map/pieces/ppermute | solution.py:283
  73.0 6.1 %all-to-all-start.3 = ((bf16[4,64,512]{2,1,0:T(8,128)(2,1)}), bf16[4,64,512]{2,1,0:T(8,128)(2,1)S(1)}, u32[]{:S(2)}, u32[]{:S(2)}) async-start(bf16[4,64,512]{2,1,0:T(8,128)(2,1)} %hidden.1), calls=%async_computation.3 | async-start | bytes 524288 | tf_op jit(solution)/shard_map/hidden/all_to_all | solution.py:278
  79.9 19.1 %all_gather.3.cot_ref = bf16[256,512]{1,0:T(8,128)(2,1)S(1)} all-gather(bf16[64,512]{1,0:T(8,128)(2,1)S(1)} %bitcast.38), channel_id=1, replica_groups={{0,4,8,12},{1,5,9,13},{2,6,10,14},{3,7,11,15},{16,20,24,28},{17,21,25,2..., dimensions={0}, use_global_device_ids=true | all-gather | bytes 327680 | tf_op jit(solution)/shard_map/cotangent/all_gather | solution.py:289
  100.7 11.9 %all-to-all-start.5 = ((bf16[32,32,128]{2,1,0:T(8,128)(2,1)}), bf16[32,32,128]{2,1,0:T(8,128)(2,1)S(1)}, u32[]{:S(2)}, u32[]{:S(2)}) async-start(bf16[32,32,128]{2,1,0:T(8,128)(2,1)} %get-tuple-element.8), calls=%async_computation.5 | async-start | bytes 524288 | tf_op jit(solution)/shard_map/grads/all_to_all | solution.py:278
  113.7 7.8 %all-to-all-done.5.terms_ref = bf16[32,32,128]{2,1,0:T(8,128)(2,1)S(1)} async-done(((bf16[32,32,128]{2,1,0:T(8,128)(2,1)}), bf16[32,32,128]{2,1,0:T(8,128)(2,1)S(1)}, u32[]{:S(2)}, u32[]{:S(2)}) %all-to-all-start.5) | async-done | bytes 262176 | tf_op jit(solution)/shard_map/grads/all_to_all | solution.py:278
  121.5 6.4 %all-to-all-start.4 = ((bf16[4,64,512]{2,1,0:T(8,128)(2,1)}), bf16[4,64,512]{2,1,0:T(8,128)(2,1)S(1)}, u32[]{:S(2)}, u32[]{:S(2)}) async-start(bf16[4,64,512]{2,1,0:T(8,128)(2,1)} %second.2), calls=%async_computation.4 | async-start | bytes 524288 | tf_op jit(solution)/shard_map/second/all_to_all | solution.py:278
  127.9 5.7 %collective-permute-start.6 = (f32[8,128]{1,0:T(8,128)S(1)}, f32[8,128]{1,0:T(8,128)S(1)}, u32[]{:S(2)}, u32[]{:S(2)}) collective-permute-start(f32[8,128]{1,0:T(8,128)S(1)} %get-tuple-element.21), channel_id=1, source_target_pairs={{0,1},{1,0},{2,3},{3,2},{4,5},{5,4},{6,7},{7,6},{8,9},{9,8},{10,11... | collective-permute-start | bytes 12296 | tf_op jit(solution)/shard_map/grads/ppermute | solution.py:283
  133.6 2.7 %collective-permute-start.7 = (f32[8,128]{1,0:T(8,128)S(1)}, f32[8,128]{1,0:T(8,128)S(1)}, u32[]{:S(2)}, u32[]{:S(2)}) collective-permute-start(f32[8,128]{1,0:T(8,128)S(1)} %get-tuple-element.20), channel_id=1, source_target_pairs={{0,2},{1,3},{2,0},{3,1},{4,6},{5,7},{6,4},{7,5},{8,10},{9,11},{10,... | collective-permute-start | bytes 12296 | tf_op jit(solution)/shard_map/grads/ppermute | solution.py:283
  136.3 3.2 %collective-permute-start.8 = (f32[8,128]{1,0:T(8,128)S(1)}, f32[8,128]{1,0:T(8,128)S(1)}, u32[]{:S(2)}, u32[]{:S(2)}) collective-permute-start(f32[8,128]{1,0:T(8,128)S(1)} %get-tuple-element.19), channel_id=1, source_target_pairs={{0,3},{1,2},{2,1},{3,0},{4,7},{5,6},{6,5},{7,4},{8,11},{9,10},{10,... | collective-permute-start | bytes 12296 | tf_op jit(solution)/shard_map/grads/ppermute | solution.py:283
  140.6 2.3 %collective-permute-done.8.p3_ref = f32[8,128]{1,0:T(8,128)S(1)} collective-permute-done((f32[8,128]{1,0:T(8,128)S(1)}, f32[8,128]{1,0:T(8,128)S(1)}, u32[]{:S(2)}, u32[]{:S(2)}) %collective-permute-start.8) | collective-permute-done | bytes 4128 | tf_op jit(solution)/shard_map/grads/ppermute | solution.py:283
  143.7 10.5 %all-to-all-start.6 = ((f32[32,32,128]{2,1,0:T(8,128)}), f32[32,32,128]{2,1,0:T(8,128)S(1)}, u32[]{:S(2)}, u32[]{:S(2)}) async-start(f32[32,32,128]{2,1,0:T(8,128)} %place.2), calls=%async_computation.6 | async-start | bytes 1048576 | tf_op jit(solution)/shard_map/place/all_to_all | solution.py:278
  155.7 10.1 %all-to-all-done.6.pieces_ref = f32[32,32,128]{2,1,0:T(8,128)S(1)} async-done(((f32[32,32,128]{2,1,0:T(8,128)}), f32[32,32,128]{2,1,0:T(8,128)S(1)}, u32[]{:S(2)}, u32[]{:S(2)}) %all-to-all-start.6) | async-done | bytes 524320 | tf_op jit(solution)/shard_map/place/all_to_all | solution.py:278
  (53 shorter events, 15.8 us)
Async XLA Ops:
  5.6 10.6 %copy-start.3 = (bf16[48,1024]{1,0:T(8,128)(2,1)S(1)}, bf16[48,1024]{1,0:T(8,128)(2,1)}, u32[]{:S(2)}) copy-start(bf16[48,1024]{1,0:T(8,128)(2,1)} %neigh_ref.2) | copy-start | bytes 294916
  5.6 10.6 %copy-start.4 = (bf16[48,1024]{1,0:T(8,128)(2,1)S(1)}, bf16[48,1024]{1,0:T(8,128)(2,1)}, u32[]{:S(2)}) copy-start(bf16[48,1024]{1,0:T(8,128)(2,1)} %own_ref.2) | copy-start | bytes 294916
  5.6 10.6 %copy-start.5 = (bf16[512,48]{0,1:T(8,128)(2,1)S(1)}, bf16[512,48]{0,1:T(8,128)(2,1)}, u32[]{:S(2)}) copy-start(bf16[512,48]{0,1:T(8,128)(2,1)} %param.15) | copy-start | bytes 147460
  5.6 24.7 %all-to-all-start = ((bf16[32,64,128]{2,1,0:T(8,128)(2,1)}), bf16[32,64,128]{2,1,0:T(8,128)(2,1)S(1)}, u32[]{:S(2)}, u32[]{:S(2)}) async-start(bf16[32,64,128]{2,1,0:T(8,128)(2,1)} %edges.1.late_ref), calls=%async_computation | async-start | bytes 1048576 | tf_op jit(solution)/shard_map/edges/all_to_all | solution.py:278
  16.4 9.3 %collective-permute-start = (bf16[192,256]{1,0:T(8,128)(2,1)S(1)}, bf16[192,256]{1,0:T(8,128)(2,1)S(1)}, u32[]{:S(2)}, u32[]{:S(2)}) collective-permute-start(bf16[192,256]{1,0:T(8,128)(2,1)S(1)} %get-tuple-element.14), channel_id=1, source_target_pairs={{0,1},{1,0},{2,3},{3,2},{4,5},{5,4},{6,7},{7,6},{8,9},{9,8},{10,11... | collective-permute-start | bytes 294920 | tf_op jit(solution)/shard_map/pieces/ppermute | solution.py:283
  18.3 9.5 %collective-permute-start.1 = (bf16[192,256]{1,0:T(8,128)(2,1)S(1)}, bf16[192,256]{1,0:T(8,128)(2,1)S(1)}, u32[]{:S(2)}, u32[]{:S(2)}) collective-permute-start(bf16[192,256]{1,0:T(8,128)(2,1)S(1)} %get-tuple-element.13), channel_id=1, source_target_pairs={{0,2},{1,3},{2,0},{3,1},{4,6},{5,7},{6,4},{7,5},{8,10},{9,11},{10,... | collective-permute-start | bytes 294920 | tf_op jit(solution)/shard_map/pieces/ppermute | solution.py:283
  23.0 7.3 %collective-permute-start.2 = (bf16[192,256]{1,0:T(8,128)(2,1)S(1)}, bf16[192,256]{1,0:T(8,128)(2,1)S(1)}, u32[]{:S(2)}, u32[]{:S(2)}) collective-permute-start(bf16[192,256]{1,0:T(8,128)(2,1)S(1)} %get-tuple-element.12), channel_id=1, source_target_pairs={{0,3},{1,2},{2,1},{3,0},{4,7},{5,6},{6,5},{7,4},{8,11},{9,10},{10,... | collective-permute-start | bytes 294920 | tf_op jit(solution)/shard_map/pieces/ppermute | solution.py:283
  42.2 13.2 %copy-start.1 = (bf16[64,1024]{1,0:T(8,128)(2,1)S(1)}, bf16[64,1024]{1,0:T(8,128)(2,1)}, u32[]{:S(2)}) copy-start(bf16[64,1024]{1,0:T(8,128)(2,1)} %neigh_ref.3) | copy-start | bytes 393220
  42.2 13.2 %copy-start.2 = (bf16[64,1024]{1,0:T(8,128)(2,1)S(1)}, bf16[64,1024]{1,0:T(8,128)(2,1)}, u32[]{:S(2)}) copy-start(bf16[64,1024]{1,0:T(8,128)(2,1)} %own_ref.3) | copy-start | bytes 393220
  42.2 30.0 %all-to-all-start.2 = ((bf16[4,64,512]{2,1,0:T(8,128)(2,1)}), bf16[4,64,512]{2,1,0:T(8,128)(2,1)S(1)}, u32[]{:S(2)}, u32[]{:S(2)}) async-start(bf16[4,64,512]{2,1,0:T(8,128)(2,1)} %first.1.late_ref), calls=%async_computation.2 | async-start | bytes 524288 | tf_op jit(solution)/shard_map/first/all_to_all | solution.py:278
  55.6 11.3 %collective-permute-start.3 = (bf16[128,256]{1,0:T(8,128)(2,1)S(1)}, bf16[128,256]{1,0:T(8,128)(2,1)S(1)}, u32[]{:S(2)}, u32[]{:S(2)}) collective-permute-start(bf16[128,256]{1,0:T(8,128)(2,1)S(1)} %get-tuple-element.18), channel_id=1, source_target_pairs={{0,1},{1,0},{2,3},{3,2},{4,5},{5,4},{6,7},{7,6},{8,9},{9,8},{10,11... | collective-permute-start | bytes 196616 | tf_op jit(solution)/shard_map/pieces/ppermute | solution.py:283
  58.1 9.6 %collective-permute-start.4 = (bf16[128,256]{1,0:T(8,128)(2,1)S(1)}, bf16[128,256]{1,0:T(8,128)(2,1)S(1)}, u32[]{:S(2)}, u32[]{:S(2)}) collective-permute-start(bf16[128,256]{1,0:T(8,128)(2,1)S(1)} %get-tuple-element.17), channel_id=1, source_target_pairs={{0,2},{1,3},{2,0},{3,1},{4,6},{5,7},{6,4},{7,5},{8,10},{9,11},{10,... | collective-permute-start | bytes 196616 | tf_op jit(solution)/shard_map/pieces/ppermute | solution.py:283
  62.6 2.3 %copy-start.11 = (f32[64]{0:T(128)S(1)}, f32[64]{0:T(128)}, u32[]{:S(2)}) copy-start(f32[64]{0:T(128)} %param.18) | copy-start | bytes 772
  62.6 9.6 %collective-permute-start.5 = (bf16[128,256]{1,0:T(8,128)(2,1)S(1)}, bf16[128,256]{1,0:T(8,128)(2,1)S(1)}, u32[]{:S(2)}, u32[]{:S(2)}) collective-permute-start(bf16[128,256]{1,0:T(8,128)(2,1)S(1)} %get-tuple-element.16), channel_id=1, source_target_pairs={{0,3},{1,2},{2,1},{3,0},{4,7},{5,6},{6,5},{7,4},{8,11},{9,10},{10,... | collective-permute-start | bytes 196616 | tf_op jit(solution)/shard_map/pieces/ppermute | solution.py:283
  73.0 6.1 %copy-start.10 = (s32[4,2]{0,1:T(2,128)S(1)}, s32[4,2]{0,1:T(2,128)}, u32[]{:S(2)}) copy-start(s32[4,2]{0,1:T(2,128)} %param.19) | copy-start | bytes 100
  73.0 6.8 %copy-start.8 = (bf16[512,64]{0,1:T(8,128)(2,1)S(1)}, bf16[512,64]{0,1:T(8,128)(2,1)}, u32[]{:S(2)}) copy-start(bf16[512,64]{0,1:T(8,128)(2,1)} %param.25) | copy-start | bytes 196612
  73.0 25.9 %all-to-all-start.3 = ((bf16[4,64,512]{2,1,0:T(8,128)(2,1)}), bf16[4,64,512]{2,1,0:T(8,128)(2,1)S(1)}, u32[]{:S(2)}, u32[]{:S(2)}) async-start(bf16[4,64,512]{2,1,0:T(8,128)(2,1)} %hidden.1), calls=%async_computation.3 | async-start | bytes 524288 | tf_op jit(solution)/shard_map/hidden/all_to_all | solution.py:278
  79.9 19.1 %copy-start = (bf16[4,128,128]{2,1,0:T(8,128)(2,1)S(1)}, bf16[4,128,128]{2,1,0:T(8,128)(2,1)}, u32[]{:S(2)}) copy-start(bf16[4,128,128]{2,1,0:T(8,128)(2,1)} %values_ref.1) | copy-start | bytes 393220
  100.7 20.8 %all-to-all-start.5 = ((bf16[32,32,128]{2,1,0:T(8,128)(2,1)}), bf16[32,32,128]{2,1,0:T(8,128)(2,1)S(1)}, u32[]{:S(2)}, u32[]{:S(2)}) async-start(bf16[32,32,128]{2,1,0:T(8,128)(2,1)} %get-tuple-element.8), calls=%async_computation.5 | async-start | bytes 524288 | tf_op jit(solution)/shard_map/grads/all_to_all | solution.py:278
  121.5 21.4 %all-to-all-start.4 = ((bf16[4,64,512]{2,1,0:T(8,128)(2,1)}), bf16[4,64,512]{2,1,0:T(8,128)(2,1)S(1)}, u32[]{:S(2)}, u32[]{:S(2)}) async-start(bf16[4,64,512]{2,1,0:T(8,128)(2,1)} %second.2), calls=%async_computation.4 | async-start | bytes 524288 | tf_op jit(solution)/shard_map/second/all_to_all | solution.py:278
  127.9 12.6 %collective-permute-start.6 = (f32[8,128]{1,0:T(8,128)S(1)}, f32[8,128]{1,0:T(8,128)S(1)}, u32[]{:S(2)}, u32[]{:S(2)}) collective-permute-start(f32[8,128]{1,0:T(8,128)S(1)} %get-tuple-element.21), channel_id=1, source_target_pairs={{0,1},{1,0},{2,3},{3,2},{4,5},{5,4},{6,7},{7,6},{8,9},{9,8},{10,11... | collective-permute-start | bytes 12296 | tf_op jit(solution)/shard_map/grads/ppermute | solution.py:283
  133.6 6.9 %collective-permute-start.7 = (f32[8,128]{1,0:T(8,128)S(1)}, f32[8,128]{1,0:T(8,128)S(1)}, u32[]{:S(2)}, u32[]{:S(2)}) collective-permute-start(f32[8,128]{1,0:T(8,128)S(1)} %get-tuple-element.20), channel_id=1, source_target_pairs={{0,2},{1,3},{2,0},{3,1},{4,6},{5,7},{6,4},{7,5},{8,10},{9,11},{10,... | collective-permute-start | bytes 12296 | tf_op jit(solution)/shard_map/grads/ppermute | solution.py:283
  136.3 6.6 %collective-permute-start.8 = (f32[8,128]{1,0:T(8,128)S(1)}, f32[8,128]{1,0:T(8,128)S(1)}, u32[]{:S(2)}, u32[]{:S(2)}) collective-permute-start(f32[8,128]{1,0:T(8,128)S(1)} %get-tuple-element.19), channel_id=1, source_target_pairs={{0,3},{1,2},{2,1},{3,0},{4,7},{5,6},{6,5},{7,4},{8,11},{9,10},{10,... | collective-permute-start | bytes 12296 | tf_op jit(solution)/shard_map/grads/ppermute | solution.py:283
  143.7 22.1 %all-to-all-start.6 = ((f32[32,32,128]{2,1,0:T(8,128)}), f32[32,32,128]{2,1,0:T(8,128)S(1)}, u32[]{:S(2)}, u32[]{:S(2)}) async-start(f32[32,32,128]{2,1,0:T(8,128)} %place.2), calls=%async_computation.6 | async-start | bytes 1048576 | tf_op jit(solution)/shard_map/place/all_to_all | solution.py:278
  (4 other events, 3.0 us)

commit v6 on v5

--- a/solution.py
+++ b/solution.py
@@ -144,103 +144,98 @@
         out_ref[z] = total[z * cols : (z + 1) * cols, :].astype(BF)
 
 
-def hidden_kernel(parts_ref, bias_ref, late1_ref, late2_ref, late3_ref, out_ref):
-    del late1_ref, late2_ref, late3_ref
+def hidden_kernel(
+    parts_ref, bias_ref, index_ref, values_ref, live_ref, pieces_ref, pay_ref, left_ref, source, acc
+):
+    cols, targets = bias_ref.shape[0], live_ref.shape[1]
+    width = values_ref.shape[1]
+    wide = pay_ref.shape[2]
     total = parts_ref[0].astype(F32)
     for k in range(1, parts_ref.shape[0]):
         total = total + parts_ref[k].astype(F32)
     hidden = jnp.maximum(total + bias_ref[...], 0.0).astype(BF)
-    for c in range(out_ref.shape[0]):
-        out_ref[c] = hidden
-
-
-def grad_kernel(index_ref, hid_ref, values_ref, live_ref, cot_ref, agg_ref, out_ref, left, acc):
-    group, cols, targets = hid_ref.shape
-    width = values_ref.shape[1]
-    wide = group * cols
+    for k in range(pay_ref.shape[0]):
+        pay_ref[k, :cols, :] = hidden[:, :wide]
+        pay_ref[k, cols : 2 * cols, :] = hidden[:, wide:]
+        pay_ref[k, 2 * cols :, :] = pieces_ref[k]
+    live = live_ref[...].astype(BF)
+    for t in range(targets // width):
+        source[t] = hidden[:, t * width : (t + 1) * width]
     acc[...] = jnp.zeros_like(acc)
     for k in range(values_ref.shape[0]):
-        source = index_ref[k, 1]
-        at = pl.ds(pl.multiple_of(source * width, width), width)
-        rows = jnp.concatenate([hid_ref[j, :, at] for j in range(group)], axis=0)
         target = index_ref[k, 0]
-        acc[target] += lax.dot_general(rows, values_ref[k], NT, preferred_element_type=F32)
-    live = live_ref[...].astype(BF)
+        acc[target] += lax.dot_general(
+            source[index_ref[k, 1]], values_ref[k], NT, preferred_element_type=F32
+        )
     for t in range(targets // width):
         at = slice(t * width, (t + 1) * width)
-        tile = acc[t].astype(BF)
-        agg_ref[:, at] = tile
-        left[:wide, at] = tile * live[:, at]
-    for j in range(group):
-        left[wide + j * cols : wide + (j + 1) * cols, :] = hid_ref[j] * live
-    block = lax.dot_general(left[...], cot_ref[...], NT, preferred_element_type=F32)
-    at = 0
-    for w in range(2):
-        for r in range(0, cols, 8):
-            for c in range(0, cot_ref.shape[0], 128):
-                rows_of = [
-                    block[w * wide + j * cols + r : w * wide + j * cols + r + 8, c : c + 128]
-                    for j in range(group)
-                ]
-                out_ref[at] = jnp.concatenate(rows_of, axis=0).astype(BF)
-                at += 1
-
-
-def second_kernel(mine_ref, agg_ref, hid_ref, p0_ref, p1_ref, p2_ref, p3_ref, out_ref, weight, acts):
-    mine = mine_ref[0]
-    group, rows, targets = hid_ref.shape
-    for k, piece in enumerate((p0_ref, p1_ref, p2_ref, p3_ref)):
-        weight[jnp.bitwise_xor(mine, k)] = piece[...]
-    for j in range(group):
-        acts[2 * rows * j : 2 * rows * j + rows, :] = agg_ref[j * rows : (j + 1) * rows, :]
-        acts[2 * rows * j + rows : 2 * rows * (j + 1), :] = hid_ref[j]
-    both = jnp.concatenate([weight[j] for j in range(group)], axis=0)
-    total = lax.dot_general(both, acts[...], TN, preferred_element_type=F32)
-    n, cols, _ = out_ref.shape
+        left_ref[:cols, at] = acc[t].astype(BF) * live[:, at]
+    left_ref[cols:, :] = hidden * live
+
+
+def grad_kernel(left_ref, cot_ref, out_ref):
+    pieces, piece_rows, piece_cols = out_ref.shape
+    quarters = left_ref.shape[0] // piece_rows
+    for c in range(pieces // quarters):
+        cot = cot_ref[c * piece_cols : (c + 1) * piece_cols, :]
+        block = lax.dot_general(left_ref[...], cot, NT, preferred_element_type=F32).astype(BF)
+        for q in range(quarters):
+            out_ref[c * quarters + q] = block[q * piece_rows : (q + 1) * piece_rows, :]
+
+
+def second_kernel(
+    across_ref, index_ref, values_ref, p0_ref, p1_ref, p2_ref, p3_ref, out_ref, weight, acts, source, acc
+):
+    across = across_ref[0]
+    n, cols, targets = out_ref.shape
+    wide = p0_ref.shape[1]
+    width = values_ref.shape[1]
+    group = 4
+    for k, ref in enumerate((p0_ref, p1_ref, p2_ref, p3_ref)):
+        mine = slice(k * cols, (k + 1) * cols)
+        acts[mine, :wide] = ref[:cols, :]
+        acts[mine, wide:] = ref[cols : 2 * cols, :]
+        weight[mine, :] = ref[3 * cols :, :]
+        weight[(group + k) * cols : (group + k + 1) * cols, :] = ref[2 * cols : 3 * cols, :]
+        for t in range(targets // width):
+            half, at = divmod(t * width, wide)
+            source[t, mine, :] = ref[half * cols : (half + 1) * cols, at : at + width]
+    acc[...] = jnp.zeros_like(acc)
+    for k in range(values_ref.shape[0]):
+        target = index_ref[k, 0]
+        acc[target] += lax.dot_general(
+            source[index_ref[k, 1]], values_ref[k], NT, preferred_element_type=F32
+        )
+    for t in range(targets // width):
+        acts[group * cols :, t * width : (t + 1) * width] = acc[t].astype(BF)
+    total = lax.dot_general(weight[...], acts[...], TN, preferred_element_type=F32)
     for z in range(n):
-        out_ref[z] = total[z * cols : (z + 1) * cols, :].astype(BF)
-
-
-def sum_kernel(mine_ref, terms_ref, out_ref):
-    mine = mine_ref[0]
+        out_ref[jnp.bitwise_xor(across, z)] = total[z * cols : (z + 1) * cols, :].astype(BF)
+
+
+def copies_kernel(terms_ref, out_ref):
     total = terms_ref[0].astype(F32)
     for d in range(1, terms_ref.shape[0]):
         total = total + terms_ref[d].astype(F32)
-    rows = out_ref.shape[1]
-    for j in range(out_ref.shape[0]):
-        out_ref[jnp.bitwise_xor(mine, j)] = total[j * rows : (j + 1) * rows, :]
-
-
-def copies_kernel(p0_ref, p1_ref, p2_ref, p3_ref, late_ref, out_ref):
-    del late_ref
-    whole = jnp.concatenate([p0_ref[...], p1_ref[...], p2_ref[...], p3_ref[...]], axis=0)
     for d in range(out_ref.shape[0]):
-        out_ref[d] = whole
-
-
-def place_kernel(mine_ref, pieces_ref, neigh_ref, self_ref):
-    mine = mine_ref[0]
-    half = 64
-    at = 0
-    for out_ref in (neigh_ref, self_ref):
-        for r in range(0, out_ref.shape[0], 8):
-            for c in range(2):
-                parts = [
-                    pieces_ref[at, pl.ds(pl.multiple_of(jnp.bitwise_xor(mine, h) * 8, 8), 8), :]
-                    for h in range(4)
+        out_ref[d] = total
+
+
+def place_kernel(pieces_ref, neigh_ref, self_ref):
+    pieces, rows, cols = pieces_ref.shape
+    halves = neigh_ref.shape[0] // rows
+    quarters = 2 * halves
+    for i, out_ref in enumerate((neigh_ref, self_ref)):
+        for c in range(pieces // quarters):
+            for h in range(halves):
+                out_ref[h * rows : (h + 1) * rows, c * cols : (c + 1) * cols] = pieces_ref[
+                    c * quarters + i * halves + h
                 ]
-                for e in range(2):
-                    for p in range(2):
-                        pair = [parts[2 * p + i][:, e * half : (e + 1) * half] for i in range(2)]
-                        to = (8 * c + 4 * e + 2 * p) * half
-                        out_ref[r : r + 8, to : to + 2 * half] = jnp.concatenate(pair, axis=1)
-                at += 1
-
-
-def out_kernel(parts_ref, bias_ref, live_ref, out_ref):
-    total = parts_ref[0].astype(F32)
-    for k in range(1, parts_ref.shape[0]):
-        total = total + parts_ref[k].astype(F32)
+
+
+def out_kernel(p0_ref, p1_ref, p2_ref, p3_ref, bias_ref, live_ref, out_ref):
+    total = p0_ref[...].astype(F32) + p1_ref[...].astype(F32)
+    total = total + (p2_ref[...].astype(F32) + p3_ref[...].astype(F32))
     out_ref[...] = ((total + bias_ref[...]) * live_ref[...]).astype(BF)
 
 
@@ -272,6 +267,7 @@
     far = [[i + GROUP * j for j in range(blocks)] for i in range(GROUP)]
     z = lax.axis_index("feat")
     mine = (z % GROUP).reshape(1)
+    across = (z // GROUP).reshape(1)
     live = seed_live.reshape(1, targets).astype(F32)
 
     def swap(x, axis, among=None):
@@ -286,7 +282,7 @@
         return jax.ShapeDtypeStruct(dims, dtype)
 
     with jax.named_scope("cotangent"):
-        cot = lax.all_gather(cotangent.T, "feat", axis=0, tiled=True, axis_index_groups=far)
+        cot = lax.all_gather(cotangent.T, "feat", axis=0, tiled=True)
     with jax.named_scope("edges"):
         send = call(
             functools.partial(pack_kernel, groups, targets),
@@ -337,56 +333,58 @@
             late=(3,),
             nbytes=1 << 20,
         )(mine, neigh_two, self_two, first)
-        got = [trade(pieces[k], k) for k in range(1, GROUP)]
     with jax.named_scope("hidden"):
-        hidden = call(
-            hidden_kernel, shape(GROUP, hid, targets), 5, late=(2, 3, 4), nbytes=1 << 20
-        )(parts, bias_one.reshape(hid, 1), *got)
-        hidden = swap(hidden, "feat", near)
+        pay, left = call(
+            hidden_kernel,
+            (shape(GROUP, 4 * hid, wide), shape(2 * hid, targets)),
+            6,
+            scratch=[
+                pltpu.VMEM((targets // 128, hid, 128), BF),
+                pltpu.VMEM((targets // 128, hid, 128), F32),
+            ],
+            smem=(2,),
+            nbytes=1 << 20,
+        )(parts, bias_one.reshape(hid, 1), tile_index, tile_values, live, pieces)
+        got = [trade(pay[k], k) for k in range(1, GROUP)]
     with jax.named_scope("grads"):
-        agg, terms = call(
+        piece_rows = 2 * hid * full // 128 // groups
+        terms = call(
             grad_kernel,
-            (shape(wide, targets), shape(groups, GROUP * 8, 128)),
-            5,
-            scratch=[
-                pltpu.VMEM((2 * wide, targets), BF),
-                pltpu.VMEM((targets // 128, wide, 128), F32),
-            ],
-            smem=(0,),
-            flops=2 * 2 * wide * targets * wide,
-            nbytes=4 << 20,
-        )(tile_index, hidden, tile_values, live, cot)
+            shape(groups, piece_rows, 128),
+            2,
+            flops=2 * 2 * hid * targets * full,
+            nbytes=2 << 20,
+        )(left, cot)
         terms = swap(terms, "dp")
-        mine_sum = call(
-            sum_kernel, shape(GROUP, 8, 128, dtype=F32), 2, smem=(0,), nbytes=1 << 20
-        )(mine, terms)
-        sums = [mine_sum[0]] + [trade(mine_sum[k], k) for k in range(1, GROUP)]
+        spread = call(
+            copies_kernel, shape(groups, piece_rows, 128, dtype=F32), 1, nbytes=1 << 20
+        )(terms)
+        spread = swap(spread, "dp")
+        grad_neigh, grad_self = call(
+            place_kernel,
+            (shape(hid, full, dtype=F32), shape(hid, full, dtype=F32)),
+            1,
+            nbytes=1 << 20,
+        )(spread)
     with jax.named_scope("second"):
         second = call(
             second_kernel,
             shape(blocks, hid, targets),
             7,
-            scratch=[pltpu.VMEM((GROUP, 2 * hid, wide), BF), pltpu.VMEM((2 * wide, targets), BF)],
-            smem=(0,),
+            scratch=[
+                pltpu.VMEM((2 * wide, wide), BF),
+                pltpu.VMEM((2 * wide, targets), BF),
+                pltpu.VMEM((targets // 128, wide, 128), BF),
+                pltpu.VMEM((targets // 128, wide, 128), F32),
+            ],
+            smem=(0, 1),
             flops=2 * 2 * wide * wide * targets,
             nbytes=2 << 20,
-        )(mine, agg, hidden, pieces[0], *got)
-        second = swap(second, "feat", far)
-        second_out = call(out_kernel, shape(hid, targets), 3, nbytes=1 << 20)(
-            second, bias_two.reshape(hid, 1), live
+        )(across, tile_index, tile_values, pay[0], *got)
+        sums = [second[0]] + [trade(second[k], GROUP * k) for k in range(1, blocks)]
+        second_out = call(out_kernel, shape(hid, targets), 6, nbytes=1 << 20)(
+            *sums, bias_two.reshape(hid, 1), live
         ).T
-    with jax.named_scope("place"):
-        spread = call(
-            copies_kernel, shape(groups, GROUP * 8, 128, dtype=F32), 5, late=(4,), nbytes=1 << 20
-        )(*sums, second)
-        spread = swap(spread, "dp")
-        grad_neigh, grad_self = call(
-            place_kernel,
-            (shape(hid, full, dtype=F32), shape(hid, full, dtype=F32)),
-            2,
-            smem=(0,),
-            nbytes=1 << 20,
-        )(mine, spread)
     return (second_out, grad_neigh, grad_self)
 
 

time: 168 us -> 169 us (level)
  starting transfers between devices: 88.7 us -> 62.6 us
  between operations: 0.86 us -> 14.3 us
  waiting for transfers between devices: 33.1 us -> 40.9 us
  blocking collectives: 28.6 us -> 34.2 us
    all_to_all x6 -> x3, starting transfers between devices: 58.6 us -> 27.8 us  [swap(): lax.all_to_all(x, axis, split_axis=0, concat_axis=0, tiled=True, axis_ind...]
    all_to_all x1 -> x2, blocking collectives: 9.55 us -> 34.2 us  [swap(): lax.all_to_all(x, axis, split_axis=0, concat_axis=0, tiled=True, axis_ind...]
    all_gather x1 -> x0, blocking collectives: 19.1 us -> none  [body(): lax.all_gather(cotangent.T, 'feat', axis=0, tiled=True, axis_index_groups...]
    ppermute x9, waiting for transfers between devices: 15.1 us -> 21 us  [trade(): return lax.ppermute(x, 'feat', [(i, i ^ k) for i in range(n_feat)])]
    ppermute x9, starting transfers between devices: 30.1 us -> 34.7 us  [trade(): return lax.ppermute(x, 'feat', [(i, i ^ k) for i in range(n_feat)])]
    all_gather x0 -> x1, waiting for transfers between devices: none -> 3.71 us  [body(): cot = lax.all_gather(cotangent.T, 'feat', axis=0, tiled=True)]
    all_to_all x6 -> x3, waiting for transfers between devices: 17.9 us -> 15.5 us  [swap(): lax.all_to_all(x, axis, split_axis=0, concat_axis=0, tiled=True, axis_ind...]
    pallas_call x5 -> x4, Pallas kernels: 4.22 us -> 2.87 us  [the longest x1 0.88 us: body(): call(copies_kernel, shape(groups, piece_rows, 128, dtype=F32), 1, nbytes=...]
  transfers between devices with their start and end apart: 15 -> 13, of which waited for: 9 -> 7; matrix products, arithmetic and copies ran while one was open for 0% -> 0% of each run, Pallas kernels for 1% -> 5%
where the time goes in v6:
time: 169 us; the launch traced here: 167 us
  starting transfers between devices  62.6 us (37%)
  waiting for transfers between devices  40.9 us (24%)
  blocking collectives  34.2 us (20%)
  between operations  14.3 us (8%)
  Pallas kernels  10.8 us (6%)
  local copies, waits for them, and re-layouts  3.89 us (2%)
    ppermute x9, starting transfers between devices, trade(): return lax.ppermute(x, 'feat', [(i, i ^ k) for i in range(n_feat)])  34.7 us
    all_to_all x2, blocking collectives, swap(): lax.all_to_all(x, axis, split_axis=0, concat_axis=0, tiled=True, axis_ind...  34.2 us
    all_to_all x3, starting transfers between devices, swap(): lax.all_to_all(x, axis, split_axis=0, concat_axis=0, tiled=True, axis_ind...  27.8 us
    ppermute x9, waiting for transfers between devices, trade(): return lax.ppermute(x, 'feat', [(i, i ^ k) for i in range(n_feat)])  21 us
    all_to_all x3, waiting for transfers between devices, swap(): lax.all_to_all(x, axis, split_axis=0, concat_axis=0, tiled=True, axis_ind...  15.5 us
    all_gather x1, waiting for transfers between devices, body(): cot = lax.all_gather(cotangent.T, 'feat', axis=0, tiled=True)  3.71 us
    unnamed x27, local copies, waits for them, and re-layouts  3.61 us
  transfers between devices with their start and end apart: 13, of which 7 were waited for; matrix products, arithmetic and copies ran while one was open for 0% of the time, Pallas kernels for 5%

profile of v6, /device:TPU:1, one launch (start us, length us, event | category | flops | bytes accessed | tf_op | source)
XLA Modules:
  0.0 166.7 jit_solution(8343019792500690277)
XLA Ops:
  8.8 3.3 %edges.1.late_ref = bf16[32,64,128]{2,1,0:T(8,128)(2,1)} custom-call(bf16[48,2048]{1,0:T(8,128)(2,1)S(1)} %bitcast.37, s32[16,128]{1,0:T(8,128)S(1)} %bitcast.38), custom_call_target="tpu_custom_call" | custom-call | flops 1073741824 | bytes 8388608 | tf_op jit(solution)/shard_map/edges/pallas_call | solution.py:287
  12.2 10.5 %all-to-all-start = ((bf16[32,64,128]{2,1,0:T(8,128)(2,1)}), bf16[32,64,128]{2,1,0:T(8,128)(2,1)S(1)}, u32[]{:S(2)}, u32[]{:S(2)}) async-start(bf16[32,64,128]{2,1,0:T(8,128)(2,1)} %edges.1.late_ref), calls=%async_computation | async-start | bytes 1048576 | tf_op jit(solution)/shard_map/edges/all_to_all | solution.py:274
  22.9 1.9 %collective-permute-start = (bf16[192,256]{1,0:T(8,128)(2,1)S(1)}, bf16[192,256]{1,0:T(8,128)(2,1)S(1)}, u32[]{:S(2)}, u32[]{:S(2)}) collective-permute-start(bf16[192,256]{1,0:T(8,128)(2,1)S(1)} %get-tuple-element.18), channel_id=1, source_target_pairs={{0,1},{1,0},{2,3},{3,2},{4,5},{5,4},{6,7},{7,6},{8,9},{9,8},{10,11... | collective-permute-start | bytes 294920 | tf_op jit(solution)/shard_map/pieces/ppermute | solution.py:279
  24.9 4.7 %collective-permute-start.1 = (bf16[192,256]{1,0:T(8,128)(2,1)S(1)}, bf16[192,256]{1,0:T(8,128)(2,1)S(1)}, u32[]{:S(2)}, u32[]{:S(2)}) collective-permute-start(bf16[192,256]{1,0:T(8,128)(2,1)S(1)} %get-tuple-element.17), channel_id=1, source_target_pairs={{0,2},{1,3},{2,0},{3,1},{4,6},{5,7},{6,4},{7,5},{8,10},{9,11},{10,... | collective-permute-start | bytes 294920 | tf_op jit(solution)/shard_map/pieces/ppermute | solution.py:279
  29.6 2.7 %collective-permute-start.2 = (bf16[192,256]{1,0:T(8,128)(2,1)S(1)}, bf16[192,256]{1,0:T(8,128)(2,1)S(1)}, u32[]{:S(2)}, u32[]{:S(2)}) collective-permute-start(bf16[192,256]{1,0:T(8,128)(2,1)S(1)} %get-tuple-element.16), channel_id=1, source_target_pairs={{0,3},{1,2},{2,1},{3,0},{4,7},{5,6},{6,5},{7,4},{8,11},{9,10},{10,... | collective-permute-start | bytes 294920 | tf_op jit(solution)/shard_map/pieces/ppermute | solution.py:279
  32.2 2.1 %collective-permute-done.1.late2_ref.p2_ref = bf16[192,256]{1,0:T(8,128)(2,1)S(1)} collective-permute-done((bf16[192,256]{1,0:T(8,128)(2,1)S(1)}, bf16[192,256]{1,0:T(8,128)(2,1)S(1)}, u32[]{:S(2)}, u32[]{:S(2)}) %collective-permute-start.1) | collective-permute-done | bytes 98336 | tf_op jit(solution)/shard_map/pieces/ppermute | solution.py:279
  34.4 3.7 %collective-permute-done.2.late3_ref.p3_ref = bf16[192,256]{1,0:T(8,128)(2,1)S(1)} collective-permute-done((bf16[192,256]{1,0:T(8,128)(2,1)S(1)}, bf16[192,256]{1,0:T(8,128)(2,1)S(1)}, u32[]{:S(2)}, u32[]{:S(2)}) %collective-permute-start.2) | collective-permute-done | bytes 98336 | tf_op jit(solution)/shard_map/pieces/ppermute | solution.py:279
  38.0 1.4 mean.1
  39.4 10.0 %all_to_all.25.mean_ref = bf16[4,48,512]{2,1,0:T(8,128)(2,1)S(1)} all-to-all(bf16[4,48,512]{2,1,0:T(8,128)(2,1)S(1)} %mean.1), channel_id=1, replica_groups={{0,1,2,3},{4,5,6,7},{8,9,10,11},{12,13,14,15},{16,17,18,19},{20,21,22,2..., dimensions={0} | all-to-all | bytes 393216 | tf_op jit(solution)/shard_map/mean/all_to_all | solution.py:274
  50.5 13.5 %all-to-all-start.2 = ((bf16[4,64,512]{2,1,0:T(8,128)(2,1)}), bf16[4,64,512]{2,1,0:T(8,128)(2,1)S(1)}, u32[]{:S(2)}, u32[]{:S(2)}) async-start(bf16[4,64,512]{2,1,0:T(8,128)(2,1)} %first.1.late_ref), calls=%async_computation.2 | async-start | bytes 524288 | tf_op jit(solution)/shard_map/first/all_to_all | solution.py:274
  65.7 15.5 %all-to-all-done.2.parts_ref = bf16[4,64,512]{2,1,0:T(8,128)(2,1)S(1)} async-done(((bf16[4,64,512]{2,1,0:T(8,128)(2,1)}), bf16[4,64,512]{2,1,0:T(8,128)(2,1)S(1)}, u32[]{:S(2)}, u32[]{:S(2)}) %all-to-all-start.2) | async-done | bytes 262176 | tf_op jit(solution)/shard_map/first/all_to_all | solution.py:274
  82.1 3.7 %all-gather.2.cloned.1.call-done.cot_ref = bf16[1024,512]{1,0:T(8,128)(2,1)} async-done(((bf16[64,512]{1,0:T(8,128)(2,1)}), bf16[1024,512]{1,0:T(8,128)(2,1)}) %all-gather.2.cloned.1.call-update) | async-done | bytes 1048592 | tf_op jit(solution)/shard_map/cotangent/all_gather | solution.py:285
  85.8 1.2 copy-done
  87.4 24.1 %all_to_all.26.terms_ref = bf16[32,32,128]{2,1,0:T(8,128)(2,1)S(1)} all-to-all(bf16[32,32,128]{2,1,0:T(8,128)(2,1)S(1)} %grads.3), channel_id=1, replica_groups=mesh['dp'=32,'feat'=16] {'dp'}, dimensions={0} | all-to-all | bytes 524288 | tf_op jit(solution)/shard_map/grads/all_to_all | solution.py:274
  112.5 3.8 %all-to-all-start.4 = ((f32[32,32,128]{2,1,0:T(8,128)}), f32[32,32,128]{2,1,0:T(8,128)S(1)}, u32[]{:S(2)}, u32[]{:S(2)}) async-start(f32[32,32,128]{2,1,0:T(8,128)} %grads.4), calls=%async_computation.4 | async-start | bytes 1048576 | tf_op jit(solution)/shard_map/grads/all_to_all | solution.py:274
  116.3 1.9 %collective-permute-start.3 = (bf16[256,256]{1,0:T(8,128)(2,1)S(1)}, bf16[256,256]{1,0:T(8,128)(2,1)S(1)}, u32[]{:S(2)}, u32[]{:S(2)}) collective-permute-start(bf16[256,256]{1,0:T(8,128)(2,1)S(1)} %get-tuple-element.13), channel_id=1, source_target_pairs={{0,1},{1,0},{2,3},{3,2},{4,5},{5,4},{6,7},{7,6},{8,9},{9,8},{10,11... | collective-permute-start | bytes 393224 | tf_op jit(solution)/shard_map/hidden/ppermute | solution.py:279
  118.2 3.1 %collective-permute-start.4 = (bf16[256,256]{1,0:T(8,128)(2,1)S(1)}, bf16[256,256]{1,0:T(8,128)(2,1)S(1)}, u32[]{:S(2)}, u32[]{:S(2)}) collective-permute-start(bf16[256,256]{1,0:T(8,128)(2,1)S(1)} %get-tuple-element.12), channel_id=1, source_target_pairs={{0,2},{1,3},{2,0},{3,1},{4,6},{5,7},{6,4},{7,5},{8,10},{9,11},{10,... | collective-permute-start | bytes 393224 | tf_op jit(solution)/shard_map/hidden/ppermute | solution.py:279
  121.3 4.3 %collective-permute-start.5 = (bf16[256,256]{1,0:T(8,128)(2,1)S(1)}, bf16[256,256]{1,0:T(8,128)(2,1)S(1)}, u32[]{:S(2)}, u32[]{:S(2)}) collective-permute-start(bf16[256,256]{1,0:T(8,128)(2,1)S(1)} %get-tuple-element.11), channel_id=1, source_target_pairs={{0,3},{1,2},{2,1},{3,0},{4,7},{5,6},{6,5},{7,4},{8,11},{9,10},{10,... | collective-permute-start | bytes 393224 | tf_op jit(solution)/shard_map/hidden/ppermute | solution.py:279
  125.6 5.8 %collective-permute-done.4.p2_ref = bf16[256,256]{1,0:T(8,128)(2,1)S(1)} collective-permute-done((bf16[256,256]{1,0:T(8,128)(2,1)S(1)}, bf16[256,256]{1,0:T(8,128)(2,1)S(1)}, u32[]{:S(2)}, u32[]{:S(2)}) %collective-permute-start.4) | collective-permute-done | bytes 131104 | tf_op jit(solution)/shard_map/hidden/ppermute | solution.py:279
  132.5 4.8 %collective-permute-start.6 = (bf16[64,512]{1,0:T(8,128)(2,1)S(1)}, bf16[64,512]{1,0:T(8,128)(2,1)S(1)}, u32[]{:S(2)}, u32[]{:S(2)}) collective-permute-start(bf16[64,512]{1,0:T(8,128)(2,1)S(1)} %get-tuple-element.21), channel_id=1, source_target_pairs={{0,4},{1,5},{2,6},{3,7},{4,0},{5,1},{6,2},{7,3},{8,12},{9,13},{10,... | collective-permute-start | bytes 196616 | tf_op jit(solution)/shard_map/second/ppermute | solution.py:279
  137.3 7.1 %collective-permute-start.7 = (bf16[64,512]{1,0:T(8,128)(2,1)S(1)}, bf16[64,512]{1,0:T(8,128)(2,1)S(1)}, u32[]{:S(2)}, u32[]{:S(2)}) collective-permute-start(bf16[64,512]{1,0:T(8,128)(2,1)S(1)} %get-tuple-element.20), channel_id=1, source_target_pairs={{0,8},{1,9},{2,10},{3,11},{4,12},{5,13},{6,14},{7,15},{8,0},{9,1},... | collective-permute-start | bytes 196616 | tf_op jit(solution)/shard_map/second/ppermute | solution.py:279
  144.4 4.3 %collective-permute-start.8 = (bf16[64,512]{1,0:T(8,128)(2,1)S(1)}, bf16[64,512]{1,0:T(8,128)(2,1)S(1)}, u32[]{:S(2)}, u32[]{:S(2)}) collective-permute-start(bf16[64,512]{1,0:T(8,128)(2,1)S(1)} %get-tuple-element.19), channel_id=1, source_target_pairs={{0,12},{1,13},{2,14},{3,15},{4,8},{5,9},{6,10},{7,11},{8,4},{9,5},... | collective-permute-start | bytes 196616 | tf_op jit(solution)/shard_map/second/ppermute | solution.py:279
  148.8 3.0 %collective-permute-done.7.p2_ref = bf16[64,512]{1,0:T(8,128)(2,1)S(1)} collective-permute-done((bf16[64,512]{1,0:T(8,128)(2,1)S(1)}, bf16[64,512]{1,0:T(8,128)(2,1)S(1)}, u32[]{:S(2)}, u32[]{:S(2)}) %collective-permute-start.7) | collective-permute-done | bytes 65568 | tf_op jit(solution)/shard_map/second/ppermute | solution.py:279
  151.8 6.5 %collective-permute-done.8.p3_ref = bf16[64,512]{1,0:T(8,128)(2,1)S(1)} collective-permute-done((bf16[64,512]{1,0:T(8,128)(2,1)S(1)}, bf16[64,512]{1,0:T(8,128)(2,1)S(1)}, u32[]{:S(2)}, u32[]{:S(2)}) %collective-permute-start.8) | collective-permute-done | bytes 65568 | tf_op jit(solution)/shard_map/second/ppermute | solution.py:279
  (49 shorter events, 9.5 us)
Async XLA Ops:
  7.2 78.6 %all-gather.2.cloned.1.call-start = ((), (), s32[]{:S(2)}) async-start(), calls=%async_computation.5 | async-start | bytes 1114112 | tf_op jit(solution)/shard_map/cotangent/all_gather | solution.py:285
  7.2 0.7 copy-start.8
  7.9 0.9 copy-start.7
  12.2 10.6 %copy-start.4 = (bf16[48,1024]{1,0:T(8,128)(2,1)S(1)}, bf16[48,1024]{1,0:T(8,128)(2,1)}, u32[]{:S(2)}) copy-start(bf16[48,1024]{1,0:T(8,128)(2,1)} %neigh_ref.2) | copy-start | bytes 294916
  12.2 10.6 %copy-start.5 = (bf16[48,1024]{1,0:T(8,128)(2,1)S(1)}, bf16[48,1024]{1,0:T(8,128)(2,1)}, u32[]{:S(2)}) copy-start(bf16[48,1024]{1,0:T(8,128)(2,1)} %own_ref.2) | copy-start | bytes 294916
  12.2 10.6 %copy-start.6 = (bf16[512,48]{0,1:T(8,128)(2,1)S(1)}, bf16[512,48]{0,1:T(8,128)(2,1)}, u32[]{:S(2)}) copy-start(bf16[512,48]{0,1:T(8,128)(2,1)} %param.15) | copy-start | bytes 147460
  12.2 25.9 %all-to-all-start = ((bf16[32,64,128]{2,1,0:T(8,128)(2,1)}), bf16[32,64,128]{2,1,0:T(8,128)(2,1)S(1)}, u32[]{:S(2)}, u32[]{:S(2)}) async-start(bf16[32,64,128]{2,1,0:T(8,128)(2,1)} %edges.1.late_ref), calls=%async_computation | async-start | bytes 1048576 | tf_op jit(solution)/shard_map/edges/all_to_all | solution.py:274
  22.9 9.3 %collective-permute-start = (bf16[192,256]{1,0:T(8,128)(2,1)S(1)}, bf16[192,256]{1,0:T(8,128)(2,1)S(1)}, u32[]{:S(2)}, u32[]{:S(2)}) collective-permute-start(bf16[192,256]{1,0:T(8,128)(2,1)S(1)} %get-tuple-element.18), channel_id=1, source_target_pairs={{0,1},{1,0},{2,3},{3,2},{4,5},{5,4},{6,7},{7,6},{8,9},{9,8},{10,11... | collective-permute-start | bytes 294920 | tf_op jit(solution)/shard_map/pieces/ppermute | solution.py:279
  24.9 9.5 %collective-permute-start.1 = (bf16[192,256]{1,0:T(8,128)(2,1)S(1)}, bf16[192,256]{1,0:T(8,128)(2,1)S(1)}, u32[]{:S(2)}, u32[]{:S(2)}) collective-permute-start(bf16[192,256]{1,0:T(8,128)(2,1)S(1)} %get-tuple-element.17), channel_id=1, source_target_pairs={{0,2},{1,3},{2,0},{3,1},{4,6},{5,7},{6,4},{7,5},{8,10},{9,11},{10,... | collective-permute-start | bytes 294920 | tf_op jit(solution)/shard_map/pieces/ppermute | solution.py:279
  29.6 8.5 %collective-permute-start.2 = (bf16[192,256]{1,0:T(8,128)(2,1)S(1)}, bf16[192,256]{1,0:T(8,128)(2,1)S(1)}, u32[]{:S(2)}, u32[]{:S(2)}) collective-permute-start(bf16[192,256]{1,0:T(8,128)(2,1)S(1)} %get-tuple-element.16), channel_id=1, source_target_pairs={{0,3},{1,2},{2,1},{3,0},{4,7},{5,6},{6,5},{7,4},{8,11},{9,10},{10,... | collective-permute-start | bytes 294920 | tf_op jit(solution)/shard_map/pieces/ppermute | solution.py:279
  50.5 13.5 %copy-start.9 = (s32[512]{0:T(512)S(1)}, s32[512]{0:T(512)}, u32[]{:S(2)}) copy-start(s32[512]{0:T(512)} %param.21) | copy-start | bytes 6148
  50.5 15.1 %copy-start.2 = (bf16[64,1024]{1,0:T(8,128)(2,1)S(1)}, bf16[64,1024]{1,0:T(8,128)(2,1)}, u32[]{:S(2)}) copy-start(bf16[64,1024]{1,0:T(8,128)(2,1)} %neigh_ref.3) | copy-start | bytes 393220
  50.5 15.1 %copy-start.3 = (bf16[64,1024]{1,0:T(8,128)(2,1)S(1)}, bf16[64,1024]{1,0:T(8,128)(2,1)}, u32[]{:S(2)}) copy-start(bf16[64,1024]{1,0:T(8,128)(2,1)} %own_ref.3) | copy-start | bytes 393220
  50.5 30.7 %all-to-all-start.2 = ((bf16[4,64,512]{2,1,0:T(8,128)(2,1)}), bf16[4,64,512]{2,1,0:T(8,128)(2,1)S(1)}, u32[]{:S(2)}, u32[]{:S(2)}) async-start(bf16[4,64,512]{2,1,0:T(8,128)(2,1)} %first.1.late_ref), calls=%async_computation.2 | async-start | bytes 524288 | tf_op jit(solution)/shard_map/first/all_to_all | solution.py:274
  65.6 15.6 %copy-start.1 = (bf16[4,128,128]{2,1,0:T(8,128)(2,1)S(1)}, bf16[4,128,128]{2,1,0:T(8,128)(2,1)}, u32[]{:S(2)}) copy-start(bf16[4,128,128]{2,1,0:T(8,128)(2,1)} %values_ref.3) | copy-start | bytes 393220
  85.8 1.2 copy-start
  112.5 46.6 %all-to-all-start.4 = ((f32[32,32,128]{2,1,0:T(8,128)}), f32[32,32,128]{2,1,0:T(8,128)S(1)}, u32[]{:S(2)}, u32[]{:S(2)}) async-start(f32[32,32,128]{2,1,0:T(8,128)} %grads.4), calls=%async_computation.4 | async-start | bytes 1048576 | tf_op jit(solution)/shard_map/grads/all_to_all | solution.py:274
  116.3 9.3 %collective-permute-start.3 = (bf16[256,256]{1,0:T(8,128)(2,1)S(1)}, bf16[256,256]{1,0:T(8,128)(2,1)S(1)}, u32[]{:S(2)}, u32[]{:S(2)}) collective-permute-start(bf16[256,256]{1,0:T(8,128)(2,1)S(1)} %get-tuple-element.13), channel_id=1, source_target_pairs={{0,1},{1,0},{2,3},{3,2},{4,5},{5,4},{6,7},{7,6},{8,9},{9,8},{10,11... | collective-permute-start | bytes 393224 | tf_op jit(solution)/shard_map/hidden/ppermute | solution.py:279
  118.2 13.1 %collective-permute-start.4 = (bf16[256,256]{1,0:T(8,128)(2,1)S(1)}, bf16[256,256]{1,0:T(8,128)(2,1)S(1)}, u32[]{:S(2)}, u32[]{:S(2)}) collective-permute-start(bf16[256,256]{1,0:T(8,128)(2,1)S(1)} %get-tuple-element.12), channel_id=1, source_target_pairs={{0,2},{1,3},{2,0},{3,1},{4,6},{5,7},{6,4},{7,5},{8,10},{9,11},{10,... | collective-permute-start | bytes 393224 | tf_op jit(solution)/shard_map/hidden/ppermute | solution.py:279
  121.3 10.1 %collective-permute-start.5 = (bf16[256,256]{1,0:T(8,128)(2,1)S(1)}, bf16[256,256]{1,0:T(8,128)(2,1)S(1)}, u32[]{:S(2)}, u32[]{:S(2)}) collective-permute-start(bf16[256,256]{1,0:T(8,128)(2,1)S(1)} %get-tuple-element.11), channel_id=1, source_target_pairs={{0,3},{1,2},{2,1},{3,0},{4,7},{5,6},{6,5},{7,4},{8,11},{9,10},{10,... | collective-permute-start | bytes 393224 | tf_op jit(solution)/shard_map/hidden/ppermute | solution.py:279
  132.5 16.3 %collective-permute-start.6 = (bf16[64,512]{1,0:T(8,128)(2,1)S(1)}, bf16[64,512]{1,0:T(8,128)(2,1)S(1)}, u32[]{:S(2)}, u32[]{:S(2)}) collective-permute-start(bf16[64,512]{1,0:T(8,128)(2,1)S(1)} %get-tuple-element.21), channel_id=1, source_target_pairs={{0,4},{1,5},{2,6},{3,7},{4,0},{5,1},{6,2},{7,3},{8,12},{9,13},{10,... | collective-permute-start | bytes 196616 | tf_op jit(solution)/shard_map/second/ppermute | solution.py:279
  137.3 14.5 %collective-permute-start.7 = (bf16[64,512]{1,0:T(8,128)(2,1)S(1)}, bf16[64,512]{1,0:T(8,128)(2,1)S(1)}, u32[]{:S(2)}, u32[]{:S(2)}) collective-permute-start(bf16[64,512]{1,0:T(8,128)(2,1)S(1)} %get-tuple-element.20), channel_id=1, source_target_pairs={{0,8},{1,9},{2,10},{3,11},{4,12},{5,13},{6,14},{7,15},{8,0},{9,1},... | collective-permute-start | bytes 196616 | tf_op jit(solution)/shard_map/second/ppermute | solution.py:279
  144.4 4.3 %copy-start.12 = (f32[64]{0:T(128)S(1)}, f32[64]{0:T(128)}, u32[]{:S(2)}) copy-start(f32[64]{0:T(128)} %param.24) | copy-start | bytes 772
  144.4 13.9 %collective-permute-start.8 = (bf16[64,512]{1,0:T(8,128)(2,1)S(1)}, bf16[64,512]{1,0:T(8,128)(2,1)S(1)}, u32[]{:S(2)}, u32[]{:S(2)}) collective-permute-start(bf16[64,512]{1,0:T(8,128)(2,1)S(1)} %get-tuple-element.19), channel_id=1, source_target_pairs={{0,12},{1,13},{2,14},{3,15},{4,8},{5,9},{6,10},{7,11},{8,4},{9,5},... | collective-permute-start | bytes 196616 | tf_op jit(solution)/shard_map/second/ppermute | solution.py:279
  (2 other events, 1.3 us)
Sparse Core Ops, SparseCore 0:
  10.1 75.6 all-gather.1

commit v7 on v6

--- a/solution.py
+++ b/solution.py
@@ -213,7 +213,8 @@
         out_ref[jnp.bitwise_xor(across, z)] = total[z * cols : (z + 1) * cols, :].astype(BF)
 
 
-def copies_kernel(terms_ref, out_ref):
+def copies_kernel(terms_ref, late1_ref, late2_ref, late3_ref, out_ref):
+    del late1_ref, late2_ref, late3_ref
     total = terms_ref[0].astype(F32)
     for d in range(1, terms_ref.shape[0]):
         total = total + terms_ref[d].astype(F32)
@@ -357,8 +358,12 @@
         )(left, cot)
         terms = swap(terms, "dp")
         spread = call(
-            copies_kernel, shape(groups, piece_rows, 128, dtype=F32), 1, nbytes=1 << 20
-        )(terms)
+            copies_kernel,
+            shape(groups, piece_rows, 128, dtype=F32),
+            4,
+            late=(1, 2, 3),
+            nbytes=1 << 20,
+        )(terms, *got)
         spread = swap(spread, "dp")
         grad_neigh, grad_self = call(
             place_kernel,

time: 169 us -> 164 us (0.970)
  blocking collectives: 34.2 us -> 10 us
  starting transfers between devices: 62.6 us -> 84.5 us
  waiting for transfers between devices: 40.9 us -> 38.9 us
    all_to_all x2 -> x1, blocking collectives: 34.2 us -> 10 us  [swap(): lax.all_to_all(x, axis, split_axis=0, concat_axis=0, tiled=True, axis_ind...]
    all_to_all x3 -> x4, starting transfers between devices: 27.8 us -> 49.7 us  [swap(): lax.all_to_all(x, axis, split_axis=0, concat_axis=0, tiled=True, axis_ind...]
    all_to_all x3 -> x4, waiting for transfers between devices: 15.5 us -> 15.3 us  [swap(): lax.all_to_all(x, axis, split_axis=0, concat_axis=0, tiled=True, axis_ind...]
  transfers between devices with their start and end apart: 13 -> 14, of which waited for: 7 -> 7; matrix products, arithmetic and copies ran while one was open for 0% -> 0% of each run, Pallas kernels for 5% -> 5%
where the time goes in v7:
time: 164 us; the launch traced here: 163 us
  starting transfers between devices  84.5 us (52%)
  waiting for transfers between devices  38.9 us (24%)
  between operations  14.3 us (9%)
  Pallas kernels  11.5 us (7%)
  blocking collectives  10 us (6%)
  local copies, waits for them, and re-layouts  3.8 us (2%)
    all_to_all x4, starting transfers between devices, swap(): lax.all_to_all(x, axis, split_axis=0, concat_axis=0, tiled=True, axis_ind...  49.7 us
    ppermute x9, starting transfers between devices, trade(): return lax.ppermute(x, 'feat', [(i, i ^ k) for i in range(n_feat)])  34.7 us
    ppermute x9, waiting for transfers between devices, trade(): return lax.ppermute(x, 'feat', [(i, i ^ k) for i in range(n_feat)])  20.3 us
    all_to_all x4, waiting for transfers between devices, swap(): lax.all_to_all(x, axis, split_axis=0, concat_axis=0, tiled=True, axis_ind...  15.3 us
    all_to_all x1, blocking collectives, swap(): lax.all_to_all(x, axis, split_axis=0, concat_axis=0, tiled=True, axis_ind...  10 us
    unnamed x27, local copies, waits for them, and re-layouts  3.52 us
    pallas_call x1, Pallas kernels, body(): call(functools.partial(pack_kernel, groups, targets), shape(groups, ROWS,...  3.33 us
  transfers between devices with their start and end apart: 14, of which 7 were waited for; matrix products, arithmetic and copies ran while one was open for 0% of the time, Pallas kernels for 5%

profile of v7, /device:TPU:1, one launch (start us, length us, event | category | flops | bytes accessed | tf_op | source)
XLA Modules:
  0.0 162.9 jit_solution(17697838712768528649)
XLA Ops:
  8.8 3.3 %edges.1.late_ref = bf16[32,64,128]{2,1,0:T(8,128)(2,1)} custom-call(bf16[48,2048]{1,0:T(8,128)(2,1)S(1)} %bitcast.37, s32[16,128]{1,0:T(8,128)S(1)} %bitcast.38), custom_call_target="tpu_custom_call" | custom-call | flops 1073741824 | bytes 8388608 | tf_op jit(solution)/shard_map/edges/pallas_call | solution.py:288
  12.2 10.5 %all-to-all-start = ((bf16[32,64,128]{2,1,0:T(8,128)(2,1)}), bf16[32,64,128]{2,1,0:T(8,128)(2,1)S(1)}, u32[]{:S(2)}, u32[]{:S(2)}) async-start(bf16[32,64,128]{2,1,0:T(8,128)(2,1)} %edges.1.late_ref), calls=%async_computation | async-start | bytes 1048576 | tf_op jit(solution)/shard_map/edges/all_to_all | solution.py:275
  22.9 1.9 %collective-permute-start = (bf16[192,256]{1,0:T(8,128)(2,1)S(1)}, bf16[192,256]{1,0:T(8,128)(2,1)S(1)}, u32[]{:S(2)}, u32[]{:S(2)}) collective-permute-start(bf16[192,256]{1,0:T(8,128)(2,1)S(1)} %get-tuple-element.18), channel_id=1, source_target_pairs={{0,1},{1,0},{2,3},{3,2},{4,5},{5,4},{6,7},{7,6},{8,9},{9,8},{10,11... | collective-permute-start | bytes 294920 | tf_op jit(solution)/shard_map/pieces/ppermute | solution.py:280
  24.9 4.7 %collective-permute-start.1 = (bf16[192,256]{1,0:T(8,128)(2,1)S(1)}, bf16[192,256]{1,0:T(8,128)(2,1)S(1)}, u32[]{:S(2)}, u32[]{:S(2)}) collective-permute-start(bf16[192,256]{1,0:T(8,128)(2,1)S(1)} %get-tuple-element.17), channel_id=1, source_target_pairs={{0,2},{1,3},{2,0},{3,1},{4,6},{5,7},{6,4},{7,5},{8,10},{9,11},{10,... | collective-permute-start | bytes 294920 | tf_op jit(solution)/shard_map/pieces/ppermute | solution.py:280
  29.6 2.7 %collective-permute-start.2 = (bf16[192,256]{1,0:T(8,128)(2,1)S(1)}, bf16[192,256]{1,0:T(8,128)(2,1)S(1)}, u32[]{:S(2)}, u32[]{:S(2)}) collective-permute-start(bf16[192,256]{1,0:T(8,128)(2,1)S(1)} %get-tuple-element.16), channel_id=1, source_target_pairs={{0,3},{1,2},{2,1},{3,0},{4,7},{5,6},{6,5},{7,4},{8,11},{9,10},{10,... | collective-permute-start | bytes 294920 | tf_op jit(solution)/shard_map/pieces/ppermute | solution.py:280
  32.2 2.1 %collective-permute-done.1.late2_ref.p2_ref = bf16[192,256]{1,0:T(8,128)(2,1)S(1)} collective-permute-done((bf16[192,256]{1,0:T(8,128)(2,1)S(1)}, bf16[192,256]{1,0:T(8,128)(2,1)S(1)}, u32[]{:S(2)}, u32[]{:S(2)}) %collective-permute-start.1) | collective-permute-done | bytes 98336 | tf_op jit(solution)/shard_map/pieces/ppermute | solution.py:280
  34.4 3.7 %collective-permute-done.2.late3_ref.p3_ref = bf16[192,256]{1,0:T(8,128)(2,1)S(1)} collective-permute-done((bf16[192,256]{1,0:T(8,128)(2,1)S(1)}, bf16[192,256]{1,0:T(8,128)(2,1)S(1)}, u32[]{:S(2)}, u32[]{:S(2)}) %collective-permute-start.2) | collective-permute-done | bytes 98336 | tf_op jit(solution)/shard_map/pieces/ppermute | solution.py:280
  38.0 1.4 mean.1
  39.4 10.0 %all_to_all.25.mean_ref = bf16[4,48,512]{2,1,0:T(8,128)(2,1)S(1)} all-to-all(bf16[4,48,512]{2,1,0:T(8,128)(2,1)S(1)} %mean.1), channel_id=1, replica_groups={{0,1,2,3},{4,5,6,7},{8,9,10,11},{12,13,14,15},{16,17,18,19},{20,21,22,2..., dimensions={0} | all-to-all | bytes 393216 | tf_op jit(solution)/shard_map/mean/all_to_all | solution.py:275
  50.5 13.8 %all-to-all-start.2 = ((bf16[4,64,512]{2,1,0:T(8,128)(2,1)}), bf16[4,64,512]{2,1,0:T(8,128)(2,1)S(1)}, u32[]{:S(2)}, u32[]{:S(2)}) async-start(bf16[4,64,512]{2,1,0:T(8,128)(2,1)} %first.1.late_ref), calls=%async_computation.2 | async-start | bytes 524288 | tf_op jit(solution)/shard_map/first/all_to_all | solution.py:275
  65.9 15.3 %all-to-all-done.2.parts_ref = bf16[4,64,512]{2,1,0:T(8,128)(2,1)S(1)} async-done(((bf16[4,64,512]{2,1,0:T(8,128)(2,1)}), bf16[4,64,512]{2,1,0:T(8,128)(2,1)S(1)}, u32[]{:S(2)}, u32[]{:S(2)}) %all-to-all-start.2) | async-done | bytes 262176 | tf_op jit(solution)/shard_map/first/all_to_all | solution.py:275
  82.1 2.6 %all-gather.2.cloned.1.call-done.cot_ref = bf16[1024,512]{1,0:T(8,128)(2,1)} async-done(((bf16[64,512]{1,0:T(8,128)(2,1)}), bf16[1024,512]{1,0:T(8,128)(2,1)}) %all-gather.2.cloned.1.call-update) | async-done | bytes 1048592 | tf_op jit(solution)/shard_map/cotangent/all_gather | solution.py:286
  84.7 1.2 copy-done
  87.0 16.4 %all-to-all-start.3 = ((bf16[32,32,128]{2,1,0:T(8,128)(2,1)}), bf16[32,32,128]{2,1,0:T(8,128)(2,1)S(1)}, u32[]{:S(2)}, u32[]{:S(2)}) async-start(bf16[32,32,128]{2,1,0:T(8,128)(2,1)} %grads.3), calls=%async_computation.3 | async-start | bytes 524288 | tf_op jit(solution)/shard_map/grads/all_to_all | solution.py:275
  103.5 2.4 %collective-permute-start.3 = (bf16[256,256]{1,0:T(8,128)(2,1)S(1)}, bf16[256,256]{1,0:T(8,128)(2,1)S(1)}, u32[]{:S(2)}, u32[]{:S(2)}) collective-permute-start(bf16[256,256]{1,0:T(8,128)(2,1)S(1)} %get-tuple-element.13), channel_id=1, source_target_pairs={{0,1},{1,0},{2,3},{3,2},{4,5},{5,4},{6,7},{7,6},{8,9},{9,8},{10,11... | collective-permute-start | bytes 393224 | tf_op jit(solution)/shard_map/hidden/ppermute | solution.py:280
  105.9 3.2 %collective-permute-start.4 = (bf16[256,256]{1,0:T(8,128)(2,1)S(1)}, bf16[256,256]{1,0:T(8,128)(2,1)S(1)}, u32[]{:S(2)}, u32[]{:S(2)}) collective-permute-start(bf16[256,256]{1,0:T(8,128)(2,1)S(1)} %get-tuple-element.12), channel_id=1, source_target_pairs={{0,2},{1,3},{2,0},{3,1},{4,6},{5,7},{6,4},{7,5},{8,10},{9,11},{10,... | collective-permute-start | bytes 393224 | tf_op jit(solution)/shard_map/hidden/ppermute | solution.py:280
  109.1 3.7 %collective-permute-start.5 = (bf16[256,256]{1,0:T(8,128)(2,1)S(1)}, bf16[256,256]{1,0:T(8,128)(2,1)S(1)}, u32[]{:S(2)}, u32[]{:S(2)}) collective-permute-start(bf16[256,256]{1,0:T(8,128)(2,1)S(1)} %get-tuple-element.11), channel_id=1, source_target_pairs={{0,3},{1,2},{2,1},{3,0},{4,7},{5,6},{6,5},{7,4},{8,11},{9,10},{10,... | collective-permute-start | bytes 393224 | tf_op jit(solution)/shard_map/hidden/ppermute | solution.py:280
  112.8 6.3 %collective-permute-done.4.p2_ref.late2_ref = bf16[256,256]{1,0:T(8,128)(2,1)S(1)} collective-permute-done((bf16[256,256]{1,0:T(8,128)(2,1)S(1)}, bf16[256,256]{1,0:T(8,128)(2,1)S(1)}, u32[]{:S(2)}, u32[]{:S(2)}) %collective-permute-start.4) | collective-permute-done | bytes 131104 | tf_op jit(solution)/shard_map/hidden/ppermute | solution.py:280
  120.0 8.9 %all-to-all-start.4 = ((f32[32,32,128]{2,1,0:T(8,128)}), f32[32,32,128]{2,1,0:T(8,128)S(1)}, u32[]{:S(2)}, u32[]{:S(2)}) async-start(f32[32,32,128]{2,1,0:T(8,128)} %grads.4), calls=%async_computation.4 | async-start | bytes 1048576 | tf_op jit(solution)/shard_map/grads/all_to_all | solution.py:275
  130.1 4.7 %collective-permute-start.6 = (bf16[64,512]{1,0:T(8,128)(2,1)S(1)}, bf16[64,512]{1,0:T(8,128)(2,1)S(1)}, u32[]{:S(2)}, u32[]{:S(2)}) collective-permute-start(bf16[64,512]{1,0:T(8,128)(2,1)S(1)} %get-tuple-element.21), channel_id=1, source_target_pairs={{0,4},{1,5},{2,6},{3,7},{4,0},{5,1},{6,2},{7,3},{8,12},{9,13},{10,... | collective-permute-start | bytes 196616 | tf_op jit(solution)/shard_map/second/ppermute | solution.py:280
  134.8 7.0 %collective-permute-start.7 = (bf16[64,512]{1,0:T(8,128)(2,1)S(1)}, bf16[64,512]{1,0:T(8,128)(2,1)S(1)}, u32[]{:S(2)}, u32[]{:S(2)}) collective-permute-start(bf16[64,512]{1,0:T(8,128)(2,1)S(1)} %get-tuple-element.20), channel_id=1, source_target_pairs={{0,8},{1,9},{2,10},{3,11},{4,12},{5,13},{6,14},{7,15},{8,0},{9,1},... | collective-permute-start | bytes 196616 | tf_op jit(solution)/shard_map/second/ppermute | solution.py:280
  141.8 4.5 %collective-permute-start.8 = (bf16[64,512]{1,0:T(8,128)(2,1)S(1)}, bf16[64,512]{1,0:T(8,128)(2,1)S(1)}, u32[]{:S(2)}, u32[]{:S(2)}) collective-permute-start(bf16[64,512]{1,0:T(8,128)(2,1)S(1)} %get-tuple-element.19), channel_id=1, source_target_pairs={{0,12},{1,13},{2,14},{3,15},{4,8},{5,9},{6,10},{7,11},{8,4},{9,5},... | collective-permute-start | bytes 196616 | tf_op jit(solution)/shard_map/second/ppermute | solution.py:280
  146.4 2.2 %collective-permute-done.7.p2_ref = bf16[64,512]{1,0:T(8,128)(2,1)S(1)} collective-permute-done((bf16[64,512]{1,0:T(8,128)(2,1)S(1)}, bf16[64,512]{1,0:T(8,128)(2,1)S(1)}, u32[]{:S(2)}, u32[]{:S(2)}) %collective-permute-start.7) | collective-permute-done | bytes 65568 | tf_op jit(solution)/shard_map/second/ppermute | solution.py:280
  148.6 5.9 %collective-permute-done.8.p3_ref = bf16[64,512]{1,0:T(8,128)(2,1)S(1)} collective-permute-done((bf16[64,512]{1,0:T(8,128)(2,1)S(1)}, bf16[64,512]{1,0:T(8,128)(2,1)S(1)}, u32[]{:S(2)}, u32[]{:S(2)}) %collective-permute-start.8) | collective-permute-done | bytes 65568 | tf_op jit(solution)/shard_map/second/ppermute | solution.py:280
  (50 shorter events, 10.1 us)
Async XLA Ops:
  7.2 77.5 %all-gather.2.cloned.1.call-start = ((), (), s32[]{:S(2)}) async-start(), calls=%async_computation.5 | async-start | bytes 1114112 | tf_op jit(solution)/shard_map/cotangent/all_gather | solution.py:286
  7.9 0.9 copy-start.7
  12.2 10.6 %copy-start.4 = (bf16[48,1024]{1,0:T(8,128)(2,1)S(1)}, bf16[48,1024]{1,0:T(8,128)(2,1)}, u32[]{:S(2)}) copy-start(bf16[48,1024]{1,0:T(8,128)(2,1)} %neigh_ref.2) | copy-start | bytes 294916
  12.2 10.6 %copy-start.5 = (bf16[48,1024]{1,0:T(8,128)(2,1)S(1)}, bf16[48,1024]{1,0:T(8,128)(2,1)}, u32[]{:S(2)}) copy-start(bf16[48,1024]{1,0:T(8,128)(2,1)} %own_ref.2) | copy-start | bytes 294916
  12.2 10.6 %copy-start.6 = (bf16[512,48]{0,1:T(8,128)(2,1)S(1)}, bf16[512,48]{0,1:T(8,128)(2,1)}, u32[]{:S(2)}) copy-start(bf16[512,48]{0,1:T(8,128)(2,1)} %param.15) | copy-start | bytes 147460
  12.2 25.9 %all-to-all-start = ((bf16[32,64,128]{2,1,0:T(8,128)(2,1)}), bf16[32,64,128]{2,1,0:T(8,128)(2,1)S(1)}, u32[]{:S(2)}, u32[]{:S(2)}) async-start(bf16[32,64,128]{2,1,0:T(8,128)(2,1)} %edges.1.late_ref), calls=%async_computation | async-start | bytes 1048576 | tf_op jit(solution)/shard_map/edges/all_to_all | solution.py:275
  22.9 9.3 %collective-permute-start = (bf16[192,256]{1,0:T(8,128)(2,1)S(1)}, bf16[192,256]{1,0:T(8,128)(2,1)S(1)}, u32[]{:S(2)}, u32[]{:S(2)}) collective-permute-start(bf16[192,256]{1,0:T(8,128)(2,1)S(1)} %get-tuple-element.18), channel_id=1, source_target_pairs={{0,1},{1,0},{2,3},{3,2},{4,5},{5,4},{6,7},{7,6},{8,9},{9,8},{10,11... | collective-permute-start | bytes 294920 | tf_op jit(solution)/shard_map/pieces/ppermute | solution.py:280
  24.9 9.5 %collective-permute-start.1 = (bf16[192,256]{1,0:T(8,128)(2,1)S(1)}, bf16[192,256]{1,0:T(8,128)(2,1)S(1)}, u32[]{:S(2)}, u32[]{:S(2)}) collective-permute-start(bf16[192,256]{1,0:T(8,128)(2,1)S(1)} %get-tuple-element.17), channel_id=1, source_target_pairs={{0,2},{1,3},{2,0},{3,1},{4,6},{5,7},{6,4},{7,5},{8,10},{9,11},{10,... | collective-permute-start | bytes 294920 | tf_op jit(solution)/shard_map/pieces/ppermute | solution.py:280
  29.6 8.5 %collective-permute-start.2 = (bf16[192,256]{1,0:T(8,128)(2,1)S(1)}, bf16[192,256]{1,0:T(8,128)(2,1)S(1)}, u32[]{:S(2)}, u32[]{:S(2)}) collective-permute-start(bf16[192,256]{1,0:T(8,128)(2,1)S(1)} %get-tuple-element.16), channel_id=1, source_target_pairs={{0,3},{1,2},{2,1},{3,0},{4,7},{5,6},{6,5},{7,4},{8,11},{9,10},{10,... | collective-permute-start | bytes 294920 | tf_op jit(solution)/shard_map/pieces/ppermute | solution.py:280
  50.5 13.8 %copy-start.10 = (s32[4,2]{0,1:T(2,128)S(1)}, s32[4,2]{0,1:T(2,128)}, u32[]{:S(2)}) copy-start(s32[4,2]{0,1:T(2,128)} %param.19) | copy-start | bytes 100
  50.5 15.2 %copy-start.2 = (bf16[64,1024]{1,0:T(8,128)(2,1)S(1)}, bf16[64,1024]{1,0:T(8,128)(2,1)}, u32[]{:S(2)}) copy-start(bf16[64,1024]{1,0:T(8,128)(2,1)} %neigh_ref.3) | copy-start | bytes 393220
  50.5 15.2 %copy-start.3 = (bf16[64,1024]{1,0:T(8,128)(2,1)S(1)}, bf16[64,1024]{1,0:T(8,128)(2,1)}, u32[]{:S(2)}) copy-start(bf16[64,1024]{1,0:T(8,128)(2,1)} %own_ref.3) | copy-start | bytes 393220
  50.5 30.7 %all-to-all-start.2 = ((bf16[4,64,512]{2,1,0:T(8,128)(2,1)}), bf16[4,64,512]{2,1,0:T(8,128)(2,1)S(1)}, u32[]{:S(2)}, u32[]{:S(2)}) async-start(bf16[4,64,512]{2,1,0:T(8,128)(2,1)} %first.1.late_ref), calls=%async_computation.2 | async-start | bytes 524288 | tf_op jit(solution)/shard_map/first/all_to_all | solution.py:275
  65.7 15.5 %copy-start.1 = (bf16[4,128,128]{2,1,0:T(8,128)(2,1)S(1)}, bf16[4,128,128]{2,1,0:T(8,128)(2,1)}, u32[]{:S(2)}) copy-start(bf16[4,128,128]{2,1,0:T(8,128)(2,1)} %values_ref.3) | copy-start | bytes 393220
  84.7 1.2 copy-start
  87.0 32.1 %all-to-all-start.3 = ((bf16[32,32,128]{2,1,0:T(8,128)(2,1)}), bf16[32,32,128]{2,1,0:T(8,128)(2,1)S(1)}, u32[]{:S(2)}, u32[]{:S(2)}) async-start(bf16[32,32,128]{2,1,0:T(8,128)(2,1)} %grads.3), calls=%async_computation.3 | async-start | bytes 524288 | tf_op jit(solution)/shard_map/grads/all_to_all | solution.py:275
  103.5 9.3 %collective-permute-start.3 = (bf16[256,256]{1,0:T(8,128)(2,1)S(1)}, bf16[256,256]{1,0:T(8,128)(2,1)S(1)}, u32[]{:S(2)}, u32[]{:S(2)}) collective-permute-start(bf16[256,256]{1,0:T(8,128)(2,1)S(1)} %get-tuple-element.13), channel_id=1, source_target_pairs={{0,1},{1,0},{2,3},{3,2},{4,5},{5,4},{6,7},{7,6},{8,9},{9,8},{10,11... | collective-permute-start | bytes 393224 | tf_op jit(solution)/shard_map/hidden/ppermute | solution.py:280
  105.9 13.2 %collective-permute-start.4 = (bf16[256,256]{1,0:T(8,128)(2,1)S(1)}, bf16[256,256]{1,0:T(8,128)(2,1)S(1)}, u32[]{:S(2)}, u32[]{:S(2)}) collective-permute-start(bf16[256,256]{1,0:T(8,128)(2,1)S(1)} %get-tuple-element.12), channel_id=1, source_target_pairs={{0,2},{1,3},{2,0},{3,1},{4,6},{5,7},{6,4},{7,5},{8,10},{9,11},{10,... | collective-permute-start | bytes 393224 | tf_op jit(solution)/shard_map/hidden/ppermute | solution.py:280
  109.1 10.0 %collective-permute-start.5 = (bf16[256,256]{1,0:T(8,128)(2,1)S(1)}, bf16[256,256]{1,0:T(8,128)(2,1)S(1)}, u32[]{:S(2)}, u32[]{:S(2)}) collective-permute-start(bf16[256,256]{1,0:T(8,128)(2,1)S(1)} %get-tuple-element.11), channel_id=1, source_target_pairs={{0,3},{1,2},{2,1},{3,0},{4,7},{5,6},{6,5},{7,4},{8,11},{9,10},{10,... | collective-permute-start | bytes 393224 | tf_op jit(solution)/shard_map/hidden/ppermute | solution.py:280
  120.0 35.3 %all-to-all-start.4 = ((f32[32,32,128]{2,1,0:T(8,128)}), f32[32,32,128]{2,1,0:T(8,128)S(1)}, u32[]{:S(2)}, u32[]{:S(2)}) async-start(f32[32,32,128]{2,1,0:T(8,128)} %grads.4), calls=%async_computation.4 | async-start | bytes 1048576 | tf_op jit(solution)/shard_map/grads/all_to_all | solution.py:275
  130.1 16.3 %collective-permute-start.6 = (bf16[64,512]{1,0:T(8,128)(2,1)S(1)}, bf16[64,512]{1,0:T(8,128)(2,1)S(1)}, u32[]{:S(2)}, u32[]{:S(2)}) collective-permute-start(bf16[64,512]{1,0:T(8,128)(2,1)S(1)} %get-tuple-element.21), channel_id=1, source_target_pairs={{0,4},{1,5},{2,6},{3,7},{4,0},{5,1},{6,2},{7,3},{8,12},{9,13},{10,... | collective-permute-start | bytes 196616 | tf_op jit(solution)/shard_map/second/ppermute | solution.py:280
  134.8 13.8 %collective-permute-start.7 = (bf16[64,512]{1,0:T(8,128)(2,1)S(1)}, bf16[64,512]{1,0:T(8,128)(2,1)S(1)}, u32[]{:S(2)}, u32[]{:S(2)}) collective-permute-start(bf16[64,512]{1,0:T(8,128)(2,1)S(1)} %get-tuple-element.20), channel_id=1, source_target_pairs={{0,8},{1,9},{2,10},{3,11},{4,12},{5,13},{6,14},{7,15},{8,0},{9,1},... | collective-permute-start | bytes 196616 | tf_op jit(solution)/shard_map/second/ppermute | solution.py:280
  141.8 4.5 %copy-start.12 = (f32[64]{0:T(128)S(1)}, f32[64]{0:T(128)}, u32[]{:S(2)}) copy-start(f32[64]{0:T(128)} %param.24) | copy-start | bytes 772
  141.8 12.8 %collective-permute-start.8 = (bf16[64,512]{1,0:T(8,128)(2,1)S(1)}, bf16[64,512]{1,0:T(8,128)(2,1)S(1)}, u32[]{:S(2)}, u32[]{:S(2)}) collective-permute-start(bf16[64,512]{1,0:T(8,128)(2,1)S(1)} %get-tuple-element.19), channel_id=1, source_target_pairs={{0,12},{1,13},{2,14},{3,15},{4,8},{5,9},{6,10},{7,11},{8,4},{9,5},... | collective-permute-start | bytes 196616 | tf_op jit(solution)/shard_map/second/ppermute | solution.py:280
  (3 other events, 2.0 us)
Sparse Core Ops, SparseCore 0:
  10.1 74.5 all-gather.1

commit v8 on v5

--- a/solution.py
+++ b/solution.py
@@ -80,33 +80,29 @@
     return sets
 
 
-def first_pieces_kernel(mine_ref, neigh_ref, own_ref, self_ref, late_ref, out_ref):
+def first_pieces_kernel(neigh_ref, own_ref, self_ref, cot_ref, late_ref, out_ref, cot_out_ref):
     del late_ref
-    mine = mine_ref[0]
     rows = neigh_ref.shape[0]
     group, _, width = out_ref.shape
     both = zip(column_sets(neigh_ref[...], group), column_sets(own_ref[...], group))
     for j, (neigh, own) in enumerate(both):
-        to = jnp.bitwise_xor(mine, j)
-        out_ref[to, :rows, :] = neigh
-        out_ref[to, rows : 2 * rows, :] = own
-        out_ref[to, 2 * rows : 3 * rows, :] = self_ref[:, :width]
-        out_ref[to, 3 * rows :, :] = self_ref[:, width:]
-
-
-def second_pieces_kernel(mine_ref, neigh_ref, own_ref, late_ref, out_ref):
+        out_ref[j, :rows, : width // 2] = neigh
+        out_ref[j, :rows, width // 2 :] = own
+        out_ref[j, rows:, :] = self_ref[...]
+    cot_out_ref[...] = cot_ref[...]
+
+
+def second_pieces_kernel(neigh_ref, own_ref, late_ref, out_ref):
     del late_ref
-    mine = mine_ref[0]
-    rows = neigh_ref.shape[0]
-    both = zip(column_sets(neigh_ref[...], out_ref.shape[0]), column_sets(own_ref[...], out_ref.shape[0]))
+    group, _, width = out_ref.shape
+    both = zip(column_sets(neigh_ref[...], group), column_sets(own_ref[...], group))
     for j, (neigh, own) in enumerate(both):
-        to = jnp.bitwise_xor(mine, j)
-        out_ref[to, :rows, :] = neigh
-        out_ref[to, rows:, :] = own
-
-
-def mean_kernel(cols, recv_ref, late1_ref, late2_ref, late3_ref, out_ref):
-    del late1_ref, late2_ref, late3_ref
+        out_ref[j, :, : width // 2] = neigh
+        out_ref[j, :, width // 2 :] = own
+
+
+def mean_kernel(cols, recv_ref, pieces_ref, late_ref, out_ref):
+    del late_ref
     groups, rows, cap = recv_ref.shape
     targets = out_ref.shape[2]
     half = targets // 2
@@ -122,57 +118,61 @@
     degree = jnp.maximum(acc[cols + 1 : cols + 2, :], 1.0)
     mean = (acc[:cols, :] / degree).astype(BF)
     for j in range(out_ref.shape[0]):
-        out_ref[j] = mean
-
-
-def first_kernel(
-    mine_ref, mean_ref, p0_ref, p1_ref, p2_ref, p3_ref, out_ref, weight, acts
-):
-    mine = mine_ref[0]
-    group, rows, targets = mean_ref.shape
+        out_ref[j, :cols, :] = mean
+        out_ref[j, cols:, :] = pieces_ref[j]
+
+
+def first_kernel(got_ref, out_ref, weight, acts):
+    group, rows, targets = got_ref.shape
+    rows = rows // 3
     width = targets // 2
-    for k, piece in enumerate((p0_ref, p1_ref, p2_ref, p3_ref)):
-        at = slice(2 * rows * k, 2 * rows * (k + 1))
-        mid = 2 * rows * k + rows
-        weight[at, :] = piece[: 2 * rows, :]
-        acts[2 * rows * k : mid, :] = mean_ref[jnp.bitwise_xor(mine, k)]
-        acts[mid : mid + rows, :width] = piece[2 * rows : 3 * rows, :]
-        acts[mid : mid + rows, width:] = piece[3 * rows :, :]
+    for j in range(group):
+        low, mid, high = 2 * rows * j, 2 * rows * j + rows, 2 * rows * (j + 1)
+        acts[low:mid, :] = got_ref[j, :rows, :]
+        weight[low:mid, :] = got_ref[j, rows : 2 * rows, :width]
+        weight[mid:high, :] = got_ref[j, rows : 2 * rows, width:]
+        acts[mid:high, :] = got_ref[j, 2 * rows :, :]
     total = lax.dot_general(weight[...], acts[...], TN, preferred_element_type=F32)
     cols = out_ref.shape[1]
     for z in range(out_ref.shape[0]):
         out_ref[z] = total[z * cols : (z + 1) * cols, :].astype(BF)
 
 
-def hidden_kernel(parts_ref, bias_ref, late1_ref, late2_ref, late3_ref, out_ref):
-    del late1_ref, late2_ref, late3_ref
+def hidden_kernel(parts_ref, bias_ref, pieces_ref, out_ref):
+    cols = bias_ref.shape[0]
     total = parts_ref[0].astype(F32)
     for k in range(1, parts_ref.shape[0]):
         total = total + parts_ref[k].astype(F32)
     hidden = jnp.maximum(total + bias_ref[...], 0.0).astype(BF)
     for c in range(out_ref.shape[0]):
-        out_ref[c] = hidden
-
-
-def grad_kernel(index_ref, hid_ref, values_ref, live_ref, cot_ref, agg_ref, out_ref, left, acc):
-    group, cols, targets = hid_ref.shape
+        out_ref[c, :cols, :] = hidden
+        out_ref[c, cols:, :] = pieces_ref[c]
+
+
+def grad_kernel(
+    index_ref, got_ref, values_ref, live_ref, cot_ref, agg_ref, out_ref, left, source, acc
+):
+    group, cols, targets = got_ref.shape
+    cols = cols // 2
     width = values_ref.shape[1]
     wide = group * cols
+    for t in range(targets // width):
+        for j in range(group):
+            at = slice(j * cols, (j + 1) * cols)
+            source[t, at, :] = got_ref[j, :cols, t * width : (t + 1) * width]
     acc[...] = jnp.zeros_like(acc)
     for k in range(values_ref.shape[0]):
-        source = index_ref[k, 1]
-        at = pl.ds(pl.multiple_of(source * width, width), width)
-        rows = jnp.concatenate([hid_ref[j, :, at] for j in range(group)], axis=0)
         target = index_ref[k, 0]
-        acc[target] += lax.dot_general(rows, values_ref[k], NT, preferred_element_type=F32)
+        acc[target] += lax.dot_general(
+            source[index_ref[k, 1]], values_ref[k], NT, preferred_element_type=F32
+        )
     live = live_ref[...].astype(BF)
     for t in range(targets // width):
         at = slice(t * width, (t + 1) * width)
         tile = acc[t].astype(BF)
         agg_ref[:, at] = tile
         left[:wide, at] = tile * live[:, at]
-    for j in range(group):
-        left[wide + j * cols : wide + (j + 1) * cols, :] = hid_ref[j] * live
+        left[wide:, at] = source[t] * live[:, at]
     block = lax.dot_general(left[...], cot_ref[...], NT, preferred_element_type=F32)
     at = 0
     for w in range(2):
@@ -186,16 +186,17 @@
                 at += 1
 
 
-def second_kernel(mine_ref, agg_ref, hid_ref, p0_ref, p1_ref, p2_ref, p3_ref, out_ref, weight, acts):
-    mine = mine_ref[0]
-    group, rows, targets = hid_ref.shape
-    for k, piece in enumerate((p0_ref, p1_ref, p2_ref, p3_ref)):
-        weight[jnp.bitwise_xor(mine, k)] = piece[...]
+def second_kernel(agg_ref, got_ref, out_ref, weight, acts):
+    group, rows, targets = got_ref.shape
+    rows = rows // 2
+    width = targets // 2
     for j in range(group):
-        acts[2 * rows * j : 2 * rows * j + rows, :] = agg_ref[j * rows : (j + 1) * rows, :]
-        acts[2 * rows * j + rows : 2 * rows * (j + 1), :] = hid_ref[j]
-    both = jnp.concatenate([weight[j] for j in range(group)], axis=0)
-    total = lax.dot_general(both, acts[...], TN, preferred_element_type=F32)
+        low, mid, high = 2 * rows * j, 2 * rows * j + rows, 2 * rows * (j + 1)
+        weight[low:mid, :] = got_ref[j, rows:, :width]
+        acts[low:mid, :] = agg_ref[j * rows : (j + 1) * rows, :]
+        weight[mid:high, :] = got_ref[j, rows:, width:]
+        acts[mid:high, :] = got_ref[j, :rows, :]
+    total = lax.dot_general(weight[...], acts[...], TN, preferred_element_type=F32)
     n, cols, _ = out_ref.shape
     for z in range(n):
         out_ref[z] = total[z * cols : (z + 1) * cols, :].astype(BF)
@@ -285,8 +286,6 @@
     def shape(*dims, dtype=BF):
         return jax.ShapeDtypeStruct(dims, dtype)
 
-    with jax.named_scope("cotangent"):
-        cot = lax.all_gather(cotangent.T, "feat", axis=0, tiled=True, axis_index_groups=far)
     with jax.named_scope("edges"):
         send = call(
             functools.partial(pack_kernel, groups, targets),
@@ -298,50 +297,42 @@
         )(edge_feats.T, edge_dst.reshape(-1, 128))
         recv = swap(send, "dp")
     with jax.named_scope("pieces"):
-        pieces = call(
+        pieces, cot = call(
             first_pieces_kernel,
-            shape(GROUP, 4 * cols, wide),
+            (shape(GROUP, 2 * cols, targets), shape(hid, targets)),
             5,
-            smem=(0,),
             late=(4,),
             nbytes=2 << 20,
-        )(mine, neigh_one, self_one, self_feats.T, send)
-        got = [trade(pieces[k], k) for k in range(1, GROUP)]
+        )(neigh_one, self_one, self_feats.T, cotangent.T, send)
+        cot = lax.all_gather(cot, "feat", axis=0, tiled=True, axis_index_groups=far)
     with jax.named_scope("mean"):
-        mean = call(
+        acts = call(
             functools.partial(mean_kernel, cols),
-            shape(GROUP, cols, targets),
-            4,
-            late=(1, 2, 3),
+            shape(GROUP, 3 * cols, targets),
+            3,
+            late=(2,),
             flops=2 * groups * ROWS * cap * targets,
             nbytes=8 << 20,
-        )(recv, *got)
-        mean = swap(mean, "feat", near)
+        )(recv, pieces, cot)
+        acts = swap(acts, "feat", near)
     with jax.named_scope("first"):
         first = call(
             first_kernel,
             shape(blocks, hid, targets),
-            6,
+            1,
             scratch=[pltpu.VMEM((8 * cols, wide), BF), pltpu.VMEM((8 * cols, targets), BF)],
-            smem=(0,),
             flops=2 * 8 * cols * wide * targets,
             nbytes=2 << 20,
-        )(mine, mean, pieces[0], *got)
+        )(acts)
         parts = swap(first, "feat", far)
     with jax.named_scope("pieces"):
         pieces = call(
-            second_pieces_kernel,
-            shape(GROUP, 2 * hid, wide),
-            4,
-            smem=(0,),
-            late=(3,),
-            nbytes=1 << 20,
-        )(mine, neigh_two, self_two, first)
-        got = [trade(pieces[k], k) for k in range(1, GROUP)]
+            second_pieces_kernel, shape(GROUP, hid, targets), 3, late=(2,), nbytes=1 << 20
+        )(neigh_two, self_two, first)
     with jax.named_scope("hidden"):
-        hidden = call(
-            hidden_kernel, shape(GROUP, hid, targets), 5, late=(2, 3, 4), nbytes=1 << 20
-        )(parts, bias_one.reshape(hid, 1), *got)
+        hidden = call(hidden_kernel, shape(GROUP, 2 * hid, targets), 3, nbytes=1 << 20)(
+            parts, bias_one.reshape(hid, 1), pieces
+        )
         hidden = swap(hidden, "feat", near)
     with jax.named_scope("grads"):
         agg, terms = call(
@@ -350,6 +341,7 @@
             5,
             scratch=[
                 pltpu.VMEM((2 * wide, targets), BF),
+                pltpu.VMEM((targets // 128, wide, 128), BF),
                 pltpu.VMEM((targets // 128, wide, 128), F32),
             ],
             smem=(0,),
@@ -365,12 +357,11 @@
         second = call(
             second_kernel,
             shape(blocks, hid, targets),
-            7,
-            scratch=[pltpu.VMEM((GROUP, 2 * hid, wide), BF), pltpu.VMEM((2 * wide, targets), BF)],
-            smem=(0,),
+            2,
+            scratch=[pltpu.VMEM((2 * wide, wide), BF), pltpu.VMEM((2 * wide, targets), BF)],
             flops=2 * 2 * wide * wide * targets,
             nbytes=2 << 20,
-        )(mine, agg, hidden, pieces[0], *got)
+        )(agg, hidden)
         second = swap(second, "feat", far)
         second_out = call(out_kernel, shape(hid, targets), 3, nbytes=1 << 20)(
             second, bias_two.reshape(hid, 1), live

time: 168 us -> 164 us (0.976)
  starting transfers between devices: 88.7 us -> 58.7 us
  waiting for transfers between devices: 33.1 us -> 47.4 us
  blocking collectives: 28.6 us -> 39.7 us
    all_to_all x6, waiting for transfers between devices: 17.9 us -> 43.4 us  [swap(): lax.all_to_all(x, axis, split_axis=0, concat_axis=0, tiled=True, axis_ind...]
    ppermute x9 -> x3, starting transfers between devices: 30.1 us -> 9.27 us  [trade(): return lax.ppermute(x, 'feat', [(i, i ^ k) for i in range(n_feat)])]
    ppermute x9 -> x3, waiting for transfers between devices: 15.1 us -> 4 us  [trade(): return lax.ppermute(x, 'feat', [(i, i ^ k) for i in range(n_feat)])]
    all_to_all x6, starting transfers between devices: 58.6 us -> 49.4 us  [swap(): lax.all_to_all(x, axis, split_axis=0, concat_axis=0, tiled=True, axis_ind...]
    all_to_all x1, blocking collectives: 9.55 us -> 16.8 us  [swap(): lax.all_to_all(x, axis, split_axis=0, concat_axis=0, tiled=True, axis_ind...]
    all_gather x1, blocking collectives: 19.1 us -> 22.9 us  [body(): cot = lax.all_gather(cot, 'feat', axis=0, tiled=True, axis_index_groups=far)]
  transfers between devices with their start and end apart: 15 -> 9, of which waited for: 9 -> 6; matrix products, arithmetic and copies ran while one was open for 0% -> 0% of each run, Pallas kernels for 1% -> 1%
where the time goes in v8:
time: 164 us; the launch traced here: 163 us
  starting transfers between devices  58.7 us (36%)
  waiting for transfers between devices  47.4 us (29%)
  blocking collectives  39.7 us (24%)
  Pallas kernels  12.4 us (8%)
  local copies, waits for them, and re-layouts  3.9 us (2%)
    all_to_all x6, starting transfers between devices, swap(): lax.all_to_all(x, axis, split_axis=0, concat_axis=0, tiled=True, axis_ind...  49.4 us
    all_to_all x6, waiting for transfers between devices, swap(): lax.all_to_all(x, axis, split_axis=0, concat_axis=0, tiled=True, axis_ind...  43.4 us
    all_gather x1, blocking collectives, body(): cot = lax.all_gather(cot, 'feat', axis=0, tiled=True, axis_index_groups=far)  22.9 us
    all_to_all x1, blocking collectives, swap(): lax.all_to_all(x, axis, split_axis=0, concat_axis=0, tiled=True, axis_ind...  16.8 us
    ppermute x3, starting transfers between devices, trade(): return lax.ppermute(x, 'feat', [(i, i ^ k) for i in range(n_feat)])  9.27 us
    ppermute x3, waiting for transfers between devices, trade(): return lax.ppermute(x, 'feat', [(i, i ^ k) for i in range(n_feat)])  4 us
    unnamed x27, local copies, waits for them, and re-layouts  3.71 us
    pallas_call x1, Pallas kernels, body(): call(functools.partial(pack_kernel, groups, targets), shape(groups, ROWS,...  3.34 us
  transfers between devices with their start and end apart: 9, of which 6 were waited for; matrix products, arithmetic and copies ran while one was open for 0% of the time, Pallas kernels for 1%

profile of v8, /device:TPU:1, one launch (start us, length us, event | category | flops | bytes accessed | tf_op | source)
XLA Modules:
  0.0 162.8 jit_solution(397863671390664072)
XLA Ops:
  0.6 0.9 copy-done.7
  2.3 3.3 %edges.1.late_ref = bf16[32,64,128]{2,1,0:T(8,128)(2,1)} custom-call(bf16[48,2048]{1,0:T(8,128)(2,1)S(1)} %bitcast.21, s32[16,128]{1,0:T(8,128)S(1)} %bitcast.22), custom_call_target="tpu_custom_call" | custom-call | flops 1073741824 | bytes 8388608 | tf_op jit(solution)/shard_map/edges/pallas_call | solution.py:290
  5.6 10.6 %all-to-all-start = ((bf16[32,64,128]{2,1,0:T(8,128)(2,1)}), bf16[32,64,128]{2,1,0:T(8,128)(2,1)S(1)}, u32[]{:S(2)}, u32[]{:S(2)}) async-start(bf16[32,64,128]{2,1,0:T(8,128)(2,1)} %edges.1.late_ref), calls=%async_computation | async-start | bytes 1048576 | tf_op jit(solution)/shard_map/edges/all_to_all | solution.py:279
  16.3 22.9 %all_gather.3.late_ref.cot_ref = bf16[256,512]{1,0:T(8,128)(2,1)S(1)} all-gather(bf16[64,512]{1,0:T(8,128)(2,1)S(1)} %get-tuple-element.10), channel_id=1, replica_groups={{0,4,8,12},{1,5,9,13},{2,6,10,14},{3,7,11,15},{16,20,24,28},{17,21,25,2..., dimensions={0}, use_global_device_ids=true | all-gather | bytes 327680 | tf_op jit(solution)/shard_map/pieces/all_gather | solution.py:307
  39.3 1.4 mean.1
  40.7 16.8 %all_to_all.35.got_ref = bf16[4,144,512]{2,1,0:T(8,128)(2,1)S(1)} all-to-all(bf16[4,144,512]{2,1,0:T(8,128)(2,1)S(1)} %mean.1), channel_id=1, replica_groups={{0,1,2,3},{4,5,6,7},{8,9,10,11},{12,13,14,15},{16,17,18,19},{20,21,22,2..., dimensions={0} | all-to-all | bytes 1179648 | tf_op jit(solution)/shard_map/mean/all_to_all | solution.py:279
  57.5 1.0 first.1.late_ref
  58.5 6.7 %all-to-all-start.2 = ((bf16[4,64,512]{2,1,0:T(8,128)(2,1)}), bf16[4,64,512]{2,1,0:T(8,128)(2,1)S(1)}, u32[]{:S(2)}, u32[]{:S(2)}) async-start(bf16[4,64,512]{2,1,0:T(8,128)(2,1)} %first.1.late_ref), calls=%async_computation.2 | async-start | bytes 524288 | tf_op jit(solution)/shard_map/first/all_to_all | solution.py:279
  66.1 14.6 %all-to-all-done.2.parts_ref = bf16[4,64,512]{2,1,0:T(8,128)(2,1)S(1)} async-done(((bf16[4,64,512]{2,1,0:T(8,128)(2,1)}), bf16[4,64,512]{2,1,0:T(8,128)(2,1)S(1)}, u32[]{:S(2)}, u32[]{:S(2)}) %all-to-all-start.2) | async-done | bytes 262176 | tf_op jit(solution)/shard_map/first/all_to_all | solution.py:279
  80.7 0.9 hidden.1
  81.6 3.6 %all-to-all-start.3 = ((bf16[4,128,512]{2,1,0:T(8,128)(2,1)}), bf16[4,128,512]{2,1,0:T(8,128)(2,1)S(1)}, u32[]{:S(2)}, u32[]{:S(2)}) async-start(bf16[4,128,512]{2,1,0:T(8,128)(2,1)} %hidden.1), calls=%async_computation.3 | async-start | bytes 1048576 | tf_op jit(solution)/shard_map/hidden/all_to_all | solution.py:279
  86.0 10.0 %all-to-all-done.3.got_ref = bf16[4,128,512]{2,1,0:T(8,128)(2,1)S(1)} async-done(((bf16[4,128,512]{2,1,0:T(8,128)(2,1)}), bf16[4,128,512]{2,1,0:T(8,128)(2,1)S(1)}, u32[]{:S(2)}, u32[]{:S(2)}) %all-to-all-start.3) | async-done | bytes 524320 | tf_op jit(solution)/shard_map/hidden/all_to_all | solution.py:279
  96.0 1.9 %grads.2 = (bf16[256,512]{1,0:T(8,128)(2,1)S(1)}, bf16[32,32,128]{2,1,0:T(8,128)(2,1)}) custom-call(s32[4,2]{1,0:T(4,128)S(1)} %copy.17.index_ref, bf16[4,128,512]{2,1,0:T(8,128)(2,1)S(1)} %all-to-all-done.3.got_ref, bf16[4,128,128]{2,1,0:T(8,128)(2,1)S(1)} %copy-done, f32[1,512]{1,0:T(1,128)S(1)} %bitcast.19, bf16[256,512]{1,0:T(8,128)(2,1)S(1)} %all_gather.3.late_ref.cot_ref), custom_call_target="tpu_custom_call" | custom-call | flops 134217728 | bytes 4194304 | tf_op jit(solution)/shard_map/grads/pallas_call | solution.py:338
  97.9 11.8 %all-to-all-start.5 = ((bf16[32,32,128]{2,1,0:T(8,128)(2,1)}), bf16[32,32,128]{2,1,0:T(8,128)(2,1)S(1)}, u32[]{:S(2)}, u32[]{:S(2)}) async-start(bf16[32,32,128]{2,1,0:T(8,128)(2,1)} %get-tuple-element.12), calls=%async_computation.5 | async-start | bytes 524288 | tf_op jit(solution)/shard_map/grads/all_to_all | solution.py:279
  109.7 1.0 second.2
  110.7 7.9 %all-to-all-done.5.terms_ref = bf16[32,32,128]{2,1,0:T(8,128)(2,1)S(1)} async-done(((bf16[32,32,128]{2,1,0:T(8,128)(2,1)}), bf16[32,32,128]{2,1,0:T(8,128)(2,1)S(1)}, u32[]{:S(2)}, u32[]{:S(2)}) %all-to-all-start.5) | async-done | bytes 262176 | tf_op jit(solution)/shard_map/grads/all_to_all | solution.py:279
  118.6 6.7 %all-to-all-start.4 = ((bf16[4,64,512]{2,1,0:T(8,128)(2,1)}), bf16[4,64,512]{2,1,0:T(8,128)(2,1)S(1)}, u32[]{:S(2)}, u32[]{:S(2)}) async-start(bf16[4,64,512]{2,1,0:T(8,128)(2,1)} %second.2), calls=%async_computation.4 | async-start | bytes 524288 | tf_op jit(solution)/shard_map/second/all_to_all | solution.py:279
  125.3 1.9 %collective-permute-start = (f32[8,128]{1,0:T(8,128)S(1)}, f32[8,128]{1,0:T(8,128)S(1)}, u32[]{:S(2)}, u32[]{:S(2)}) collective-permute-start(f32[8,128]{1,0:T(8,128)S(1)} %get-tuple-element.17), channel_id=1, source_target_pairs={{0,1},{1,0},{2,3},{3,2},{4,5},{5,4},{6,7},{7,6},{8,9},{9,8},{10,11... | collective-permute-start | bytes 12296 | tf_op jit(solution)/shard_map/grads/ppermute | solution.py:284
  127.3 3.4 %collective-permute-start.1 = (f32[8,128]{1,0:T(8,128)S(1)}, f32[8,128]{1,0:T(8,128)S(1)}, u32[]{:S(2)}, u32[]{:S(2)}) collective-permute-start(f32[8,128]{1,0:T(8,128)S(1)} %get-tuple-element.16), channel_id=1, source_target_pairs={{0,2},{1,3},{2,0},{3,1},{4,6},{5,7},{6,4},{7,5},{8,10},{9,11},{10,... | collective-permute-start | bytes 12296 | tf_op jit(solution)/shard_map/grads/ppermute | solution.py:284
  130.6 4.0 %collective-permute-start.2 = (f32[8,128]{1,0:T(8,128)S(1)}, f32[8,128]{1,0:T(8,128)S(1)}, u32[]{:S(2)}, u32[]{:S(2)}) collective-permute-start(f32[8,128]{1,0:T(8,128)S(1)} %get-tuple-element.15), channel_id=1, source_target_pairs={{0,3},{1,2},{2,1},{3,0},{4,7},{5,6},{6,5},{7,4},{8,11},{9,10},{10,... | collective-permute-start | bytes 12296 | tf_op jit(solution)/shard_map/grads/ppermute | solution.py:284
  134.7 4.0 %collective-permute-done.2.p3_ref = f32[8,128]{1,0:T(8,128)S(1)} collective-permute-done((f32[8,128]{1,0:T(8,128)S(1)}, f32[8,128]{1,0:T(8,128)S(1)}, u32[]{:S(2)}, u32[]{:S(2)}) %collective-permute-start.2) | collective-permute-done | bytes 4128 | tf_op jit(solution)/shard_map/grads/ppermute | solution.py:284
  140.4 10.0 %all-to-all-start.6 = ((f32[32,32,128]{2,1,0:T(8,128)}), f32[32,32,128]{2,1,0:T(8,128)S(1)}, u32[]{:S(2)}, u32[]{:S(2)}) async-start(f32[32,32,128]{2,1,0:T(8,128)} %place.2), calls=%async_computation.6 | async-start | bytes 1048576 | tf_op jit(solution)/shard_map/place/all_to_all | solution.py:279
  151.8 10.1 %all-to-all-done.6.pieces_ref = f32[32,32,128]{2,1,0:T(8,128)S(1)} async-done(((f32[32,32,128]{2,1,0:T(8,128)}), f32[32,32,128]{2,1,0:T(8,128)S(1)}, u32[]{:S(2)}, u32[]{:S(2)}) %all-to-all-start.6) | async-done | bytes 524320 | tf_op jit(solution)/shard_map/place/all_to_all | solution.py:279
  161.9 0.9 place.3
  (39 shorter events, 5.7 us)
Async XLA Ops:
  0.6 0.9 copy-start.7
  1.6 0.7 copy-start.8
  5.6 10.6 %copy-start.3 = (bf16[48,1024]{1,0:T(8,128)(2,1)S(1)}, bf16[48,1024]{1,0:T(8,128)(2,1)}, u32[]{:S(2)}) copy-start(bf16[48,1024]{1,0:T(8,128)(2,1)} %neigh_ref.2) | copy-start | bytes 294916
  5.6 10.6 %copy-start.4 = (bf16[48,1024]{1,0:T(8,128)(2,1)S(1)}, bf16[48,1024]{1,0:T(8,128)(2,1)}, u32[]{:S(2)}) copy-start(bf16[48,1024]{1,0:T(8,128)(2,1)} %own_ref.2) | copy-start | bytes 294916
  5.6 10.6 %copy-start.5 = (bf16[512,64]{0,1:T(8,128)(2,1)S(1)}, bf16[512,64]{0,1:T(8,128)(2,1)}, u32[]{:S(2)}) copy-start(bf16[512,64]{0,1:T(8,128)(2,1)} %param.25) | copy-start | bytes 196612
  5.6 10.6 %copy-start.6 = (bf16[512,48]{0,1:T(8,128)(2,1)S(1)}, bf16[512,48]{0,1:T(8,128)(2,1)}, u32[]{:S(2)}) copy-start(bf16[512,48]{0,1:T(8,128)(2,1)} %param.15) | copy-start | bytes 147460
  5.6 33.7 %all-to-all-start = ((bf16[32,64,128]{2,1,0:T(8,128)(2,1)}), bf16[32,64,128]{2,1,0:T(8,128)(2,1)S(1)}, u32[]{:S(2)}, u32[]{:S(2)}) async-start(bf16[32,64,128]{2,1,0:T(8,128)(2,1)} %edges.1.late_ref), calls=%async_computation | async-start | bytes 1048576 | tf_op jit(solution)/shard_map/edges/all_to_all | solution.py:279
  58.5 7.5 %copy-start.1 = (bf16[64,1024]{1,0:T(8,128)(2,1)S(1)}, bf16[64,1024]{1,0:T(8,128)(2,1)}, u32[]{:S(2)}) copy-start(bf16[64,1024]{1,0:T(8,128)(2,1)} %neigh_ref.3) | copy-start | bytes 393220
  58.5 7.5 %copy-start.2 = (bf16[64,1024]{1,0:T(8,128)(2,1)S(1)}, bf16[64,1024]{1,0:T(8,128)(2,1)}, u32[]{:S(2)}) copy-start(bf16[64,1024]{1,0:T(8,128)(2,1)} %own_ref.3) | copy-start | bytes 393220
  58.5 22.2 %all-to-all-start.2 = ((bf16[4,64,512]{2,1,0:T(8,128)(2,1)}), bf16[4,64,512]{2,1,0:T(8,128)(2,1)S(1)}, u32[]{:S(2)}, u32[]{:S(2)}) async-start(bf16[4,64,512]{2,1,0:T(8,128)(2,1)} %first.1.late_ref), calls=%async_computation.2 | async-start | bytes 524288 | tf_op jit(solution)/shard_map/first/all_to_all | solution.py:279
  65.2 0.7 copy-start.11
  81.6 3.6 %copy-start.9 = (s32[512]{0:T(512)S(1)}, s32[512]{0:T(512)}, u32[]{:S(2)}) copy-start(s32[512]{0:T(512)} %param.21) | copy-start | bytes 6148
  81.6 14.4 %copy-start = (bf16[4,128,128]{2,1,0:T(8,128)(2,1)S(1)}, bf16[4,128,128]{2,1,0:T(8,128)(2,1)}, u32[]{:S(2)}) copy-start(bf16[4,128,128]{2,1,0:T(8,128)(2,1)} %values_ref.1) | copy-start | bytes 393220
  81.6 14.4 %all-to-all-start.3 = ((bf16[4,128,512]{2,1,0:T(8,128)(2,1)}), bf16[4,128,512]{2,1,0:T(8,128)(2,1)S(1)}, u32[]{:S(2)}, u32[]{:S(2)}) async-start(bf16[4,128,512]{2,1,0:T(8,128)(2,1)} %hidden.1), calls=%async_computation.3 | async-start | bytes 1048576 | tf_op jit(solution)/shard_map/hidden/all_to_all | solution.py:279
  85.2 0.7 copy-start.10
  97.9 20.8 %all-to-all-start.5 = ((bf16[32,32,128]{2,1,0:T(8,128)(2,1)}), bf16[32,32,128]{2,1,0:T(8,128)(2,1)S(1)}, u32[]{:S(2)}, u32[]{:S(2)}) async-start(bf16[32,32,128]{2,1,0:T(8,128)(2,1)} %get-tuple-element.12), calls=%async_computation.5 | async-start | bytes 524288 | tf_op jit(solution)/shard_map/grads/all_to_all | solution.py:279
  118.6 20.9 %all-to-all-start.4 = ((bf16[4,64,512]{2,1,0:T(8,128)(2,1)}), bf16[4,64,512]{2,1,0:T(8,128)(2,1)S(1)}, u32[]{:S(2)}, u32[]{:S(2)}) async-start(bf16[4,64,512]{2,1,0:T(8,128)(2,1)} %second.2), calls=%async_computation.4 | async-start | bytes 524288 | tf_op jit(solution)/shard_map/second/all_to_all | solution.py:279
  125.3 9.3 %collective-permute-start = (f32[8,128]{1,0:T(8,128)S(1)}, f32[8,128]{1,0:T(8,128)S(1)}, u32[]{:S(2)}, u32[]{:S(2)}) collective-permute-start(f32[8,128]{1,0:T(8,128)S(1)} %get-tuple-element.17), channel_id=1, source_target_pairs={{0,1},{1,0},{2,3},{3,2},{4,5},{5,4},{6,7},{7,6},{8,9},{9,8},{10,11... | collective-permute-start | bytes 12296 | tf_op jit(solution)/shard_map/grads/ppermute | solution.py:284
  127.3 7.4 %collective-permute-start.1 = (f32[8,128]{1,0:T(8,128)S(1)}, f32[8,128]{1,0:T(8,128)S(1)}, u32[]{:S(2)}, u32[]{:S(2)}) collective-permute-start(f32[8,128]{1,0:T(8,128)S(1)} %get-tuple-element.16), channel_id=1, source_target_pairs={{0,2},{1,3},{2,0},{3,1},{4,6},{5,7},{6,4},{7,5},{8,10},{9,11},{10,... | collective-permute-start | bytes 12296 | tf_op jit(solution)/shard_map/grads/ppermute | solution.py:284
  130.6 8.0 %collective-permute-start.2 = (f32[8,128]{1,0:T(8,128)S(1)}, f32[8,128]{1,0:T(8,128)S(1)}, u32[]{:S(2)}, u32[]{:S(2)}) collective-permute-start(f32[8,128]{1,0:T(8,128)S(1)} %get-tuple-element.15), channel_id=1, source_target_pairs={{0,3},{1,2},{2,1},{3,0},{4,7},{5,6},{6,5},{7,4},{8,11},{9,10},{10,... | collective-permute-start | bytes 12296 | tf_op jit(solution)/shard_map/grads/ppermute | solution.py:284
  140.4 21.6 %all-to-all-start.6 = ((f32[32,32,128]{2,1,0:T(8,128)}), f32[32,32,128]{2,1,0:T(8,128)S(1)}, u32[]{:S(2)}, u32[]{:S(2)}) async-start(f32[32,32,128]{2,1,0:T(8,128)} %place.2), calls=%async_computation.6 | async-start | bytes 1048576 | tf_op jit(solution)/shard_map/place/all_to_all | solution.py:279
  150.4 0.7 copy-start.12

commit v9 on v8

--- a/solution.py
+++ b/solution.py
@@ -101,8 +101,7 @@
         out_ref[j, :, width // 2 :] = own
 
 
-def mean_kernel(cols, recv_ref, pieces_ref, late_ref, out_ref):
-    del late_ref
+def mean_kernel(cols, recv_ref, pieces_ref, cot_ref, far_ref, out_ref, cots_ref):
     groups, rows, cap = recv_ref.shape
     targets = out_ref.shape[2]
     half = targets // 2
@@ -120,9 +119,12 @@
     for j in range(out_ref.shape[0]):
         out_ref[j, :cols, :] = mean
         out_ref[j, cols:, :] = pieces_ref[j]
-
-
-def first_kernel(got_ref, out_ref, weight, acts):
+    cots_ref[0] = cot_ref[...]
+    cots_ref[1] = far_ref[...]
+
+
+def first_kernel(got_ref, late_ref, out_ref, weight, acts):
+    del late_ref
     group, rows, targets = got_ref.shape
     rows = rows // 3
     width = targets // 2
@@ -150,7 +152,19 @@
 
 
 def grad_kernel(
-    index_ref, got_ref, values_ref, live_ref, cot_ref, agg_ref, out_ref, left, source, acc
+    across_ref,
+    index_ref,
+    got_ref,
+    values_ref,
+    live_ref,
+    cots_ref,
+    others_ref,
+    agg_ref,
+    out_ref,
+    left,
+    source,
+    acc,
+    cot,
 ):
     group, cols, targets = got_ref.shape
     cols = cols // 2
@@ -160,6 +174,9 @@
         for j in range(group):
             at = slice(j * cols, (j + 1) * cols)
             source[t, at, :] = got_ref[j, :cols, t * width : (t + 1) * width]
+    across = across_ref[0]
+    for k, ref in enumerate((cots_ref, others_ref, cots_ref, others_ref)):
+        cot[jnp.bitwise_xor(across, k)] = ref[k // 2]
     acc[...] = jnp.zeros_like(acc)
     for k in range(values_ref.shape[0]):
         target = index_ref[k, 0]
@@ -173,11 +190,12 @@
         agg_ref[:, at] = tile
         left[:wide, at] = tile * live[:, at]
         left[wide:, at] = source[t] * live[:, at]
-    block = lax.dot_general(left[...], cot_ref[...], NT, preferred_element_type=F32)
+    right = jnp.concatenate([cot[z] for z in range(cot.shape[0])], axis=0)
+    block = lax.dot_general(left[...], right, NT, preferred_element_type=F32)
     at = 0
     for w in range(2):
         for r in range(0, cols, 8):
-            for c in range(0, cot_ref.shape[0], 128):
+            for c in range(0, right.shape[0], 128):
                 rows_of = [
                     block[w * wide + j * cols + r : w * wide + j * cols + r + 8, c : c + 128]
                     for j in range(group)
@@ -273,6 +291,7 @@
     far = [[i + GROUP * j for j in range(blocks)] for i in range(GROUP)]
     z = lax.axis_index("feat")
     mine = (z % GROUP).reshape(1)
+    across = (z // GROUP).reshape(1)
     live = seed_live.reshape(1, targets).astype(F32)
 
     def swap(x, axis, among=None):
@@ -304,26 +323,27 @@
             late=(4,),
             nbytes=2 << 20,
         )(neigh_one, self_one, self_feats.T, cotangent.T, send)
-        cot = lax.all_gather(cot, "feat", axis=0, tiled=True, axis_index_groups=far)
+        cot_far = trade(cot, 2 * GROUP)
     with jax.named_scope("mean"):
-        acts = call(
+        acts, cots = call(
             functools.partial(mean_kernel, cols),
-            shape(GROUP, 3 * cols, targets),
-            3,
-            late=(2,),
+            (shape(GROUP, 3 * cols, targets), shape(2, hid, targets)),
+            4,
             flops=2 * groups * ROWS * cap * targets,
             nbytes=8 << 20,
-        )(recv, pieces, cot)
+        )(recv, pieces, cot, cot_far)
+        others = trade(cots, GROUP)
         acts = swap(acts, "feat", near)
     with jax.named_scope("first"):
         first = call(
             first_kernel,
             shape(blocks, hid, targets),
-            1,
+            2,
+            late=(1,),
             scratch=[pltpu.VMEM((8 * cols, wide), BF), pltpu.VMEM((8 * cols, targets), BF)],
             flops=2 * 8 * cols * wide * targets,
             nbytes=2 << 20,
-        )(acts)
+        )(acts, others)
         parts = swap(first, "feat", far)
     with jax.named_scope("pieces"):
         pieces = call(
@@ -338,16 +358,17 @@
         agg, terms = call(
             grad_kernel,
             (shape(wide, targets), shape(groups, GROUP * 8, 128)),
-            5,
+            7,
             scratch=[
                 pltpu.VMEM((2 * wide, targets), BF),
                 pltpu.VMEM((targets // 128, wide, 128), BF),
                 pltpu.VMEM((targets // 128, wide, 128), F32),
+                pltpu.VMEM((blocks, hid, targets), BF),
             ],
-            smem=(0,),
+            smem=(0, 1),
             flops=2 * 2 * wide * targets * wide,
             nbytes=4 << 20,
-        )(tile_index, hidden, tile_values, live, cot)
+        )(across, tile_index, hidden, tile_values, live, cots, others)
         terms = swap(terms, "dp")
         mine_sum = call(
             sum_kernel, shape(GROUP, 8, 128, dtype=F32), 2, smem=(0,), nbytes=1 << 20

time: 164 us -> 167 us (1.018)
  blocking collectives: 39.7 us -> 0 us
  starting transfers between devices: 58.7 us -> 86.7 us
  waiting for transfers between devices: 47.4 us -> 60.4 us
    ppermute x3 -> x5, starting transfers between devices: 9.27 us -> 32.3 us  [trade(): return lax.ppermute(x, 'feat', [(i, i ^ k) for i in range(n_feat)])]
    all_gather x1 -> x0, blocking collectives: 22.9 us -> none  [body(): cot = lax.all_gather(cot, 'feat', axis=0, tiled=True, axis_index_groups=far)]
    all_to_all x1 -> x0, blocking collectives: 16.8 us -> none  [swap(): lax.all_to_all(x, axis, split_axis=0, concat_axis=0, tiled=True, axis_ind...]
    all_to_all x6 -> x7, waiting for transfers between devices: 43.4 us -> 52.1 us  [swap(): lax.all_to_all(x, axis, split_axis=0, concat_axis=0, tiled=True, axis_ind...]
    all_to_all x6 -> x7, starting transfers between devices: 49.4 us -> 54.4 us  [swap(): lax.all_to_all(x, axis, split_axis=0, concat_axis=0, tiled=True, axis_ind...]
    ppermute x3 -> x5, waiting for transfers between devices: 4 us -> 8.22 us  [trade(): return lax.ppermute(x, 'feat', [(i, i ^ k) for i in range(n_feat)])]
  transfers between devices with their start and end apart: 9 -> 12, of which waited for: 6 -> 9; matrix products, arithmetic and copies ran while one was open for 0% -> 0% of each run, Pallas kernels for 1% -> 1%
where the time goes in v9:
time: 167 us; the launch traced here: 166 us
  starting transfers between devices  86.7 us (52%)
  waiting for transfers between devices  60.4 us (36%)
  Pallas kernels  13.2 us (8%)
  local copies, waits for them, and re-layouts  4.59 us (3%)
    all_to_all x7, starting transfers between devices, swap(): lax.all_to_all(x, axis, split_axis=0, concat_axis=0, tiled=True, axis_ind...  54.4 us
    all_to_all x7, waiting for transfers between devices, swap(): lax.all_to_all(x, axis, split_axis=0, concat_axis=0, tiled=True, axis_ind...  52.1 us
    ppermute x5, starting transfers between devices, trade(): return lax.ppermute(x, 'feat', [(i, i ^ k) for i in range(n_feat)])  32.3 us
    ppermute x5, waiting for transfers between devices, trade(): return lax.ppermute(x, 'feat', [(i, i ^ k) for i in range(n_feat)])  8.22 us
    unnamed x27, local copies, waits for them, and re-layouts  4.4 us
  transfers between devices with their start and end apart: 12, of which 9 were waited for; matrix products, arithmetic and copies ran while one was open for 0% of the time, Pallas kernels for 1%

profile of v9, /device:TPU:1, one launch (start us, length us, event | category | flops | bytes accessed | tf_op | source)
XLA Modules:
  0.0 165.6 jit_solution(1772262305521955860)
XLA Ops:
  2.3 3.3 %edges.1.late_ref = bf16[32,64,128]{2,1,0:T(8,128)(2,1)} custom-call(bf16[48,2048]{1,0:T(8,128)(2,1)S(1)} %bitcast.22, s32[16,128]{1,0:T(8,128)S(1)} %bitcast.23), custom_call_target="tpu_custom_call" | custom-call | flops 1073741824 | bytes 8388608 | tf_op jit(solution)/shard_map/edges/pallas_call | solution.py:309
  5.6 10.6 %all-to-all-start = ((bf16[32,64,128]{2,1,0:T(8,128)(2,1)}), bf16[32,64,128]{2,1,0:T(8,128)(2,1)S(1)}, u32[]{:S(2)}, u32[]{:S(2)}) async-start(bf16[32,64,128]{2,1,0:T(8,128)(2,1)} %edges.1.late_ref), calls=%async_computation | async-start | bytes 1048576 | tf_op jit(solution)/shard_map/edges/all_to_all | solution.py:298
  16.3 13.6 %collective-permute-start = (bf16[64,512]{1,0:T(8,128)(2,1)S(1)}, bf16[64,512]{1,0:T(8,128)(2,1)S(1)}, u32[]{:S(2)}, u32[]{:S(2)}) collective-permute-start(bf16[64,512]{1,0:T(8,128)(2,1)S(1)} %get-tuple-element.12.cot_ref), channel_id=1, source_target_pairs={{0,8},{1,9},{2,10},{3,11},{4,12},{5,13},{6,14},{7,15},{8,0},{9,1},... | collective-permute-start | bytes 196616 | tf_op jit(solution)/shard_map/pieces/ppermute | solution.py:303
  30.0 2.3 %collective-permute-done.far_ref = bf16[64,512]{1,0:T(8,128)(2,1)S(1)} collective-permute-done((bf16[64,512]{1,0:T(8,128)(2,1)S(1)}, bf16[64,512]{1,0:T(8,128)(2,1)S(1)}, u32[]{:S(2)}, u32[]{:S(2)}) %collective-permute-start) | collective-permute-done | bytes 65568 | tf_op jit(solution)/shard_map/pieces/ppermute | solution.py:303
  32.3 2.2 %mean.1 = (bf16[4,144,512]{2,1,0:T(8,128)(2,1)}, bf16[2,64,512]{2,1,0:T(8,128)(2,1)S(1)}) custom-call(bf16[32,64,128]{2,1,0:T(8,128)(2,1)S(1)} %all-to-all-done.recv_ref, bf16[4,96,512]{2,1,0:T(8,128)(2,1)S(1)} %get-tuple-element.11.pieces_ref, bf16[64,512]{1,0:T(8,128)(2,1)S(1)} %get-tuple-element.12.cot_ref, bf16[64,512]{1,0:T(8,128)(2,1)S(1)} %collective-permute-done.far_ref), custom_call_target="tpu_custom_call" | custom-call | flops 268435456 | bytes 8388608 | tf_op jit(solution)/shard_map/mean/pallas_call | solution.py:328
  34.5 3.9 %all-to-all-start.1 = ((bf16[4,144,512]{2,1,0:T(8,128)(2,1)}), bf16[4,144,512]{2,1,0:T(8,128)(2,1)S(1)}, u32[]{:S(2)}, u32[]{:S(2)}) async-start(bf16[4,144,512]{2,1,0:T(8,128)(2,1)} %get-tuple-element.13), calls=%async_computation.1 | async-start | bytes 1179648 | tf_op jit(solution)/shard_map/mean/all_to_all | solution.py:298
  38.4 9.4 %collective-permute-start.1 = (bf16[2,64,512]{2,1,0:T(8,128)(2,1)S(1)}, bf16[2,64,512]{2,1,0:T(8,128)(2,1)S(1)}, u32[]{:S(2)}, u32[]{:S(2)}) collective-permute-start(bf16[2,64,512]{2,1,0:T(8,128)(2,1)S(1)} %get-tuple-element.14.cots_ref), channel_id=1, source_target_pairs={{0,4},{1,5},{2,6},{3,7},{4,0},{5,1},{6,2},{7,3},{8,12},{9,13},{10,... | collective-permute-start | bytes 393224 | tf_op jit(solution)/shard_map/mean/ppermute | solution.py:303
  47.8 3.1 %collective-permute-done.1.late_ref.others_ref = bf16[2,64,512]{2,1,0:T(8,128)(2,1)S(1)} collective-permute-done((bf16[2,64,512]{2,1,0:T(8,128)(2,1)S(1)}, bf16[2,64,512]{2,1,0:T(8,128)(2,1)S(1)}, u32[]{:S(2)}, u32[]{:S(2)}) %collective-permute-start.1) | collective-permute-done | bytes 131104 | tf_op jit(solution)/shard_map/mean/ppermute | solution.py:303
  50.8 8.5 %all-to-all-done.1.got_ref = bf16[4,144,512]{2,1,0:T(8,128)(2,1)S(1)} async-done(((bf16[4,144,512]{2,1,0:T(8,128)(2,1)}), bf16[4,144,512]{2,1,0:T(8,128)(2,1)S(1)}, u32[]{:S(2)}, u32[]{:S(2)}) %all-to-all-start.1) | async-done | bytes 589856 | tf_op jit(solution)/shard_map/mean/all_to_all | solution.py:298
  60.4 7.2 %all-to-all-start.2 = ((bf16[4,64,512]{2,1,0:T(8,128)(2,1)}), bf16[4,64,512]{2,1,0:T(8,128)(2,1)S(1)}, u32[]{:S(2)}, u32[]{:S(2)}) async-start(bf16[4,64,512]{2,1,0:T(8,128)(2,1)} %first.1.late_ref), calls=%async_computation.2 | async-start | bytes 524288 | tf_op jit(solution)/shard_map/first/all_to_all | solution.py:298
  68.5 13.9 %all-to-all-done.2.parts_ref = bf16[4,64,512]{2,1,0:T(8,128)(2,1)S(1)} async-done(((bf16[4,64,512]{2,1,0:T(8,128)(2,1)}), bf16[4,64,512]{2,1,0:T(8,128)(2,1)S(1)}, u32[]{:S(2)}, u32[]{:S(2)}) %all-to-all-start.2) | async-done | bytes 262176 | tf_op jit(solution)/shard_map/first/all_to_all | solution.py:298
  83.2 8.8 %all-to-all-start.3 = ((bf16[4,128,512]{2,1,0:T(8,128)(2,1)}), bf16[4,128,512]{2,1,0:T(8,128)(2,1)S(1)}, u32[]{:S(2)}, u32[]{:S(2)}) async-start(bf16[4,128,512]{2,1,0:T(8,128)(2,1)} %hidden.1), calls=%async_computation.3 | async-start | bytes 1048576 | tf_op jit(solution)/shard_map/hidden/all_to_all | solution.py:298
  93.4 9.7 %all-to-all-done.3.got_ref = bf16[4,128,512]{2,1,0:T(8,128)(2,1)S(1)} async-done(((bf16[4,128,512]{2,1,0:T(8,128)(2,1)}), bf16[4,128,512]{2,1,0:T(8,128)(2,1)S(1)}, u32[]{:S(2)}, u32[]{:S(2)}) %all-to-all-start.3) | async-done | bytes 524320 | tf_op jit(solution)/shard_map/hidden/all_to_all | solution.py:298
  103.2 1.9 %grads.2 = (bf16[256,512]{1,0:T(8,128)(2,1)S(1)}, bf16[32,32,128]{2,1,0:T(8,128)(2,1)}) custom-call(s32[1]{0:T(128)} %bitcast.across_ref, s32[4,2]{1,0:T(4,128)S(1)} %copy.17.index_ref, bf16[4,128,512]{2,1,0:T(8,128)(2,1)S(1)} %all-to-all-done.3.got_ref, bf16[4,128,128]{2,1,0:T(8,128)(2,1)S(1)} %copy-done, f32[1,512]{1,0:T(1,128)S(1)} %bitcast.20, ...), custom_call_target="tpu_custom_call" | custom-call | flops 134217728 | bytes 4194304 | tf_op jit(solution)/shard_map/grads/pallas_call | solution.py:358
  105.0 11.1 %all-to-all-start.5 = ((bf16[32,32,128]{2,1,0:T(8,128)(2,1)}), bf16[32,32,128]{2,1,0:T(8,128)(2,1)S(1)}, u32[]{:S(2)}, u32[]{:S(2)}) async-start(bf16[32,32,128]{2,1,0:T(8,128)(2,1)} %get-tuple-element.16), calls=%async_computation.5 | async-start | bytes 524288 | tf_op jit(solution)/shard_map/grads/all_to_all | solution.py:298
  117.2 7.9 %all-to-all-done.5.terms_ref = bf16[32,32,128]{2,1,0:T(8,128)(2,1)S(1)} async-done(((bf16[32,32,128]{2,1,0:T(8,128)(2,1)}), bf16[32,32,128]{2,1,0:T(8,128)(2,1)S(1)}, u32[]{:S(2)}, u32[]{:S(2)}) %all-to-all-start.5) | async-done | bytes 262176 | tf_op jit(solution)/shard_map/grads/all_to_all | solution.py:298
  125.1 3.4 %all-to-all-start.4 = ((bf16[4,64,512]{2,1,0:T(8,128)(2,1)}), bf16[4,64,512]{2,1,0:T(8,128)(2,1)S(1)}, u32[]{:S(2)}, u32[]{:S(2)}) async-start(bf16[4,64,512]{2,1,0:T(8,128)(2,1)} %second.2), calls=%async_computation.4 | async-start | bytes 524288 | tf_op jit(solution)/shard_map/second/all_to_all | solution.py:298
  128.6 1.9 %collective-permute-start.2 = (f32[8,128]{1,0:T(8,128)S(1)}, f32[8,128]{1,0:T(8,128)S(1)}, u32[]{:S(2)}, u32[]{:S(2)}) collective-permute-start(f32[8,128]{1,0:T(8,128)S(1)} %get-tuple-element.21), channel_id=1, source_target_pairs={{0,1},{1,0},{2,3},{3,2},{4,5},{5,4},{6,7},{7,6},{8,9},{9,8},{10,11... | collective-permute-start | bytes 12296 | tf_op jit(solution)/shard_map/grads/ppermute | solution.py:303
  130.5 3.4 %collective-permute-start.3 = (f32[8,128]{1,0:T(8,128)S(1)}, f32[8,128]{1,0:T(8,128)S(1)}, u32[]{:S(2)}, u32[]{:S(2)}) collective-permute-start(f32[8,128]{1,0:T(8,128)S(1)} %get-tuple-element.20), channel_id=1, source_target_pairs={{0,2},{1,3},{2,0},{3,1},{4,6},{5,7},{6,4},{7,5},{8,10},{9,11},{10,... | collective-permute-start | bytes 12296 | tf_op jit(solution)/shard_map/grads/ppermute | solution.py:303
  133.9 4.0 %collective-permute-start.4 = (f32[8,128]{1,0:T(8,128)S(1)}, f32[8,128]{1,0:T(8,128)S(1)}, u32[]{:S(2)}, u32[]{:S(2)}) collective-permute-start(f32[8,128]{1,0:T(8,128)S(1)} %get-tuple-element.19), channel_id=1, source_target_pairs={{0,3},{1,2},{2,1},{3,0},{4,7},{5,6},{6,5},{7,4},{8,11},{9,10},{10,... | collective-permute-start | bytes 12296 | tf_op jit(solution)/shard_map/grads/ppermute | solution.py:303
  137.9 2.8 %collective-permute-done.4.p3_ref = f32[8,128]{1,0:T(8,128)S(1)} collective-permute-done((f32[8,128]{1,0:T(8,128)S(1)}, f32[8,128]{1,0:T(8,128)S(1)}, u32[]{:S(2)}, u32[]{:S(2)}) %collective-permute-start.4) | collective-permute-done | bytes 4128 | tf_op jit(solution)/shard_map/grads/ppermute | solution.py:303
  140.7 2.0 %all-to-all-done.4.parts_ref.late_ref = bf16[4,64,512]{2,1,0:T(8,128)(2,1)S(1)} async-done(((bf16[4,64,512]{2,1,0:T(8,128)(2,1)}), bf16[4,64,512]{2,1,0:T(8,128)(2,1)S(1)}, u32[]{:S(2)}, u32[]{:S(2)}) %all-to-all-start.4) | async-done | bytes 262176 | tf_op jit(solution)/shard_map/second/all_to_all | solution.py:298
  143.6 9.6 %all-to-all-start.6 = ((f32[32,32,128]{2,1,0:T(8,128)}), f32[32,32,128]{2,1,0:T(8,128)S(1)}, u32[]{:S(2)}, u32[]{:S(2)}) async-start(f32[32,32,128]{2,1,0:T(8,128)} %place.2), calls=%async_computation.6 | async-start | bytes 1048576 | tf_op jit(solution)/shard_map/place/all_to_all | solution.py:298
  154.6 10.1 %all-to-all-done.6.pieces_ref = f32[32,32,128]{2,1,0:T(8,128)S(1)} async-done(((f32[32,32,128]{2,1,0:T(8,128)}), f32[32,32,128]{2,1,0:T(8,128)S(1)}, u32[]{:S(2)}, u32[]{:S(2)}) %all-to-all-start.6) | async-done | bytes 524320 | tf_op jit(solution)/shard_map/place/all_to_all | solution.py:298
  (43 shorter events, 10.3 us)
Async XLA Ops:
  0.6 0.9 copy-start.7
  1.6 0.7 copy-start.8
  5.6 10.6 %copy-start.3 = (bf16[48,1024]{1,0:T(8,128)(2,1)S(1)}, bf16[48,1024]{1,0:T(8,128)(2,1)}, u32[]{:S(2)}) copy-start(bf16[48,1024]{1,0:T(8,128)(2,1)} %neigh_ref.2) | copy-start | bytes 294916
  5.6 10.6 %copy-start.4 = (bf16[48,1024]{1,0:T(8,128)(2,1)S(1)}, bf16[48,1024]{1,0:T(8,128)(2,1)}, u32[]{:S(2)}) copy-start(bf16[48,1024]{1,0:T(8,128)(2,1)} %own_ref.2) | copy-start | bytes 294916
  5.6 10.6 %copy-start.5 = (bf16[512,64]{0,1:T(8,128)(2,1)S(1)}, bf16[512,64]{0,1:T(8,128)(2,1)}, u32[]{:S(2)}) copy-start(bf16[512,64]{0,1:T(8,128)(2,1)} %param.25) | copy-start | bytes 196612
  5.6 10.6 %copy-start.6 = (bf16[512,48]{0,1:T(8,128)(2,1)S(1)}, bf16[512,48]{0,1:T(8,128)(2,1)}, u32[]{:S(2)}) copy-start(bf16[512,48]{0,1:T(8,128)(2,1)} %param.15) | copy-start | bytes 147460
  5.6 26.7 %all-to-all-start = ((bf16[32,64,128]{2,1,0:T(8,128)(2,1)}), bf16[32,64,128]{2,1,0:T(8,128)(2,1)S(1)}, u32[]{:S(2)}, u32[]{:S(2)}) async-start(bf16[32,64,128]{2,1,0:T(8,128)(2,1)} %edges.1.late_ref), calls=%async_computation | async-start | bytes 1048576 | tf_op jit(solution)/shard_map/edges/all_to_all | solution.py:298
  16.3 15.9 %collective-permute-start = (bf16[64,512]{1,0:T(8,128)(2,1)S(1)}, bf16[64,512]{1,0:T(8,128)(2,1)S(1)}, u32[]{:S(2)}, u32[]{:S(2)}) collective-permute-start(bf16[64,512]{1,0:T(8,128)(2,1)S(1)} %get-tuple-element.12.cot_ref), channel_id=1, source_target_pairs={{0,8},{1,9},{2,10},{3,11},{4,12},{5,13},{6,14},{7,15},{8,0},{9,1},... | collective-permute-start | bytes 196616 | tf_op jit(solution)/shard_map/pieces/ppermute | solution.py:303
  34.5 24.9 %all-to-all-start.1 = ((bf16[4,144,512]{2,1,0:T(8,128)(2,1)}), bf16[4,144,512]{2,1,0:T(8,128)(2,1)S(1)}, u32[]{:S(2)}, u32[]{:S(2)}) async-start(bf16[4,144,512]{2,1,0:T(8,128)(2,1)} %get-tuple-element.13), calls=%async_computation.1 | async-start | bytes 1179648 | tf_op jit(solution)/shard_map/mean/all_to_all | solution.py:298
  38.4 12.5 %collective-permute-start.1 = (bf16[2,64,512]{2,1,0:T(8,128)(2,1)S(1)}, bf16[2,64,512]{2,1,0:T(8,128)(2,1)S(1)}, u32[]{:S(2)}, u32[]{:S(2)}) collective-permute-start(bf16[2,64,512]{2,1,0:T(8,128)(2,1)S(1)} %get-tuple-element.14.cots_ref), channel_id=1, source_target_pairs={{0,4},{1,5},{2,6},{3,7},{4,0},{5,1},{6,2},{7,3},{8,12},{9,13},{10,... | collective-permute-start | bytes 393224 | tf_op jit(solution)/shard_map/mean/ppermute | solution.py:303
  60.4 7.9 %copy-start.1 = (bf16[64,1024]{1,0:T(8,128)(2,1)S(1)}, bf16[64,1024]{1,0:T(8,128)(2,1)}, u32[]{:S(2)}) copy-start(bf16[64,1024]{1,0:T(8,128)(2,1)} %neigh_ref.3) | copy-start | bytes 393220
  60.4 7.9 %copy-start.2 = (bf16[64,1024]{1,0:T(8,128)(2,1)S(1)}, bf16[64,1024]{1,0:T(8,128)(2,1)}, u32[]{:S(2)}) copy-start(bf16[64,1024]{1,0:T(8,128)(2,1)} %own_ref.3) | copy-start | bytes 393220
  60.4 21.9 %all-to-all-start.2 = ((bf16[4,64,512]{2,1,0:T(8,128)(2,1)}), bf16[4,64,512]{2,1,0:T(8,128)(2,1)S(1)}, u32[]{:S(2)}, u32[]{:S(2)}) async-start(bf16[4,64,512]{2,1,0:T(8,128)(2,1)} %first.1.late_ref), calls=%async_computation.2 | async-start | bytes 524288 | tf_op jit(solution)/shard_map/first/all_to_all | solution.py:298
  83.2 20.0 %copy-start = (bf16[4,128,128]{2,1,0:T(8,128)(2,1)S(1)}, bf16[4,128,128]{2,1,0:T(8,128)(2,1)}, u32[]{:S(2)}) copy-start(bf16[4,128,128]{2,1,0:T(8,128)(2,1)} %values_ref.1) | copy-start | bytes 393220
  83.2 20.0 %all-to-all-start.3 = ((bf16[4,128,512]{2,1,0:T(8,128)(2,1)}), bf16[4,128,512]{2,1,0:T(8,128)(2,1)S(1)}, u32[]{:S(2)}, u32[]{:S(2)}) async-start(bf16[4,128,512]{2,1,0:T(8,128)(2,1)} %hidden.1), calls=%async_computation.3 | async-start | bytes 1048576 | tf_op jit(solution)/shard_map/hidden/all_to_all | solution.py:298
  92.0 0.7 copy-start.9
  92.7 0.7 copy-start.10
  105.0 20.0 %all-to-all-start.5 = ((bf16[32,32,128]{2,1,0:T(8,128)(2,1)}), bf16[32,32,128]{2,1,0:T(8,128)(2,1)S(1)}, u32[]{:S(2)}, u32[]{:S(2)}) async-start(bf16[32,32,128]{2,1,0:T(8,128)(2,1)} %get-tuple-element.16), calls=%async_computation.5 | async-start | bytes 524288 | tf_op jit(solution)/shard_map/grads/all_to_all | solution.py:298
  125.1 17.6 %all-to-all-start.4 = ((bf16[4,64,512]{2,1,0:T(8,128)(2,1)}), bf16[4,64,512]{2,1,0:T(8,128)(2,1)S(1)}, u32[]{:S(2)}, u32[]{:S(2)}) async-start(bf16[4,64,512]{2,1,0:T(8,128)(2,1)} %second.2), calls=%async_computation.4 | async-start | bytes 524288 | tf_op jit(solution)/shard_map/second/all_to_all | solution.py:298
  128.6 9.3 %collective-permute-start.2 = (f32[8,128]{1,0:T(8,128)S(1)}, f32[8,128]{1,0:T(8,128)S(1)}, u32[]{:S(2)}, u32[]{:S(2)}) collective-permute-start(f32[8,128]{1,0:T(8,128)S(1)} %get-tuple-element.21), channel_id=1, source_target_pairs={{0,1},{1,0},{2,3},{3,2},{4,5},{5,4},{6,7},{7,6},{8,9},{9,8},{10,11... | collective-permute-start | bytes 12296 | tf_op jit(solution)/shard_map/grads/ppermute | solution.py:303
  130.5 7.4 %collective-permute-start.3 = (f32[8,128]{1,0:T(8,128)S(1)}, f32[8,128]{1,0:T(8,128)S(1)}, u32[]{:S(2)}, u32[]{:S(2)}) collective-permute-start(f32[8,128]{1,0:T(8,128)S(1)} %get-tuple-element.20), channel_id=1, source_target_pairs={{0,2},{1,3},{2,0},{3,1},{4,6},{5,7},{6,4},{7,5},{8,10},{9,11},{10,... | collective-permute-start | bytes 12296 | tf_op jit(solution)/shard_map/grads/ppermute | solution.py:303
  133.9 6.8 %collective-permute-start.4 = (f32[8,128]{1,0:T(8,128)S(1)}, f32[8,128]{1,0:T(8,128)S(1)}, u32[]{:S(2)}, u32[]{:S(2)}) collective-permute-start(f32[8,128]{1,0:T(8,128)S(1)} %get-tuple-element.19), channel_id=1, source_target_pairs={{0,3},{1,2},{2,1},{3,0},{4,7},{5,6},{6,5},{7,4},{8,11},{9,10},{10,... | collective-permute-start | bytes 12296 | tf_op jit(solution)/shard_map/grads/ppermute | solution.py:303
  143.6 21.2 %all-to-all-start.6 = ((f32[32,32,128]{2,1,0:T(8,128)}), f32[32,32,128]{2,1,0:T(8,128)S(1)}, u32[]{:S(2)}, u32[]{:S(2)}) async-start(f32[32,32,128]{2,1,0:T(8,128)} %place.2), calls=%async_computation.6 | async-start | bytes 1048576 | tf_op jit(solution)/shard_map/place/all_to_all | solution.py:298
  153.1 0.7 copy-start.12
  (1 other events, 0.7 us)

commit v10 on v6

--- a/solution.py
+++ b/solution.py
@@ -94,15 +94,13 @@
         out_ref[to, 3 * rows :, :] = self_ref[:, width:]
 
 
-def second_pieces_kernel(mine_ref, neigh_ref, own_ref, late_ref, out_ref):
+def second_pieces_kernel(neigh_ref, own_ref, late_ref, out_ref):
     del late_ref
-    mine = mine_ref[0]
-    rows = neigh_ref.shape[0]
-    both = zip(column_sets(neigh_ref[...], out_ref.shape[0]), column_sets(own_ref[...], out_ref.shape[0]))
+    group, _, width = out_ref.shape
+    both = zip(column_sets(neigh_ref[...], group), column_sets(own_ref[...], group))
     for j, (neigh, own) in enumerate(both):
-        to = jnp.bitwise_xor(mine, j)
-        out_ref[to, :rows, :] = neigh
-        out_ref[to, rows:, :] = own
+        out_ref[j, :, : width // 2] = neigh
+        out_ref[j, :, width // 2 :] = own
 
 
 def mean_kernel(cols, recv_ref, late1_ref, late2_ref, late3_ref, out_ref):
@@ -149,15 +147,13 @@
 ):
     cols, targets = bias_ref.shape[0], live_ref.shape[1]
     width = values_ref.shape[1]
-    wide = pay_ref.shape[2]
     total = parts_ref[0].astype(F32)
     for k in range(1, parts_ref.shape[0]):
         total = total + parts_ref[k].astype(F32)
     hidden = jnp.maximum(total + bias_ref[...], 0.0).astype(BF)
     for k in range(pay_ref.shape[0]):
-        pay_ref[k, :cols, :] = hidden[:, :wide]
-        pay_ref[k, cols : 2 * cols, :] = hidden[:, wide:]
-        pay_ref[k, 2 * cols :, :] = pieces_ref[k]
+        pay_ref[k, :cols, :] = hidden
+        pay_ref[k, cols:, :] = pieces_ref[k]
     live = live_ref[...].astype(BF)
     for t in range(targets // width):
         source[t] = hidden[:, t * width : (t + 1) * width]
@@ -173,7 +169,8 @@
     left_ref[cols:, :] = hidden * live
 
 
-def grad_kernel(left_ref, cot_ref, out_ref):
+def grad_kernel(left_ref, cot_ref, late_ref, out_ref):
+    del late_ref
     pieces, piece_rows, piece_cols = out_ref.shape
     quarters = left_ref.shape[0] // piece_rows
     for c in range(pieces // quarters):
@@ -184,22 +181,21 @@
 
 
 def second_kernel(
-    across_ref, index_ref, values_ref, p0_ref, p1_ref, p2_ref, p3_ref, out_ref, weight, acts, source, acc
+    across_ref, index_ref, values_ref, got_ref, out_ref, weight, acts, source, acc
 ):
     across = across_ref[0]
-    n, cols, targets = out_ref.shape
-    wide = p0_ref.shape[1]
+    group, cols, targets = got_ref.shape
+    cols = cols // 2
+    half = targets // 2
     width = values_ref.shape[1]
-    group = 4
-    for k, ref in enumerate((p0_ref, p1_ref, p2_ref, p3_ref)):
-        mine = slice(k * cols, (k + 1) * cols)
-        acts[mine, :wide] = ref[:cols, :]
-        acts[mine, wide:] = ref[cols : 2 * cols, :]
-        weight[mine, :] = ref[3 * cols :, :]
-        weight[(group + k) * cols : (group + k + 1) * cols, :] = ref[2 * cols : 3 * cols, :]
+    wide = group * cols
+    for j in range(group):
+        mine = slice(j * cols, (j + 1) * cols)
+        acts[mine, :] = got_ref[j, :cols, :]
+        weight[mine, :] = got_ref[j, cols:, half:]
+        weight[wide + j * cols : wide + (j + 1) * cols, :] = got_ref[j, cols:, :half]
         for t in range(targets // width):
-            half, at = divmod(t * width, wide)
-            source[t, mine, :] = ref[half * cols : (half + 1) * cols, at : at + width]
+            source[t, mine, :] = got_ref[j, :cols, t * width : (t + 1) * width]
     acc[...] = jnp.zeros_like(acc)
     for k in range(values_ref.shape[0]):
         target = index_ref[k, 0]
@@ -207,13 +203,14 @@
             source[index_ref[k, 1]], values_ref[k], NT, preferred_element_type=F32
         )
     for t in range(targets // width):
-        acts[group * cols :, t * width : (t + 1) * width] = acc[t].astype(BF)
+        acts[wide:, t * width : (t + 1) * width] = acc[t].astype(BF)
     total = lax.dot_general(weight[...], acts[...], TN, preferred_element_type=F32)
-    for z in range(n):
+    for z in range(out_ref.shape[0]):
         out_ref[jnp.bitwise_xor(across, z)] = total[z * cols : (z + 1) * cols, :].astype(BF)
 
 
-def copies_kernel(terms_ref, out_ref):
+def copies_kernel(terms_ref, late_ref, out_ref):
+    del late_ref
     total = terms_ref[0].astype(F32)
     for d in range(1, terms_ref.shape[0]):
         total = total + terms_ref[d].astype(F32)
@@ -326,17 +323,12 @@
         parts = swap(first, "feat", far)
     with jax.named_scope("pieces"):
         pieces = call(
-            second_pieces_kernel,
-            shape(GROUP, 2 * hid, wide),
-            4,
-            smem=(0,),
-            late=(3,),
-            nbytes=1 << 20,
-        )(mine, neigh_two, self_two, first)
+            second_pieces_kernel, shape(GROUP, hid, targets), 3, late=(2,), nbytes=1 << 20
+        )(neigh_two, self_two, first)
     with jax.named_scope("hidden"):
         pay, left = call(
             hidden_kernel,
-            (shape(GROUP, 4 * hid, wide), shape(2 * hid, targets)),
+            (shape(GROUP, 2 * hid, targets), shape(2 * hid, targets)),
             6,
             scratch=[
                 pltpu.VMEM((targets // 128, hid, 128), BF),
@@ -345,32 +337,23 @@
             smem=(2,),
             nbytes=1 << 20,
         )(parts, bias_one.reshape(hid, 1), tile_index, tile_values, live, pieces)
-        got = [trade(pay[k], k) for k in range(1, GROUP)]
+        pay = swap(pay, "feat", near)
     with jax.named_scope("grads"):
         piece_rows = 2 * hid * full // 128 // groups
         terms = call(
             grad_kernel,
             shape(groups, piece_rows, 128),
-            2,
+            3,
+            late=(2,),
             flops=2 * 2 * hid * targets * full,
             nbytes=2 << 20,
-        )(left, cot)
+        )(left, cot, pay)
         terms = swap(terms, "dp")
-        spread = call(
-            copies_kernel, shape(groups, piece_rows, 128, dtype=F32), 1, nbytes=1 << 20
-        )(terms)
-        spread = swap(spread, "dp")
-        grad_neigh, grad_self = call(
-            place_kernel,
-            (shape(hid, full, dtype=F32), shape(hid, full, dtype=F32)),
-            1,
-            nbytes=1 << 20,
-        )(spread)
     with jax.named_scope("second"):
         second = call(
             second_kernel,
             shape(blocks, hid, targets),
-            7,
+            4,
             scratch=[
                 pltpu.VMEM((2 * wide, wide), BF),
                 pltpu.VMEM((2 * wide, targets), BF),
@@ -380,11 +363,26 @@
             smem=(0, 1),
             flops=2 * 2 * wide * wide * targets,
             nbytes=2 << 20,
-        )(across, tile_index, tile_values, pay[0], *got)
+        )(across, tile_index, tile_values, pay)
         sums = [second[0]] + [trade(second[k], GROUP * k) for k in range(1, blocks)]
         second_out = call(out_kernel, shape(hid, targets), 6, nbytes=1 << 20)(
             *sums, bias_two.reshape(hid, 1), live
         ).T
+    with jax.named_scope("spread"):
+        spread = call(
+            copies_kernel,
+            shape(groups, piece_rows, 128, dtype=F32),
+            2,
+            late=(1,),
+            nbytes=1 << 20,
+        )(terms, sums[1])
+        spread = swap(spread, "dp")
+        grad_neigh, grad_self = call(
+            place_kernel,
+            (shape(hid, full, dtype=F32), shape(hid, full, dtype=F32)),
+            1,
+            nbytes=1 << 20,
+        )(spread)
     return (second_out, grad_neigh, grad_self)
 
 

time: 169 us -> 206 us (1.22)
  waiting for transfers between devices: 40.9 us -> 83.6 us
  blocking collectives: 34.2 us -> 9.55 us
  starting transfers between devices: 62.6 us -> 81.5 us
    all_gather x1, waiting for transfers between devices: 3.71 us -> 48.5 us  [body(): cot = lax.all_gather(cotangent.T, 'feat', axis=0, tiled=True)]
    all_to_all x3 -> x5, starting transfers between devices: 27.8 us -> 57.3 us  [swap(): lax.all_to_all(x, axis, split_axis=0, concat_axis=0, tiled=True, axis_ind...]
    all_to_all x2 -> x1, blocking collectives: 34.2 us -> 9.55 us  [swap(): lax.all_to_all(x, axis, split_axis=0, concat_axis=0, tiled=True, axis_ind...]
    ppermute x9 -> x6, starting transfers between devices: 34.7 us -> 24.2 us  [trade(): return lax.ppermute(x, 'feat', [(i, i ^ k) for i in range(n_feat)])]
    all_to_all x3 -> x5, waiting for transfers between devices: 15.5 us -> 13.8 us  [swap(): lax.all_to_all(x, axis, split_axis=0, concat_axis=0, tiled=True, axis_ind...]
    ppermute x9 -> x6, waiting for transfers between devices: 21 us -> 20.6 us  [trade(): return lax.ppermute(x, 'feat', [(i, i ^ k) for i in range(n_feat)])]
  transfers between devices with their start and end apart: 13 -> 12, of which waited for: 7 -> 6; matrix products, arithmetic and copies ran while one was open for 0% -> 0% of each run, Pallas kernels for 5% -> 2%
where the time goes in v10:
time: 206 us
  waiting for transfers between devices  83.6 us (41%)
  starting transfers between devices  81.5 us (40%)
  between operations  14.3 us (7%)
  Pallas kernels  12.1 us (6%)
  blocking collectives  9.55 us (5%)
  local copies, waits for them, and re-layouts  4.53 us (2%)
    all_to_all x5, starting transfers between devices, swap(): lax.all_to_all(x, axis, split_axis=0, concat_axis=0, tiled=True, axis_ind...  57.3 us
    all_gather x1, waiting for transfers between devices, body(): cot = lax.all_gather(cotangent.T, 'feat', axis=0, tiled=True)  48.5 us
    ppermute x6, starting transfers between devices, trade(): return lax.ppermute(x, 'feat', [(i, i ^ k) for i in range(n_feat)])  24.2 us
    ppermute x6, waiting for transfers between devices, trade(): return lax.ppermute(x, 'feat', [(i, i ^ k) for i in range(n_feat)])  20.6 us
    all_to_all x5, waiting for transfers between devices, swap(): lax.all_to_all(x, axis, split_axis=0, concat_axis=0, tiled=True, axis_ind...  13.8 us
    all_to_all x1, blocking collectives, swap(): lax.all_to_all(x, axis, split_axis=0, concat_axis=0, tiled=True, axis_ind...  9.55 us
    unnamed x27, local copies, waits for them, and re-layouts  4.29 us
  transfers between devices with their start and end apart: 12, of which 6 were waited for; matrix products, arithmetic and copies ran while one was open for 0% of the time, Pallas kernels for 2%

profile of v10, /device:TPU:1, one launch (start us, length us, event | category | flops | bytes accessed | tf_op | source)
XLA Modules:
  0.0 205.6 jit_solution(12337009959522722165)
XLA Ops:
  8.8 3.3 %edges.1.late_ref = bf16[32,64,128]{2,1,0:T(8,128)(2,1)} custom-call(bf16[48,2048]{1,0:T(8,128)(2,1)S(1)} %bitcast.29, s32[16,128]{1,0:T(8,128)S(1)} %bitcast.30), custom_call_target="tpu_custom_call" | custom-call | flops 1073741824 | bytes 8388608 | tf_op jit(solution)/shard_map/edges/pallas_call | solution.py:284
  12.1 10.6 %all-to-all-start = ((bf16[32,64,128]{2,1,0:T(8,128)(2,1)}), bf16[32,64,128]{2,1,0:T(8,128)(2,1)S(1)}, u32[]{:S(2)}, u32[]{:S(2)}) async-start(bf16[32,64,128]{2,1,0:T(8,128)(2,1)} %edges.1.late_ref), calls=%async_computation | async-start | bytes 1048576 | tf_op jit(solution)/shard_map/edges/all_to_all | solution.py:271
  22.9 1.9 collective-permute-start
  24.8 4.7 %collective-permute-start.1 = (bf16[192,256]{1,0:T(8,128)(2,1)S(1)}, bf16[192,256]{1,0:T(8,128)(2,1)S(1)}, u32[]{:S(2)}, u32[]{:S(2)}) collective-permute-start(bf16[192,256]{1,0:T(8,128)(2,1)S(1)} %get-tuple-element.13), channel_id=1, source_target_pairs={{0,2},{1,3},{2,0},{3,1},{4,6},{5,7},{6,4},{7,5},{8,10},{9,11},{10,... | collective-permute-start | bytes 294920 | tf_op jit(solution)/shard_map/pieces/ppermute | solution.py:276
  29.5 2.7 %collective-permute-start.2 = (bf16[192,256]{1,0:T(8,128)(2,1)S(1)}, bf16[192,256]{1,0:T(8,128)(2,1)S(1)}, u32[]{:S(2)}, u32[]{:S(2)}) collective-permute-start(bf16[192,256]{1,0:T(8,128)(2,1)S(1)} %get-tuple-element.12), channel_id=1, source_target_pairs={{0,3},{1,2},{2,1},{3,0},{4,7},{5,6},{6,5},{7,4},{8,11},{9,10},{10,... | collective-permute-start | bytes 294920 | tf_op jit(solution)/shard_map/pieces/ppermute | solution.py:276
  32.2 2.1 %collective-permute-done.1.late2_ref.p2_ref = bf16[192,256]{1,0:T(8,128)(2,1)S(1)} collective-permute-done((bf16[192,256]{1,0:T(8,128)(2,1)S(1)}, bf16[192,256]{1,0:T(8,128)(2,1)S(1)}, u32[]{:S(2)}, u32[]{:S(2)}) %collective-permute-start.1) | collective-permute-done | bytes 98336 | tf_op jit(solution)/shard_map/pieces/ppermute | solution.py:276
  34.3 2.5 %collective-permute-done.2.late3_ref.p3_ref = bf16[192,256]{1,0:T(8,128)(2,1)S(1)} collective-permute-done((bf16[192,256]{1,0:T(8,128)(2,1)S(1)}, bf16[192,256]{1,0:T(8,128)(2,1)S(1)}, u32[]{:S(2)}, u32[]{:S(2)}) %collective-permute-start.2) | collective-permute-done | bytes 98336 | tf_op jit(solution)/shard_map/pieces/ppermute | solution.py:276
  36.8 1.4 mean.1
  38.2 9.5 %all_to_all.30.mean_ref = bf16[4,48,512]{2,1,0:T(8,128)(2,1)S(1)} all-to-all(bf16[4,48,512]{2,1,0:T(8,128)(2,1)S(1)} %mean.1), channel_id=1, replica_groups={{0,1,2,3},{4,5,6,7},{8,9,10,11},{12,13,14,15},{16,17,18,19},{20,21,22,2..., dimensions={0} | all-to-all | bytes 393216 | tf_op jit(solution)/shard_map/mean/all_to_all | solution.py:271
  48.8 13.2 %all-to-all-start.2 = ((bf16[4,64,512]{2,1,0:T(8,128)(2,1)}), bf16[4,64,512]{2,1,0:T(8,128)(2,1)S(1)}, u32[]{:S(2)}, u32[]{:S(2)}) async-start(bf16[4,64,512]{2,1,0:T(8,128)(2,1)} %first.1.late_ref), calls=%async_computation.2 | async-start | bytes 524288 | tf_op jit(solution)/shard_map/first/all_to_all | solution.py:271
  64.4 13.8 %all-to-all-done.2.parts_ref = bf16[4,64,512]{2,1,0:T(8,128)(2,1)S(1)} async-done(((bf16[4,64,512]{2,1,0:T(8,128)(2,1)}), bf16[4,64,512]{2,1,0:T(8,128)(2,1)S(1)}, u32[]{:S(2)}, u32[]{:S(2)}) %all-to-all-start.2) | async-done | bytes 262176 | tf_op jit(solution)/shard_map/first/all_to_all | solution.py:271
  78.2 1.5 hidden.1
  79.7 5.9 %all-to-all-start.3 = ((bf16[4,128,512]{2,1,0:T(8,128)(2,1)}), bf16[4,128,512]{2,1,0:T(8,128)(2,1)S(1)}, u32[]{:S(2)}, u32[]{:S(2)}) async-start(bf16[4,128,512]{2,1,0:T(8,128)(2,1)} %get-tuple-element.7), calls=%async_computation.3 | async-start | bytes 1048576 | tf_op jit(solution)/shard_map/hidden/all_to_all | solution.py:271
  85.5 48.5 %all-gather.2.cloned.1.call-done.cot_ref = bf16[1024,512]{1,0:T(8,128)(2,1)} async-done(((bf16[64,512]{1,0:T(8,128)(2,1)}), bf16[1024,512]{1,0:T(8,128)(2,1)}) %all-gather.2.cloned.1.call-update) | async-done | bytes 1048592 | tf_op jit(solution)/shard_map/cotangent/all_gather | solution.py:282
  134.0 1.2 copy-done
  135.3 1.1 grads.1
  136.4 15.3 %all-to-all-start.4 = ((bf16[32,32,128]{2,1,0:T(8,128)(2,1)}), bf16[32,32,128]{2,1,0:T(8,128)(2,1)S(1)}, u32[]{:S(2)}, u32[]{:S(2)}) async-start(bf16[32,32,128]{2,1,0:T(8,128)(2,1)} %grads.1), calls=%async_computation.4 | async-start | bytes 524288 | tf_op jit(solution)/shard_map/grads/all_to_all | solution.py:271
  151.7 1.1 second.2
  152.8 5.1 %collective-permute-start.3 = (bf16[64,512]{1,0:T(8,128)(2,1)S(1)}, bf16[64,512]{1,0:T(8,128)(2,1)S(1)}, u32[]{:S(2)}, u32[]{:S(2)}) collective-permute-start(bf16[64,512]{1,0:T(8,128)(2,1)S(1)} %get-tuple-element.17), channel_id=1, source_target_pairs={{0,4},{1,5},{2,6},{3,7},{4,0},{5,1},{6,2},{7,3},{8,12},{9,13},{10,... | collective-permute-start | bytes 196616 | tf_op jit(solution)/shard_map/second/ppermute | solution.py:276
  158.0 4.1 %collective-permute-done.3.p1_ref.late_ref = bf16[64,512]{1,0:T(8,128)(2,1)S(1)} collective-permute-done((bf16[64,512]{1,0:T(8,128)(2,1)S(1)}, bf16[64,512]{1,0:T(8,128)(2,1)S(1)}, u32[]{:S(2)}, u32[]{:S(2)}) %collective-permute-start.3) | collective-permute-done | bytes 65568 | tf_op jit(solution)/shard_map/second/ppermute | solution.py:276
  163.0 12.4 %all-to-all-start.5 = ((f32[32,32,128]{2,1,0:T(8,128)}), f32[32,32,128]{2,1,0:T(8,128)S(1)}, u32[]{:S(2)}, u32[]{:S(2)}) async-start(f32[32,32,128]{2,1,0:T(8,128)} %spread.2), calls=%async_computation.5 | async-start | bytes 1048576 | tf_op jit(solution)/shard_map/spread/all_to_all | solution.py:271
  175.4 7.9 %collective-permute-start.4 = (bf16[64,512]{1,0:T(8,128)(2,1)S(1)}, bf16[64,512]{1,0:T(8,128)(2,1)S(1)}, u32[]{:S(2)}, u32[]{:S(2)}) collective-permute-start(bf16[64,512]{1,0:T(8,128)(2,1)S(1)} %get-tuple-element.16), channel_id=1, source_target_pairs={{0,8},{1,9},{2,10},{3,11},{4,12},{5,13},{6,14},{7,15},{8,0},{9,1},... | collective-permute-start | bytes 196616 | tf_op jit(solution)/shard_map/second/ppermute | solution.py:276
  183.3 1.9 collective-permute-start.5
  185.3 11.8 %collective-permute-done.4.p2_ref = bf16[64,512]{1,0:T(8,128)(2,1)S(1)} collective-permute-done((bf16[64,512]{1,0:T(8,128)(2,1)S(1)}, bf16[64,512]{1,0:T(8,128)(2,1)S(1)}, u32[]{:S(2)}, u32[]{:S(2)}) %collective-permute-start.4) | collective-permute-done | bytes 65568 | tf_op jit(solution)/shard_map/second/ppermute | solution.py:276
  (45 shorter events, 7.7 us)
Async XLA Ops:
  7.2 0.9 copy-start.7
  8.1 0.7 copy-start.8
  12.1 10.6 %copy-start.4 = (bf16[48,1024]{1,0:T(8,128)(2,1)S(1)}, bf16[48,1024]{1,0:T(8,128)(2,1)}, u32[]{:S(2)}) copy-start(bf16[48,1024]{1,0:T(8,128)(2,1)} %neigh_ref.2) | copy-start | bytes 294916
  12.1 10.6 %copy-start.5 = (bf16[48,1024]{1,0:T(8,128)(2,1)S(1)}, bf16[48,1024]{1,0:T(8,128)(2,1)}, u32[]{:S(2)}) copy-start(bf16[48,1024]{1,0:T(8,128)(2,1)} %own_ref.2) | copy-start | bytes 294916
  12.1 10.6 %copy-start.6 = (bf16[512,48]{0,1:T(8,128)(2,1)S(1)}, bf16[512,48]{0,1:T(8,128)(2,1)}, u32[]{:S(2)}) copy-start(bf16[512,48]{0,1:T(8,128)(2,1)} %param.15) | copy-start | bytes 147460
  12.1 24.7 %all-to-all-start = ((bf16[32,64,128]{2,1,0:T(8,128)(2,1)}), bf16[32,64,128]{2,1,0:T(8,128)(2,1)S(1)}, u32[]{:S(2)}, u32[]{:S(2)}) async-start(bf16[32,64,128]{2,1,0:T(8,128)(2,1)} %edges.1.late_ref), calls=%async_computation | async-start | bytes 1048576 | tf_op jit(solution)/shard_map/edges/all_to_all | solution.py:271
  22.9 9.3 %collective-permute-start = (bf16[192,256]{1,0:T(8,128)(2,1)S(1)}, bf16[192,256]{1,0:T(8,128)(2,1)S(1)}, u32[]{:S(2)}, u32[]{:S(2)}) collective-permute-start(bf16[192,256]{1,0:T(8,128)(2,1)S(1)} %get-tuple-element.14), channel_id=1, source_target_pairs={{0,1},{1,0},{2,3},{3,2},{4,5},{5,4},{6,7},{7,6},{8,9},{9,8},{10,11... | collective-permute-start | bytes 294920 | tf_op jit(solution)/shard_map/pieces/ppermute | solution.py:276
  24.8 9.5 %collective-permute-start.1 = (bf16[192,256]{1,0:T(8,128)(2,1)S(1)}, bf16[192,256]{1,0:T(8,128)(2,1)S(1)}, u32[]{:S(2)}, u32[]{:S(2)}) collective-permute-start(bf16[192,256]{1,0:T(8,128)(2,1)S(1)} %get-tuple-element.13), channel_id=1, source_target_pairs={{0,2},{1,3},{2,0},{3,1},{4,6},{5,7},{6,4},{7,5},{8,10},{9,11},{10,... | collective-permute-start | bytes 294920 | tf_op jit(solution)/shard_map/pieces/ppermute | solution.py:276
  29.5 7.3 %collective-permute-start.2 = (bf16[192,256]{1,0:T(8,128)(2,1)S(1)}, bf16[192,256]{1,0:T(8,128)(2,1)S(1)}, u32[]{:S(2)}, u32[]{:S(2)}) collective-permute-start(bf16[192,256]{1,0:T(8,128)(2,1)S(1)} %get-tuple-element.12), channel_id=1, source_target_pairs={{0,3},{1,2},{2,1},{3,0},{4,7},{5,6},{6,5},{7,4},{8,11},{9,10},{10,... | collective-permute-start | bytes 294920 | tf_op jit(solution)/shard_map/pieces/ppermute | solution.py:276
  48.8 15.4 %copy-start.2 = (bf16[64,1024]{1,0:T(8,128)(2,1)S(1)}, bf16[64,1024]{1,0:T(8,128)(2,1)}, u32[]{:S(2)}) copy-start(bf16[64,1024]{1,0:T(8,128)(2,1)} %neigh_ref.3) | copy-start | bytes 393220
  48.8 15.4 %copy-start.3 = (bf16[64,1024]{1,0:T(8,128)(2,1)S(1)}, bf16[64,1024]{1,0:T(8,128)(2,1)}, u32[]{:S(2)}) copy-start(bf16[64,1024]{1,0:T(8,128)(2,1)} %own_ref.3) | copy-start | bytes 393220
  48.8 29.4 %all-to-all-start.2 = ((bf16[4,64,512]{2,1,0:T(8,128)(2,1)}), bf16[4,64,512]{2,1,0:T(8,128)(2,1)S(1)}, u32[]{:S(2)}, u32[]{:S(2)}) async-start(bf16[4,64,512]{2,1,0:T(8,128)(2,1)} %first.1.late_ref), calls=%async_computation.2 | async-start | bytes 524288 | tf_op jit(solution)/shard_map/first/all_to_all | solution.py:271
  62.0 72.1 %all-gather.2.cloned.1.call-start = ((), (), s32[]{:S(2)}) async-start(), calls=%async_computation.6 | async-start | bytes 1114112 | tf_op jit(solution)/shard_map/cotangent/all_gather | solution.py:282
  62.0 0.7 copy-start.9
  62.7 0.7 copy-start.10
  64.2 13.9 %copy-start.1 = (bf16[4,128,128]{2,1,0:T(8,128)(2,1)S(1)}, bf16[4,128,128]{2,1,0:T(8,128)(2,1)}, u32[]{:S(2)}) copy-start(bf16[4,128,128]{2,1,0:T(8,128)(2,1)} %values_ref.3) | copy-start | bytes 393220
  79.7 54.4 %all-to-all-start.3 = ((bf16[4,128,512]{2,1,0:T(8,128)(2,1)}), bf16[4,128,512]{2,1,0:T(8,128)(2,1)S(1)}, u32[]{:S(2)}, u32[]{:S(2)}) async-start(bf16[4,128,512]{2,1,0:T(8,128)(2,1)} %get-tuple-element.7), calls=%async_computation.3 | async-start | bytes 1048576 | tf_op jit(solution)/shard_map/hidden/all_to_all | solution.py:271
  134.0 1.2 copy-start
  136.4 25.7 %all-to-all-start.4 = ((bf16[32,32,128]{2,1,0:T(8,128)(2,1)}), bf16[32,32,128]{2,1,0:T(8,128)(2,1)S(1)}, u32[]{:S(2)}, u32[]{:S(2)}) async-start(bf16[32,32,128]{2,1,0:T(8,128)(2,1)} %grads.1), calls=%async_computation.4 | async-start | bytes 524288 | tf_op jit(solution)/shard_map/grads/all_to_all | solution.py:271
  152.8 9.3 %collective-permute-start.3 = (bf16[64,512]{1,0:T(8,128)(2,1)S(1)}, bf16[64,512]{1,0:T(8,128)(2,1)S(1)}, u32[]{:S(2)}, u32[]{:S(2)}) collective-permute-start(bf16[64,512]{1,0:T(8,128)(2,1)S(1)} %get-tuple-element.17), channel_id=1, source_target_pairs={{0,4},{1,5},{2,6},{3,7},{4,0},{5,1},{6,2},{7,3},{8,12},{9,13},{10,... | collective-permute-start | bytes 196616 | tf_op jit(solution)/shard_map/second/ppermute | solution.py:276
  163.0 34.9 %all-to-all-start.5 = ((f32[32,32,128]{2,1,0:T(8,128)}), f32[32,32,128]{2,1,0:T(8,128)S(1)}, u32[]{:S(2)}, u32[]{:S(2)}) async-start(f32[32,32,128]{2,1,0:T(8,128)} %spread.2), calls=%async_computation.5 | async-start | bytes 1048576 | tf_op jit(solution)/shard_map/spread/all_to_all | solution.py:271
  175.4 21.8 %collective-permute-start.4 = (bf16[64,512]{1,0:T(8,128)(2,1)S(1)}, bf16[64,512]{1,0:T(8,128)(2,1)S(1)}, u32[]{:S(2)}, u32[]{:S(2)}) collective-permute-start(bf16[64,512]{1,0:T(8,128)(2,1)S(1)} %get-tuple-element.16), channel_id=1, source_target_pairs={{0,8},{1,9},{2,10},{3,11},{4,12},{5,13},{6,14},{7,15},{8,0},{9,1},... | collective-permute-start | bytes 196616 | tf_op jit(solution)/shard_map/second/ppermute | solution.py:276
  183.3 1.9 copy-start.12
  183.3 13.9 %collective-permute-start.5 = (bf16[64,512]{1,0:T(8,128)(2,1)S(1)}, bf16[64,512]{1,0:T(8,128)(2,1)S(1)}, u32[]{:S(2)}, u32[]{:S(2)}) collective-permute-start(bf16[64,512]{1,0:T(8,128)(2,1)S(1)} %get-tuple-element.15), channel_id=1, source_target_pairs={{0,12},{1,13},{2,14},{3,15},{4,8},{5,9},{6,10},{7,11},{8,4},{9,5},... | collective-permute-start | bytes 196616 | tf_op jit(solution)/shard_map/second/ppermute | solution.py:276
  (1 other events, 0.7 us)
Sparse Core Ops, SparseCore 0:
  64.9 69.1 all-gather.1

commit v11 on v8

--- a/solution.py
+++ b/solution.py
@@ -70,35 +70,43 @@
             send_ref[g * some + j] = out[j * ROWS : (j + 1) * ROWS, :]
 
 
+def far_place(block, column):
+    return (block + column) % GROUP
+
+
 def column_sets(weight, group):
     half = 64
     n = weight.shape[1] // half
     sets = []
-    for j in range(group):
-        blocks = [weight[:, b * half : (b + 1) * half] for b in range(j, n, group)]
-        sets.append(jnp.concatenate(blocks, axis=1))
+    for h in range(group):
+        at = [group * i + far_place(i, h) for i in range(n // group)]
+        sets.append(jnp.concatenate([weight[:, b * half : (b + 1) * half] for b in at], axis=1))
     return sets
 
 
-def first_pieces_kernel(neigh_ref, own_ref, self_ref, cot_ref, late_ref, out_ref, cot_out_ref):
+def first_pieces_kernel(
+    block_ref, neigh_ref, own_ref, self_ref, cot_ref, late_ref, out_ref, cot_out_ref
+):
     del late_ref
     rows = neigh_ref.shape[0]
     group, _, width = out_ref.shape
     both = zip(column_sets(neigh_ref[...], group), column_sets(own_ref[...], group))
-    for j, (neigh, own) in enumerate(both):
-        out_ref[j, :rows, : width // 2] = neigh
-        out_ref[j, :rows, width // 2 :] = own
-        out_ref[j, rows:, :] = self_ref[...]
+    for h, (neigh, own) in enumerate(both):
+        to = far_place(block_ref[0], h)
+        out_ref[to, :rows, : width // 2] = neigh
+        out_ref[to, :rows, width // 2 :] = own
+        out_ref[to, rows:, :] = self_ref[...]
     cot_out_ref[...] = cot_ref[...]
 
 
-def second_pieces_kernel(neigh_ref, own_ref, late_ref, out_ref):
+def second_pieces_kernel(block_ref, neigh_ref, own_ref, late_ref, out_ref):
     del late_ref
     group, _, width = out_ref.shape
     both = zip(column_sets(neigh_ref[...], group), column_sets(own_ref[...], group))
-    for j, (neigh, own) in enumerate(both):
-        out_ref[j, :, : width // 2] = neigh
-        out_ref[j, :, width // 2 :] = own
+    for h, (neigh, own) in enumerate(both):
+        to = far_place(block_ref[0], h)
+        out_ref[to, :, : width // 2] = neigh
+        out_ref[to, :, width // 2 :] = own
 
 
 def mean_kernel(cols, recv_ref, pieces_ref, late_ref, out_ref):
@@ -219,21 +227,25 @@
         out_ref[d] = whole
 
 
-def place_kernel(mine_ref, pieces_ref, neigh_ref, self_ref):
-    mine = mine_ref[0]
+def place_kernel(mine_ref, block_ref, pieces_ref, neigh_ref, self_ref):
     half = 64
+    starts = []
+    for h in range(GROUP):
+        from_me = jnp.bitwise_xor(mine_ref[0], far_place(block_ref[0], h))
+        starts.append(pl.multiple_of(from_me * 8, 8))
     at = 0
     for out_ref in (neigh_ref, self_ref):
         for r in range(0, out_ref.shape[0], 8):
             for c in range(2):
-                parts = [
-                    pieces_ref[at, pl.ds(pl.multiple_of(jnp.bitwise_xor(mine, h) * 8, 8), 8), :]
-                    for h in range(4)
-                ]
+                parts = [pieces_ref[at, pl.ds(start, 8), :] for start in starts]
                 for e in range(2):
-                    for p in range(2):
-                        pair = [parts[2 * p + i][:, e * half : (e + 1) * half] for i in range(2)]
-                        to = (8 * c + 4 * e + 2 * p) * half
+                    block = 2 * c + e
+                    for p in range(0, GROUP, 2):
+                        pair = [
+                            parts[(p + i - block) % GROUP][:, e * half : (e + 1) * half]
+                            for i in range(2)
+                        ]
+                        to = (GROUP * block + p) * half
                         out_ref[r : r + 8, to : to + 2 * half] = jnp.concatenate(pair, axis=1)
                 at += 1
 
@@ -270,9 +282,10 @@
     blocks = n_feat // GROUP
     wide = full // GROUP
     near = [[GROUP * i + j for j in range(GROUP)] for i in range(blocks)]
-    far = [[i + GROUP * j for j in range(blocks)] for i in range(GROUP)]
+    far = [[GROUP * i + far_place(i, h) for i in range(blocks)] for h in range(GROUP)]
     z = lax.axis_index("feat")
     mine = (z % GROUP).reshape(1)
+    block = (z // GROUP).reshape(1)
     live = seed_live.reshape(1, targets).astype(F32)
 
     def swap(x, axis, among=None):
@@ -300,10 +313,11 @@
         pieces, cot = call(
             first_pieces_kernel,
             (shape(GROUP, 2 * cols, targets), shape(hid, targets)),
-            5,
-            late=(4,),
+            6,
+            smem=(0,),
+            late=(5,),
             nbytes=2 << 20,
-        )(neigh_one, self_one, self_feats.T, cotangent.T, send)
+        )(block, neigh_one, self_one, self_feats.T, cotangent.T, send)
         cot = lax.all_gather(cot, "feat", axis=0, tiled=True, axis_index_groups=far)
     with jax.named_scope("mean"):
         acts = call(
@@ -327,8 +341,13 @@
         parts = swap(first, "feat", far)
     with jax.named_scope("pieces"):
         pieces = call(
-            second_pieces_kernel, shape(GROUP, hid, targets), 3, late=(2,), nbytes=1 << 20
-        )(neigh_two, self_two, first)
+            second_pieces_kernel,
+            shape(GROUP, hid, targets),
+            4,
+            smem=(0,),
+            late=(3,),
+            nbytes=1 << 20,
+        )(block, neigh_two, self_two, first)
     with jax.named_scope("hidden"):
         hidden = call(hidden_kernel, shape(GROUP, 2 * hid, targets), 3, nbytes=1 << 20)(
             parts, bias_one.reshape(hid, 1), pieces
@@ -374,10 +393,10 @@
         grad_neigh, grad_self = call(
             place_kernel,
             (shape(hid, full, dtype=F32), shape(hid, full, dtype=F32)),
-            2,
-            smem=(0,),
+            3,
+            smem=(0, 1),
             nbytes=1 << 20,
-        )(mine, spread)
+        )(mine, block, spread)
     return (second_out, grad_neigh, grad_self)
 
 

time: 164 us -> 159 us (0.970)
  starting transfers between devices: 58.7 us -> 54.9 us
    all_to_all x6, starting transfers between devices: 49.4 us -> 45.3 us  [swap(): lax.all_to_all(x, axis, split_axis=0, concat_axis=0, tiled=True, axis_ind...]
    all_to_all x1, blocking collectives: 16.8 us -> 14.5 us  [swap(): lax.all_to_all(x, axis, split_axis=0, concat_axis=0, tiled=True, axis_ind...]
  transfers between devices with their start and end apart: 9 -> 9, of which waited for: 6 -> 7; matrix products, arithmetic and copies ran while one was open for 0% -> 0% of each run, Pallas kernels for 1% -> 1%
where the time goes in v11:
time: 159 us; the launch traced here: 158 us
  starting transfers between devices  54.9 us (35%)
  waiting for transfers between devices  46.8 us (29%)
  blocking collectives  38.9 us (24%)
  Pallas kernels  12.3 us (8%)
  local copies, waits for them, and re-layouts  3.91 us (2%)
    all_to_all x6, starting transfers between devices, swap(): lax.all_to_all(x, axis, split_axis=0, concat_axis=0, tiled=True, axis_ind...  45.3 us
    all_to_all x6, waiting for transfers between devices, swap(): lax.all_to_all(x, axis, split_axis=0, concat_axis=0, tiled=True, axis_ind...  42.4 us
    all_gather x1, blocking collectives, body(): cot = lax.all_gather(cot, 'feat', axis=0, tiled=True, axis_index_groups=far)  24.4 us
    all_to_all x1, blocking collectives, swap(): lax.all_to_all(x, axis, split_axis=0, concat_axis=0, tiled=True, axis_ind...  14.5 us
    ppermute x3, starting transfers between devices, trade(): return lax.ppermute(x, 'feat', [(i, i ^ k) for i in range(n_feat)])  9.55 us
    ppermute x3, waiting for transfers between devices, trade(): return lax.ppermute(x, 'feat', [(i, i ^ k) for i in range(n_feat)])  4.37 us
    unnamed x27, local copies, waits for them, and re-layouts  3.72 us
    pallas_call x1, Pallas kernels, body(): call(functools.partial(pack_kernel, groups, targets), shape(groups, ROWS,...  3.34 us
  transfers between devices with their start and end apart: 9, of which 7 were waited for; matrix products, arithmetic and copies ran while one was open for 0% of the time, Pallas kernels for 1%

profile of v11, /device:TPU:1, one launch (start us, length us, event | category | flops | bytes accessed | tf_op | source)
XLA Modules:
  0.0 157.7 jit_solution(16327039729188281486)
XLA Ops:
  0.6 0.9 copy-done.7
  2.3 3.3 %edges.1.late_ref = bf16[32,64,128]{2,1,0:T(8,128)(2,1)} custom-call(bf16[48,2048]{1,0:T(8,128)(2,1)S(1)} %bitcast.22, s32[16,128]{1,0:T(8,128)S(1)} %bitcast.23), custom_call_target="tpu_custom_call" | custom-call | flops 1073741824 | bytes 8388608 | tf_op jit(solution)/shard_map/edges/pallas_call | solution.py:303
  5.6 10.6 %all-to-all-start = ((bf16[32,64,128]{2,1,0:T(8,128)(2,1)}), bf16[32,64,128]{2,1,0:T(8,128)(2,1)S(1)}, u32[]{:S(2)}, u32[]{:S(2)}) async-start(bf16[32,64,128]{2,1,0:T(8,128)(2,1)} %edges.1.late_ref), calls=%async_computation | async-start | bytes 1048576 | tf_op jit(solution)/shard_map/edges/all_to_all | solution.py:292
  16.4 24.4 %all_gather.3.late_ref.cot_ref = bf16[256,512]{1,0:T(8,128)(2,1)S(1)} all-gather(bf16[64,512]{1,0:T(8,128)(2,1)S(1)} %get-tuple-element.10), channel_id=1, replica_groups={{0,5,10,15},{1,6,11,12},{2,7,8,13},{3,4,9,14},{16,21,26,31},{17,22,27,2..., dimensions={0}, use_global_device_ids=true | all-gather | bytes 327680 | tf_op jit(solution)/shard_map/pieces/all_gather | solution.py:321
  40.8 1.4 mean.1
  42.2 14.5 %all_to_all.35.got_ref = bf16[4,144,512]{2,1,0:T(8,128)(2,1)S(1)} all-to-all(bf16[4,144,512]{2,1,0:T(8,128)(2,1)S(1)} %mean.1), channel_id=1, replica_groups={{0,1,2,3},{4,5,6,7},{8,9,10,11},{12,13,14,15},{16,17,18,19},{20,21,22,2..., dimensions={0} | all-to-all | bytes 1179648 | tf_op jit(solution)/shard_map/mean/all_to_all | solution.py:292
  56.7 1.0 first.1.late_ref
  57.8 5.7 %all-to-all-start.2 = ((bf16[4,64,512]{2,1,0:T(8,128)(2,1)}), bf16[4,64,512]{2,1,0:T(8,128)(2,1)S(1)}, u32[]{:S(2)}, u32[]{:S(2)}) async-start(bf16[4,64,512]{2,1,0:T(8,128)(2,1)} %first.1.late_ref), calls=%async_computation.2 | async-start | bytes 524288 | tf_op jit(solution)/shard_map/first/all_to_all | solution.py:292
  64.4 11.0 %all-to-all-done.2.parts_ref = bf16[4,64,512]{2,1,0:T(8,128)(2,1)S(1)} async-done(((bf16[4,64,512]{2,1,0:T(8,128)(2,1)}), bf16[4,64,512]{2,1,0:T(8,128)(2,1)S(1)}, u32[]{:S(2)}, u32[]{:S(2)}) %all-to-all-start.2) | async-done | bytes 262176 | tf_op jit(solution)/shard_map/first/all_to_all | solution.py:292
  76.3 8.6 %all-to-all-start.3 = ((bf16[4,128,512]{2,1,0:T(8,128)(2,1)}), bf16[4,128,512]{2,1,0:T(8,128)(2,1)S(1)}, u32[]{:S(2)}, u32[]{:S(2)}) async-start(bf16[4,128,512]{2,1,0:T(8,128)(2,1)} %hidden.1), calls=%async_computation.3 | async-start | bytes 1048576 | tf_op jit(solution)/shard_map/hidden/all_to_all | solution.py:292
  85.7 10.4 %all-to-all-done.3.got_ref = bf16[4,128,512]{2,1,0:T(8,128)(2,1)S(1)} async-done(((bf16[4,128,512]{2,1,0:T(8,128)(2,1)}), bf16[4,128,512]{2,1,0:T(8,128)(2,1)S(1)}, u32[]{:S(2)}, u32[]{:S(2)}) %all-to-all-start.3) | async-done | bytes 524320 | tf_op jit(solution)/shard_map/hidden/all_to_all | solution.py:292
  96.1 1.9 %grads.2 = (bf16[256,512]{1,0:T(8,128)(2,1)S(1)}, bf16[32,32,128]{2,1,0:T(8,128)(2,1)}) custom-call(s32[4,2]{1,0:T(4,128)S(1)} %copy.17.index_ref, bf16[4,128,512]{2,1,0:T(8,128)(2,1)S(1)} %all-to-all-done.3.got_ref, bf16[4,128,128]{2,1,0:T(8,128)(2,1)S(1)} %copy-done, f32[1,512]{1,0:T(1,128)S(1)} %bitcast.20, bf16[256,512]{1,0:T(8,128)(2,1)S(1)} %all_gather.3.late_ref.cot_ref), custom_call_target="tpu_custom_call" | custom-call | flops 134217728 | bytes 4194304 | tf_op jit(solution)/shard_map/grads/pallas_call | solution.py:357
  97.9 12.3 %all-to-all-start.5 = ((bf16[32,32,128]{2,1,0:T(8,128)(2,1)}), bf16[32,32,128]{2,1,0:T(8,128)(2,1)S(1)}, u32[]{:S(2)}, u32[]{:S(2)}) async-start(bf16[32,32,128]{2,1,0:T(8,128)(2,1)} %get-tuple-element.12), calls=%async_computation.5 | async-start | bytes 524288 | tf_op jit(solution)/shard_map/grads/all_to_all | solution.py:292
  110.2 1.0 second.2
  111.2 7.9 %all-to-all-done.5.terms_ref = bf16[32,32,128]{2,1,0:T(8,128)(2,1)S(1)} async-done(((bf16[32,32,128]{2,1,0:T(8,128)(2,1)}), bf16[32,32,128]{2,1,0:T(8,128)(2,1)S(1)}, u32[]{:S(2)}, u32[]{:S(2)}) %all-to-all-start.5) | async-done | bytes 262176 | tf_op jit(solution)/shard_map/grads/all_to_all | solution.py:292
  119.1 3.4 %all-to-all-start.4 = ((bf16[4,64,512]{2,1,0:T(8,128)(2,1)}), bf16[4,64,512]{2,1,0:T(8,128)(2,1)S(1)}, u32[]{:S(2)}, u32[]{:S(2)}) async-start(bf16[4,64,512]{2,1,0:T(8,128)(2,1)} %second.2), calls=%async_computation.4 | async-start | bytes 524288 | tf_op jit(solution)/shard_map/second/all_to_all | solution.py:292
  122.6 3.6 %collective-permute-start = (f32[8,128]{1,0:T(8,128)S(1)}, f32[8,128]{1,0:T(8,128)S(1)}, u32[]{:S(2)}, u32[]{:S(2)}) collective-permute-start(f32[8,128]{1,0:T(8,128)S(1)} %get-tuple-element.17), channel_id=1, source_target_pairs={{0,1},{1,0},{2,3},{3,2},{4,5},{5,4},{6,7},{7,6},{8,9},{9,8},{10,11... | collective-permute-start | bytes 12296 | tf_op jit(solution)/shard_map/grads/ppermute | solution.py:297
  126.3 2.4 %collective-permute-start.1 = (f32[8,128]{1,0:T(8,128)S(1)}, f32[8,128]{1,0:T(8,128)S(1)}, u32[]{:S(2)}, u32[]{:S(2)}) collective-permute-start(f32[8,128]{1,0:T(8,128)S(1)} %get-tuple-element.16), channel_id=1, source_target_pairs={{0,2},{1,3},{2,0},{3,1},{4,6},{5,7},{6,4},{7,5},{8,10},{9,11},{10,... | collective-permute-start | bytes 12296 | tf_op jit(solution)/shard_map/grads/ppermute | solution.py:297
  128.7 3.5 %collective-permute-start.2 = (f32[8,128]{1,0:T(8,128)S(1)}, f32[8,128]{1,0:T(8,128)S(1)}, u32[]{:S(2)}, u32[]{:S(2)}) collective-permute-start(f32[8,128]{1,0:T(8,128)S(1)} %get-tuple-element.15), channel_id=1, source_target_pairs={{0,3},{1,2},{2,1},{3,0},{4,7},{5,6},{6,5},{7,4},{8,11},{9,10},{10,... | collective-permute-start | bytes 12296 | tf_op jit(solution)/shard_map/grads/ppermute | solution.py:297
  132.2 1.4 collective-permute-done.p1_ref
  133.6 3.0 %collective-permute-done.2.p3_ref = f32[8,128]{1,0:T(8,128)S(1)} collective-permute-done((f32[8,128]{1,0:T(8,128)S(1)}, f32[8,128]{1,0:T(8,128)S(1)}, u32[]{:S(2)}, u32[]{:S(2)}) %collective-permute-start.2) | collective-permute-done | bytes 4128 | tf_op jit(solution)/shard_map/grads/ppermute | solution.py:297
  136.6 3.0 %all-to-all-done.4.parts_ref.late_ref = bf16[4,64,512]{2,1,0:T(8,128)(2,1)S(1)} async-done(((bf16[4,64,512]{2,1,0:T(8,128)(2,1)}), bf16[4,64,512]{2,1,0:T(8,128)(2,1)S(1)}, u32[]{:S(2)}, u32[]{:S(2)}) %all-to-all-start.4) | async-done | bytes 262176 | tf_op jit(solution)/shard_map/second/all_to_all | solution.py:292
  140.4 4.8 %all-to-all-start.6 = ((f32[32,32,128]{2,1,0:T(8,128)}), f32[32,32,128]{2,1,0:T(8,128)S(1)}, u32[]{:S(2)}, u32[]{:S(2)}) async-start(f32[32,32,128]{2,1,0:T(8,128)} %place.2), calls=%async_computation.6 | async-start | bytes 1048576 | tf_op jit(solution)/shard_map/place/all_to_all | solution.py:292
  146.7 10.2 %all-to-all-done.6.pieces_ref = f32[32,32,128]{2,1,0:T(8,128)S(1)} async-done(((f32[32,32,128]{2,1,0:T(8,128)}), f32[32,32,128]{2,1,0:T(8,128)S(1)}, u32[]{:S(2)}, u32[]{:S(2)}) %all-to-all-start.6) | async-done | bytes 524320 | tf_op jit(solution)/shard_map/place/all_to_all | solution.py:292
  (39 shorter events, 6.7 us)
Async XLA Ops:
  0.6 0.9 copy-start.7
  1.6 0.7 copy-start.8
  5.6 10.6 %copy-start.3 = (bf16[48,1024]{1,0:T(8,128)(2,1)S(1)}, bf16[48,1024]{1,0:T(8,128)(2,1)}, u32[]{:S(2)}) copy-start(bf16[48,1024]{1,0:T(8,128)(2,1)} %neigh_ref.2) | copy-start | bytes 294916
  5.6 10.6 %copy-start.4 = (bf16[48,1024]{1,0:T(8,128)(2,1)S(1)}, bf16[48,1024]{1,0:T(8,128)(2,1)}, u32[]{:S(2)}) copy-start(bf16[48,1024]{1,0:T(8,128)(2,1)} %own_ref.2) | copy-start | bytes 294916
  5.6 10.6 %copy-start.5 = (bf16[512,64]{0,1:T(8,128)(2,1)S(1)}, bf16[512,64]{0,1:T(8,128)(2,1)}, u32[]{:S(2)}) copy-start(bf16[512,64]{0,1:T(8,128)(2,1)} %param.25) | copy-start | bytes 196612
  5.6 10.6 %copy-start.6 = (bf16[512,48]{0,1:T(8,128)(2,1)S(1)}, bf16[512,48]{0,1:T(8,128)(2,1)}, u32[]{:S(2)}) copy-start(bf16[512,48]{0,1:T(8,128)(2,1)} %param.15) | copy-start | bytes 147460
  5.6 35.2 %all-to-all-start = ((bf16[32,64,128]{2,1,0:T(8,128)(2,1)}), bf16[32,64,128]{2,1,0:T(8,128)(2,1)S(1)}, u32[]{:S(2)}, u32[]{:S(2)}) async-start(bf16[32,64,128]{2,1,0:T(8,128)(2,1)} %edges.1.late_ref), calls=%async_computation | async-start | bytes 1048576 | tf_op jit(solution)/shard_map/edges/all_to_all | solution.py:292
  57.8 6.5 %copy-start.1 = (bf16[64,1024]{1,0:T(8,128)(2,1)S(1)}, bf16[64,1024]{1,0:T(8,128)(2,1)}, u32[]{:S(2)}) copy-start(bf16[64,1024]{1,0:T(8,128)(2,1)} %neigh_ref.3) | copy-start | bytes 393220
  57.8 6.5 %copy-start.2 = (bf16[64,1024]{1,0:T(8,128)(2,1)S(1)}, bf16[64,1024]{1,0:T(8,128)(2,1)}, u32[]{:S(2)}) copy-start(bf16[64,1024]{1,0:T(8,128)(2,1)} %own_ref.3) | copy-start | bytes 393220
  57.8 17.6 %all-to-all-start.2 = ((bf16[4,64,512]{2,1,0:T(8,128)(2,1)}), bf16[4,64,512]{2,1,0:T(8,128)(2,1)S(1)}, u32[]{:S(2)}, u32[]{:S(2)}) async-start(bf16[4,64,512]{2,1,0:T(8,128)(2,1)} %first.1.late_ref), calls=%async_computation.2 | async-start | bytes 524288 | tf_op jit(solution)/shard_map/first/all_to_all | solution.py:292
  63.5 0.7 copy-start.11
  76.3 8.6 %copy-start.9 = (s32[512]{0:T(512)S(1)}, s32[512]{0:T(512)}, u32[]{:S(2)}) copy-start(s32[512]{0:T(512)} %param.21) | copy-start | bytes 6148
  76.3 19.8 %copy-start = (bf16[4,128,128]{2,1,0:T(8,128)(2,1)S(1)}, bf16[4,128,128]{2,1,0:T(8,128)(2,1)}, u32[]{:S(2)}) copy-start(bf16[4,128,128]{2,1,0:T(8,128)(2,1)} %values_ref.1) | copy-start | bytes 393220
  76.3 19.8 %all-to-all-start.3 = ((bf16[4,128,512]{2,1,0:T(8,128)(2,1)}), bf16[4,128,512]{2,1,0:T(8,128)(2,1)S(1)}, u32[]{:S(2)}, u32[]{:S(2)}) async-start(bf16[4,128,512]{2,1,0:T(8,128)(2,1)} %hidden.1), calls=%async_computation.3 | async-start | bytes 1048576 | tf_op jit(solution)/shard_map/hidden/all_to_all | solution.py:292
  84.9 0.7 copy-start.10
  97.9 21.2 %all-to-all-start.5 = ((bf16[32,32,128]{2,1,0:T(8,128)(2,1)}), bf16[32,32,128]{2,1,0:T(8,128)(2,1)S(1)}, u32[]{:S(2)}, u32[]{:S(2)}) async-start(bf16[32,32,128]{2,1,0:T(8,128)(2,1)} %get-tuple-element.12), calls=%async_computation.5 | async-start | bytes 524288 | tf_op jit(solution)/shard_map/grads/all_to_all | solution.py:292
  119.1 20.4 %all-to-all-start.4 = ((bf16[4,64,512]{2,1,0:T(8,128)(2,1)}), bf16[4,64,512]{2,1,0:T(8,128)(2,1)S(1)}, u32[]{:S(2)}, u32[]{:S(2)}) async-start(bf16[4,64,512]{2,1,0:T(8,128)(2,1)} %second.2), calls=%async_computation.4 | async-start | bytes 524288 | tf_op jit(solution)/shard_map/second/all_to_all | solution.py:292
  122.6 11.0 %collective-permute-start = (f32[8,128]{1,0:T(8,128)S(1)}, f32[8,128]{1,0:T(8,128)S(1)}, u32[]{:S(2)}, u32[]{:S(2)}) collective-permute-start(f32[8,128]{1,0:T(8,128)S(1)} %get-tuple-element.17), channel_id=1, source_target_pairs={{0,1},{1,0},{2,3},{3,2},{4,5},{5,4},{6,7},{7,6},{8,9},{9,8},{10,11... | collective-permute-start | bytes 12296 | tf_op jit(solution)/shard_map/grads/ppermute | solution.py:297
  126.3 7.3 %collective-permute-start.1 = (f32[8,128]{1,0:T(8,128)S(1)}, f32[8,128]{1,0:T(8,128)S(1)}, u32[]{:S(2)}, u32[]{:S(2)}) collective-permute-start(f32[8,128]{1,0:T(8,128)S(1)} %get-tuple-element.16), channel_id=1, source_target_pairs={{0,2},{1,3},{2,0},{3,1},{4,6},{5,7},{6,4},{7,5},{8,10},{9,11},{10,... | collective-permute-start | bytes 12296 | tf_op jit(solution)/shard_map/grads/ppermute | solution.py:297
  128.7 7.9 %collective-permute-start.2 = (f32[8,128]{1,0:T(8,128)S(1)}, f32[8,128]{1,0:T(8,128)S(1)}, u32[]{:S(2)}, u32[]{:S(2)}) collective-permute-start(f32[8,128]{1,0:T(8,128)S(1)} %get-tuple-element.15), channel_id=1, source_target_pairs={{0,3},{1,2},{2,1},{3,0},{4,7},{5,6},{6,5},{7,4},{8,11},{9,10},{10,... | collective-permute-start | bytes 12296 | tf_op jit(solution)/shard_map/grads/ppermute | solution.py:297
  140.4 16.4 %all-to-all-start.6 = ((f32[32,32,128]{2,1,0:T(8,128)}), f32[32,32,128]{2,1,0:T(8,128)S(1)}, u32[]{:S(2)}, u32[]{:S(2)}) async-start(f32[32,32,128]{2,1,0:T(8,128)} %place.2), calls=%async_computation.6 | async-start | bytes 1048576 | tf_op jit(solution)/shard_map/place/all_to_all | solution.py:292
  145.2 0.7 copy-start.12

commit v12 on v11

--- a/solution.py
+++ b/solution.py
@@ -5,6 +5,7 @@
 from jax import lax
 from jax.experimental import pallas as pl
 from jax.experimental.pallas import tpu as pltpu
+from jax.sharding import Mesh
 from jax.sharding import PartitionSpec as P
 
 BF = jnp.bfloat16
@@ -13,6 +14,7 @@
 TN = (((0,), (0,)), ((), ()))
 ROWS = 64
 GROUP = 4
+FEAT = ("blk", "mem")
 VMEM_LIMIT = 48 * 1024 * 1024
 
 
@@ -84,9 +86,7 @@
     return sets
 
 
-def first_pieces_kernel(
-    block_ref, neigh_ref, own_ref, self_ref, cot_ref, late_ref, out_ref, cot_out_ref
-):
+def first_pieces_kernel(block_ref, neigh_ref, own_ref, self_ref, late_ref, out_ref):
     del late_ref
     rows = neigh_ref.shape[0]
     group, _, width = out_ref.shape
@@ -96,7 +96,6 @@
         out_ref[to, :rows, : width // 2] = neigh
         out_ref[to, :rows, width // 2 :] = own
         out_ref[to, rows:, :] = self_ref[...]
-    cot_out_ref[...] = cot_ref[...]
 
 
 def second_pieces_kernel(block_ref, neigh_ref, own_ref, late_ref, out_ref):
@@ -109,8 +108,7 @@
         out_ref[to, :, width // 2 :] = own
 
 
-def mean_kernel(cols, recv_ref, pieces_ref, late_ref, out_ref):
-    del late_ref
+def mean_kernel(cols, recv_ref, pieces_ref, out_ref):
     groups, rows, cap = recv_ref.shape
     targets = out_ref.shape[2]
     half = targets // 2
@@ -130,7 +128,7 @@
         out_ref[j, cols:, :] = pieces_ref[j]
 
 
-def first_kernel(got_ref, out_ref, weight, acts):
+def first_kernel(got_ref, cot_ref, out_ref, weight, acts):
     group, rows, targets = got_ref.shape
     rows = rows // 3
     width = targets // 2
@@ -141,16 +139,17 @@
         weight[mid:high, :] = got_ref[j, rows : 2 * rows, width:]
         acts[mid:high, :] = got_ref[j, 2 * rows :, :]
     total = lax.dot_general(weight[...], acts[...], TN, preferred_element_type=F32)
-    cols = out_ref.shape[1]
+    cols = cot_ref.shape[0]
     for z in range(out_ref.shape[0]):
-        out_ref[z] = total[z * cols : (z + 1) * cols, :].astype(BF)
+        out_ref[z, :cols, :] = total[z * cols : (z + 1) * cols, :].astype(BF)
+        out_ref[z, cols:, :] = cot_ref[...]
 
 
 def hidden_kernel(parts_ref, bias_ref, pieces_ref, out_ref):
     cols = bias_ref.shape[0]
-    total = parts_ref[0].astype(F32)
+    total = parts_ref[0, :cols, :].astype(F32)
     for k in range(1, parts_ref.shape[0]):
-        total = total + parts_ref[k].astype(F32)
+        total = total + parts_ref[k, :cols, :].astype(F32)
     hidden = jnp.maximum(total + bias_ref[...], 0.0).astype(BF)
     for c in range(out_ref.shape[0]):
         out_ref[c, :cols, :] = hidden
@@ -158,7 +157,7 @@
 
 
 def grad_kernel(
-    index_ref, got_ref, values_ref, live_ref, cot_ref, agg_ref, out_ref, left, source, acc
+    index_ref, got_ref, values_ref, live_ref, parts_ref, agg_ref, out_ref, left, source, acc
 ):
     group, cols, targets = got_ref.shape
     cols = cols // 2
@@ -181,11 +180,12 @@
         agg_ref[:, at] = tile
         left[:wide, at] = tile * live[:, at]
         left[wide:, at] = source[t] * live[:, at]
-    block = lax.dot_general(left[...], cot_ref[...], NT, preferred_element_type=F32)
+    right = jnp.concatenate([parts_ref[z, cols:, :] for z in range(parts_ref.shape[0])], axis=0)
+    block = lax.dot_general(left[...], right, NT, preferred_element_type=F32)
     at = 0
     for w in range(2):
         for r in range(0, cols, 8):
-            for c in range(0, cot_ref.shape[0], 128):
+            for c in range(0, right.shape[0], 128):
                 rows_of = [
                     block[w * wide + j * cols + r : w * wide + j * cols + r + 8, c : c + 128]
                     for j in range(group)
@@ -210,29 +210,18 @@
         out_ref[z] = total[z * cols : (z + 1) * cols, :].astype(BF)
 
 
-def sum_kernel(mine_ref, terms_ref, out_ref):
-    mine = mine_ref[0]
+def sum_kernel(terms_ref, out_ref):
     total = terms_ref[0].astype(F32)
     for d in range(1, terms_ref.shape[0]):
         total = total + terms_ref[d].astype(F32)
-    rows = out_ref.shape[1]
-    for j in range(out_ref.shape[0]):
-        out_ref[jnp.bitwise_xor(mine, j)] = total[j * rows : (j + 1) * rows, :]
-
-
-def copies_kernel(p0_ref, p1_ref, p2_ref, p3_ref, late_ref, out_ref):
-    del late_ref
-    whole = jnp.concatenate([p0_ref[...], p1_ref[...], p2_ref[...], p3_ref[...]], axis=0)
-    for d in range(out_ref.shape[0]):
-        out_ref[d] = whole
-
-
-def place_kernel(mine_ref, block_ref, pieces_ref, neigh_ref, self_ref):
+    out_ref[...] = total
+
+
+def place_kernel(block_ref, pieces_ref, neigh_ref, self_ref):
     half = 64
     starts = []
     for h in range(GROUP):
-        from_me = jnp.bitwise_xor(mine_ref[0], far_place(block_ref[0], h))
-        starts.append(pl.multiple_of(from_me * 8, 8))
+        starts.append(pl.multiple_of(far_place(block_ref[0], h) * 8, 8))
     at = 0
     for out_ref in (neigh_ref, self_ref):
         for r in range(0, out_ref.shape[0], 8):
@@ -273,28 +262,21 @@
     cotangent,
 ):
     groups = lax.axis_size("dp")
-    n_feat = lax.axis_size("feat")
+    blocks = lax.axis_size("blk")
     edges, cols = edge_feats.shape
     targets = self_feats.shape[0]
     hid = bias_one.shape[0]
     full = neigh_one.shape[1]
     cap = 2 * edges // groups
-    blocks = n_feat // GROUP
     wide = full // GROUP
-    near = [[GROUP * i + j for j in range(GROUP)] for i in range(blocks)]
     far = [[GROUP * i + far_place(i, h) for i in range(blocks)] for h in range(GROUP)]
-    z = lax.axis_index("feat")
-    mine = (z % GROUP).reshape(1)
-    block = (z // GROUP).reshape(1)
+    block = lax.axis_index("blk").reshape(1)
     live = seed_live.reshape(1, targets).astype(F32)
 
     def swap(x, axis, among=None):
         return lax.all_to_all(
             x, axis, split_axis=0, concat_axis=0, tiled=True, axis_index_groups=among
         )
-
-    def trade(x, k):
-        return lax.ppermute(x, "feat", [(i, i ^ k) for i in range(n_feat)])
 
     def shape(*dims, dtype=BF):
         return jax.ShapeDtypeStruct(dims, dtype)
@@ -310,35 +292,33 @@
         )(edge_feats.T, edge_dst.reshape(-1, 128))
         recv = swap(send, "dp")
     with jax.named_scope("pieces"):
-        pieces, cot = call(
+        pieces = call(
             first_pieces_kernel,
-            (shape(GROUP, 2 * cols, targets), shape(hid, targets)),
-            6,
+            shape(GROUP, 2 * cols, targets),
+            5,
             smem=(0,),
-            late=(5,),
+            late=(4,),
             nbytes=2 << 20,
-        )(block, neigh_one, self_one, self_feats.T, cotangent.T, send)
-        cot = lax.all_gather(cot, "feat", axis=0, tiled=True, axis_index_groups=far)
+        )(block, neigh_one, self_one, self_feats.T, send)
     with jax.named_scope("mean"):
         acts = call(
             functools.partial(mean_kernel, cols),
             shape(GROUP, 3 * cols, targets),
-            3,
-            late=(2,),
+            2,
             flops=2 * groups * ROWS * cap * targets,
             nbytes=8 << 20,
-        )(recv, pieces, cot)
-        acts = swap(acts, "feat", near)
+        )(recv, pieces)
+        acts = swap(acts, "mem")
     with jax.named_scope("first"):
         first = call(
             first_kernel,
-            shape(blocks, hid, targets),
-            1,
+            shape(blocks, 2 * hid, targets),
+            2,
             scratch=[pltpu.VMEM((8 * cols, wide), BF), pltpu.VMEM((8 * cols, targets), BF)],
             flops=2 * 8 * cols * wide * targets,
             nbytes=2 << 20,
-        )(acts)
-        parts = swap(first, "feat", far)
+        )(acts, cotangent.T)
+        parts = swap(first, FEAT, far)
     with jax.named_scope("pieces"):
         pieces = call(
             second_pieces_kernel,
@@ -352,7 +332,7 @@
         hidden = call(hidden_kernel, shape(GROUP, 2 * hid, targets), 3, nbytes=1 << 20)(
             parts, bias_one.reshape(hid, 1), pieces
         )
-        hidden = swap(hidden, "feat", near)
+        hidden = swap(hidden, "mem")
     with jax.named_scope("grads"):
         agg, terms = call(
             grad_kernel,
@@ -366,12 +346,11 @@
             smem=(0,),
             flops=2 * 2 * wide * targets * wide,
             nbytes=4 << 20,
-        )(tile_index, hidden, tile_values, live, cot)
-        terms = swap(terms, "dp")
-        mine_sum = call(
-            sum_kernel, shape(GROUP, 8, 128, dtype=F32), 2, smem=(0,), nbytes=1 << 20
-        )(mine, terms)
-        sums = [mine_sum[0]] + [trade(mine_sum[k], k) for k in range(1, GROUP)]
+        )(tile_index, hidden, tile_values, live, parts)
+        terms = swap(terms.reshape(GROUP * groups, 8, 128), ("dp", "mem"))
+        mine = call(sum_kernel, shape(GROUP * 8, 128, dtype=F32), 1, nbytes=1 << 20)(
+            terms.reshape(groups, GROUP * 8, 128)
+        )
     with jax.named_scope("second"):
         second = call(
             second_kernel,
@@ -381,40 +360,40 @@
             flops=2 * 2 * wide * wide * targets,
             nbytes=2 << 20,
         )(agg, hidden)
-        second = swap(second, "feat", far)
+        second = swap(second, FEAT, far)
         second_out = call(out_kernel, shape(hid, targets), 3, nbytes=1 << 20)(
             second, bias_two.reshape(hid, 1), live
         ).T
     with jax.named_scope("place"):
-        spread = call(
-            copies_kernel, shape(groups, GROUP * 8, 128, dtype=F32), 5, late=(4,), nbytes=1 << 20
-        )(*sums, second)
-        spread = swap(spread, "dp")
+        spread = lax.all_gather(mine, "dp", axis=0)
         grad_neigh, grad_self = call(
             place_kernel,
             (shape(hid, full, dtype=F32), shape(hid, full, dtype=F32)),
-            3,
-            smem=(0, 1),
+            2,
+            smem=(0,),
             nbytes=1 << 20,
-        )(mine, block, spread)
+        )(block, spread)
     return (second_out, grad_neigh, grad_self)
 
 
 def solution(mesh):
+    shards = mesh.devices.shape
+    blocks = mesh.devices.reshape(shards[0], shards[1] // GROUP, GROUP)
+    mesh = Mesh(blocks, ("dp",) + FEAT)
     in_specs = (
-        P("dp", "feat"),
+        P("dp", FEAT),
         P("dp"),
-        P("dp", "feat"),
-        P("feat", None),
-        P("feat", None),
-        P("feat"),
+        P("dp", FEAT),
+        P(FEAT, None),
+        P(FEAT, None),
+        P(FEAT),
         P("dp", None),
         P("dp", None, None),
         P("dp"),
-        P("feat", None),
-        P("feat", None),
-        P("feat"),
-        P("dp", "feat"),
+        P(FEAT, None),
+        P(FEAT, None),
+        P(FEAT),
+        P("dp", FEAT),
     )
-    out_specs = (P("dp", "feat"), P("feat", None), P("feat", None))
+    out_specs = (P("dp", FEAT), P(FEAT, None), P(FEAT, None))
     return jax.shard_map(body, mesh=mesh, in_specs=in_specs, out_specs=out_specs, check_vma=False)

time: 159 us -> 179 us (1.13)
  blocking collectives: 38.9 us -> 56.5 us
  waiting for transfers between devices: 46.8 us -> 61.9 us
  starting transfers between devices: 54.9 us -> 44.1 us
    all_to_all x6 -> x4, waiting for transfers between devices: 42.4 us -> 61.9 us  [swap(): lax.all_to_all(x, axis, split_axis=0, concat_axis=0, tiled=True, axis_ind...]
    all_to_all x1 -> x2, blocking collectives: 14.5 us -> 33.3 us  [swap(): lax.all_to_all(x, axis, split_axis=0, concat_axis=0, tiled=True, axis_ind...]
    ppermute x3 -> x0, starting transfers between devices: 9.55 us -> none  [trade(): return lax.ppermute(x, 'feat', [(i, i ^ k) for i in range(n_feat)])]
    ppermute x3 -> x0, waiting for transfers between devices: 4.37 us -> none  [trade(): return lax.ppermute(x, 'feat', [(i, i ^ k) for i in range(n_feat)])]
    all_to_all x6 -> x4, starting transfers between devices: 45.3 us -> 44.1 us  [swap(): lax.all_to_all(x, axis, split_axis=0, concat_axis=0, tiled=True, axis_ind...]
  transfers between devices with their start and end apart: 9 -> 4, of which waited for: 7 -> 4; matrix products, arithmetic and copies ran while one was open for 0% -> 0% of each run, Pallas kernels for 1% -> 1%
where the time goes in v12:
time: 179 us; the launch traced here: 178 us
  waiting for transfers between devices  61.9 us (35%)
  blocking collectives  56.5 us (32%)
  starting transfers between devices  44.1 us (25%)
  Pallas kernels  10.9 us (6%)
  local copies, waits for them, and re-layouts  3.91 us (2%)
    all_to_all x4, waiting for transfers between devices, swap(): lax.all_to_all(x, axis, split_axis=0, concat_axis=0, tiled=True, axis_ind...  61.9 us
    all_to_all x4, starting transfers between devices, swap(): lax.all_to_all(x, axis, split_axis=0, concat_axis=0, tiled=True, axis_ind...  44.1 us
    all_to_all x2, blocking collectives, swap(): lax.all_to_all(x, axis, split_axis=0, concat_axis=0, tiled=True, axis_ind...  33.3 us
    all_gather x1, blocking collectives, body(): spread = lax.all_gather(mine, 'dp', axis=0)  23.2 us
    unnamed x27, local copies, waits for them, and re-layouts  3.72 us
  transfers between devices with their start and end apart: 4, of which 4 were waited for; matrix products, arithmetic and copies ran while one was open for 0% of the time, Pallas kernels for 1%

profile of v12, /device:TPU:1, one launch (start us, length us, event | category | flops | bytes accessed | tf_op | source)
XLA Modules:
  0.0 178.0 jit_solution(18436615458084296562)
XLA Ops:
  0.6 0.9 copy-done.7
  1.6 0.7 copy-done.8
  2.3 3.3 %edges.1.late_ref = bf16[32,64,128]{2,1,0:T(8,128)(2,1)} custom-call(bf16[48,2048]{1,0:T(8,128)(2,1)S(1)} %bitcast.18, s32[16,128]{1,0:T(8,128)S(1)} %bitcast.19), custom_call_target="tpu_custom_call" | custom-call | flops 1073741824 | bytes 8388608 | tf_op jit(solution)/shard_map/edges/pallas_call | solution.py:285
  5.6 10.6 %all-to-all-start = ((bf16[32,64,128]{2,1,0:T(8,128)(2,1)}), bf16[32,64,128]{2,1,0:T(8,128)(2,1)S(1)}, u32[]{:S(2)}, u32[]{:S(2)}) async-start(bf16[32,64,128]{2,1,0:T(8,128)(2,1)} %edges.1.late_ref), calls=%async_computation | async-start | bytes 1048576 | tf_op jit(solution)/shard_map/edges/all_to_all | solution.py:277
  16.3 11.5 %all-to-all-done.recv_ref = bf16[32,64,128]{2,1,0:T(8,128)(2,1)S(1)} async-done(((bf16[32,64,128]{2,1,0:T(8,128)(2,1)}), bf16[32,64,128]{2,1,0:T(8,128)(2,1)S(1)}, u32[]{:S(2)}, u32[]{:S(2)}) %all-to-all-start) | async-done | bytes 524320 | tf_op jit(solution)/shard_map/edges/all_to_all | solution.py:277
  27.8 1.4 mean.1
  29.2 19.0 %all_to_all.30.got_ref = bf16[4,144,512]{2,1,0:T(8,128)(2,1)S(1)} all-to-all(bf16[4,144,512]{2,1,0:T(8,128)(2,1)S(1)} %mean.1), channel_id=1, replica_groups=mesh['dp'=32,'blk'=4,'mem'=4] {'mem'}, dimensions={0} | all-to-all | bytes 1179648 | tf_op jit(solution)/shard_map/mean/all_to_all | solution.py:277
  48.2 1.1 first.1.late_ref
  49.4 10.6 %all-to-all-start.2 = ((bf16[4,128,512]{2,1,0:T(8,128)(2,1)}), bf16[4,128,512]{2,1,0:T(8,128)(2,1)S(1)}, u32[]{:S(2)}, u32[]{:S(2)}) async-start(bf16[4,128,512]{2,1,0:T(8,128)(2,1)} %first.1.late_ref), calls=%async_computation.2 | async-start | bytes 1048576 | tf_op jit(solution)/shard_map/first/all_to_all | solution.py:277
  60.0 0.7 copy-done.11
  60.9 25.2 %all-to-all-done.2.parts_ref = bf16[4,128,512]{2,1,0:T(8,128)(2,1)S(1)} async-done(((bf16[4,128,512]{2,1,0:T(8,128)(2,1)}), bf16[4,128,512]{2,1,0:T(8,128)(2,1)S(1)}, u32[]{:S(2)}, u32[]{:S(2)}) %all-to-all-start.2) | async-done | bytes 524320 | tf_op jit(solution)/shard_map/first/all_to_all | solution.py:277
  86.1 0.9 hidden.1
  87.0 7.1 %all-to-all-start.3 = ((bf16[4,128,512]{2,1,0:T(8,128)(2,1)}), bf16[4,128,512]{2,1,0:T(8,128)(2,1)S(1)}, u32[]{:S(2)}, u32[]{:S(2)}) async-start(bf16[4,128,512]{2,1,0:T(8,128)(2,1)} %hidden.1), calls=%async_computation.3 | async-start | bytes 1048576 | tf_op jit(solution)/shard_map/hidden/all_to_all | solution.py:277
  94.1 0.7 copy-done.10
  94.9 13.2 %all-to-all-done.3.got_ref = bf16[4,128,512]{2,1,0:T(8,128)(2,1)S(1)} async-done(((bf16[4,128,512]{2,1,0:T(8,128)(2,1)}), bf16[4,128,512]{2,1,0:T(8,128)(2,1)S(1)}, u32[]{:S(2)}, u32[]{:S(2)}) %all-to-all-start.3) | async-done | bytes 524320 | tf_op jit(solution)/shard_map/hidden/all_to_all | solution.py:277
  108.1 1.9 %grads.2 = (bf16[256,512]{1,0:T(8,128)(2,1)S(1)}, bf16[32,32,128]{2,1,0:T(8,128)(2,1)}) custom-call(s32[4,2]{1,0:T(4,128)S(1)} %copy.17.index_ref, bf16[4,128,512]{2,1,0:T(8,128)(2,1)S(1)} %all-to-all-done.3.got_ref, bf16[4,128,128]{2,1,0:T(8,128)(2,1)S(1)} %copy-done, f32[1,512]{1,0:T(1,128)S(1)} %bitcast.16, bf16[4,128,512]{2,1,0:T(8,128)(2,1)S(1)} %all-to-all-done.2.parts_ref), custom_call_target="tpu_custom_call" | custom-call | flops 134217728 | bytes 4194304 | tf_op jit(solution)/shard_map/grads/pallas_call | solution.py:337
  110.0 0.3 second.2
  110.3 14.3 %all_to_all.31.parts_ref = bf16[4,64,512]{2,1,0:T(8,128)(2,1)S(1)} all-to-all(bf16[4,64,512]{2,1,0:T(8,128)(2,1)S(1)} %second.2), channel_id=1, replica_groups={{0,5,10,15},{1,6,11,12},{2,7,8,13},{3,4,9,14},{16,21,26,31},{17,22,27,2..., dimensions={0} | all-to-all | bytes 524288 | tf_op jit(solution)/shard_map/second/all_to_all | solution.py:277
  124.6 15.8 %all-to-all-start.5 = ((bf16[128,8,128]{2,1,0:T(8,128)(2,1)}), bf16[128,8,128]{2,1,0:T(8,128)(2,1)S(1)}, u32[]{:S(2)}, u32[]{:S(2)}) async-start(bf16[128,8,128]{2,1,0:T(8,128)(2,1)} %bitcast.9), calls=%async_computation.5 | async-start | bytes 524288 | tf_op jit(solution)/shard_map/grads/all_to_all | solution.py:277
  140.5 0.6 copy-done.12
  141.2 0.7 second.3
  141.9 11.9 %all-to-all-done.5 = bf16[128,8,128]{2,1,0:T(8,128)(2,1)S(1)} async-done(((bf16[128,8,128]{2,1,0:T(8,128)(2,1)}), bf16[128,8,128]{2,1,0:T(8,128)(2,1)S(1)}, u32[]{:S(2)}, u32[]{:S(2)}) %all-to-all-start.5) | async-done | bytes 262176 | tf_op jit(solution)/shard_map/grads/all_to_all | solution.py:277
  153.9 23.2 %all-gather = f32[1024,128]{1,0:T(8,128)S(1)} all-gather(f32[32,128]{1,0:T(8,128)S(1)} %grads.3), channel_id=2, replica_groups=mesh['dp'=32,'blk'=4,'mem'=4] {'dp'}, dimensions={0}, use_global_device_ids=true | all-gather | bytes 540672 | tf_op jit(solution)/shard_map/place/all_gather | solution.py:368
  177.1 0.9 place.1
  (28 shorter events, 0.6 us)
Async XLA Ops:
  0.6 0.9 copy-start.7
  1.6 0.7 copy-start.8
  5.6 10.6 %copy-start.3 = (bf16[48,1024]{1,0:T(8,128)(2,1)S(1)}, bf16[48,1024]{1,0:T(8,128)(2,1)}, u32[]{:S(2)}) copy-start(bf16[48,1024]{1,0:T(8,128)(2,1)} %neigh_ref.2) | copy-start | bytes 294916
  5.6 10.6 %copy-start.4 = (bf16[48,1024]{1,0:T(8,128)(2,1)S(1)}, bf16[48,1024]{1,0:T(8,128)(2,1)}, u32[]{:S(2)}) copy-start(bf16[48,1024]{1,0:T(8,128)(2,1)} %own_ref.2) | copy-start | bytes 294916
  5.6 10.6 %copy-start.6 = (bf16[512,48]{0,1:T(8,128)(2,1)S(1)}, bf16[512,48]{0,1:T(8,128)(2,1)}, u32[]{:S(2)}) copy-start(bf16[512,48]{0,1:T(8,128)(2,1)} %param.15) | copy-start | bytes 147460
  5.6 22.2 %all-to-all-start = ((bf16[32,64,128]{2,1,0:T(8,128)(2,1)}), bf16[32,64,128]{2,1,0:T(8,128)(2,1)S(1)}, u32[]{:S(2)}, u32[]{:S(2)}) async-start(bf16[32,64,128]{2,1,0:T(8,128)(2,1)} %edges.1.late_ref), calls=%async_computation | async-start | bytes 1048576 | tf_op jit(solution)/shard_map/edges/all_to_all | solution.py:277
  29.2 19.0 %copy-start.5 = (bf16[512,64]{0,1:T(8,128)(2,1)S(1)}, bf16[512,64]{0,1:T(8,128)(2,1)}, u32[]{:S(2)}) copy-start(bf16[512,64]{0,1:T(8,128)(2,1)} %param.25) | copy-start | bytes 196612
  49.4 11.4 %copy-start.1 = (bf16[64,1024]{1,0:T(8,128)(2,1)S(1)}, bf16[64,1024]{1,0:T(8,128)(2,1)}, u32[]{:S(2)}) copy-start(bf16[64,1024]{1,0:T(8,128)(2,1)} %neigh_ref.3) | copy-start | bytes 393220
  49.4 11.4 %copy-start.2 = (bf16[64,1024]{1,0:T(8,128)(2,1)S(1)}, bf16[64,1024]{1,0:T(8,128)(2,1)}, u32[]{:S(2)}) copy-start(bf16[64,1024]{1,0:T(8,128)(2,1)} %own_ref.3) | copy-start | bytes 393220
  49.4 36.7 %all-to-all-start.2 = ((bf16[4,128,512]{2,1,0:T(8,128)(2,1)}), bf16[4,128,512]{2,1,0:T(8,128)(2,1)S(1)}, u32[]{:S(2)}, u32[]{:S(2)}) async-start(bf16[4,128,512]{2,1,0:T(8,128)(2,1)} %first.1.late_ref), calls=%async_computation.2 | async-start | bytes 1048576 | tf_op jit(solution)/shard_map/first/all_to_all | solution.py:277
  60.0 0.7 copy-start.11
  87.0 7.1 %copy-start.9 = (s32[512]{0:T(512)S(1)}, s32[512]{0:T(512)}, u32[]{:S(2)}) copy-start(s32[512]{0:T(512)} %param.21) | copy-start | bytes 6148
  87.0 21.1 %copy-start = (bf16[4,128,128]{2,1,0:T(8,128)(2,1)S(1)}, bf16[4,128,128]{2,1,0:T(8,128)(2,1)}, u32[]{:S(2)}) copy-start(bf16[4,128,128]{2,1,0:T(8,128)(2,1)} %values_ref.1) | copy-start | bytes 393220
  87.0 21.1 %all-to-all-start.3 = ((bf16[4,128,512]{2,1,0:T(8,128)(2,1)}), bf16[4,128,512]{2,1,0:T(8,128)(2,1)S(1)}, u32[]{:S(2)}, u32[]{:S(2)}) async-start(bf16[4,128,512]{2,1,0:T(8,128)(2,1)} %hidden.1), calls=%async_computation.3 | async-start | bytes 1048576 | tf_op jit(solution)/shard_map/hidden/all_to_all | solution.py:277
  94.1 0.7 copy-start.10
  124.6 29.2 %all-to-all-start.5 = ((bf16[128,8,128]{2,1,0:T(8,128)(2,1)}), bf16[128,8,128]{2,1,0:T(8,128)(2,1)S(1)}, u32[]{:S(2)}, u32[]{:S(2)}) async-start(bf16[128,8,128]{2,1,0:T(8,128)(2,1)} %bitcast.9), calls=%async_computation.5 | async-start | bytes 524288 | tf_op jit(solution)/shard_map/grads/all_to_all | solution.py:277
  140.5 0.7 copy-start.12

commit v13 on v6

--- a/solution.py
+++ b/solution.py
@@ -70,37 +70,41 @@
             send_ref[g * some + j] = out[j * ROWS : (j + 1) * ROWS, :]
 
 
+def far_place(block, column):
+    return (block + column) % GROUP
+
+
 def column_sets(weight, group):
     half = 64
     n = weight.shape[1] // half
     sets = []
-    for j in range(group):
-        blocks = [weight[:, b * half : (b + 1) * half] for b in range(j, n, group)]
-        sets.append(jnp.concatenate(blocks, axis=1))
+    for h in range(group):
+        at = [group * i + far_place(i, h) for i in range(n // group)]
+        sets.append(jnp.concatenate([weight[:, b * half : (b + 1) * half] for b in at], axis=1))
     return sets
 
 
-def first_pieces_kernel(mine_ref, neigh_ref, own_ref, self_ref, late_ref, out_ref):
+def first_pieces_kernel(mine_ref, block_ref, neigh_ref, own_ref, self_ref, late_ref, out_ref):
     del late_ref
     mine = mine_ref[0]
     rows = neigh_ref.shape[0]
     group, _, width = out_ref.shape
     both = zip(column_sets(neigh_ref[...], group), column_sets(own_ref[...], group))
-    for j, (neigh, own) in enumerate(both):
-        to = jnp.bitwise_xor(mine, j)
+    for h, (neigh, own) in enumerate(both):
+        to = jnp.bitwise_xor(mine, far_place(block_ref[0], h))
         out_ref[to, :rows, :] = neigh
         out_ref[to, rows : 2 * rows, :] = own
         out_ref[to, 2 * rows : 3 * rows, :] = self_ref[:, :width]
         out_ref[to, 3 * rows :, :] = self_ref[:, width:]
 
 
-def second_pieces_kernel(mine_ref, neigh_ref, own_ref, late_ref, out_ref):
+def second_pieces_kernel(mine_ref, block_ref, neigh_ref, own_ref, late_ref, out_ref):
     del late_ref
     mine = mine_ref[0]
     rows = neigh_ref.shape[0]
     both = zip(column_sets(neigh_ref[...], out_ref.shape[0]), column_sets(own_ref[...], out_ref.shape[0]))
-    for j, (neigh, own) in enumerate(both):
-        to = jnp.bitwise_xor(mine, j)
+    for h, (neigh, own) in enumerate(both):
+        to = jnp.bitwise_xor(mine, far_place(block_ref[0], h))
         out_ref[to, :rows, :] = neigh
         out_ref[to, rows:, :] = own
 
@@ -173,7 +177,8 @@
     left_ref[cols:, :] = hidden * live
 
 
-def grad_kernel(left_ref, cot_ref, out_ref):
+def grad_kernel(left_ref, cot_ref, late1_ref, late2_ref, late3_ref, out_ref):
+    del late1_ref, late2_ref, late3_ref
     pieces, piece_rows, piece_cols = out_ref.shape
     quarters = left_ref.shape[0] // piece_rows
     for c in range(pieces // quarters):
@@ -213,7 +218,8 @@
         out_ref[jnp.bitwise_xor(across, z)] = total[z * cols : (z + 1) * cols, :].astype(BF)
 
 
-def copies_kernel(terms_ref, out_ref):
+def copies_kernel(terms_ref, late_ref, out_ref):
+    del late_ref
     total = terms_ref[0].astype(F32)
     for d in range(1, terms_ref.shape[0]):
         total = total + terms_ref[d].astype(F32)
@@ -264,10 +270,10 @@
     blocks = n_feat // GROUP
     wide = full // GROUP
     near = [[GROUP * i + j for j in range(GROUP)] for i in range(blocks)]
-    far = [[i + GROUP * j for j in range(blocks)] for i in range(GROUP)]
+    far = [[GROUP * i + far_place(i, h) for i in range(blocks)] for h in range(GROUP)]
     z = lax.axis_index("feat")
     mine = (z % GROUP).reshape(1)
-    across = (z // GROUP).reshape(1)
+    block = (z // GROUP).reshape(1)
     live = seed_live.reshape(1, targets).astype(F32)
 
     def swap(x, axis, among=None):
@@ -277,6 +283,10 @@
 
     def trade(x, k):
         return lax.ppermute(x, "feat", [(i, i ^ k) for i in range(n_feat)])
+
+    def trade_far(x, k):
+        pairs = [(group[i], group[i ^ k]) for group in far for i in range(blocks)]
+        return lax.ppermute(x, "feat", pairs)
 
     def shape(*dims, dtype=BF):
         return jax.ShapeDtypeStruct(dims, dtype)
@@ -297,11 +307,11 @@
         pieces = call(
             first_pieces_kernel,
             shape(GROUP, 4 * cols, wide),
-            5,
-            smem=(0,),
-            late=(4,),
+            6,
+            smem=(0, 1),
+            late=(5,),
             nbytes=2 << 20,
-        )(mine, neigh_one, self_one, self_feats.T, send)
+        )(mine, block, neigh_one, self_one, self_feats.T, send)
         got = [trade(pieces[k], k) for k in range(1, GROUP)]
     with jax.named_scope("mean"):
         mean = call(
@@ -328,11 +338,11 @@
         pieces = call(
             second_pieces_kernel,
             shape(GROUP, 2 * hid, wide),
-            4,
-            smem=(0,),
-            late=(3,),
+            5,
+            smem=(0, 1),
+            late=(4,),
             nbytes=1 << 20,
-        )(mine, neigh_two, self_two, first)
+        )(mine, block, neigh_two, self_two, first)
     with jax.named_scope("hidden"):
         pay, left = call(
             hidden_kernel,
@@ -351,21 +361,12 @@
         terms = call(
             grad_kernel,
             shape(groups, piece_rows, 128),
-            2,
+            5,
+            late=(2, 3, 4),
             flops=2 * 2 * hid * targets * full,
             nbytes=2 << 20,
-        )(left, cot)
+        )(left, cot, *got)
         terms = swap(terms, "dp")
-        spread = call(
-            copies_kernel, shape(groups, piece_rows, 128, dtype=F32), 1, nbytes=1 << 20
-        )(terms)
-        spread = swap(spread, "dp")
-        grad_neigh, grad_self = call(
-            place_kernel,
-            (shape(hid, full, dtype=F32), shape(hid, full, dtype=F32)),
-            1,
-            nbytes=1 << 20,
-        )(spread)
     with jax.named_scope("second"):
         second = call(
             second_kernel,
@@ -380,11 +381,26 @@
             smem=(0, 1),
             flops=2 * 2 * wide * wide * targets,
             nbytes=2 << 20,
-        )(across, tile_index, tile_values, pay[0], *got)
-        sums = [second[0]] + [trade(second[k], GROUP * k) for k in range(1, blocks)]
+        )(block, tile_index, tile_values, pay[0], *got)
+        sums = [second[0]] + [trade_far(second[k], k) for k in range(1, blocks)]
         second_out = call(out_kernel, shape(hid, targets), 6, nbytes=1 << 20)(
             *sums, bias_two.reshape(hid, 1), live
         ).T
+    with jax.named_scope("spread"):
+        spread = call(
+            copies_kernel,
+            shape(groups, piece_rows, 128, dtype=F32),
+            2,
+            late=(1,),
+            nbytes=1 << 20,
+        )(terms, second)
+        spread = swap(spread, "dp")
+        grad_neigh, grad_self = call(
+            place_kernel,
+            (shape(hid, full, dtype=F32), shape(hid, full, dtype=F32)),
+            1,
+            nbytes=1 << 20,
+        )(spread)
     return (second_out, grad_neigh, grad_self)
 
 

time: 169 us -> 164 us (0.970)
  blocking collectives: 34.2 us -> 10.8 us
  starting transfers between devices: 62.6 us -> 79.7 us
    all_to_all x2 -> x1, blocking collectives: 34.2 us -> 10.8 us  [swap(): lax.all_to_all(x, axis, split_axis=0, concat_axis=0, tiled=True, axis_ind...]
    ppermute x0 -> x3, starting transfers between devices: none -> 15.2 us  [trade_far(): return lax.ppermute(x, 'feat', pairs)]
    ppermute x0 -> x3, waiting for transfers between devices: none -> 9.46 us  [trade_far(): return lax.ppermute(x, 'feat', pairs)]
    ppermute x9 -> x6, waiting for transfers between devices: 21 us -> 12.4 us  [trade(): return lax.ppermute(x, 'feat', [(i, i ^ k) for i in range(n_feat)])]
    all_to_all x3 -> x4, starting transfers between devices: 27.8 us -> 36.3 us  [swap(): lax.all_to_all(x, axis, split_axis=0, concat_axis=0, tiled=True, axis_ind...]
    ppermute x9 -> x6, starting transfers between devices: 34.7 us -> 28.2 us  [trade(): return lax.ppermute(x, 'feat', [(i, i ^ k) for i in range(n_feat)])]
    all_to_all x3 -> x4, waiting for transfers between devices: 15.5 us -> 18.7 us  [swap(): lax.all_to_all(x, axis, split_axis=0, concat_axis=0, tiled=True, axis_ind...]
    all_gather x1, waiting for transfers between devices: 3.71 us -> 0.57 us  [body(): cot = lax.all_gather(cotangent.T, 'feat', axis=0, tiled=True)]
  transfers between devices with their start and end apart: 13 -> 14, of which waited for: 7 -> 8; matrix products, arithmetic and copies ran while one was open for 0% -> 0% of each run, Pallas kernels for 5% -> 3%
where the time goes in v13:
time: 164 us; the launch traced here: 163 us
  starting transfers between devices  79.7 us (49%)
  waiting for transfers between devices  41.8 us (25%)
  between operations  14.3 us (9%)
  Pallas kernels  11.5 us (7%)
  blocking collectives  10.8 us (7%)
  local copies, waits for them, and re-layouts  4.68 us (3%)
    all_to_all x4, starting transfers between devices, swap(): lax.all_to_all(x, axis, split_axis=0, concat_axis=0, tiled=True, axis_ind...  36.3 us
    ppermute x6, starting transfers between devices, trade(): return lax.ppermute(x, 'feat', [(i, i ^ k) for i in range(n_feat)])  28.2 us
    all_to_all x4, waiting for transfers between devices, swap(): lax.all_to_all(x, axis, split_axis=0, concat_axis=0, tiled=True, axis_ind...  18.7 us
    ppermute x3, starting transfers between devices, trade_far(): return lax.ppermute(x, 'feat', pairs)  15.2 us
    ppermute x6, waiting for transfers between devices, trade(): return lax.ppermute(x, 'feat', [(i, i ^ k) for i in range(n_feat)])  12.4 us
    all_to_all x1, blocking collectives, swap(): lax.all_to_all(x, axis, split_axis=0, concat_axis=0, tiled=True, axis_ind...  10.8 us
    ppermute x3, waiting for transfers between devices, trade_far(): return lax.ppermute(x, 'feat', pairs)  9.46 us
    unnamed x27, local copies, waits for them, and re-layouts  4.4 us
  transfers between devices with their start and end apart: 14, of which 8 were waited for; matrix products, arithmetic and copies ran while one was open for 0% of the time, Pallas kernels for 3%

profile of v13, /device:TPU:1, one launch (start us, length us, event | category | flops | bytes accessed | tf_op | source)
XLA Modules:
  0.0 162.7 jit_solution(17906464247386551505)
XLA Ops:
  8.8 3.3 %edges.1.late_ref = bf16[32,64,128]{2,1,0:T(8,128)(2,1)} custom-call(bf16[48,2048]{1,0:T(8,128)(2,1)S(1)} %bitcast.37, s32[16,128]{1,0:T(8,128)S(1)} %bitcast.38), custom_call_target="tpu_custom_call" | custom-call | flops 1073741824 | bytes 8388608 | tf_op jit(solution)/shard_map/edges/pallas_call | solution.py:297
  12.1 10.6 %all-to-all-start = ((bf16[32,64,128]{2,1,0:T(8,128)(2,1)}), bf16[32,64,128]{2,1,0:T(8,128)(2,1)S(1)}, u32[]{:S(2)}, u32[]{:S(2)}) async-start(bf16[32,64,128]{2,1,0:T(8,128)(2,1)} %edges.1.late_ref), calls=%async_computation | async-start | bytes 1048576 | tf_op jit(solution)/shard_map/edges/all_to_all | solution.py:280
  23.7 1.9 %collective-permute-start = (bf16[192,256]{1,0:T(8,128)(2,1)S(1)}, bf16[192,256]{1,0:T(8,128)(2,1)S(1)}, u32[]{:S(2)}, u32[]{:S(2)}) collective-permute-start(bf16[192,256]{1,0:T(8,128)(2,1)S(1)} %get-tuple-element.18), channel_id=1, source_target_pairs={{0,1},{1,0},{2,3},{3,2},{4,5},{5,4},{6,7},{7,6},{8,9},{9,8},{10,11... | collective-permute-start | bytes 294920 | tf_op jit(solution)/shard_map/pieces/ppermute | solution.py:285
  25.7 4.7 %collective-permute-start.1 = (bf16[192,256]{1,0:T(8,128)(2,1)S(1)}, bf16[192,256]{1,0:T(8,128)(2,1)S(1)}, u32[]{:S(2)}, u32[]{:S(2)}) collective-permute-start(bf16[192,256]{1,0:T(8,128)(2,1)S(1)} %get-tuple-element.17), channel_id=1, source_target_pairs={{0,2},{1,3},{2,0},{3,1},{4,6},{5,7},{6,4},{7,5},{8,10},{9,11},{10,... | collective-permute-start | bytes 294920 | tf_op jit(solution)/shard_map/pieces/ppermute | solution.py:285
  30.4 2.7 %collective-permute-start.2 = (bf16[192,256]{1,0:T(8,128)(2,1)S(1)}, bf16[192,256]{1,0:T(8,128)(2,1)S(1)}, u32[]{:S(2)}, u32[]{:S(2)}) collective-permute-start(bf16[192,256]{1,0:T(8,128)(2,1)S(1)} %get-tuple-element.16), channel_id=1, source_target_pairs={{0,3},{1,2},{2,1},{3,0},{4,7},{5,6},{6,5},{7,4},{8,11},{9,10},{10,... | collective-permute-start | bytes 294920 | tf_op jit(solution)/shard_map/pieces/ppermute | solution.py:285
  33.0 2.1 %collective-permute-done.1.late2_ref.p2_ref = bf16[192,256]{1,0:T(8,128)(2,1)S(1)} collective-permute-done((bf16[192,256]{1,0:T(8,128)(2,1)S(1)}, bf16[192,256]{1,0:T(8,128)(2,1)S(1)}, u32[]{:S(2)}, u32[]{:S(2)}) %collective-permute-start.1) | collective-permute-done | bytes 98336 | tf_op jit(solution)/shard_map/pieces/ppermute | solution.py:285
  35.2 2.5 %collective-permute-done.2.late3_ref.p3_ref = bf16[192,256]{1,0:T(8,128)(2,1)S(1)} collective-permute-done((bf16[192,256]{1,0:T(8,128)(2,1)S(1)}, bf16[192,256]{1,0:T(8,128)(2,1)S(1)}, u32[]{:S(2)}, u32[]{:S(2)}) %collective-permute-start.2) | collective-permute-done | bytes 98336 | tf_op jit(solution)/shard_map/pieces/ppermute | solution.py:285
  37.6 1.4 mean.1
  39.0 10.8 %all_to_all.25.mean_ref = bf16[4,48,512]{2,1,0:T(8,128)(2,1)S(1)} all-to-all(bf16[4,48,512]{2,1,0:T(8,128)(2,1)S(1)} %mean.1), channel_id=1, replica_groups={{0,1,2,3},{4,5,6,7},{8,9,10,11},{12,13,14,15},{16,17,18,19},{20,21,22,2..., dimensions={0} | all-to-all | bytes 393216 | tf_op jit(solution)/shard_map/mean/all_to_all | solution.py:280
  50.9 11.3 %all-to-all-start.2 = ((bf16[4,64,512]{2,1,0:T(8,128)(2,1)}), bf16[4,64,512]{2,1,0:T(8,128)(2,1)S(1)}, u32[]{:S(2)}, u32[]{:S(2)}) async-start(bf16[4,64,512]{2,1,0:T(8,128)(2,1)} %first.1.late_ref), calls=%async_computation.2 | async-start | bytes 524288 | tf_op jit(solution)/shard_map/first/all_to_all | solution.py:280
  63.8 10.9 %all-to-all-done.2.parts_ref = bf16[4,64,512]{2,1,0:T(8,128)(2,1)S(1)} async-done(((bf16[4,64,512]{2,1,0:T(8,128)(2,1)}), bf16[4,64,512]{2,1,0:T(8,128)(2,1)S(1)}, u32[]{:S(2)}, u32[]{:S(2)}) %all-to-all-start.2) | async-done | bytes 262176 | tf_op jit(solution)/shard_map/first/all_to_all | solution.py:280
  75.6 13.0 %collective-permute-start.3 = (bf16[256,256]{1,0:T(8,128)(2,1)S(1)}, bf16[256,256]{1,0:T(8,128)(2,1)S(1)}, u32[]{:S(2)}, u32[]{:S(2)}) collective-permute-start(bf16[256,256]{1,0:T(8,128)(2,1)S(1)} %get-tuple-element.13), channel_id=1, source_target_pairs={{0,1},{1,0},{2,3},{3,2},{4,5},{5,4},{6,7},{7,6},{8,9},{9,8},{10,11... | collective-permute-start | bytes 393224 | tf_op jit(solution)/shard_map/hidden/ppermute | solution.py:285
  88.6 1.9 %collective-permute-start.4 = (bf16[256,256]{1,0:T(8,128)(2,1)S(1)}, bf16[256,256]{1,0:T(8,128)(2,1)S(1)}, u32[]{:S(2)}, u32[]{:S(2)}) collective-permute-start(bf16[256,256]{1,0:T(8,128)(2,1)S(1)} %get-tuple-element.12), channel_id=1, source_target_pairs={{0,2},{1,3},{2,0},{3,1},{4,6},{5,7},{6,4},{7,5},{8,10},{9,11},{10,... | collective-permute-start | bytes 393224 | tf_op jit(solution)/shard_map/hidden/ppermute | solution.py:285
  90.5 4.0 %collective-permute-start.5 = (bf16[256,256]{1,0:T(8,128)(2,1)S(1)}, bf16[256,256]{1,0:T(8,128)(2,1)S(1)}, u32[]{:S(2)}, u32[]{:S(2)}) collective-permute-start(bf16[256,256]{1,0:T(8,128)(2,1)S(1)} %get-tuple-element.11), channel_id=1, source_target_pairs={{0,3},{1,2},{2,1},{3,0},{4,7},{5,6},{6,5},{7,4},{8,11},{9,10},{10,... | collective-permute-start | bytes 393224 | tf_op jit(solution)/shard_map/hidden/ppermute | solution.py:285
  95.1 7.8 %collective-permute-done.4.p2_ref.late2_ref = bf16[256,256]{1,0:T(8,128)(2,1)S(1)} collective-permute-done((bf16[256,256]{1,0:T(8,128)(2,1)S(1)}, bf16[256,256]{1,0:T(8,128)(2,1)S(1)}, u32[]{:S(2)}, u32[]{:S(2)}) %collective-permute-start.4) | collective-permute-done | bytes 131104 | tf_op jit(solution)/shard_map/hidden/ppermute | solution.py:285
  102.9 1.2 copy-done
  104.1 1.1 grads.1
  105.2 10.7 %all-to-all-start.3 = ((bf16[32,32,128]{2,1,0:T(8,128)(2,1)}), bf16[32,32,128]{2,1,0:T(8,128)(2,1)S(1)}, u32[]{:S(2)}, u32[]{:S(2)}) async-start(bf16[32,32,128]{2,1,0:T(8,128)(2,1)} %grads.1), calls=%async_computation.3 | async-start | bytes 524288 | tf_op jit(solution)/shard_map/grads/all_to_all | solution.py:280
  117.0 7.8 %all-to-all-done.3.terms_ref = bf16[32,32,128]{2,1,0:T(8,128)(2,1)S(1)} async-done(((bf16[32,32,128]{2,1,0:T(8,128)(2,1)}), bf16[32,32,128]{2,1,0:T(8,128)(2,1)S(1)}, u32[]{:S(2)}, u32[]{:S(2)}) %all-to-all-start.3) | async-done | bytes 262176 | tf_op jit(solution)/shard_map/grads/all_to_all | solution.py:280
  125.7 3.8 %all-to-all-start.4 = ((f32[32,32,128]{2,1,0:T(8,128)}), f32[32,32,128]{2,1,0:T(8,128)S(1)}, u32[]{:S(2)}, u32[]{:S(2)}) async-start(f32[32,32,128]{2,1,0:T(8,128)} %spread.2), calls=%async_computation.4 | async-start | bytes 1048576 | tf_op jit(solution)/shard_map/spread/all_to_all | solution.py:280
  129.5 4.0 %collective-permute-start.6 = (bf16[64,512]{1,0:T(8,128)(2,1)S(1)}, bf16[64,512]{1,0:T(8,128)(2,1)S(1)}, u32[]{:S(2)}, u32[]{:S(2)}) collective-permute-start(bf16[64,512]{1,0:T(8,128)(2,1)S(1)} %get-tuple-element.21), channel_id=1, source_target_pairs={{0,5},{5,0},{10,15},{15,10},{1,6},{6,1},{11,12},{12,11},{2,7},{7,2... | collective-permute-start | bytes 196616 | tf_op jit(solution)/shard_map/second/ppermute | solution.py:289
  133.6 9.3 %collective-permute-start.7 = (bf16[64,512]{1,0:T(8,128)(2,1)S(1)}, bf16[64,512]{1,0:T(8,128)(2,1)S(1)}, u32[]{:S(2)}, u32[]{:S(2)}) collective-permute-start(bf16[64,512]{1,0:T(8,128)(2,1)S(1)} %get-tuple-element.20), channel_id=1, source_target_pairs={{0,10},{5,15},{10,0},{15,5},{1,11},{6,12},{11,1},{12,6},{2,8},{7,1... | collective-permute-start | bytes 196616 | tf_op jit(solution)/shard_map/second/ppermute | solution.py:289
  142.9 1.9 %collective-permute-start.8 = (bf16[64,512]{1,0:T(8,128)(2,1)S(1)}, bf16[64,512]{1,0:T(8,128)(2,1)S(1)}, u32[]{:S(2)}, u32[]{:S(2)}) collective-permute-start(bf16[64,512]{1,0:T(8,128)(2,1)S(1)} %get-tuple-element.19), channel_id=1, source_target_pairs={{0,15},{5,10},{10,5},{15,0},{1,12},{6,11},{11,6},{12,1},{2,13},{7,... | collective-permute-start | bytes 196616 | tf_op jit(solution)/shard_map/second/ppermute | solution.py:289
  145.7 8.6 %collective-permute-done.8.p3_ref = bf16[64,512]{1,0:T(8,128)(2,1)S(1)} collective-permute-done((bf16[64,512]{1,0:T(8,128)(2,1)S(1)}, bf16[64,512]{1,0:T(8,128)(2,1)S(1)}, u32[]{:S(2)}, u32[]{:S(2)}) %collective-permute-start.8) | collective-permute-done | bytes 65568 | tf_op jit(solution)/shard_map/second/ppermute | solution.py:289
  (50 shorter events, 11.2 us)
Async XLA Ops:
  7.2 0.9 copy-start.7
  12.1 11.3 %copy-start.5 = (bf16[48,1024]{1,0:T(8,128)(2,1)S(1)}, bf16[48,1024]{1,0:T(8,128)(2,1)}, u32[]{:S(2)}) copy-start(bf16[48,1024]{1,0:T(8,128)(2,1)} %own_ref.2) | copy-start | bytes 294916
  12.1 11.3 %copy-start.6 = (bf16[512,48]{0,1:T(8,128)(2,1)S(1)}, bf16[512,48]{0,1:T(8,128)(2,1)}, u32[]{:S(2)}) copy-start(bf16[512,48]{0,1:T(8,128)(2,1)} %param.15) | copy-start | bytes 147460
  12.1 25.5 %all-to-all-start = ((bf16[32,64,128]{2,1,0:T(8,128)(2,1)}), bf16[32,64,128]{2,1,0:T(8,128)(2,1)S(1)}, u32[]{:S(2)}, u32[]{:S(2)}) async-start(bf16[32,64,128]{2,1,0:T(8,128)(2,1)} %edges.1.late_ref), calls=%async_computation | async-start | bytes 1048576 | tf_op jit(solution)/shard_map/edges/all_to_all | solution.py:280
  22.7 0.9 copy-start.4
  22.7 72.4 %all-gather.2.cloned.1.call-start = ((), (), s32[]{:S(2)}) async-start(), calls=%async_computation.5 | async-start | bytes 1114112 | tf_op jit(solution)/shard_map/cotangent/all_gather | solution.py:295
  23.7 9.3 %collective-permute-start = (bf16[192,256]{1,0:T(8,128)(2,1)S(1)}, bf16[192,256]{1,0:T(8,128)(2,1)S(1)}, u32[]{:S(2)}, u32[]{:S(2)}) collective-permute-start(bf16[192,256]{1,0:T(8,128)(2,1)S(1)} %get-tuple-element.18), channel_id=1, source_target_pairs={{0,1},{1,0},{2,3},{3,2},{4,5},{5,4},{6,7},{7,6},{8,9},{9,8},{10,11... | collective-permute-start | bytes 294920 | tf_op jit(solution)/shard_map/pieces/ppermute | solution.py:285
  25.7 9.5 %collective-permute-start.1 = (bf16[192,256]{1,0:T(8,128)(2,1)S(1)}, bf16[192,256]{1,0:T(8,128)(2,1)S(1)}, u32[]{:S(2)}, u32[]{:S(2)}) collective-permute-start(bf16[192,256]{1,0:T(8,128)(2,1)S(1)} %get-tuple-element.17), channel_id=1, source_target_pairs={{0,2},{1,3},{2,0},{3,1},{4,6},{5,7},{6,4},{7,5},{8,10},{9,11},{10,... | collective-permute-start | bytes 294920 | tf_op jit(solution)/shard_map/pieces/ppermute | solution.py:285
  30.4 7.3 %collective-permute-start.2 = (bf16[192,256]{1,0:T(8,128)(2,1)S(1)}, bf16[192,256]{1,0:T(8,128)(2,1)S(1)}, u32[]{:S(2)}, u32[]{:S(2)}) collective-permute-start(bf16[192,256]{1,0:T(8,128)(2,1)S(1)} %get-tuple-element.16), channel_id=1, source_target_pairs={{0,3},{1,2},{2,1},{3,0},{4,7},{5,6},{6,5},{7,4},{8,11},{9,10},{10,... | collective-permute-start | bytes 294920 | tf_op jit(solution)/shard_map/pieces/ppermute | solution.py:285
  50.9 11.3 %copy-start.9 = (s32[512]{0:T(512)S(1)}, s32[512]{0:T(512)}, u32[]{:S(2)}) copy-start(s32[512]{0:T(512)} %param.21) | copy-start | bytes 6148
  50.9 12.8 %copy-start.2 = (bf16[64,1024]{1,0:T(8,128)(2,1)S(1)}, bf16[64,1024]{1,0:T(8,128)(2,1)}, u32[]{:S(2)}) copy-start(bf16[64,1024]{1,0:T(8,128)(2,1)} %neigh_ref.3) | copy-start | bytes 393220
  50.9 12.8 %copy-start.3 = (bf16[64,1024]{1,0:T(8,128)(2,1)S(1)}, bf16[64,1024]{1,0:T(8,128)(2,1)}, u32[]{:S(2)}) copy-start(bf16[64,1024]{1,0:T(8,128)(2,1)} %own_ref.3) | copy-start | bytes 393220
  50.9 23.8 %all-to-all-start.2 = ((bf16[4,64,512]{2,1,0:T(8,128)(2,1)}), bf16[4,64,512]{2,1,0:T(8,128)(2,1)S(1)}, u32[]{:S(2)}, u32[]{:S(2)}) async-start(bf16[4,64,512]{2,1,0:T(8,128)(2,1)} %first.1.late_ref), calls=%async_computation.2 | async-start | bytes 524288 | tf_op jit(solution)/shard_map/first/all_to_all | solution.py:280
  63.7 11.0 %copy-start.1 = (bf16[4,128,128]{2,1,0:T(8,128)(2,1)S(1)}, bf16[4,128,128]{2,1,0:T(8,128)(2,1)}, u32[]{:S(2)}) copy-start(bf16[4,128,128]{2,1,0:T(8,128)(2,1)} %values_ref.3) | copy-start | bytes 393220
  75.6 19.5 %collective-permute-start.3 = (bf16[256,256]{1,0:T(8,128)(2,1)S(1)}, bf16[256,256]{1,0:T(8,128)(2,1)S(1)}, u32[]{:S(2)}, u32[]{:S(2)}) collective-permute-start(bf16[256,256]{1,0:T(8,128)(2,1)S(1)} %get-tuple-element.13), channel_id=1, source_target_pairs={{0,1},{1,0},{2,3},{3,2},{4,5},{5,4},{6,7},{7,6},{8,9},{9,8},{10,11... | collective-permute-start | bytes 393224 | tf_op jit(solution)/shard_map/hidden/ppermute | solution.py:285
  88.6 14.3 %collective-permute-start.4 = (bf16[256,256]{1,0:T(8,128)(2,1)S(1)}, bf16[256,256]{1,0:T(8,128)(2,1)S(1)}, u32[]{:S(2)}, u32[]{:S(2)}) collective-permute-start(bf16[256,256]{1,0:T(8,128)(2,1)S(1)} %get-tuple-element.12), channel_id=1, source_target_pairs={{0,2},{1,3},{2,0},{3,1},{4,6},{5,7},{6,4},{7,5},{8,10},{9,11},{10,... | collective-permute-start | bytes 393224 | tf_op jit(solution)/shard_map/hidden/ppermute | solution.py:285
  90.5 12.4 %collective-permute-start.5 = (bf16[256,256]{1,0:T(8,128)(2,1)S(1)}, bf16[256,256]{1,0:T(8,128)(2,1)S(1)}, u32[]{:S(2)}, u32[]{:S(2)}) collective-permute-start(bf16[256,256]{1,0:T(8,128)(2,1)S(1)} %get-tuple-element.11), channel_id=1, source_target_pairs={{0,3},{1,2},{2,1},{3,0},{4,7},{5,6},{6,5},{7,4},{8,11},{9,10},{10,... | collective-permute-start | bytes 393224 | tf_op jit(solution)/shard_map/hidden/ppermute | solution.py:285
  102.9 1.2 copy-start
  105.2 19.6 %all-to-all-start.3 = ((bf16[32,32,128]{2,1,0:T(8,128)(2,1)}), bf16[32,32,128]{2,1,0:T(8,128)(2,1)S(1)}, u32[]{:S(2)}, u32[]{:S(2)}) async-start(bf16[32,32,128]{2,1,0:T(8,128)(2,1)} %grads.1), calls=%async_computation.3 | async-start | bytes 524288 | tf_op jit(solution)/shard_map/grads/all_to_all | solution.py:280
  125.7 29.4 %all-to-all-start.4 = ((f32[32,32,128]{2,1,0:T(8,128)}), f32[32,32,128]{2,1,0:T(8,128)S(1)}, u32[]{:S(2)}, u32[]{:S(2)}) async-start(f32[32,32,128]{2,1,0:T(8,128)} %spread.2), calls=%async_computation.4 | async-start | bytes 1048576 | tf_op jit(solution)/shard_map/spread/all_to_all | solution.py:280
  129.5 15.4 %collective-permute-start.6 = (bf16[64,512]{1,0:T(8,128)(2,1)S(1)}, bf16[64,512]{1,0:T(8,128)(2,1)S(1)}, u32[]{:S(2)}, u32[]{:S(2)}) collective-permute-start(bf16[64,512]{1,0:T(8,128)(2,1)S(1)} %get-tuple-element.21), channel_id=1, source_target_pairs={{0,5},{5,0},{10,15},{15,10},{1,6},{6,1},{11,12},{12,11},{2,7},{7,2... | collective-permute-start | bytes 196616 | tf_op jit(solution)/shard_map/second/ppermute | solution.py:289
  133.6 12.2 %collective-permute-start.7 = (bf16[64,512]{1,0:T(8,128)(2,1)S(1)}, bf16[64,512]{1,0:T(8,128)(2,1)S(1)}, u32[]{:S(2)}, u32[]{:S(2)}) collective-permute-start(bf16[64,512]{1,0:T(8,128)(2,1)S(1)} %get-tuple-element.20), channel_id=1, source_target_pairs={{0,10},{5,15},{10,0},{15,5},{1,11},{6,12},{11,1},{12,6},{2,8},{7,1... | collective-permute-start | bytes 196616 | tf_op jit(solution)/shard_map/second/ppermute | solution.py:289
  142.8 1.9 %copy-start.12 = (f32[64]{0:T(128)S(1)}, f32[64]{0:T(128)}, u32[]{:S(2)}) copy-start(f32[64]{0:T(128)} %param.24) | copy-start | bytes 772
  142.9 11.5 %collective-permute-start.8 = (bf16[64,512]{1,0:T(8,128)(2,1)S(1)}, bf16[64,512]{1,0:T(8,128)(2,1)S(1)}, u32[]{:S(2)}, u32[]{:S(2)}) collective-permute-start(bf16[64,512]{1,0:T(8,128)(2,1)S(1)} %get-tuple-element.19), channel_id=1, source_target_pairs={{0,15},{5,10},{10,5},{15,0},{1,12},{6,11},{11,6},{12,1},{2,13},{7,... | collective-permute-start | bytes 196616 | tf_op jit(solution)/shard_map/second/ppermute | solution.py:289
  (3 other events, 2.0 us)
Sparse Core Ops, SparseCore 0:
  25.6 69.4 all-gather.1

commit v14 on v13

--- a/solution.py
+++ b/solution.py
@@ -112,7 +112,7 @@
 def mean_kernel(cols, recv_ref, late1_ref, late2_ref, late3_ref, out_ref):
     del late1_ref, late2_ref, late3_ref
     groups, rows, cap = recv_ref.shape
-    targets = out_ref.shape[2]
+    targets = out_ref.shape[1]
     half = targets // 2
     vertex = lax.broadcasted_iota(jnp.int32, (targets, 1), 0)
     vertex = jnp.where(vertex < half, vertex - half, vertex - (half - 1)).astype(F32)
@@ -124,24 +124,21 @@
         hot = (vertex == code).astype(F32).astype(BF)
         acc = acc + lax.dot_general(part, hot, NT, preferred_element_type=F32)
     degree = jnp.maximum(acc[cols + 1 : cols + 2, :], 1.0)
-    mean = (acc[:cols, :] / degree).astype(BF)
-    for j in range(out_ref.shape[0]):
-        out_ref[j] = mean
+    out_ref[...] = (acc[:cols, :] / degree).astype(BF)
 
 
 def first_kernel(
-    mine_ref, mean_ref, p0_ref, p1_ref, p2_ref, p3_ref, out_ref, weight, acts
+    m0_ref, m1_ref, m2_ref, m3_ref, p0_ref, p1_ref, p2_ref, p3_ref, out_ref, weight, acts
 ):
-    mine = mine_ref[0]
-    group, rows, targets = mean_ref.shape
+    rows, targets = m0_ref.shape
     width = targets // 2
-    for k, piece in enumerate((p0_ref, p1_ref, p2_ref, p3_ref)):
-        at = slice(2 * rows * k, 2 * rows * (k + 1))
-        mid = 2 * rows * k + rows
-        weight[at, :] = piece[: 2 * rows, :]
-        acts[2 * rows * k : mid, :] = mean_ref[jnp.bitwise_xor(mine, k)]
-        acts[mid : mid + rows, :width] = piece[2 * rows : 3 * rows, :]
-        acts[mid : mid + rows, width:] = piece[3 * rows :, :]
+    means = (m0_ref, m1_ref, m2_ref, m3_ref)
+    for k, (mean, piece) in enumerate(zip(means, (p0_ref, p1_ref, p2_ref, p3_ref))):
+        low, mid, high = 2 * rows * k, 2 * rows * k + rows, 2 * rows * (k + 1)
+        weight[low:high, :] = piece[: 2 * rows, :]
+        acts[low:mid, :] = mean[...]
+        acts[mid:high, :width] = piece[2 * rows : 3 * rows, :]
+        acts[mid:high, width:] = piece[3 * rows :, :]
     total = lax.dot_general(weight[...], acts[...], TN, preferred_element_type=F32)
     cols = out_ref.shape[1]
     for z in range(out_ref.shape[0]):
@@ -269,7 +266,6 @@
     cap = 2 * edges // groups
     blocks = n_feat // GROUP
     wide = full // GROUP
-    near = [[GROUP * i + j for j in range(GROUP)] for i in range(blocks)]
     far = [[GROUP * i + far_place(i, h) for i in range(blocks)] for h in range(GROUP)]
     z = lax.axis_index("feat")
     mine = (z % GROUP).reshape(1)
@@ -316,23 +312,22 @@
     with jax.named_scope("mean"):
         mean = call(
             functools.partial(mean_kernel, cols),
-            shape(GROUP, cols, targets),
+            shape(cols, targets),
             4,
             late=(1, 2, 3),
             flops=2 * groups * ROWS * cap * targets,
             nbytes=8 << 20,
         )(recv, *got)
-        mean = swap(mean, "feat", near)
+        means = [mean] + [trade(mean, k) for k in range(1, GROUP)]
     with jax.named_scope("first"):
         first = call(
             first_kernel,
             shape(blocks, hid, targets),
-            6,
+            8,
             scratch=[pltpu.VMEM((8 * cols, wide), BF), pltpu.VMEM((8 * cols, targets), BF)],
-            smem=(0,),
             flops=2 * 8 * cols * wide * targets,
             nbytes=2 << 20,
-        )(mine, mean, pieces[0], *got)
+        )(*means, pieces[0], *got)
         parts = swap(first, "feat", far)
     with jax.named_scope("pieces"):
         pieces = call(

time: 164 us -> 162 us (0.988)
  the two profiles are of different devices: /device:TPU:1 before, /device:TPU:35 now
where the time goes in v14:
time: 162 us; the launch traced here: 161 us
  starting transfers between devices  76.8 us (47%)
  waiting for transfers between devices  54.6 us (34%)
  between operations  14.3 us (9%)
  Pallas kernels  11.5 us (7%)
  local copies, waits for them, and re-layouts  3.89 us (2%)
    all_to_all x4, starting transfers between devices, swap(): lax.all_to_all(x, axis, split_axis=0, concat_axis=0, tiled=True, axis_ind...  34.7 us
    ppermute x9, starting transfers between devices, trade(): return lax.ppermute(x, 'feat', [(i, i ^ k) for i in range(n_feat)])  25.9 us
    all_to_all x4, waiting for transfers between devices, swap(): lax.all_to_all(x, axis, split_axis=0, concat_axis=0, tiled=True, axis_ind...  25.5 us
    ppermute x9, waiting for transfers between devices, trade(): return lax.ppermute(x, 'feat', [(i, i ^ k) for i in range(n_feat)])  21.2 us
    ppermute x3, starting transfers between devices, trade_far(): return lax.ppermute(x, 'feat', pairs)  16.2 us
    ppermute x3, waiting for transfers between devices, trade_far(): return lax.ppermute(x, 'feat', pairs)  7.17 us
    unnamed x27, local copies, waits for them, and re-layouts  3.61 us
    pallas_call x1, Pallas kernels, body(): call(functools.partial(pack_kernel, groups, targets), shape(groups, ROWS,...  3.33 us
  transfers between devices with their start and end apart: 17, of which 8 were waited for; matrix products, arithmetic and copies ran while one was open for 0% of the time, Pallas kernels for 5%

profile of v14, /device:TPU:35, one launch (start us, length us, event | category | flops | bytes accessed | tf_op | source)
XLA Modules:
  0.0 161.1 jit_solution(893424865007723273)
XLA Ops:
  8.8 3.3 %edges.1.late_ref = bf16[32,64,128]{2,1,0:T(8,128)(2,1)} custom-call(bf16[48,2048]{1,0:T(8,128)(2,1)S(1)} %bitcast.37, s32[16,128]{1,0:T(8,128)S(1)} %bitcast.38), custom_call_target="tpu_custom_call" | custom-call | flops 1073741824 | bytes 8388608 | tf_op jit(solution)/shard_map/edges/pallas_call | solution.py:293
  12.2 8.1 %all-to-all-start = ((bf16[32,64,128]{2,1,0:T(8,128)(2,1)}), bf16[32,64,128]{2,1,0:T(8,128)(2,1)S(1)}, u32[]{:S(2)}, u32[]{:S(2)}) async-start(bf16[32,64,128]{2,1,0:T(8,128)(2,1)} %edges.1.late_ref), calls=%async_computation | async-start | bytes 1048576 | tf_op jit(solution)/shard_map/edges/all_to_all | solution.py:276
  20.5 3.6 %collective-permute-start = (bf16[192,256]{1,0:T(8,128)(2,1)S(1)}, bf16[192,256]{1,0:T(8,128)(2,1)S(1)}, u32[]{:S(2)}, u32[]{:S(2)}) collective-permute-start(bf16[192,256]{1,0:T(8,128)(2,1)S(1)} %get-tuple-element.18), channel_id=1, source_target_pairs={{0,1},{1,0},{2,3},{3,2},{4,5},{5,4},{6,7},{7,6},{8,9},{9,8},{10,11... | collective-permute-start | bytes 294920 | tf_op jit(solution)/shard_map/pieces/ppermute | solution.py:281
  24.0 3.2 %collective-permute-start.1 = (bf16[192,256]{1,0:T(8,128)(2,1)S(1)}, bf16[192,256]{1,0:T(8,128)(2,1)S(1)}, u32[]{:S(2)}, u32[]{:S(2)}) collective-permute-start(bf16[192,256]{1,0:T(8,128)(2,1)S(1)} %get-tuple-element.17), channel_id=1, source_target_pairs={{0,2},{1,3},{2,0},{3,1},{4,6},{5,7},{6,4},{7,5},{8,10},{9,11},{10,... | collective-permute-start | bytes 294920 | tf_op jit(solution)/shard_map/pieces/ppermute | solution.py:281
  27.3 2.2 %collective-permute-start.2 = (bf16[192,256]{1,0:T(8,128)(2,1)S(1)}, bf16[192,256]{1,0:T(8,128)(2,1)S(1)}, u32[]{:S(2)}, u32[]{:S(2)}) collective-permute-start(bf16[192,256]{1,0:T(8,128)(2,1)S(1)} %get-tuple-element.16), channel_id=1, source_target_pairs={{0,3},{1,2},{2,1},{3,0},{4,7},{5,6},{6,5},{7,4},{8,11},{9,10},{10,... | collective-permute-start | bytes 294920 | tf_op jit(solution)/shard_map/pieces/ppermute | solution.py:281
  30.6 6.8 %collective-permute-done.2.late3_ref.p3_ref = bf16[192,256]{1,0:T(8,128)(2,1)S(1)} collective-permute-done((bf16[192,256]{1,0:T(8,128)(2,1)S(1)}, bf16[192,256]{1,0:T(8,128)(2,1)S(1)}, u32[]{:S(2)}, u32[]{:S(2)}) %collective-permute-start.2) | collective-permute-done | bytes 98336 | tf_op jit(solution)/shard_map/pieces/ppermute | solution.py:281
  37.4 1.4 mean.1.m0_ref
  38.8 1.9 %collective-permute-start.3 = (bf16[48,512]{1,0:T(8,128)(2,1)S(1)}, bf16[48,512]{1,0:T(8,128)(2,1)S(1)}, u32[]{:S(2)}, u32[]{:S(2)}) collective-permute-start(bf16[48,512]{1,0:T(8,128)(2,1)S(1)} %mean.1.m0_ref), channel_id=1, source_target_pairs={{0,1},{1,0},{2,3},{3,2},{4,5},{5,4},{6,7},{7,6},{8,9},{9,8},{10,11... | collective-permute-start | bytes 147464 | tf_op jit(solution)/shard_map/mean/ppermute | solution.py:281
  40.7 4.6 %collective-permute-start.4 = (bf16[48,512]{1,0:T(8,128)(2,1)S(1)}, bf16[48,512]{1,0:T(8,128)(2,1)S(1)}, u32[]{:S(2)}, u32[]{:S(2)}) collective-permute-start(bf16[48,512]{1,0:T(8,128)(2,1)S(1)} %mean.1.m0_ref), channel_id=1, source_target_pairs={{0,2},{1,3},{2,0},{3,1},{4,6},{5,7},{6,4},{7,5},{8,10},{9,11},{10,... | collective-permute-start | bytes 147464 | tf_op jit(solution)/shard_map/mean/ppermute | solution.py:281
  45.4 1.9 %collective-permute-start.5 = (bf16[48,512]{1,0:T(8,128)(2,1)S(1)}, bf16[48,512]{1,0:T(8,128)(2,1)S(1)}, u32[]{:S(2)}, u32[]{:S(2)}) collective-permute-start(bf16[48,512]{1,0:T(8,128)(2,1)S(1)} %mean.1.m0_ref), channel_id=1, source_target_pairs={{0,3},{1,2},{2,1},{3,0},{4,7},{5,6},{6,5},{7,4},{8,11},{9,10},{10,... | collective-permute-start | bytes 147464 | tf_op jit(solution)/shard_map/mean/ppermute | solution.py:281
  47.3 4.3 %collective-permute-done.5.m3_ref = bf16[48,512]{1,0:T(8,128)(2,1)S(1)} collective-permute-done((bf16[48,512]{1,0:T(8,128)(2,1)S(1)}, bf16[48,512]{1,0:T(8,128)(2,1)S(1)}, u32[]{:S(2)}, u32[]{:S(2)}) %collective-permute-start.5) | collective-permute-done | bytes 49184 | tf_op jit(solution)/shard_map/mean/ppermute | solution.py:281
  52.6 12.5 %all-to-all-start.1 = ((bf16[4,64,512]{2,1,0:T(8,128)(2,1)}), bf16[4,64,512]{2,1,0:T(8,128)(2,1)S(1)}, u32[]{:S(2)}, u32[]{:S(2)}) async-start(bf16[4,64,512]{2,1,0:T(8,128)(2,1)} %first.1.late_ref), calls=%async_computation.1 | async-start | bytes 524288 | tf_op jit(solution)/shard_map/first/all_to_all | solution.py:276
  66.9 18.6 %all-to-all-done.1.parts_ref = bf16[4,64,512]{2,1,0:T(8,128)(2,1)S(1)} async-done(((bf16[4,64,512]{2,1,0:T(8,128)(2,1)}), bf16[4,64,512]{2,1,0:T(8,128)(2,1)S(1)}, u32[]{:S(2)}, u32[]{:S(2)}) %all-to-all-start.1) | async-done | bytes 262176 | tf_op jit(solution)/shard_map/first/all_to_all | solution.py:276
  86.4 1.9 %collective-permute-start.6 = (bf16[256,256]{1,0:T(8,128)(2,1)S(1)}, bf16[256,256]{1,0:T(8,128)(2,1)S(1)}, u32[]{:S(2)}, u32[]{:S(2)}) collective-permute-start(bf16[256,256]{1,0:T(8,128)(2,1)S(1)} %get-tuple-element.13), channel_id=1, source_target_pairs={{0,1},{1,0},{2,3},{3,2},{4,5},{5,4},{6,7},{7,6},{8,9},{9,8},{10,11... | collective-permute-start | bytes 393224 | tf_op jit(solution)/shard_map/hidden/ppermute | solution.py:281
  88.3 1.9 %collective-permute-start.7 = (bf16[256,256]{1,0:T(8,128)(2,1)S(1)}, bf16[256,256]{1,0:T(8,128)(2,1)S(1)}, u32[]{:S(2)}, u32[]{:S(2)}) collective-permute-start(bf16[256,256]{1,0:T(8,128)(2,1)S(1)} %get-tuple-element.12), channel_id=1, source_target_pairs={{0,2},{1,3},{2,0},{3,1},{4,6},{5,7},{6,4},{7,5},{8,10},{9,11},{10,... | collective-permute-start | bytes 393224 | tf_op jit(solution)/shard_map/hidden/ppermute | solution.py:281
  90.2 4.5 %collective-permute-start.8 = (bf16[256,256]{1,0:T(8,128)(2,1)S(1)}, bf16[256,256]{1,0:T(8,128)(2,1)S(1)}, u32[]{:S(2)}, u32[]{:S(2)}) collective-permute-start(bf16[256,256]{1,0:T(8,128)(2,1)S(1)} %get-tuple-element.11), channel_id=1, source_target_pairs={{0,3},{1,2},{2,1},{3,0},{4,7},{5,6},{6,5},{7,4},{8,11},{9,10},{10,... | collective-permute-start | bytes 393224 | tf_op jit(solution)/shard_map/hidden/ppermute | solution.py:281
  95.7 8.1 %collective-permute-done.8.p3_ref.late3_ref = bf16[256,256]{1,0:T(8,128)(2,1)S(1)} collective-permute-done((bf16[256,256]{1,0:T(8,128)(2,1)S(1)}, bf16[256,256]{1,0:T(8,128)(2,1)S(1)}, u32[]{:S(2)}, u32[]{:S(2)}) %collective-permute-start.8) | collective-permute-done | bytes 131104 | tf_op jit(solution)/shard_map/hidden/ppermute | solution.py:281
  106.2 9.4 %all-to-all-start.2 = ((bf16[32,32,128]{2,1,0:T(8,128)(2,1)}), bf16[32,32,128]{2,1,0:T(8,128)(2,1)S(1)}, u32[]{:S(2)}, u32[]{:S(2)}) async-start(bf16[32,32,128]{2,1,0:T(8,128)(2,1)} %grads.1), calls=%async_computation.2 | async-start | bytes 524288 | tf_op jit(solution)/shard_map/grads/all_to_all | solution.py:276
  116.7 6.9 %all-to-all-done.2.terms_ref = bf16[32,32,128]{2,1,0:T(8,128)(2,1)S(1)} async-done(((bf16[32,32,128]{2,1,0:T(8,128)(2,1)}), bf16[32,32,128]{2,1,0:T(8,128)(2,1)S(1)}, u32[]{:S(2)}, u32[]{:S(2)}) %all-to-all-start.2) | async-done | bytes 262176 | tf_op jit(solution)/shard_map/grads/all_to_all | solution.py:276
  124.5 4.7 %all-to-all-start.3 = ((f32[32,32,128]{2,1,0:T(8,128)}), f32[32,32,128]{2,1,0:T(8,128)S(1)}, u32[]{:S(2)}, u32[]{:S(2)}) async-start(f32[32,32,128]{2,1,0:T(8,128)} %spread.2), calls=%async_computation.3 | async-start | bytes 1048576 | tf_op jit(solution)/shard_map/spread/all_to_all | solution.py:276
  129.2 1.9 %collective-permute-start.10 = (bf16[64,512]{1,0:T(8,128)(2,1)S(1)}, bf16[64,512]{1,0:T(8,128)(2,1)S(1)}, u32[]{:S(2)}, u32[]{:S(2)}) collective-permute-start(bf16[64,512]{1,0:T(8,128)(2,1)S(1)} %get-tuple-element.20), channel_id=1, source_target_pairs={{0,10},{5,15},{10,0},{15,5},{1,11},{6,12},{11,1},{12,6},{2,8},{7,1... | collective-permute-start | bytes 196616 | tf_op jit(solution)/shard_map/second/ppermute | solution.py:285
  131.2 9.3 %collective-permute-start.11 = (bf16[64,512]{1,0:T(8,128)(2,1)S(1)}, bf16[64,512]{1,0:T(8,128)(2,1)S(1)}, u32[]{:S(2)}, u32[]{:S(2)}) collective-permute-start(bf16[64,512]{1,0:T(8,128)(2,1)S(1)} %get-tuple-element.19), channel_id=1, source_target_pairs={{0,15},{5,10},{10,5},{15,0},{1,12},{6,11},{11,6},{12,1},{2,13},{7,... | collective-permute-start | bytes 196616 | tf_op jit(solution)/shard_map/second/ppermute | solution.py:285
  140.5 5.0 %collective-permute-start.9 = (bf16[64,512]{1,0:T(8,128)(2,1)S(1)}, bf16[64,512]{1,0:T(8,128)(2,1)S(1)}, u32[]{:S(2)}, u32[]{:S(2)}) collective-permute-start(bf16[64,512]{1,0:T(8,128)(2,1)S(1)} %get-tuple-element.21), channel_id=1, source_target_pairs={{0,5},{5,0},{10,15},{15,10},{1,6},{6,1},{11,12},{12,11},{2,7},{7,2... | collective-permute-start | bytes 196616 | tf_op jit(solution)/shard_map/second/ppermute | solution.py:285
  145.6 7.2 %collective-permute-done.9.p1_ref = bf16[64,512]{1,0:T(8,128)(2,1)S(1)} collective-permute-done((bf16[64,512]{1,0:T(8,128)(2,1)S(1)}, bf16[64,512]{1,0:T(8,128)(2,1)S(1)}, u32[]{:S(2)}, u32[]{:S(2)}) %collective-permute-start.9) | collective-permute-done | bytes 65568 | tf_op jit(solution)/shard_map/second/ppermute | solution.py:285
  (55 shorter events, 13.4 us)
Async XLA Ops:
  7.2 96.7 %all-gather.2.cloned.1.call-start = ((), (), s32[]{:S(2)}) async-start(), calls=%async_computation.4 | async-start | bytes 1114112 | tf_op jit(solution)/shard_map/cotangent/all_gather | solution.py:291
  12.2 8.1 %copy-start.4 = (bf16[48,1024]{1,0:T(8,128)(2,1)S(1)}, bf16[48,1024]{1,0:T(8,128)(2,1)}, u32[]{:S(2)}) copy-start(bf16[48,1024]{1,0:T(8,128)(2,1)} %neigh_ref.2) | copy-start | bytes 294916
  12.2 8.1 %copy-start.5 = (bf16[48,1024]{1,0:T(8,128)(2,1)S(1)}, bf16[48,1024]{1,0:T(8,128)(2,1)}, u32[]{:S(2)}) copy-start(bf16[48,1024]{1,0:T(8,128)(2,1)} %own_ref.2) | copy-start | bytes 294916
  12.2 8.1 %copy-start.6 = (bf16[512,48]{0,1:T(8,128)(2,1)S(1)}, bf16[512,48]{0,1:T(8,128)(2,1)}, u32[]{:S(2)}) copy-start(bf16[512,48]{0,1:T(8,128)(2,1)} %param.15) | copy-start | bytes 147460
  12.2 25.2 %all-to-all-start = ((bf16[32,64,128]{2,1,0:T(8,128)(2,1)}), bf16[32,64,128]{2,1,0:T(8,128)(2,1)S(1)}, u32[]{:S(2)}, u32[]{:S(2)}) async-start(bf16[32,64,128]{2,1,0:T(8,128)(2,1)} %edges.1.late_ref), calls=%async_computation | async-start | bytes 1048576 | tf_op jit(solution)/shard_map/edges/all_to_all | solution.py:276
  20.5 9.0 %collective-permute-start = (bf16[192,256]{1,0:T(8,128)(2,1)S(1)}, bf16[192,256]{1,0:T(8,128)(2,1)S(1)}, u32[]{:S(2)}, u32[]{:S(2)}) collective-permute-start(bf16[192,256]{1,0:T(8,128)(2,1)S(1)} %get-tuple-element.18), channel_id=1, source_target_pairs={{0,1},{1,0},{2,3},{3,2},{4,5},{5,4},{6,7},{7,6},{8,9},{9,8},{10,11... | collective-permute-start | bytes 294920 | tf_op jit(solution)/shard_map/pieces/ppermute | solution.py:281
  24.0 6.6 %collective-permute-start.1 = (bf16[192,256]{1,0:T(8,128)(2,1)S(1)}, bf16[192,256]{1,0:T(8,128)(2,1)S(1)}, u32[]{:S(2)}, u32[]{:S(2)}) collective-permute-start(bf16[192,256]{1,0:T(8,128)(2,1)S(1)} %get-tuple-element.17), channel_id=1, source_target_pairs={{0,2},{1,3},{2,0},{3,1},{4,6},{5,7},{6,4},{7,5},{8,10},{9,11},{10,... | collective-permute-start | bytes 294920 | tf_op jit(solution)/shard_map/pieces/ppermute | solution.py:281
  27.3 10.1 %collective-permute-start.2 = (bf16[192,256]{1,0:T(8,128)(2,1)S(1)}, bf16[192,256]{1,0:T(8,128)(2,1)S(1)}, u32[]{:S(2)}, u32[]{:S(2)}) collective-permute-start(bf16[192,256]{1,0:T(8,128)(2,1)S(1)} %get-tuple-element.16), channel_id=1, source_target_pairs={{0,3},{1,2},{2,1},{3,0},{4,7},{5,6},{6,5},{7,4},{8,11},{9,10},{10,... | collective-permute-start | bytes 294920 | tf_op jit(solution)/shard_map/pieces/ppermute | solution.py:281
  38.8 8.5 %collective-permute-start.3 = (bf16[48,512]{1,0:T(8,128)(2,1)S(1)}, bf16[48,512]{1,0:T(8,128)(2,1)S(1)}, u32[]{:S(2)}, u32[]{:S(2)}) collective-permute-start(bf16[48,512]{1,0:T(8,128)(2,1)S(1)} %mean.1.m0_ref), channel_id=1, source_target_pairs={{0,1},{1,0},{2,3},{3,2},{4,5},{5,4},{6,7},{7,6},{8,9},{9,8},{10,11... | collective-permute-start | bytes 147464 | tf_op jit(solution)/shard_map/mean/ppermute | solution.py:281
  40.7 6.6 %collective-permute-start.4 = (bf16[48,512]{1,0:T(8,128)(2,1)S(1)}, bf16[48,512]{1,0:T(8,128)(2,1)S(1)}, u32[]{:S(2)}, u32[]{:S(2)}) collective-permute-start(bf16[48,512]{1,0:T(8,128)(2,1)S(1)} %mean.1.m0_ref), channel_id=1, source_target_pairs={{0,2},{1,3},{2,0},{3,1},{4,6},{5,7},{6,4},{7,5},{8,10},{9,11},{10,... | collective-permute-start | bytes 147464 | tf_op jit(solution)/shard_map/mean/ppermute | solution.py:281
  45.4 6.2 %collective-permute-start.5 = (bf16[48,512]{1,0:T(8,128)(2,1)S(1)}, bf16[48,512]{1,0:T(8,128)(2,1)S(1)}, u32[]{:S(2)}, u32[]{:S(2)}) collective-permute-start(bf16[48,512]{1,0:T(8,128)(2,1)S(1)} %mean.1.m0_ref), channel_id=1, source_target_pairs={{0,3},{1,2},{2,1},{3,0},{4,7},{5,6},{6,5},{7,4},{8,11},{9,10},{10,... | collective-permute-start | bytes 147464 | tf_op jit(solution)/shard_map/mean/ppermute | solution.py:281
  52.6 12.5 %copy-start.9 = (s32[512]{0:T(512)S(1)}, s32[512]{0:T(512)}, u32[]{:S(2)}) copy-start(s32[512]{0:T(512)} %param.21) | copy-start | bytes 6148
  52.6 14.1 %copy-start.2 = (bf16[64,1024]{1,0:T(8,128)(2,1)S(1)}, bf16[64,1024]{1,0:T(8,128)(2,1)}, u32[]{:S(2)}) copy-start(bf16[64,1024]{1,0:T(8,128)(2,1)} %neigh_ref.3) | copy-start | bytes 393220
  52.6 14.1 %copy-start.3 = (bf16[64,1024]{1,0:T(8,128)(2,1)S(1)}, bf16[64,1024]{1,0:T(8,128)(2,1)}, u32[]{:S(2)}) copy-start(bf16[64,1024]{1,0:T(8,128)(2,1)} %own_ref.3) | copy-start | bytes 393220
  52.6 32.8 %all-to-all-start.1 = ((bf16[4,64,512]{2,1,0:T(8,128)(2,1)}), bf16[4,64,512]{2,1,0:T(8,128)(2,1)S(1)}, u32[]{:S(2)}, u32[]{:S(2)}) async-start(bf16[4,64,512]{2,1,0:T(8,128)(2,1)} %first.1.late_ref), calls=%async_computation.1 | async-start | bytes 524288 | tf_op jit(solution)/shard_map/first/all_to_all | solution.py:276
  66.7 18.8 %copy-start.1 = (bf16[4,128,128]{2,1,0:T(8,128)(2,1)S(1)}, bf16[4,128,128]{2,1,0:T(8,128)(2,1)}, u32[]{:S(2)}) copy-start(bf16[4,128,128]{2,1,0:T(8,128)(2,1)} %values_ref.3) | copy-start | bytes 393220
  86.4 8.4 %collective-permute-start.6 = (bf16[256,256]{1,0:T(8,128)(2,1)S(1)}, bf16[256,256]{1,0:T(8,128)(2,1)S(1)}, u32[]{:S(2)}, u32[]{:S(2)}) collective-permute-start(bf16[256,256]{1,0:T(8,128)(2,1)S(1)} %get-tuple-element.13), channel_id=1, source_target_pairs={{0,1},{1,0},{2,3},{3,2},{4,5},{5,4},{6,7},{7,6},{8,9},{9,8},{10,11... | collective-permute-start | bytes 393224 | tf_op jit(solution)/shard_map/hidden/ppermute | solution.py:281
  88.3 7.4 %collective-permute-start.7 = (bf16[256,256]{1,0:T(8,128)(2,1)S(1)}, bf16[256,256]{1,0:T(8,128)(2,1)S(1)}, u32[]{:S(2)}, u32[]{:S(2)}) collective-permute-start(bf16[256,256]{1,0:T(8,128)(2,1)S(1)} %get-tuple-element.12), channel_id=1, source_target_pairs={{0,2},{1,3},{2,0},{3,1},{4,6},{5,7},{6,4},{7,5},{8,10},{9,11},{10,... | collective-permute-start | bytes 393224 | tf_op jit(solution)/shard_map/hidden/ppermute | solution.py:281
  90.2 13.6 %collective-permute-start.8 = (bf16[256,256]{1,0:T(8,128)(2,1)S(1)}, bf16[256,256]{1,0:T(8,128)(2,1)S(1)}, u32[]{:S(2)}, u32[]{:S(2)}) collective-permute-start(bf16[256,256]{1,0:T(8,128)(2,1)S(1)} %get-tuple-element.11), channel_id=1, source_target_pairs={{0,3},{1,2},{2,1},{3,0},{4,7},{5,6},{6,5},{7,4},{8,11},{9,10},{10,... | collective-permute-start | bytes 393224 | tf_op jit(solution)/shard_map/hidden/ppermute | solution.py:281
  106.2 17.4 %all-to-all-start.2 = ((bf16[32,32,128]{2,1,0:T(8,128)(2,1)}), bf16[32,32,128]{2,1,0:T(8,128)(2,1)S(1)}, u32[]{:S(2)}, u32[]{:S(2)}) async-start(bf16[32,32,128]{2,1,0:T(8,128)(2,1)} %grads.1), calls=%async_computation.2 | async-start | bytes 524288 | tf_op jit(solution)/shard_map/grads/all_to_all | solution.py:276
  124.5 28.9 %all-to-all-start.3 = ((f32[32,32,128]{2,1,0:T(8,128)}), f32[32,32,128]{2,1,0:T(8,128)S(1)}, u32[]{:S(2)}, u32[]{:S(2)}) async-start(f32[32,32,128]{2,1,0:T(8,128)} %spread.2), calls=%async_computation.3 | async-start | bytes 1048576 | tf_op jit(solution)/shard_map/spread/all_to_all | solution.py:276
  129.2 16.3 %collective-permute-start.10 = (bf16[64,512]{1,0:T(8,128)(2,1)S(1)}, bf16[64,512]{1,0:T(8,128)(2,1)S(1)}, u32[]{:S(2)}, u32[]{:S(2)}) collective-permute-start(bf16[64,512]{1,0:T(8,128)(2,1)S(1)} %get-tuple-element.20), channel_id=1, source_target_pairs={{0,10},{5,15},{10,0},{15,5},{1,11},{6,12},{11,1},{12,6},{2,8},{7,1... | collective-permute-start | bytes 196616 | tf_op jit(solution)/shard_map/second/ppermute | solution.py:285
  131.2 14.4 %collective-permute-start.11 = (bf16[64,512]{1,0:T(8,128)(2,1)S(1)}, bf16[64,512]{1,0:T(8,128)(2,1)S(1)}, u32[]{:S(2)}, u32[]{:S(2)}) collective-permute-start(bf16[64,512]{1,0:T(8,128)(2,1)S(1)} %get-tuple-element.19), channel_id=1, source_target_pairs={{0,15},{5,10},{10,5},{15,0},{1,12},{6,11},{11,6},{12,1},{2,13},{7,... | collective-permute-start | bytes 196616 | tf_op jit(solution)/shard_map/second/ppermute | solution.py:285
  140.5 12.3 %collective-permute-start.9 = (bf16[64,512]{1,0:T(8,128)(2,1)S(1)}, bf16[64,512]{1,0:T(8,128)(2,1)S(1)}, u32[]{:S(2)}, u32[]{:S(2)}) collective-permute-start(bf16[64,512]{1,0:T(8,128)(2,1)S(1)} %get-tuple-element.21), channel_id=1, source_target_pairs={{0,5},{5,0},{10,15},{15,10},{1,6},{6,1},{11,12},{12,11},{2,7},{7,2... | collective-permute-start | bytes 196616 | tf_op jit(solution)/shard_map/second/ppermute | solution.py:285
  (6 other events, 9.2 us)
Sparse Core Ops, SparseCore 0:
  10.1 72.5 all-gather.1

commit v15 on v12

--- a/solution.py
+++ b/solution.py
@@ -86,7 +86,9 @@
     return sets
 
 
-def first_pieces_kernel(block_ref, neigh_ref, own_ref, self_ref, late_ref, out_ref):
+def first_pieces_kernel(
+    block_ref, neigh_ref, own_ref, self_ref, cot_ref, late_ref, out_ref, cot_out_ref
+):
     del late_ref
     rows = neigh_ref.shape[0]
     group, _, width = out_ref.shape
@@ -96,6 +98,7 @@
         out_ref[to, :rows, : width // 2] = neigh
         out_ref[to, :rows, width // 2 :] = own
         out_ref[to, rows:, :] = self_ref[...]
+    cot_out_ref[...] = cot_ref[...]
 
 
 def second_pieces_kernel(block_ref, neigh_ref, own_ref, late_ref, out_ref):
@@ -108,7 +111,8 @@
         out_ref[to, :, width // 2 :] = own
 
 
-def mean_kernel(cols, recv_ref, pieces_ref, out_ref):
+def mean_kernel(cols, recv_ref, pieces_ref, late_ref, out_ref):
+    del late_ref
     groups, rows, cap = recv_ref.shape
     targets = out_ref.shape[2]
     half = targets // 2
@@ -128,7 +132,7 @@
         out_ref[j, cols:, :] = pieces_ref[j]
 
 
-def first_kernel(got_ref, cot_ref, out_ref, weight, acts):
+def first_kernel(got_ref, out_ref, weight, acts):
     group, rows, targets = got_ref.shape
     rows = rows // 3
     width = targets // 2
@@ -139,17 +143,16 @@
         weight[mid:high, :] = got_ref[j, rows : 2 * rows, width:]
         acts[mid:high, :] = got_ref[j, 2 * rows :, :]
     total = lax.dot_general(weight[...], acts[...], TN, preferred_element_type=F32)
-    cols = cot_ref.shape[0]
+    cols = out_ref.shape[1]
     for z in range(out_ref.shape[0]):
-        out_ref[z, :cols, :] = total[z * cols : (z + 1) * cols, :].astype(BF)
-        out_ref[z, cols:, :] = cot_ref[...]
+        out_ref[z] = total[z * cols : (z + 1) * cols, :].astype(BF)
 
 
 def hidden_kernel(parts_ref, bias_ref, pieces_ref, out_ref):
     cols = bias_ref.shape[0]
-    total = parts_ref[0, :cols, :].astype(F32)
+    total = parts_ref[0].astype(F32)
     for k in range(1, parts_ref.shape[0]):
-        total = total + parts_ref[k, :cols, :].astype(F32)
+        total = total + parts_ref[k].astype(F32)
     hidden = jnp.maximum(total + bias_ref[...], 0.0).astype(BF)
     for c in range(out_ref.shape[0]):
         out_ref[c, :cols, :] = hidden
@@ -157,7 +160,7 @@
 
 
 def grad_kernel(
-    index_ref, got_ref, values_ref, live_ref, parts_ref, agg_ref, out_ref, left, source, acc
+    index_ref, got_ref, values_ref, live_ref, cot_ref, agg_ref, out_ref, left, source, acc
 ):
     group, cols, targets = got_ref.shape
     cols = cols // 2
@@ -180,12 +183,11 @@
         agg_ref[:, at] = tile
         left[:wide, at] = tile * live[:, at]
         left[wide:, at] = source[t] * live[:, at]
-    right = jnp.concatenate([parts_ref[z, cols:, :] for z in range(parts_ref.shape[0])], axis=0)
-    block = lax.dot_general(left[...], right, NT, preferred_element_type=F32)
+    block = lax.dot_general(left[...], cot_ref[...], NT, preferred_element_type=F32)
     at = 0
     for w in range(2):
         for r in range(0, cols, 8):
-            for c in range(0, right.shape[0], 128):
+            for c in range(0, cot_ref.shape[0], 128):
                 rows_of = [
                     block[w * wide + j * cols + r : w * wide + j * cols + r + 8, c : c + 128]
                     for j in range(group)
@@ -194,7 +196,7 @@
                 at += 1
 
 
-def second_kernel(agg_ref, got_ref, out_ref, weight, acts):
+def second_kernel(block_ref, agg_ref, got_ref, out_ref, weight, acts):
     group, rows, targets = got_ref.shape
     rows = rows // 2
     width = targets // 2
@@ -207,14 +209,16 @@
     total = lax.dot_general(weight[...], acts[...], TN, preferred_element_type=F32)
     n, cols, _ = out_ref.shape
     for z in range(n):
-        out_ref[z] = total[z * cols : (z + 1) * cols, :].astype(BF)
-
-
-def sum_kernel(terms_ref, out_ref):
+        out_ref[jnp.bitwise_xor(block_ref[0], z)] = total[z * cols : (z + 1) * cols, :].astype(BF)
+
+
+def copies_kernel(terms_ref, late1_ref, late2_ref, out_ref):
+    del late1_ref, late2_ref
     total = terms_ref[0].astype(F32)
     for d in range(1, terms_ref.shape[0]):
         total = total + terms_ref[d].astype(F32)
-    out_ref[...] = total
+    for d in range(out_ref.shape[0]):
+        out_ref[d] = total
 
 
 def place_kernel(block_ref, pieces_ref, neigh_ref, self_ref):
@@ -239,10 +243,9 @@
                 at += 1
 
 
-def out_kernel(parts_ref, bias_ref, live_ref, out_ref):
-    total = parts_ref[0].astype(F32)
-    for k in range(1, parts_ref.shape[0]):
-        total = total + parts_ref[k].astype(F32)
+def out_kernel(p0_ref, p1_ref, p2_ref, p3_ref, bias_ref, live_ref, out_ref):
+    total = p0_ref[...].astype(F32) + p1_ref[...].astype(F32)
+    total = total + (p2_ref[...].astype(F32) + p3_ref[...].astype(F32))
     out_ref[...] = ((total + bias_ref[...]) * live_ref[...]).astype(BF)
 
 
@@ -278,6 +281,10 @@
             x, axis, split_axis=0, concat_axis=0, tiled=True, axis_index_groups=among
         )
 
+    def trade_far(x, k):
+        pairs = [(group[i], group[i ^ k]) for group in far for i in range(blocks)]
+        return lax.ppermute(x, FEAT, pairs)
+
     def shape(*dims, dtype=BF):
         return jax.ShapeDtypeStruct(dims, dtype)
 
@@ -292,32 +299,34 @@
         )(edge_feats.T, edge_dst.reshape(-1, 128))
         recv = swap(send, "dp")
     with jax.named_scope("pieces"):
-        pieces = call(
+        pieces, cot = call(
             first_pieces_kernel,
-            shape(GROUP, 2 * cols, targets),
-            5,
+            (shape(GROUP, 2 * cols, targets), shape(hid, targets)),
+            6,
             smem=(0,),
-            late=(4,),
+            late=(5,),
             nbytes=2 << 20,
-        )(block, neigh_one, self_one, self_feats.T, send)
+        )(block, neigh_one, self_one, self_feats.T, cotangent.T, send)
+        cot = lax.all_gather(cot, FEAT, axis=0, tiled=True, axis_index_groups=far)
     with jax.named_scope("mean"):
         acts = call(
             functools.partial(mean_kernel, cols),
             shape(GROUP, 3 * cols, targets),
-            2,
+            3,
+            late=(2,),
             flops=2 * groups * ROWS * cap * targets,
             nbytes=8 << 20,
-        )(recv, pieces)
+        )(recv, pieces, cot)
         acts = swap(acts, "mem")
     with jax.named_scope("first"):
         first = call(
             first_kernel,
-            shape(blocks, 2 * hid, targets),
-            2,
+            shape(blocks, hid, targets),
+            1,
             scratch=[pltpu.VMEM((8 * cols, wide), BF), pltpu.VMEM((8 * cols, targets), BF)],
             flops=2 * 8 * cols * wide * targets,
             nbytes=2 << 20,
-        )(acts, cotangent.T)
+        )(acts)
         parts = swap(first, FEAT, far)
     with jax.named_scope("pieces"):
         pieces = call(
@@ -346,26 +355,31 @@
             smem=(0,),
             flops=2 * 2 * wide * targets * wide,
             nbytes=4 << 20,
-        )(tile_index, hidden, tile_values, live, parts)
+        )(tile_index, hidden, tile_values, live, cot)
         terms = swap(terms.reshape(GROUP * groups, 8, 128), ("dp", "mem"))
-        mine = call(sum_kernel, shape(GROUP * 8, 128, dtype=F32), 1, nbytes=1 << 20)(
-            terms.reshape(groups, GROUP * 8, 128)
-        )
     with jax.named_scope("second"):
         second = call(
             second_kernel,
             shape(blocks, hid, targets),
-            2,
+            3,
             scratch=[pltpu.VMEM((2 * wide, wide), BF), pltpu.VMEM((2 * wide, targets), BF)],
+            smem=(0,),
             flops=2 * 2 * wide * wide * targets,
             nbytes=2 << 20,
-        )(agg, hidden)
-        second = swap(second, FEAT, far)
-        second_out = call(out_kernel, shape(hid, targets), 3, nbytes=1 << 20)(
-            second, bias_two.reshape(hid, 1), live
+        )(block, agg, hidden)
+        sums = [second[0]] + [trade_far(second[k], k) for k in range(1, blocks)]
+        second_out = call(out_kernel, shape(hid, targets), 6, nbytes=1 << 20)(
+            *sums, bias_two.reshape(hid, 1), live
         ).T
     with jax.named_scope("place"):
-        spread = lax.all_gather(mine, "dp", axis=0)
+        spread = call(
+            copies_kernel,
+            shape(groups, GROUP * 8, 128, dtype=F32),
+            3,
+            late=(1, 2),
+            nbytes=1 << 20,
+        )(terms.reshape(groups, GROUP * 8, 128), second, sums[1])
+        spread = swap(spread, "dp")
         grad_neigh, grad_self = call(
             place_kernel,
             (shape(hid, full, dtype=F32), shape(hid, full, dtype=F32)),

time: 179 us -> 155 us (0.87)
  the two profiles are of different devices: /device:TPU:1 before, /device:TPU:2 now
where the time goes in v15:
time: 155 us; the launch traced here: 154 us
  starting transfers between devices  52 us (34%)
  blocking collectives  44.2 us (29%)
  waiting for transfers between devices  42.5 us (27%)
  Pallas kernels  11.6 us (7%)
  local copies, waits for them, and re-layouts  3.28 us (2%)
    all_to_all x5, starting transfers between devices, swap(): lax.all_to_all(x, axis, split_axis=0, concat_axis=0, tiled=True, axis_ind...  39.3 us
    all_gather x1, blocking collectives, body(): cot = lax.all_gather(cot, FEAT, axis=0, tiled=True, axis_index_groups=far)  28.8 us
    all_to_all x5, waiting for transfers between devices, swap(): lax.all_to_all(x, axis, split_axis=0, concat_axis=0, tiled=True, axis_ind...  23.7 us
    ppermute x3, waiting for transfers between devices, trade_far(): return lax.ppermute(x, FEAT, pairs)  18.8 us
    all_to_all x1, blocking collectives, swap(): lax.all_to_all(x, axis, split_axis=0, concat_axis=0, tiled=True, axis_ind...  15.4 us
    ppermute x3, starting transfers between devices, trade_far(): return lax.ppermute(x, FEAT, pairs)  12.8 us
    pallas_call x1, Pallas kernels, body(): call(functools.partial(pack_kernel, groups, targets), shape(groups, ROWS,...  3.34 us
  transfers between devices with their start and end apart: 8, of which 5 were waited for; matrix products, arithmetic and copies ran while one was open for 0% of the time, Pallas kernels for 1%

profile of v15, /device:TPU:2, one launch (start us, length us, event | category | flops | bytes accessed | tf_op | source)
XLA Modules:
  0.0 154.4 jit_solution(1343008116340975993)
XLA Ops:
  0.6 0.9 copy-done.7
  2.3 3.3 %edges.1.late_ref = bf16[32,64,128]{2,1,0:T(8,128)(2,1)} custom-call(bf16[48,2048]{1,0:T(8,128)(2,1)S(1)} %bitcast.24, s32[16,128]{1,0:T(8,128)S(1)} %bitcast.25), custom_call_target="tpu_custom_call" | custom-call | flops 1073741824 | bytes 8388608 | tf_op jit(solution)/shard_map/edges/pallas_call | solution.py:292
  5.6 9.6 %all-to-all-start = ((bf16[32,64,128]{2,1,0:T(8,128)(2,1)}), bf16[32,64,128]{2,1,0:T(8,128)(2,1)S(1)}, u32[]{:S(2)}, u32[]{:S(2)}) async-start(bf16[32,64,128]{2,1,0:T(8,128)(2,1)} %edges.1.late_ref), calls=%async_computation | async-start | bytes 1048576 | tf_op jit(solution)/shard_map/edges/all_to_all | solution.py:280
  15.4 28.8 %all_gather.3.late_ref.cot_ref = bf16[256,512]{1,0:T(8,128)(2,1)S(1)} all-gather(bf16[64,512]{1,0:T(8,128)(2,1)S(1)} %get-tuple-element.10), channel_id=1, replica_groups={{0,5,10,15},{1,6,11,12},{2,7,8,13},{3,4,9,14},{16,21,26,31},{17,22,27,2..., dimensions={0}, use_global_device_ids=true | all-gather | bytes 327680 | tf_op jit(solution)/shard_map/pieces/all_gather | solution.py:310
  44.2 1.4 mean.1
  45.6 15.4 %all_to_all.30.got_ref = bf16[4,144,512]{2,1,0:T(8,128)(2,1)S(1)} all-to-all(bf16[4,144,512]{2,1,0:T(8,128)(2,1)S(1)} %mean.1), channel_id=1, replica_groups=mesh['dp'=32,'blk'=4,'mem'=4] {'mem'}, dimensions={0} | all-to-all | bytes 1179648 | tf_op jit(solution)/shard_map/mean/all_to_all | solution.py:280
  61.0 1.0 first.1.late_ref
  62.0 4.4 %all-to-all-start.2 = ((bf16[4,64,512]{2,1,0:T(8,128)(2,1)}), bf16[4,64,512]{2,1,0:T(8,128)(2,1)S(1)}, u32[]{:S(2)}, u32[]{:S(2)}) async-start(bf16[4,64,512]{2,1,0:T(8,128)(2,1)} %first.1.late_ref), calls=%async_computation.2 | async-start | bytes 524288 | tf_op jit(solution)/shard_map/first/all_to_all | solution.py:280
  67.3 12.3 %all-to-all-done.2.parts_ref = bf16[4,64,512]{2,1,0:T(8,128)(2,1)S(1)} async-done(((bf16[4,64,512]{2,1,0:T(8,128)(2,1)}), bf16[4,64,512]{2,1,0:T(8,128)(2,1)S(1)}, u32[]{:S(2)}, u32[]{:S(2)}) %all-to-all-start.2) | async-done | bytes 262176 | tf_op jit(solution)/shard_map/first/all_to_all | solution.py:280
  79.6 0.9 hidden.1
  80.5 7.3 %all-to-all-start.3 = ((bf16[4,128,512]{2,1,0:T(8,128)(2,1)}), bf16[4,128,512]{2,1,0:T(8,128)(2,1)S(1)}, u32[]{:S(2)}, u32[]{:S(2)}) async-start(bf16[4,128,512]{2,1,0:T(8,128)(2,1)} %hidden.1), calls=%async_computation.3 | async-start | bytes 1048576 | tf_op jit(solution)/shard_map/hidden/all_to_all | solution.py:280
  88.6 11.4 %all-to-all-done.3.got_ref = bf16[4,128,512]{2,1,0:T(8,128)(2,1)S(1)} async-done(((bf16[4,128,512]{2,1,0:T(8,128)(2,1)}), bf16[4,128,512]{2,1,0:T(8,128)(2,1)S(1)}, u32[]{:S(2)}, u32[]{:S(2)}) %all-to-all-start.3) | async-done | bytes 524320 | tf_op jit(solution)/shard_map/hidden/all_to_all | solution.py:280
  100.0 1.8 %grads.1 = (bf16[256,512]{1,0:T(8,128)(2,1)S(1)}, bf16[32,32,128]{2,1,0:T(8,128)(2,1)}) custom-call(s32[4,2]{1,0:T(4,128)S(1)} %copy.17.index_ref, bf16[4,128,512]{2,1,0:T(8,128)(2,1)S(1)} %all-to-all-done.3.got_ref, bf16[4,128,128]{2,1,0:T(8,128)(2,1)S(1)} %copy-done, f32[1,512]{1,0:T(1,128)S(1)} %bitcast.22, bf16[256,512]{1,0:T(8,128)(2,1)S(1)} %all_gather.3.late_ref.cot_ref), custom_call_target="tpu_custom_call" | custom-call | flops 134217728 | bytes 4194304 | tf_op jit(solution)/shard_map/grads/pallas_call | solution.py:346
  101.8 10.2 %all-to-all-start.4 = ((bf16[128,8,128]{2,1,0:T(8,128)(2,1)}), bf16[128,8,128]{2,1,0:T(8,128)(2,1)S(1)}, u32[]{:S(2)}, u32[]{:S(2)}) async-start(bf16[128,8,128]{2,1,0:T(8,128)(2,1)} %bitcast.13), calls=%async_computation.4 | async-start | bytes 524288 | tf_op jit(solution)/shard_map/grads/all_to_all | solution.py:280
  112.4 5.6 %collective-permute-start = (bf16[64,512]{1,0:T(8,128)(2,1)S(1)}, bf16[64,512]{1,0:T(8,128)(2,1)S(1)}, u32[]{:S(2)}, u32[]{:S(2)}) collective-permute-start(bf16[64,512]{1,0:T(8,128)(2,1)S(1)} %get-tuple-element.17), channel_id=1, source_target_pairs={{0,5},{5,0},{10,15},{15,10},{1,6},{6,1},{11,12},{12,11},{2,7},{7,2... | collective-permute-start | bytes 196616 | tf_op jit(solution)/shard_map/second/ppermute | solution.py:286
  118.0 8.5 %collective-permute-done.p1_ref.late2_ref = bf16[64,512]{1,0:T(8,128)(2,1)S(1)} collective-permute-done((bf16[64,512]{1,0:T(8,128)(2,1)S(1)}, bf16[64,512]{1,0:T(8,128)(2,1)S(1)}, u32[]{:S(2)}, u32[]{:S(2)}) %collective-permute-start) | collective-permute-done | bytes 65568 | tf_op jit(solution)/shard_map/second/ppermute | solution.py:286
  126.5 0.9 place.2
  127.4 7.8 %all-to-all-start.5 = ((f32[32,32,128]{2,1,0:T(8,128)}), f32[32,32,128]{2,1,0:T(8,128)S(1)}, u32[]{:S(2)}, u32[]{:S(2)}) async-start(f32[32,32,128]{2,1,0:T(8,128)} %place.2), calls=%async_computation.5 | async-start | bytes 1048576 | tf_op jit(solution)/shard_map/place/all_to_all | solution.py:280
  135.2 3.4 %collective-permute-start.1 = (bf16[64,512]{1,0:T(8,128)(2,1)S(1)}, bf16[64,512]{1,0:T(8,128)(2,1)S(1)}, u32[]{:S(2)}, u32[]{:S(2)}) collective-permute-start(bf16[64,512]{1,0:T(8,128)(2,1)S(1)} %get-tuple-element.16), channel_id=1, source_target_pairs={{0,10},{5,15},{10,0},{15,5},{1,11},{6,12},{11,1},{12,6},{2,8},{7,1... | collective-permute-start | bytes 196616 | tf_op jit(solution)/shard_map/second/ppermute | solution.py:286
  138.7 3.7 %collective-permute-start.2 = (bf16[64,512]{1,0:T(8,128)(2,1)S(1)}, bf16[64,512]{1,0:T(8,128)(2,1)S(1)}, u32[]{:S(2)}, u32[]{:S(2)}) collective-permute-start(bf16[64,512]{1,0:T(8,128)(2,1)S(1)} %get-tuple-element.15), channel_id=1, source_target_pairs={{0,15},{5,10},{10,5},{15,0},{1,12},{6,11},{11,6},{12,1},{2,13},{7,... | collective-permute-start | bytes 196616 | tf_op jit(solution)/shard_map/second/ppermute | solution.py:286
  142.5 6.6 %collective-permute-done.1.p2_ref = bf16[64,512]{1,0:T(8,128)(2,1)S(1)} collective-permute-done((bf16[64,512]{1,0:T(8,128)(2,1)S(1)}, bf16[64,512]{1,0:T(8,128)(2,1)S(1)}, u32[]{:S(2)}, u32[]{:S(2)}) %collective-permute-start.1) | collective-permute-done | bytes 65568 | tf_op jit(solution)/shard_map/second/ppermute | solution.py:286
  149.1 3.7 %collective-permute-done.2.p3_ref = bf16[64,512]{1,0:T(8,128)(2,1)S(1)} collective-permute-done((bf16[64,512]{1,0:T(8,128)(2,1)S(1)}, bf16[64,512]{1,0:T(8,128)(2,1)S(1)}, u32[]{:S(2)}, u32[]{:S(2)}) %collective-permute-start.2) | collective-permute-done | bytes 65568 | tf_op jit(solution)/shard_map/second/ppermute | solution.py:286
  152.8 0.7 second.3
  153.5 0.9 place.3
  (36 shorter events, 3.0 us)
Async XLA Ops:
  0.6 0.9 copy-start.7
  1.6 0.7 copy-start.8
  5.6 9.6 %copy-start.3 = (bf16[48,1024]{1,0:T(8,128)(2,1)S(1)}, bf16[48,1024]{1,0:T(8,128)(2,1)}, u32[]{:S(2)}) copy-start(bf16[48,1024]{1,0:T(8,128)(2,1)} %neigh_ref.2) | copy-start | bytes 294916
  5.6 9.6 %copy-start.4 = (bf16[48,1024]{1,0:T(8,128)(2,1)S(1)}, bf16[48,1024]{1,0:T(8,128)(2,1)}, u32[]{:S(2)}) copy-start(bf16[48,1024]{1,0:T(8,128)(2,1)} %own_ref.2) | copy-start | bytes 294916
  5.6 9.6 %copy-start.5 = (bf16[512,64]{0,1:T(8,128)(2,1)S(1)}, bf16[512,64]{0,1:T(8,128)(2,1)}, u32[]{:S(2)}) copy-start(bf16[512,64]{0,1:T(8,128)(2,1)} %param.25) | copy-start | bytes 196612
  5.6 9.6 %copy-start.6 = (bf16[512,48]{0,1:T(8,128)(2,1)S(1)}, bf16[512,48]{0,1:T(8,128)(2,1)}, u32[]{:S(2)}) copy-start(bf16[512,48]{0,1:T(8,128)(2,1)} %param.15) | copy-start | bytes 147460
  5.6 38.6 %all-to-all-start = ((bf16[32,64,128]{2,1,0:T(8,128)(2,1)}), bf16[32,64,128]{2,1,0:T(8,128)(2,1)S(1)}, u32[]{:S(2)}, u32[]{:S(2)}) async-start(bf16[32,64,128]{2,1,0:T(8,128)(2,1)} %edges.1.late_ref), calls=%async_computation | async-start | bytes 1048576 | tf_op jit(solution)/shard_map/edges/all_to_all | solution.py:280
  62.0 5.1 %copy-start.1 = (bf16[64,1024]{1,0:T(8,128)(2,1)S(1)}, bf16[64,1024]{1,0:T(8,128)(2,1)}, u32[]{:S(2)}) copy-start(bf16[64,1024]{1,0:T(8,128)(2,1)} %neigh_ref.3) | copy-start | bytes 393220
  62.0 5.1 %copy-start.2 = (bf16[64,1024]{1,0:T(8,128)(2,1)S(1)}, bf16[64,1024]{1,0:T(8,128)(2,1)}, u32[]{:S(2)}) copy-start(bf16[64,1024]{1,0:T(8,128)(2,1)} %own_ref.3) | copy-start | bytes 393220
  62.0 17.6 %all-to-all-start.2 = ((bf16[4,64,512]{2,1,0:T(8,128)(2,1)}), bf16[4,64,512]{2,1,0:T(8,128)(2,1)S(1)}, u32[]{:S(2)}, u32[]{:S(2)}) async-start(bf16[4,64,512]{2,1,0:T(8,128)(2,1)} %first.1.late_ref), calls=%async_computation.2 | async-start | bytes 524288 | tf_op jit(solution)/shard_map/first/all_to_all | solution.py:280
  66.4 0.7 copy-start.11
  80.5 7.3 %copy-start.9 = (s32[512]{0:T(512)S(1)}, s32[512]{0:T(512)}, u32[]{:S(2)}) copy-start(s32[512]{0:T(512)} %param.21) | copy-start | bytes 6148
  80.5 19.5 %copy-start = (bf16[4,128,128]{2,1,0:T(8,128)(2,1)S(1)}, bf16[4,128,128]{2,1,0:T(8,128)(2,1)}, u32[]{:S(2)}) copy-start(bf16[4,128,128]{2,1,0:T(8,128)(2,1)} %values_ref.1) | copy-start | bytes 393220
  80.5 19.5 %all-to-all-start.3 = ((bf16[4,128,512]{2,1,0:T(8,128)(2,1)}), bf16[4,128,512]{2,1,0:T(8,128)(2,1)S(1)}, u32[]{:S(2)}, u32[]{:S(2)}) async-start(bf16[4,128,512]{2,1,0:T(8,128)(2,1)} %hidden.1), calls=%async_computation.3 | async-start | bytes 1048576 | tf_op jit(solution)/shard_map/hidden/all_to_all | solution.py:280
  87.8 0.7 copy-start.10
  101.8 24.7 %all-to-all-start.4 = ((bf16[128,8,128]{2,1,0:T(8,128)(2,1)}), bf16[128,8,128]{2,1,0:T(8,128)(2,1)S(1)}, u32[]{:S(2)}, u32[]{:S(2)}) async-start(bf16[128,8,128]{2,1,0:T(8,128)(2,1)} %bitcast.13), calls=%async_computation.4 | async-start | bytes 524288 | tf_op jit(solution)/shard_map/grads/all_to_all | solution.py:280
  112.4 14.1 %collective-permute-start = (bf16[64,512]{1,0:T(8,128)(2,1)S(1)}, bf16[64,512]{1,0:T(8,128)(2,1)S(1)}, u32[]{:S(2)}, u32[]{:S(2)}) collective-permute-start(bf16[64,512]{1,0:T(8,128)(2,1)S(1)} %get-tuple-element.17), channel_id=1, source_target_pairs={{0,5},{5,0},{10,15},{15,10},{1,6},{6,1},{11,12},{12,11},{2,7},{7,2... | collective-permute-start | bytes 196616 | tf_op jit(solution)/shard_map/second/ppermute | solution.py:286
  127.4 26.1 %all-to-all-start.5 = ((f32[32,32,128]{2,1,0:T(8,128)}), f32[32,32,128]{2,1,0:T(8,128)S(1)}, u32[]{:S(2)}, u32[]{:S(2)}) async-start(f32[32,32,128]{2,1,0:T(8,128)} %place.2), calls=%async_computation.5 | async-start | bytes 1048576 | tf_op jit(solution)/shard_map/place/all_to_all | solution.py:280
  135.2 13.9 %collective-permute-start.1 = (bf16[64,512]{1,0:T(8,128)(2,1)S(1)}, bf16[64,512]{1,0:T(8,128)(2,1)S(1)}, u32[]{:S(2)}, u32[]{:S(2)}) collective-permute-start(bf16[64,512]{1,0:T(8,128)(2,1)S(1)} %get-tuple-element.16), channel_id=1, source_target_pairs={{0,10},{5,15},{10,0},{15,5},{1,11},{6,12},{11,1},{12,6},{2,8},{7,1... | collective-permute-start | bytes 196616 | tf_op jit(solution)/shard_map/second/ppermute | solution.py:286
  138.7 3.7 %copy-start.12 = (f32[64]{0:T(128)S(1)}, f32[64]{0:T(128)}, u32[]{:S(2)}) copy-start(f32[64]{0:T(128)} %param.24) | copy-start | bytes 772
  138.7 14.1 %collective-permute-start.2 = (bf16[64,512]{1,0:T(8,128)(2,1)S(1)}, bf16[64,512]{1,0:T(8,128)(2,1)S(1)}, u32[]{:S(2)}, u32[]{:S(2)}) collective-permute-start(bf16[64,512]{1,0:T(8,128)(2,1)S(1)} %get-tuple-element.15), channel_id=1, source_target_pairs={{0,15},{5,10},{10,5},{15,0},{1,12},{6,11},{11,6},{12,1},{2,13},{7,... | collective-permute-start | bytes 196616 | tf_op jit(solution)/shard_map/second/ppermute | solution.py:286

commit v16 on v15

--- a/solution.py
+++ b/solution.py
@@ -86,9 +86,7 @@
     return sets
 
 
-def first_pieces_kernel(
-    block_ref, neigh_ref, own_ref, self_ref, cot_ref, late_ref, out_ref, cot_out_ref
-):
+def first_pieces_kernel(block_ref, neigh_ref, own_ref, self_ref, late_ref, out_ref):
     del late_ref
     rows = neigh_ref.shape[0]
     group, _, width = out_ref.shape
@@ -98,7 +96,6 @@
         out_ref[to, :rows, : width // 2] = neigh
         out_ref[to, :rows, width // 2 :] = own
         out_ref[to, rows:, :] = self_ref[...]
-    cot_out_ref[...] = cot_ref[...]
 
 
 def second_pieces_kernel(block_ref, neigh_ref, own_ref, late_ref, out_ref):
@@ -111,8 +108,7 @@
         out_ref[to, :, width // 2 :] = own
 
 
-def mean_kernel(cols, recv_ref, pieces_ref, late_ref, out_ref):
-    del late_ref
+def mean_kernel(cols, recv_ref, pieces_ref, out_ref):
     groups, rows, cap = recv_ref.shape
     targets = out_ref.shape[2]
     half = targets // 2
@@ -299,24 +295,22 @@
         )(edge_feats.T, edge_dst.reshape(-1, 128))
         recv = swap(send, "dp")
     with jax.named_scope("pieces"):
-        pieces, cot = call(
+        pieces = call(
             first_pieces_kernel,
-            (shape(GROUP, 2 * cols, targets), shape(hid, targets)),
-            6,
+            shape(GROUP, 2 * cols, targets),
+            5,
             smem=(0,),
-            late=(5,),
+            late=(4,),
             nbytes=2 << 20,
-        )(block, neigh_one, self_one, self_feats.T, cotangent.T, send)
-        cot = lax.all_gather(cot, FEAT, axis=0, tiled=True, axis_index_groups=far)
+        )(block, neigh_one, self_one, self_feats.T, send)
     with jax.named_scope("mean"):
         acts = call(
             functools.partial(mean_kernel, cols),
             shape(GROUP, 3 * cols, targets),
-            3,
-            late=(2,),
+            2,
             flops=2 * groups * ROWS * cap * targets,
             nbytes=8 << 20,
-        )(recv, pieces, cot)
+        )(recv, pieces)
         acts = swap(acts, "mem")
     with jax.named_scope("first"):
         first = call(
@@ -342,6 +336,8 @@
             parts, bias_one.reshape(hid, 1), pieces
         )
         hidden = swap(hidden, "mem")
+    with jax.named_scope("cotangent"):
+        cot = lax.all_gather(cotangent.T, FEAT, axis=0, tiled=True, axis_index_groups=far)
     with jax.named_scope("grads"):
         agg, terms = call(
             grad_kernel,

time: 155 us -> 166 us (1.071)
  the two profiles are of different devices: /device:TPU:2 before, /device:TPU:98 now
where the time goes in v16:
time: 166 us; the launch traced here: 165 us
  starting transfers between devices  62.1 us (37%)
  blocking collectives  44.7 us (27%)
  waiting for transfers between devices  42.8 us (26%)
  Pallas kernels  11.6 us (7%)
  local copies, waits for them, and re-layouts  3.28 us (2%)
    all_to_all x5, starting transfers between devices, swap(): lax.all_to_all(x, axis, split_axis=0, concat_axis=0, tiled=True, axis_ind...  42.6 us
    all_to_all x5, waiting for transfers between devices, swap(): lax.all_to_all(x, axis, split_axis=0, concat_axis=0, tiled=True, axis_ind...  28.1 us
    all_gather x1, blocking collectives, body(): lax.all_gather(cotangent.T, FEAT, axis=0, tiled=True, axis_index_groups=far)  25.8 us
    ppermute x3, starting transfers between devices, trade_far(): return lax.ppermute(x, FEAT, pairs)  19.5 us
    all_to_all x1, blocking collectives, swap(): lax.all_to_all(x, axis, split_axis=0, concat_axis=0, tiled=True, axis_ind...  19 us
    ppermute x3, waiting for transfers between devices, trade_far(): return lax.ppermute(x, FEAT, pairs)  14.7 us
    pallas_call x1, Pallas kernels, body(): call(functools.partial(pack_kernel, groups, targets), shape(groups, ROWS,...  3.34 us
  transfers between devices with their start and end apart: 8, of which 6 were waited for; matrix products, arithmetic and copies ran while one was open for 0% of the time, Pallas kernels for 1%

profile of v16, /device:TPU:98, one launch (start us, length us, event | category | flops | bytes accessed | tf_op | source)
XLA Modules:
  0.0 165.3 jit_solution(17218243018129208036)
XLA Ops:
  0.6 0.9 copy-done.6
  2.3 3.3 %edges.1.late_ref = bf16[32,64,128]{2,1,0:T(8,128)(2,1)} custom-call(bf16[48,2048]{1,0:T(8,128)(2,1)S(1)} %bitcast.23, s32[16,128]{1,0:T(8,128)S(1)} %bitcast.24), custom_call_target="tpu_custom_call" | custom-call | flops 1073741824 | bytes 8388608 | tf_op jit(solution)/shard_map/edges/pallas_call | solution.py:288
  5.6 7.8 %all-to-all-start = ((bf16[32,64,128]{2,1,0:T(8,128)(2,1)}), bf16[32,64,128]{2,1,0:T(8,128)(2,1)S(1)}, u32[]{:S(2)}, u32[]{:S(2)}) async-start(bf16[32,64,128]{2,1,0:T(8,128)(2,1)} %edges.1.late_ref), calls=%async_computation | async-start | bytes 1048576 | tf_op jit(solution)/shard_map/edges/all_to_all | solution.py:276
  13.5 10.3 %all-to-all-done.recv_ref = bf16[32,64,128]{2,1,0:T(8,128)(2,1)S(1)} async-done(((bf16[32,64,128]{2,1,0:T(8,128)(2,1)}), bf16[32,64,128]{2,1,0:T(8,128)(2,1)S(1)}, u32[]{:S(2)}, u32[]{:S(2)}) %all-to-all-start) | async-done | bytes 524320 | tf_op jit(solution)/shard_map/edges/all_to_all | solution.py:276
  23.9 1.4 mean.1
  25.3 19.0 %all_to_all.30.got_ref = bf16[4,144,512]{2,1,0:T(8,128)(2,1)S(1)} all-to-all(bf16[4,144,512]{2,1,0:T(8,128)(2,1)S(1)} %mean.1), channel_id=1, replica_groups=mesh['dp'=32,'blk'=4,'mem'=4] {'mem'}, dimensions={0} | all-to-all | bytes 1179648 | tf_op jit(solution)/shard_map/mean/all_to_all | solution.py:276
  44.2 1.0 first.1.late_ref
  45.3 11.4 %all-to-all-start.2 = ((bf16[4,64,512]{2,1,0:T(8,128)(2,1)}), bf16[4,64,512]{2,1,0:T(8,128)(2,1)S(1)}, u32[]{:S(2)}, u32[]{:S(2)}) async-start(bf16[4,64,512]{2,1,0:T(8,128)(2,1)} %first.1.late_ref), calls=%async_computation.2 | async-start | bytes 524288 | tf_op jit(solution)/shard_map/first/all_to_all | solution.py:276
  57.6 16.0 %all-to-all-done.2.parts_ref = bf16[4,64,512]{2,1,0:T(8,128)(2,1)S(1)} async-done(((bf16[4,64,512]{2,1,0:T(8,128)(2,1)}), bf16[4,64,512]{2,1,0:T(8,128)(2,1)S(1)}, u32[]{:S(2)}, u32[]{:S(2)}) %all-to-all-start.2) | async-done | bytes 262176 | tf_op jit(solution)/shard_map/first/all_to_all | solution.py:276
  73.6 0.9 hidden.1
  74.5 6.3 %all-to-all-start.3 = ((bf16[4,128,512]{2,1,0:T(8,128)(2,1)}), bf16[4,128,512]{2,1,0:T(8,128)(2,1)S(1)}, u32[]{:S(2)}, u32[]{:S(2)}) async-start(bf16[4,128,512]{2,1,0:T(8,128)(2,1)} %hidden.1), calls=%async_computation.3 | async-start | bytes 1048576 | tf_op jit(solution)/shard_map/hidden/all_to_all | solution.py:276
  81.6 25.8 %all_gather.3.cot_ref = bf16[256,512]{1,0:T(8,128)(2,1)S(1)} all-gather(bf16[64,512]{1,0:T(8,128)(2,1)S(1)} %bitcast.25), channel_id=1, replica_groups={{0,5,10,15},{1,6,11,12},{2,7,8,13},{3,4,9,14},{16,21,26,31},{17,22,27,2..., dimensions={0}, use_global_device_ids=true | all-gather | bytes 327680 | tf_op jit(solution)/shard_map/cotangent/all_gather | solution.py:340
  107.4 1.9 %grads.1 = (bf16[256,512]{1,0:T(8,128)(2,1)S(1)}, bf16[32,32,128]{2,1,0:T(8,128)(2,1)}) custom-call(s32[4,2]{1,0:T(4,128)S(1)} %copy.17.index_ref, bf16[4,128,512]{2,1,0:T(8,128)(2,1)S(1)} %all-to-all-done.3.got_ref, bf16[4,128,128]{2,1,0:T(8,128)(2,1)S(1)} %copy-done, f32[1,512]{1,0:T(1,128)S(1)} %bitcast.21, bf16[256,512]{1,0:T(8,128)(2,1)S(1)} %all_gather.3.cot_ref), custom_call_target="tpu_custom_call" | custom-call | flops 134217728 | bytes 4194304 | tf_op jit(solution)/shard_map/grads/pallas_call | solution.py:342
  109.2 11.0 %all-to-all-start.4 = ((bf16[128,8,128]{2,1,0:T(8,128)(2,1)}), bf16[128,8,128]{2,1,0:T(8,128)(2,1)S(1)}, u32[]{:S(2)}, u32[]{:S(2)}) async-start(bf16[128,8,128]{2,1,0:T(8,128)(2,1)} %bitcast.13), calls=%async_computation.4 | async-start | bytes 524288 | tf_op jit(solution)/shard_map/grads/all_to_all | solution.py:276
  120.6 4.3 %collective-permute-start = (bf16[64,512]{1,0:T(8,128)(2,1)S(1)}, bf16[64,512]{1,0:T(8,128)(2,1)S(1)}, u32[]{:S(2)}, u32[]{:S(2)}) collective-permute-start(bf16[64,512]{1,0:T(8,128)(2,1)S(1)} %get-tuple-element.13), channel_id=1, source_target_pairs={{0,5},{5,0},{10,15},{15,10},{1,6},{6,1},{11,12},{12,11},{2,7},{7,2... | collective-permute-start | bytes 196616 | tf_op jit(solution)/shard_map/second/ppermute | solution.py:282
  124.9 3.7 %collective-permute-done.p1_ref.late2_ref = bf16[64,512]{1,0:T(8,128)(2,1)S(1)} collective-permute-done((bf16[64,512]{1,0:T(8,128)(2,1)S(1)}, bf16[64,512]{1,0:T(8,128)(2,1)S(1)}, u32[]{:S(2)}, u32[]{:S(2)}) %collective-permute-start) | collective-permute-done | bytes 65568 | tf_op jit(solution)/shard_map/second/ppermute | solution.py:282
  128.6 1.8 %all-to-all-done.4 = bf16[128,8,128]{2,1,0:T(8,128)(2,1)S(1)} async-done(((bf16[128,8,128]{2,1,0:T(8,128)(2,1)}), bf16[128,8,128]{2,1,0:T(8,128)(2,1)S(1)}, u32[]{:S(2)}, u32[]{:S(2)}) %all-to-all-start.4) | async-done | bytes 262176 | tf_op jit(solution)/shard_map/grads/all_to_all | solution.py:276
  130.4 0.9 place.2
  131.3 6.0 %all-to-all-start.5 = ((f32[32,32,128]{2,1,0:T(8,128)}), f32[32,32,128]{2,1,0:T(8,128)S(1)}, u32[]{:S(2)}, u32[]{:S(2)}) async-start(f32[32,32,128]{2,1,0:T(8,128)} %place.2), calls=%async_computation.5 | async-start | bytes 1048576 | tf_op jit(solution)/shard_map/place/all_to_all | solution.py:276
  137.4 10.8 %collective-permute-start.1 = (bf16[64,512]{1,0:T(8,128)(2,1)S(1)}, bf16[64,512]{1,0:T(8,128)(2,1)S(1)}, u32[]{:S(2)}, u32[]{:S(2)}) collective-permute-start(bf16[64,512]{1,0:T(8,128)(2,1)S(1)} %get-tuple-element.12), channel_id=1, source_target_pairs={{0,10},{5,15},{10,0},{15,5},{1,11},{6,12},{11,1},{12,6},{2,8},{7,1... | collective-permute-start | bytes 196616 | tf_op jit(solution)/shard_map/second/ppermute | solution.py:282
  148.2 4.4 %collective-permute-start.2 = (bf16[64,512]{1,0:T(8,128)(2,1)S(1)}, bf16[64,512]{1,0:T(8,128)(2,1)S(1)}, u32[]{:S(2)}, u32[]{:S(2)}) collective-permute-start(bf16[64,512]{1,0:T(8,128)(2,1)S(1)} %get-tuple-element.11), channel_id=1, source_target_pairs={{0,15},{5,10},{10,5},{15,0},{1,12},{6,11},{11,6},{12,1},{2,13},{7,... | collective-permute-start | bytes 196616 | tf_op jit(solution)/shard_map/second/ppermute | solution.py:282
  152.7 1.5 collective-permute-done.1.p2_ref
  154.2 9.5 %collective-permute-done.2.p3_ref = bf16[64,512]{1,0:T(8,128)(2,1)S(1)} collective-permute-done((bf16[64,512]{1,0:T(8,128)(2,1)S(1)}, bf16[64,512]{1,0:T(8,128)(2,1)S(1)}, u32[]{:S(2)}, u32[]{:S(2)}) %collective-permute-start.2) | collective-permute-done | bytes 65568 | tf_op jit(solution)/shard_map/second/ppermute | solution.py:282
  164.4 0.9 place.3
  (36 shorter events, 3.7 us)
Async XLA Ops:
  0.6 0.9 copy-start.6
  1.6 0.7 copy-start.7
  5.6 7.8 %copy-start.3 = (bf16[48,1024]{1,0:T(8,128)(2,1)S(1)}, bf16[48,1024]{1,0:T(8,128)(2,1)}, u32[]{:S(2)}) copy-start(bf16[48,1024]{1,0:T(8,128)(2,1)} %neigh_ref.2) | copy-start | bytes 294916
  5.6 7.8 %copy-start.4 = (bf16[48,1024]{1,0:T(8,128)(2,1)S(1)}, bf16[48,1024]{1,0:T(8,128)(2,1)}, u32[]{:S(2)}) copy-start(bf16[48,1024]{1,0:T(8,128)(2,1)} %own_ref.2) | copy-start | bytes 294916
  5.6 7.8 %copy-start.5 = (bf16[512,48]{0,1:T(8,128)(2,1)S(1)}, bf16[512,48]{0,1:T(8,128)(2,1)}, u32[]{:S(2)}) copy-start(bf16[512,48]{0,1:T(8,128)(2,1)} %param.15) | copy-start | bytes 147460
  5.6 18.3 %all-to-all-start = ((bf16[32,64,128]{2,1,0:T(8,128)(2,1)}), bf16[32,64,128]{2,1,0:T(8,128)(2,1)S(1)}, u32[]{:S(2)}, u32[]{:S(2)}) async-start(bf16[32,64,128]{2,1,0:T(8,128)(2,1)} %edges.1.late_ref), calls=%async_computation | async-start | bytes 1048576 | tf_op jit(solution)/shard_map/edges/all_to_all | solution.py:276
  45.3 12.2 %copy-start.1 = (bf16[64,1024]{1,0:T(8,128)(2,1)S(1)}, bf16[64,1024]{1,0:T(8,128)(2,1)}, u32[]{:S(2)}) copy-start(bf16[64,1024]{1,0:T(8,128)(2,1)} %neigh_ref.3) | copy-start | bytes 393220
  45.3 12.2 %copy-start.2 = (bf16[64,1024]{1,0:T(8,128)(2,1)S(1)}, bf16[64,1024]{1,0:T(8,128)(2,1)}, u32[]{:S(2)}) copy-start(bf16[64,1024]{1,0:T(8,128)(2,1)} %own_ref.3) | copy-start | bytes 393220
  45.3 28.3 %all-to-all-start.2 = ((bf16[4,64,512]{2,1,0:T(8,128)(2,1)}), bf16[4,64,512]{2,1,0:T(8,128)(2,1)S(1)}, u32[]{:S(2)}, u32[]{:S(2)}) async-start(bf16[4,64,512]{2,1,0:T(8,128)(2,1)} %first.1.late_ref), calls=%async_computation.2 | async-start | bytes 524288 | tf_op jit(solution)/shard_map/first/all_to_all | solution.py:276
  56.7 0.7 copy-start.11
  74.5 6.3 %copy-start.9 = (s32[512]{0:T(512)S(1)}, s32[512]{0:T(512)}, u32[]{:S(2)}) copy-start(s32[512]{0:T(512)} %param.21) | copy-start | bytes 6148
  74.5 7.1 %copy-start.8 = (bf16[512,64]{0,1:T(8,128)(2,1)S(1)}, bf16[512,64]{0,1:T(8,128)(2,1)}, u32[]{:S(2)}) copy-start(bf16[512,64]{0,1:T(8,128)(2,1)} %param.25) | copy-start | bytes 196612
  74.5 32.9 %all-to-all-start.3 = ((bf16[4,128,512]{2,1,0:T(8,128)(2,1)}), bf16[4,128,512]{2,1,0:T(8,128)(2,1)S(1)}, u32[]{:S(2)}, u32[]{:S(2)}) async-start(bf16[4,128,512]{2,1,0:T(8,128)(2,1)} %hidden.1), calls=%async_computation.3 | async-start | bytes 1048576 | tf_op jit(solution)/shard_map/hidden/all_to_all | solution.py:276
  80.8 0.7 copy-start.10
  81.6 25.8 %copy-start = (bf16[4,128,128]{2,1,0:T(8,128)(2,1)S(1)}, bf16[4,128,128]{2,1,0:T(8,128)(2,1)}, u32[]{:S(2)}) copy-start(bf16[4,128,128]{2,1,0:T(8,128)(2,1)} %values_ref.1) | copy-start | bytes 393220
  109.2 21.2 %all-to-all-start.4 = ((bf16[128,8,128]{2,1,0:T(8,128)(2,1)}), bf16[128,8,128]{2,1,0:T(8,128)(2,1)S(1)}, u32[]{:S(2)}, u32[]{:S(2)}) async-start(bf16[128,8,128]{2,1,0:T(8,128)(2,1)} %bitcast.13), calls=%async_computation.4 | async-start | bytes 524288 | tf_op jit(solution)/shard_map/grads/all_to_all | solution.py:276
  120.6 8.0 %collective-permute-start = (bf16[64,512]{1,0:T(8,128)(2,1)S(1)}, bf16[64,512]{1,0:T(8,128)(2,1)S(1)}, u32[]{:S(2)}, u32[]{:S(2)}) collective-permute-start(bf16[64,512]{1,0:T(8,128)(2,1)S(1)} %get-tuple-element.13), channel_id=1, source_target_pairs={{0,5},{5,0},{10,15},{15,10},{1,6},{6,1},{11,12},{12,11},{2,7},{7,2... | collective-permute-start | bytes 196616 | tf_op jit(solution)/shard_map/second/ppermute | solution.py:282
  131.3 33.1 %all-to-all-start.5 = ((f32[32,32,128]{2,1,0:T(8,128)}), f32[32,32,128]{2,1,0:T(8,128)S(1)}, u32[]{:S(2)}, u32[]{:S(2)}) async-start(f32[32,32,128]{2,1,0:T(8,128)} %place.2), calls=%async_computation.5 | async-start | bytes 1048576 | tf_op jit(solution)/shard_map/place/all_to_all | solution.py:276
  137.4 16.8 %collective-permute-start.1 = (bf16[64,512]{1,0:T(8,128)(2,1)S(1)}, bf16[64,512]{1,0:T(8,128)(2,1)S(1)}, u32[]{:S(2)}, u32[]{:S(2)}) collective-permute-start(bf16[64,512]{1,0:T(8,128)(2,1)S(1)} %get-tuple-element.12), channel_id=1, source_target_pairs={{0,10},{5,15},{10,0},{15,5},{1,11},{6,12},{11,1},{12,6},{2,8},{7,1... | collective-permute-start | bytes 196616 | tf_op jit(solution)/shard_map/second/ppermute | solution.py:282
  148.2 4.4 %copy-start.12 = (f32[64]{0:T(128)S(1)}, f32[64]{0:T(128)}, u32[]{:S(2)}) copy-start(f32[64]{0:T(128)} %param.24) | copy-start | bytes 772
  148.2 15.5 %collective-permute-start.2 = (bf16[64,512]{1,0:T(8,128)(2,1)S(1)}, bf16[64,512]{1,0:T(8,128)(2,1)S(1)}, u32[]{:S(2)}, u32[]{:S(2)}) collective-permute-start(bf16[64,512]{1,0:T(8,128)(2,1)S(1)} %get-tuple-element.11), channel_id=1, source_target_pairs={{0,15},{5,10},{10,5},{15,0},{1,12},{6,11},{11,6},{12,1},{2,13},{7,... | collective-permute-start | bytes 196616 | tf_op jit(solution)/shard_map/second/ppermute | solution.py:282

commit v17 on v15

--- a/solution.py
+++ b/solution.py
@@ -212,8 +212,8 @@
         out_ref[jnp.bitwise_xor(block_ref[0], z)] = total[z * cols : (z + 1) * cols, :].astype(BF)
 
 
-def copies_kernel(terms_ref, late1_ref, late2_ref, out_ref):
-    del late1_ref, late2_ref
+def copies_kernel(terms_ref, late1_ref, late2_ref, late3_ref, out_ref):
+    del late1_ref, late2_ref, late3_ref
     total = terms_ref[0].astype(F32)
     for d in range(1, terms_ref.shape[0]):
         total = total + terms_ref[d].astype(F32)
@@ -375,10 +375,10 @@
         spread = call(
             copies_kernel,
             shape(groups, GROUP * 8, 128, dtype=F32),
-            3,
-            late=(1, 2),
+            4,
+            late=(1, 2, 3),
             nbytes=1 << 20,
-        )(terms.reshape(groups, GROUP * 8, 128), second, sums[1])
+        )(terms.reshape(groups, GROUP * 8, 128), second, sums[1], sums[2])
         spread = swap(spread, "dp")
         grad_neigh, grad_self = call(
             place_kernel,

time: 155 us -> 156 us (level)
  the two profiles are of different devices: /device:TPU:2 before, /device:TPU:1 now
where the time goes in v17:
time: 156 us; the launch traced here: 155 us
  starting transfers between devices  62.4 us (40%)
  blocking collectives  38.9 us (25%)
  waiting for transfers between devices  37.9 us (24%)
  Pallas kernels  11.6 us (7%)
  local copies, waits for them, and re-layouts  3.28 us (2%)
    all_to_all x5, starting transfers between devices, swap(): lax.all_to_all(x, axis, split_axis=0, concat_axis=0, tiled=True, axis_ind...  47.7 us
    all_gather x1, blocking collectives, body(): cot = lax.all_gather(cot, FEAT, axis=0, tiled=True, axis_index_groups=far)  24.4 us
    all_to_all x5, waiting for transfers between devices, swap(): lax.all_to_all(x, axis, split_axis=0, concat_axis=0, tiled=True, axis_ind...  23.8 us
    ppermute x3, starting transfers between devices, trade_far(): return lax.ppermute(x, FEAT, pairs)  14.6 us
    all_to_all x1, blocking collectives, swap(): lax.all_to_all(x, axis, split_axis=0, concat_axis=0, tiled=True, axis_ind...  14.5 us
    ppermute x3, waiting for transfers between devices, trade_far(): return lax.ppermute(x, FEAT, pairs)  14.1 us
    pallas_call x1, Pallas kernels, body(): call(functools.partial(pack_kernel, groups, targets), shape(groups, ROWS,...  3.34 us
  transfers between devices with their start and end apart: 8, of which 6 were waited for; matrix products, arithmetic and copies ran while one was open for 0% of the time, Pallas kernels for 1%

profile of v17, /device:TPU:1, one launch (start us, length us, event | category | flops | bytes accessed | tf_op | source)
XLA Modules:
  0.0 154.9 jit_solution(16901258525208771656)
XLA Ops:
  0.6 0.9 copy-done.7
  2.3 3.3 %edges.1.late_ref = bf16[32,64,128]{2,1,0:T(8,128)(2,1)} custom-call(bf16[48,2048]{1,0:T(8,128)(2,1)S(1)} %bitcast.24, s32[16,128]{1,0:T(8,128)S(1)} %bitcast.25), custom_call_target="tpu_custom_call" | custom-call | flops 1073741824 | bytes 8388608 | tf_op jit(solution)/shard_map/edges/pallas_call | solution.py:292
  5.6 10.6 %all-to-all-start = ((bf16[32,64,128]{2,1,0:T(8,128)(2,1)}), bf16[32,64,128]{2,1,0:T(8,128)(2,1)S(1)}, u32[]{:S(2)}, u32[]{:S(2)}) async-start(bf16[32,64,128]{2,1,0:T(8,128)(2,1)} %edges.1.late_ref), calls=%async_computation | async-start | bytes 1048576 | tf_op jit(solution)/shard_map/edges/all_to_all | solution.py:280
  16.4 24.4 %all_gather.3.late_ref.cot_ref = bf16[256,512]{1,0:T(8,128)(2,1)S(1)} all-gather(bf16[64,512]{1,0:T(8,128)(2,1)S(1)} %get-tuple-element.10), channel_id=1, replica_groups={{0,5,10,15},{1,6,11,12},{2,7,8,13},{3,4,9,14},{16,21,26,31},{17,22,27,2..., dimensions={0}, use_global_device_ids=true | all-gather | bytes 327680 | tf_op jit(solution)/shard_map/pieces/all_gather | solution.py:310
  40.8 1.4 mean.1
  42.2 14.5 %all_to_all.30.got_ref = bf16[4,144,512]{2,1,0:T(8,128)(2,1)S(1)} all-to-all(bf16[4,144,512]{2,1,0:T(8,128)(2,1)S(1)} %mean.1), channel_id=1, replica_groups=mesh['dp'=32,'blk'=4,'mem'=4] {'mem'}, dimensions={0} | all-to-all | bytes 1179648 | tf_op jit(solution)/shard_map/mean/all_to_all | solution.py:280
  56.7 1.0 first.1.late_ref
  57.8 5.7 %all-to-all-start.2 = ((bf16[4,64,512]{2,1,0:T(8,128)(2,1)}), bf16[4,64,512]{2,1,0:T(8,128)(2,1)S(1)}, u32[]{:S(2)}, u32[]{:S(2)}) async-start(bf16[4,64,512]{2,1,0:T(8,128)(2,1)} %first.1.late_ref), calls=%async_computation.2 | async-start | bytes 524288 | tf_op jit(solution)/shard_map/first/all_to_all | solution.py:280
  64.4 11.0 %all-to-all-done.2.parts_ref = bf16[4,64,512]{2,1,0:T(8,128)(2,1)S(1)} async-done(((bf16[4,64,512]{2,1,0:T(8,128)(2,1)}), bf16[4,64,512]{2,1,0:T(8,128)(2,1)S(1)}, u32[]{:S(2)}, u32[]{:S(2)}) %all-to-all-start.2) | async-done | bytes 262176 | tf_op jit(solution)/shard_map/first/all_to_all | solution.py:280
  75.3 0.9 hidden.1
  76.2 8.6 %all-to-all-start.3 = ((bf16[4,128,512]{2,1,0:T(8,128)(2,1)}), bf16[4,128,512]{2,1,0:T(8,128)(2,1)S(1)}, u32[]{:S(2)}, u32[]{:S(2)}) async-start(bf16[4,128,512]{2,1,0:T(8,128)(2,1)} %hidden.1), calls=%async_computation.3 | async-start | bytes 1048576 | tf_op jit(solution)/shard_map/hidden/all_to_all | solution.py:280
  85.6 10.4 %all-to-all-done.3.got_ref = bf16[4,128,512]{2,1,0:T(8,128)(2,1)S(1)} async-done(((bf16[4,128,512]{2,1,0:T(8,128)(2,1)}), bf16[4,128,512]{2,1,0:T(8,128)(2,1)S(1)}, u32[]{:S(2)}, u32[]{:S(2)}) %all-to-all-start.3) | async-done | bytes 524320 | tf_op jit(solution)/shard_map/hidden/all_to_all | solution.py:280
  96.0 1.9 %grads.1 = (bf16[256,512]{1,0:T(8,128)(2,1)S(1)}, bf16[32,32,128]{2,1,0:T(8,128)(2,1)}) custom-call(s32[4,2]{1,0:T(4,128)S(1)} %copy.17.index_ref, bf16[4,128,512]{2,1,0:T(8,128)(2,1)S(1)} %all-to-all-done.3.got_ref, bf16[4,128,128]{2,1,0:T(8,128)(2,1)S(1)} %copy-done, f32[1,512]{1,0:T(1,128)S(1)} %bitcast.22, bf16[256,512]{1,0:T(8,128)(2,1)S(1)} %all_gather.3.late_ref.cot_ref), custom_call_target="tpu_custom_call" | custom-call | flops 134217728 | bytes 4194304 | tf_op jit(solution)/shard_map/grads/pallas_call | solution.py:346
  97.9 15.1 %all-to-all-start.4 = ((bf16[128,8,128]{2,1,0:T(8,128)(2,1)}), bf16[128,8,128]{2,1,0:T(8,128)(2,1)S(1)}, u32[]{:S(2)}, u32[]{:S(2)}) async-start(bf16[128,8,128]{2,1,0:T(8,128)(2,1)} %bitcast.13), calls=%async_computation.4 | async-start | bytes 524288 | tf_op jit(solution)/shard_map/grads/all_to_all | solution.py:280
  113.4 5.5 %collective-permute-start = (bf16[64,512]{1,0:T(8,128)(2,1)S(1)}, bf16[64,512]{1,0:T(8,128)(2,1)S(1)}, u32[]{:S(2)}, u32[]{:S(2)}) collective-permute-start(bf16[64,512]{1,0:T(8,128)(2,1)S(1)} %get-tuple-element.17), channel_id=1, source_target_pairs={{0,5},{5,0},{10,15},{15,10},{1,6},{6,1},{11,12},{12,11},{2,7},{7,2... | collective-permute-start | bytes 196616 | tf_op jit(solution)/shard_map/second/ppermute | solution.py:286
  118.9 7.2 %collective-permute-start.1 = (bf16[64,512]{1,0:T(8,128)(2,1)S(1)}, bf16[64,512]{1,0:T(8,128)(2,1)S(1)}, u32[]{:S(2)}, u32[]{:S(2)}) collective-permute-start(bf16[64,512]{1,0:T(8,128)(2,1)S(1)} %get-tuple-element.16), channel_id=1, source_target_pairs={{0,10},{5,15},{10,0},{15,5},{1,11},{6,12},{11,1},{12,6},{2,8},{7,1... | collective-permute-start | bytes 196616 | tf_op jit(solution)/shard_map/second/ppermute | solution.py:286
  126.1 0.7 collective-permute-done.p1_ref.late2_ref
  126.8 7.0 %collective-permute-done.1.p2_ref.late3_ref = bf16[64,512]{1,0:T(8,128)(2,1)S(1)} collective-permute-done((bf16[64,512]{1,0:T(8,128)(2,1)S(1)}, bf16[64,512]{1,0:T(8,128)(2,1)S(1)}, u32[]{:S(2)}, u32[]{:S(2)}) %collective-permute-start.1) | collective-permute-done | bytes 65568 | tf_op jit(solution)/shard_map/second/ppermute | solution.py:286
  133.8 0.9 place.2
  134.7 7.8 %all-to-all-start.5 = ((f32[32,32,128]{2,1,0:T(8,128)}), f32[32,32,128]{2,1,0:T(8,128)S(1)}, u32[]{:S(2)}, u32[]{:S(2)}) async-start(f32[32,32,128]{2,1,0:T(8,128)} %place.2), calls=%async_computation.5 | async-start | bytes 1048576 | tf_op jit(solution)/shard_map/place/all_to_all | solution.py:280
  142.5 1.9 %collective-permute-start.2 = (bf16[64,512]{1,0:T(8,128)(2,1)S(1)}, bf16[64,512]{1,0:T(8,128)(2,1)S(1)}, u32[]{:S(2)}, u32[]{:S(2)}) collective-permute-start(bf16[64,512]{1,0:T(8,128)(2,1)S(1)} %get-tuple-element.15), channel_id=1, source_target_pairs={{0,15},{5,10},{10,5},{15,0},{1,12},{6,11},{11,6},{12,1},{2,13},{7,... | collective-permute-start | bytes 196616 | tf_op jit(solution)/shard_map/second/ppermute | solution.py:286
  144.5 6.4 %collective-permute-done.2.p3_ref = bf16[64,512]{1,0:T(8,128)(2,1)S(1)} collective-permute-done((bf16[64,512]{1,0:T(8,128)(2,1)S(1)}, bf16[64,512]{1,0:T(8,128)(2,1)S(1)}, u32[]{:S(2)}, u32[]{:S(2)}) %collective-permute-start.2) | collective-permute-done | bytes 65568 | tf_op jit(solution)/shard_map/second/ppermute | solution.py:286
  151.6 2.4 %all-to-all-done.5.pieces_ref = f32[32,32,128]{2,1,0:T(8,128)S(1)} async-done(((f32[32,32,128]{2,1,0:T(8,128)}), f32[32,32,128]{2,1,0:T(8,128)S(1)}, u32[]{:S(2)}, u32[]{:S(2)}) %all-to-all-start.5) | async-done | bytes 524320 | tf_op jit(solution)/shard_map/place/all_to_all | solution.py:280
  154.0 0.9 place.3
  (36 shorter events, 3.7 us)
Async XLA Ops:
  0.6 0.9 copy-start.7
  1.6 0.7 copy-start.8
  5.6 10.6 %copy-start.3 = (bf16[48,1024]{1,0:T(8,128)(2,1)S(1)}, bf16[48,1024]{1,0:T(8,128)(2,1)}, u32[]{:S(2)}) copy-start(bf16[48,1024]{1,0:T(8,128)(2,1)} %neigh_ref.2) | copy-start | bytes 294916
  5.6 10.6 %copy-start.4 = (bf16[48,1024]{1,0:T(8,128)(2,1)S(1)}, bf16[48,1024]{1,0:T(8,128)(2,1)}, u32[]{:S(2)}) copy-start(bf16[48,1024]{1,0:T(8,128)(2,1)} %own_ref.2) | copy-start | bytes 294916
  5.6 10.6 %copy-start.5 = (bf16[512,64]{0,1:T(8,128)(2,1)S(1)}, bf16[512,64]{0,1:T(8,128)(2,1)}, u32[]{:S(2)}) copy-start(bf16[512,64]{0,1:T(8,128)(2,1)} %param.25) | copy-start | bytes 196612
  5.6 10.6 %copy-start.6 = (bf16[512,48]{0,1:T(8,128)(2,1)S(1)}, bf16[512,48]{0,1:T(8,128)(2,1)}, u32[]{:S(2)}) copy-start(bf16[512,48]{0,1:T(8,128)(2,1)} %param.15) | copy-start | bytes 147460
  5.6 35.2 %all-to-all-start = ((bf16[32,64,128]{2,1,0:T(8,128)(2,1)}), bf16[32,64,128]{2,1,0:T(8,128)(2,1)S(1)}, u32[]{:S(2)}, u32[]{:S(2)}) async-start(bf16[32,64,128]{2,1,0:T(8,128)(2,1)} %edges.1.late_ref), calls=%async_computation | async-start | bytes 1048576 | tf_op jit(solution)/shard_map/edges/all_to_all | solution.py:280
  57.7 6.5 %copy-start.1 = (bf16[64,1024]{1,0:T(8,128)(2,1)S(1)}, bf16[64,1024]{1,0:T(8,128)(2,1)}, u32[]{:S(2)}) copy-start(bf16[64,1024]{1,0:T(8,128)(2,1)} %neigh_ref.3) | copy-start | bytes 393220
  57.7 6.5 %copy-start.2 = (bf16[64,1024]{1,0:T(8,128)(2,1)S(1)}, bf16[64,1024]{1,0:T(8,128)(2,1)}, u32[]{:S(2)}) copy-start(bf16[64,1024]{1,0:T(8,128)(2,1)} %own_ref.3) | copy-start | bytes 393220
  57.8 17.6 %all-to-all-start.2 = ((bf16[4,64,512]{2,1,0:T(8,128)(2,1)}), bf16[4,64,512]{2,1,0:T(8,128)(2,1)S(1)}, u32[]{:S(2)}, u32[]{:S(2)}) async-start(bf16[4,64,512]{2,1,0:T(8,128)(2,1)} %first.1.late_ref), calls=%async_computation.2 | async-start | bytes 524288 | tf_op jit(solution)/shard_map/first/all_to_all | solution.py:280
  63.5 0.7 copy-start.11
  76.2 8.6 %copy-start.9 = (s32[512]{0:T(512)S(1)}, s32[512]{0:T(512)}, u32[]{:S(2)}) copy-start(s32[512]{0:T(512)} %param.21) | copy-start | bytes 6148
  76.2 19.8 %copy-start = (bf16[4,128,128]{2,1,0:T(8,128)(2,1)S(1)}, bf16[4,128,128]{2,1,0:T(8,128)(2,1)}, u32[]{:S(2)}) copy-start(bf16[4,128,128]{2,1,0:T(8,128)(2,1)} %values_ref.1) | copy-start | bytes 393220
  76.2 19.8 %all-to-all-start.3 = ((bf16[4,128,512]{2,1,0:T(8,128)(2,1)}), bf16[4,128,512]{2,1,0:T(8,128)(2,1)S(1)}, u32[]{:S(2)}, u32[]{:S(2)}) async-start(bf16[4,128,512]{2,1,0:T(8,128)(2,1)} %hidden.1), calls=%async_computation.3 | async-start | bytes 1048576 | tf_op jit(solution)/shard_map/hidden/all_to_all | solution.py:280
  84.9 0.7 copy-start.10
  97.9 35.9 %all-to-all-start.4 = ((bf16[128,8,128]{2,1,0:T(8,128)(2,1)}), bf16[128,8,128]{2,1,0:T(8,128)(2,1)S(1)}, u32[]{:S(2)}, u32[]{:S(2)}) async-start(bf16[128,8,128]{2,1,0:T(8,128)(2,1)} %bitcast.13), calls=%async_computation.4 | async-start | bytes 524288 | tf_op jit(solution)/shard_map/grads/all_to_all | solution.py:280
  113.4 13.5 %collective-permute-start = (bf16[64,512]{1,0:T(8,128)(2,1)S(1)}, bf16[64,512]{1,0:T(8,128)(2,1)S(1)}, u32[]{:S(2)}, u32[]{:S(2)}) collective-permute-start(bf16[64,512]{1,0:T(8,128)(2,1)S(1)} %get-tuple-element.17), channel_id=1, source_target_pairs={{0,5},{5,0},{10,15},{15,10},{1,6},{6,1},{11,12},{12,11},{2,7},{7,2... | collective-permute-start | bytes 196616 | tf_op jit(solution)/shard_map/second/ppermute | solution.py:286
  118.9 14.9 %collective-permute-start.1 = (bf16[64,512]{1,0:T(8,128)(2,1)S(1)}, bf16[64,512]{1,0:T(8,128)(2,1)S(1)}, u32[]{:S(2)}, u32[]{:S(2)}) collective-permute-start(bf16[64,512]{1,0:T(8,128)(2,1)S(1)} %get-tuple-element.16), channel_id=1, source_target_pairs={{0,10},{5,15},{10,0},{15,5},{1,11},{6,12},{11,1},{12,6},{2,8},{7,1... | collective-permute-start | bytes 196616 | tf_op jit(solution)/shard_map/second/ppermute | solution.py:286
  134.7 19.3 %all-to-all-start.5 = ((f32[32,32,128]{2,1,0:T(8,128)}), f32[32,32,128]{2,1,0:T(8,128)S(1)}, u32[]{:S(2)}, u32[]{:S(2)}) async-start(f32[32,32,128]{2,1,0:T(8,128)} %place.2), calls=%async_computation.5 | async-start | bytes 1048576 | tf_op jit(solution)/shard_map/place/all_to_all | solution.py:280
  142.5 1.9 %copy-start.12 = (f32[64]{0:T(128)S(1)}, f32[64]{0:T(128)}, u32[]{:S(2)}) copy-start(f32[64]{0:T(128)} %param.24) | copy-start | bytes 772
  142.5 8.4 %collective-permute-start.2 = (bf16[64,512]{1,0:T(8,128)(2,1)S(1)}, bf16[64,512]{1,0:T(8,128)(2,1)S(1)}, u32[]{:S(2)}, u32[]{:S(2)}) collective-permute-start(bf16[64,512]{1,0:T(8,128)(2,1)S(1)} %get-tuple-element.15), channel_id=1, source_target_pairs={{0,15},{5,10},{10,5},{15,0},{1,12},{6,11},{11,6},{12,1},{2,13},{7,... | collective-permute-start | bytes 196616 | tf_op jit(solution)/shard_map/second/ppermute | solution.py:286

commit v18 on v17

--- a/solution.py
+++ b/solution.py
@@ -212,17 +212,19 @@
         out_ref[jnp.bitwise_xor(block_ref[0], z)] = total[z * cols : (z + 1) * cols, :].astype(BF)
 
 
-def copies_kernel(terms_ref, late1_ref, late2_ref, late3_ref, out_ref):
-    del late1_ref, late2_ref, late3_ref
+def copies_kernel(terms_ref, late1_ref, late2_ref, late3_ref, late4_ref, out_ref):
+    del late1_ref, late2_ref, late3_ref, late4_ref
     total = terms_ref[0].astype(F32)
     for d in range(1, terms_ref.shape[0]):
         total = total + terms_ref[d].astype(F32)
+    total = total.astype(BF)
     for d in range(out_ref.shape[0]):
         out_ref[d] = total
 
 
-def place_kernel(block_ref, pieces_ref, neigh_ref, self_ref):
+def place_kernel(block_ref, pieces_ref, neigh_ref, self_ref, wide):
     half = 64
+    wide[...] = pieces_ref[...].astype(F32)
     starts = []
     for h in range(GROUP):
         starts.append(pl.multiple_of(far_place(block_ref[0], h) * 8, 8))
@@ -230,7 +232,7 @@
     for out_ref in (neigh_ref, self_ref):
         for r in range(0, out_ref.shape[0], 8):
             for c in range(2):
-                parts = [pieces_ref[at, pl.ds(start, 8), :] for start in starts]
+                parts = [wide[at, pl.ds(start, 8), :] for start in starts]
                 for e in range(2):
                     block = 2 * c + e
                     for p in range(0, GROUP, 2):
@@ -374,16 +376,17 @@
     with jax.named_scope("place"):
         spread = call(
             copies_kernel,
-            shape(groups, GROUP * 8, 128, dtype=F32),
-            4,
-            late=(1, 2, 3),
+            shape(groups, GROUP * 8, 128),
+            5,
+            late=(1, 2, 3, 4),
             nbytes=1 << 20,
-        )(terms.reshape(groups, GROUP * 8, 128), second, sums[1], sums[2])
+        )(terms.reshape(groups, GROUP * 8, 128), second, *sums[1:])
         spread = swap(spread, "dp")
         grad_neigh, grad_self = call(
             place_kernel,
             (shape(hid, full, dtype=F32), shape(hid, full, dtype=F32)),
             2,
+            scratch=[pltpu.VMEM((groups, GROUP * 8, 128), F32)],
             smem=(0,),
             nbytes=1 << 20,
         )(block, spread)

time: 156 us -> 159 us (1.019)
  waiting for transfers between devices: 37.9 us -> 40 us
    all_to_all x5, waiting for transfers between devices: 23.8 us -> 28.8 us  [swap(): lax.all_to_all(x, axis, split_axis=0, concat_axis=0, tiled=True, axis_ind...]
    ppermute x3, waiting for transfers between devices: 14.1 us -> 11.2 us  [trade_far(): return lax.ppermute(x, FEAT, pairs)]
  transfers between devices with their start and end apart: 8 -> 8, of which waited for: 6 -> 5; matrix products, arithmetic and copies ran while one was open for 0% -> 0% of each run, Pallas kernels for 1% -> 1%
where the time goes in v18:
time: 159 us; the launch traced here: 158 us
  starting transfers between devices  63.3 us (40%)
  waiting for transfers between devices  40 us (25%)
  blocking collectives  38.9 us (24%)
  Pallas kernels  11.5 us (7%)
  local copies, waits for them, and re-layouts  3.93 us (2%)
    all_to_all x5, starting transfers between devices, swap(): lax.all_to_all(x, axis, split_axis=0, concat_axis=0, tiled=True, axis_ind...  48.6 us
    all_to_all x5, waiting for transfers between devices, swap(): lax.all_to_all(x, axis, split_axis=0, concat_axis=0, tiled=True, axis_ind...  28.8 us
    all_gather x1, blocking collectives, body(): cot = lax.all_gather(cot, FEAT, axis=0, tiled=True, axis_index_groups=far)  24.4 us
    ppermute x3, starting transfers between devices, trade_far(): return lax.ppermute(x, FEAT, pairs)  14.6 us
    all_to_all x1, blocking collectives, swap(): lax.all_to_all(x, axis, split_axis=0, concat_axis=0, tiled=True, axis_ind...  14.5 us
    ppermute x3, waiting for transfers between devices, trade_far(): return lax.ppermute(x, FEAT, pairs)  11.2 us
    unnamed x27, local copies, waits for them, and re-layouts  3.72 us
    pallas_call x1, Pallas kernels, body(): call(functools.partial(pack_kernel, groups, targets), shape(groups, ROWS,...  3.34 us
  transfers between devices with their start and end apart: 8, of which 5 were waited for; matrix products, arithmetic and copies ran while one was open for 0% of the time, Pallas kernels for 1%

profile of v18, /device:TPU:1, one launch (start us, length us, event | category | flops | bytes accessed | tf_op | source)
XLA Modules:
  0.0 158.5 jit_solution(1349107561486458295)
XLA Ops:
  0.6 0.9 copy-done.7
  2.3 3.3 %edges.1.late_ref = bf16[32,64,128]{2,1,0:T(8,128)(2,1)} custom-call(bf16[48,2048]{1,0:T(8,128)(2,1)S(1)} %bitcast.24, s32[16,128]{1,0:T(8,128)S(1)} %bitcast.25), custom_call_target="tpu_custom_call" | custom-call | flops 1073741824 | bytes 8388608 | tf_op jit(solution)/shard_map/edges/pallas_call | solution.py:294
  5.6 10.6 %all-to-all-start = ((bf16[32,64,128]{2,1,0:T(8,128)(2,1)}), bf16[32,64,128]{2,1,0:T(8,128)(2,1)S(1)}, u32[]{:S(2)}, u32[]{:S(2)}) async-start(bf16[32,64,128]{2,1,0:T(8,128)(2,1)} %edges.1.late_ref), calls=%async_computation | async-start | bytes 1048576 | tf_op jit(solution)/shard_map/edges/all_to_all | solution.py:282
  16.4 24.4 %all_gather.3.late_ref.cot_ref = bf16[256,512]{1,0:T(8,128)(2,1)S(1)} all-gather(bf16[64,512]{1,0:T(8,128)(2,1)S(1)} %get-tuple-element.10), channel_id=1, replica_groups={{0,5,10,15},{1,6,11,12},{2,7,8,13},{3,4,9,14},{16,21,26,31},{17,22,27,2..., dimensions={0}, use_global_device_ids=true | all-gather | bytes 327680 | tf_op jit(solution)/shard_map/pieces/all_gather | solution.py:312
  40.8 1.4 mean.1
  42.2 14.5 %all_to_all.30.got_ref = bf16[4,144,512]{2,1,0:T(8,128)(2,1)S(1)} all-to-all(bf16[4,144,512]{2,1,0:T(8,128)(2,1)S(1)} %mean.1), channel_id=1, replica_groups=mesh['dp'=32,'blk'=4,'mem'=4] {'mem'}, dimensions={0} | all-to-all | bytes 1179648 | tf_op jit(solution)/shard_map/mean/all_to_all | solution.py:282
  56.7 1.0 first.1.late_ref
  57.8 5.7 %all-to-all-start.2 = ((bf16[4,64,512]{2,1,0:T(8,128)(2,1)}), bf16[4,64,512]{2,1,0:T(8,128)(2,1)S(1)}, u32[]{:S(2)}, u32[]{:S(2)}) async-start(bf16[4,64,512]{2,1,0:T(8,128)(2,1)} %first.1.late_ref), calls=%async_computation.2 | async-start | bytes 524288 | tf_op jit(solution)/shard_map/first/all_to_all | solution.py:282
  64.4 11.0 %all-to-all-done.2.parts_ref = bf16[4,64,512]{2,1,0:T(8,128)(2,1)S(1)} async-done(((bf16[4,64,512]{2,1,0:T(8,128)(2,1)}), bf16[4,64,512]{2,1,0:T(8,128)(2,1)S(1)}, u32[]{:S(2)}, u32[]{:S(2)}) %all-to-all-start.2) | async-done | bytes 262176 | tf_op jit(solution)/shard_map/first/all_to_all | solution.py:282
  75.3 0.9 hidden.1
  76.2 8.6 %all-to-all-start.3 = ((bf16[4,128,512]{2,1,0:T(8,128)(2,1)}), bf16[4,128,512]{2,1,0:T(8,128)(2,1)S(1)}, u32[]{:S(2)}, u32[]{:S(2)}) async-start(bf16[4,128,512]{2,1,0:T(8,128)(2,1)} %hidden.1), calls=%async_computation.3 | async-start | bytes 1048576 | tf_op jit(solution)/shard_map/hidden/all_to_all | solution.py:282
  85.6 10.4 %all-to-all-done.3.got_ref = bf16[4,128,512]{2,1,0:T(8,128)(2,1)S(1)} async-done(((bf16[4,128,512]{2,1,0:T(8,128)(2,1)}), bf16[4,128,512]{2,1,0:T(8,128)(2,1)S(1)}, u32[]{:S(2)}, u32[]{:S(2)}) %all-to-all-start.3) | async-done | bytes 524320 | tf_op jit(solution)/shard_map/hidden/all_to_all | solution.py:282
  96.0 1.9 %grads.1 = (bf16[256,512]{1,0:T(8,128)(2,1)S(1)}, bf16[32,32,128]{2,1,0:T(8,128)(2,1)}) custom-call(s32[4,2]{1,0:T(4,128)S(1)} %copy.17.index_ref, bf16[4,128,512]{2,1,0:T(8,128)(2,1)S(1)} %all-to-all-done.3.got_ref, bf16[4,128,128]{2,1,0:T(8,128)(2,1)S(1)} %copy-done, f32[1,512]{1,0:T(1,128)S(1)} %bitcast.22, bf16[256,512]{1,0:T(8,128)(2,1)S(1)} %all_gather.3.late_ref.cot_ref), custom_call_target="tpu_custom_call" | custom-call | flops 134217728 | bytes 4194304 | tf_op jit(solution)/shard_map/grads/pallas_call | solution.py:348
  97.9 15.1 %all-to-all-start.4 = ((bf16[128,8,128]{2,1,0:T(8,128)(2,1)}), bf16[128,8,128]{2,1,0:T(8,128)(2,1)S(1)}, u32[]{:S(2)}, u32[]{:S(2)}) async-start(bf16[128,8,128]{2,1,0:T(8,128)(2,1)} %bitcast.13), calls=%async_computation.4 | async-start | bytes 524288 | tf_op jit(solution)/shard_map/grads/all_to_all | solution.py:282
  113.4 5.5 %collective-permute-start = (bf16[64,512]{1,0:T(8,128)(2,1)S(1)}, bf16[64,512]{1,0:T(8,128)(2,1)S(1)}, u32[]{:S(2)}, u32[]{:S(2)}) collective-permute-start(bf16[64,512]{1,0:T(8,128)(2,1)S(1)} %get-tuple-element.17), channel_id=1, source_target_pairs={{0,5},{5,0},{10,15},{15,10},{1,6},{6,1},{11,12},{12,11},{2,7},{7,2... | collective-permute-start | bytes 196616 | tf_op jit(solution)/shard_map/second/ppermute | solution.py:288
  118.9 7.2 %collective-permute-start.1 = (bf16[64,512]{1,0:T(8,128)(2,1)S(1)}, bf16[64,512]{1,0:T(8,128)(2,1)S(1)}, u32[]{:S(2)}, u32[]{:S(2)}) collective-permute-start(bf16[64,512]{1,0:T(8,128)(2,1)S(1)} %get-tuple-element.16), channel_id=1, source_target_pairs={{0,10},{5,15},{10,0},{15,5},{1,11},{6,12},{11,1},{12,6},{2,8},{7,1... | collective-permute-start | bytes 196616 | tf_op jit(solution)/shard_map/second/ppermute | solution.py:288
  126.1 1.9 %collective-permute-start.2 = (bf16[64,512]{1,0:T(8,128)(2,1)S(1)}, bf16[64,512]{1,0:T(8,128)(2,1)S(1)}, u32[]{:S(2)}, u32[]{:S(2)}) collective-permute-start(bf16[64,512]{1,0:T(8,128)(2,1)S(1)} %get-tuple-element.15), channel_id=1, source_target_pairs={{0,15},{5,10},{10,5},{15,0},{1,12},{6,11},{11,6},{12,1},{2,13},{7,... | collective-permute-start | bytes 196616 | tf_op jit(solution)/shard_map/second/ppermute | solution.py:288
  128.0 5.8 %collective-permute-done.1.p2_ref.late3_ref = bf16[64,512]{1,0:T(8,128)(2,1)S(1)} collective-permute-done((bf16[64,512]{1,0:T(8,128)(2,1)S(1)}, bf16[64,512]{1,0:T(8,128)(2,1)S(1)}, u32[]{:S(2)}, u32[]{:S(2)}) %collective-permute-start.1) | collective-permute-done | bytes 65568 | tf_op jit(solution)/shard_map/second/ppermute | solution.py:288
  133.8 5.4 %collective-permute-done.2.p3_ref.late4_ref = bf16[64,512]{1,0:T(8,128)(2,1)S(1)} collective-permute-done((bf16[64,512]{1,0:T(8,128)(2,1)S(1)}, bf16[64,512]{1,0:T(8,128)(2,1)S(1)}, u32[]{:S(2)}, u32[]{:S(2)}) %collective-permute-start.2) | collective-permute-done | bytes 65568 | tf_op jit(solution)/shard_map/second/ppermute | solution.py:288
  139.2 0.8 place.2
  140.0 8.7 %all-to-all-start.5 = ((bf16[32,32,128]{2,1,0:T(8,128)(2,1)}), bf16[32,32,128]{2,1,0:T(8,128)(2,1)S(1)}, u32[]{:S(2)}, u32[]{:S(2)}) async-start(bf16[32,32,128]{2,1,0:T(8,128)(2,1)} %place.2), calls=%async_computation.5 | async-start | bytes 524288 | tf_op jit(solution)/shard_map/place/all_to_all | solution.py:282
  149.4 0.7 second.3
  150.1 7.4 %all-to-all-done.5.pieces_ref = bf16[32,32,128]{2,1,0:T(8,128)(2,1)S(1)} async-done(((bf16[32,32,128]{2,1,0:T(8,128)(2,1)}), bf16[32,32,128]{2,1,0:T(8,128)(2,1)S(1)}, u32[]{:S(2)}, u32[]{:S(2)}) %all-to-all-start.5) | async-done | bytes 262176 | tf_op jit(solution)/shard_map/place/all_to_all | solution.py:282
  157.6 0.9 place.3
  (36 shorter events, 3.6 us)
Async XLA Ops:
  0.6 0.9 copy-start.7
  1.6 0.7 copy-start.8
  5.6 10.6 %copy-start.3 = (bf16[48,1024]{1,0:T(8,128)(2,1)S(1)}, bf16[48,1024]{1,0:T(8,128)(2,1)}, u32[]{:S(2)}) copy-start(bf16[48,1024]{1,0:T(8,128)(2,1)} %neigh_ref.2) | copy-start | bytes 294916
  5.6 10.6 %copy-start.4 = (bf16[48,1024]{1,0:T(8,128)(2,1)S(1)}, bf16[48,1024]{1,0:T(8,128)(2,1)}, u32[]{:S(2)}) copy-start(bf16[48,1024]{1,0:T(8,128)(2,1)} %own_ref.2) | copy-start | bytes 294916
  5.6 10.6 %copy-start.5 = (bf16[512,64]{0,1:T(8,128)(2,1)S(1)}, bf16[512,64]{0,1:T(8,128)(2,1)}, u32[]{:S(2)}) copy-start(bf16[512,64]{0,1:T(8,128)(2,1)} %param.25) | copy-start | bytes 196612
  5.6 10.6 %copy-start.6 = (bf16[512,48]{0,1:T(8,128)(2,1)S(1)}, bf16[512,48]{0,1:T(8,128)(2,1)}, u32[]{:S(2)}) copy-start(bf16[512,48]{0,1:T(8,128)(2,1)} %param.15) | copy-start | bytes 147460
  5.6 35.2 %all-to-all-start = ((bf16[32,64,128]{2,1,0:T(8,128)(2,1)}), bf16[32,64,128]{2,1,0:T(8,128)(2,1)S(1)}, u32[]{:S(2)}, u32[]{:S(2)}) async-start(bf16[32,64,128]{2,1,0:T(8,128)(2,1)} %edges.1.late_ref), calls=%async_computation | async-start | bytes 1048576 | tf_op jit(solution)/shard_map/edges/all_to_all | solution.py:282
  57.7 6.5 %copy-start.1 = (bf16[64,1024]{1,0:T(8,128)(2,1)S(1)}, bf16[64,1024]{1,0:T(8,128)(2,1)}, u32[]{:S(2)}) copy-start(bf16[64,1024]{1,0:T(8,128)(2,1)} %neigh_ref.3) | copy-start | bytes 393220
  57.7 6.5 %copy-start.2 = (bf16[64,1024]{1,0:T(8,128)(2,1)S(1)}, bf16[64,1024]{1,0:T(8,128)(2,1)}, u32[]{:S(2)}) copy-start(bf16[64,1024]{1,0:T(8,128)(2,1)} %own_ref.3) | copy-start | bytes 393220
  57.8 17.6 %all-to-all-start.2 = ((bf16[4,64,512]{2,1,0:T(8,128)(2,1)}), bf16[4,64,512]{2,1,0:T(8,128)(2,1)S(1)}, u32[]{:S(2)}, u32[]{:S(2)}) async-start(bf16[4,64,512]{2,1,0:T(8,128)(2,1)} %first.1.late_ref), calls=%async_computation.2 | async-start | bytes 524288 | tf_op jit(solution)/shard_map/first/all_to_all | solution.py:282
  63.5 0.7 copy-start.11
  76.2 8.6 %copy-start.9 = (s32[512]{0:T(512)S(1)}, s32[512]{0:T(512)}, u32[]{:S(2)}) copy-start(s32[512]{0:T(512)} %param.21) | copy-start | bytes 6148
  76.2 19.8 %copy-start = (bf16[4,128,128]{2,1,0:T(8,128)(2,1)S(1)}, bf16[4,128,128]{2,1,0:T(8,128)(2,1)}, u32[]{:S(2)}) copy-start(bf16[4,128,128]{2,1,0:T(8,128)(2,1)} %values_ref.1) | copy-start | bytes 393220
  76.2 19.8 %all-to-all-start.3 = ((bf16[4,128,512]{2,1,0:T(8,128)(2,1)}), bf16[4,128,512]{2,1,0:T(8,128)(2,1)S(1)}, u32[]{:S(2)}, u32[]{:S(2)}) async-start(bf16[4,128,512]{2,1,0:T(8,128)(2,1)} %hidden.1), calls=%async_computation.3 | async-start | bytes 1048576 | tf_op jit(solution)/shard_map/hidden/all_to_all | solution.py:282
  84.9 0.7 copy-start.10
  97.9 41.3 %all-to-all-start.4 = ((bf16[128,8,128]{2,1,0:T(8,128)(2,1)}), bf16[128,8,128]{2,1,0:T(8,128)(2,1)S(1)}, u32[]{:S(2)}, u32[]{:S(2)}) async-start(bf16[128,8,128]{2,1,0:T(8,128)(2,1)} %bitcast.13), calls=%async_computation.4 | async-start | bytes 524288 | tf_op jit(solution)/shard_map/grads/all_to_all | solution.py:282
  113.4 14.7 %collective-permute-start = (bf16[64,512]{1,0:T(8,128)(2,1)S(1)}, bf16[64,512]{1,0:T(8,128)(2,1)S(1)}, u32[]{:S(2)}, u32[]{:S(2)}) collective-permute-start(bf16[64,512]{1,0:T(8,128)(2,1)S(1)} %get-tuple-element.17), channel_id=1, source_target_pairs={{0,5},{5,0},{10,15},{15,10},{1,6},{6,1},{11,12},{12,11},{2,7},{7,2... | collective-permute-start | bytes 196616 | tf_op jit(solution)/shard_map/second/ppermute | solution.py:288
  118.9 14.9 %collective-permute-start.1 = (bf16[64,512]{1,0:T(8,128)(2,1)S(1)}, bf16[64,512]{1,0:T(8,128)(2,1)S(1)}, u32[]{:S(2)}, u32[]{:S(2)}) collective-permute-start(bf16[64,512]{1,0:T(8,128)(2,1)S(1)} %get-tuple-element.16), channel_id=1, source_target_pairs={{0,10},{5,15},{10,0},{15,5},{1,11},{6,12},{11,1},{12,6},{2,8},{7,1... | collective-permute-start | bytes 196616 | tf_op jit(solution)/shard_map/second/ppermute | solution.py:288
  126.1 13.1 %collective-permute-start.2 = (bf16[64,512]{1,0:T(8,128)(2,1)S(1)}, bf16[64,512]{1,0:T(8,128)(2,1)S(1)}, u32[]{:S(2)}, u32[]{:S(2)}) collective-permute-start(bf16[64,512]{1,0:T(8,128)(2,1)S(1)} %get-tuple-element.15), channel_id=1, source_target_pairs={{0,15},{5,10},{10,5},{15,0},{1,12},{6,11},{11,6},{12,1},{2,13},{7,... | collective-permute-start | bytes 196616 | tf_op jit(solution)/shard_map/second/ppermute | solution.py:288
  140.0 17.6 %all-to-all-start.5 = ((bf16[32,32,128]{2,1,0:T(8,128)(2,1)}), bf16[32,32,128]{2,1,0:T(8,128)(2,1)S(1)}, u32[]{:S(2)}, u32[]{:S(2)}) async-start(bf16[32,32,128]{2,1,0:T(8,128)(2,1)} %place.2), calls=%async_computation.5 | async-start | bytes 524288 | tf_op jit(solution)/shard_map/place/all_to_all | solution.py:282
  148.7 0.7 copy-start.12

commit v19 on v15

--- a/solution.py
+++ b/solution.py
@@ -378,7 +378,7 @@
             3,
             late=(1, 2),
             nbytes=1 << 20,
-        )(terms.reshape(groups, GROUP * 8, 128), second, sums[1])
+        )(terms.reshape(groups, GROUP * 8, 128), second, sums[3])
         spread = swap(spread, "dp")
         grad_neigh, grad_self = call(
             place_kernel,

time: 155 us -> 158 us (1.019)
  the two profiles are of different devices: /device:TPU:2 before, /device:TPU:1 now
where the time goes in v19:
time: 158 us; the launch traced here: 157 us
  starting transfers between devices  63.7 us (40%)
  blocking collectives  38.9 us (25%)
  waiting for transfers between devices  38.7 us (24%)
  Pallas kernels  11.6 us (7%)
  local copies, waits for them, and re-layouts  3.28 us (2%)
    all_to_all x5, starting transfers between devices, swap(): lax.all_to_all(x, axis, split_axis=0, concat_axis=0, tiled=True, axis_ind...  43.9 us
    all_to_all x5, waiting for transfers between devices, swap(): lax.all_to_all(x, axis, split_axis=0, concat_axis=0, tiled=True, axis_ind...  27.7 us
    all_gather x1, blocking collectives, body(): cot = lax.all_gather(cot, FEAT, axis=0, tiled=True, axis_index_groups=far)  24.4 us
    ppermute x3, starting transfers between devices, trade_far(): return lax.ppermute(x, FEAT, pairs)  19.8 us
    all_to_all x1, blocking collectives, swap(): lax.all_to_all(x, axis, split_axis=0, concat_axis=0, tiled=True, axis_ind...  14.5 us
    ppermute x3, waiting for transfers between devices, trade_far(): return lax.ppermute(x, FEAT, pairs)  11.1 us
    pallas_call x1, Pallas kernels, body(): call(functools.partial(pack_kernel, groups, targets), shape(groups, ROWS,...  3.34 us
  transfers between devices with their start and end apart: 8, of which 5 were waited for; matrix products, arithmetic and copies ran while one was open for 0% of the time, Pallas kernels for 1%

profile of v19, /device:TPU:1, one launch (start us, length us, event | category | flops | bytes accessed | tf_op | source)
XLA Modules:
  0.0 157.1 jit_solution(11892934207876612229)
XLA Ops:
  0.6 0.9 copy-done.7
  2.3 3.3 %edges.1.late_ref = bf16[32,64,128]{2,1,0:T(8,128)(2,1)} custom-call(bf16[48,2048]{1,0:T(8,128)(2,1)S(1)} %bitcast.24, s32[16,128]{1,0:T(8,128)S(1)} %bitcast.25), custom_call_target="tpu_custom_call" | custom-call | flops 1073741824 | bytes 8388608 | tf_op jit(solution)/shard_map/edges/pallas_call | solution.py:292
  5.6 10.6 %all-to-all-start = ((bf16[32,64,128]{2,1,0:T(8,128)(2,1)}), bf16[32,64,128]{2,1,0:T(8,128)(2,1)S(1)}, u32[]{:S(2)}, u32[]{:S(2)}) async-start(bf16[32,64,128]{2,1,0:T(8,128)(2,1)} %edges.1.late_ref), calls=%async_computation | async-start | bytes 1048576 | tf_op jit(solution)/shard_map/edges/all_to_all | solution.py:280
  16.4 24.4 %all_gather.3.late_ref.cot_ref = bf16[256,512]{1,0:T(8,128)(2,1)S(1)} all-gather(bf16[64,512]{1,0:T(8,128)(2,1)S(1)} %get-tuple-element.10), channel_id=1, replica_groups={{0,5,10,15},{1,6,11,12},{2,7,8,13},{3,4,9,14},{16,21,26,31},{17,22,27,2..., dimensions={0}, use_global_device_ids=true | all-gather | bytes 327680 | tf_op jit(solution)/shard_map/pieces/all_gather | solution.py:310
  40.8 1.4 mean.1
  42.2 14.5 %all_to_all.30.got_ref = bf16[4,144,512]{2,1,0:T(8,128)(2,1)S(1)} all-to-all(bf16[4,144,512]{2,1,0:T(8,128)(2,1)S(1)} %mean.1), channel_id=1, replica_groups=mesh['dp'=32,'blk'=4,'mem'=4] {'mem'}, dimensions={0} | all-to-all | bytes 1179648 | tf_op jit(solution)/shard_map/mean/all_to_all | solution.py:280
  56.7 1.0 first.1.late_ref
  57.8 5.7 %all-to-all-start.2 = ((bf16[4,64,512]{2,1,0:T(8,128)(2,1)}), bf16[4,64,512]{2,1,0:T(8,128)(2,1)S(1)}, u32[]{:S(2)}, u32[]{:S(2)}) async-start(bf16[4,64,512]{2,1,0:T(8,128)(2,1)} %first.1.late_ref), calls=%async_computation.2 | async-start | bytes 524288 | tf_op jit(solution)/shard_map/first/all_to_all | solution.py:280
  64.4 11.0 %all-to-all-done.2.parts_ref = bf16[4,64,512]{2,1,0:T(8,128)(2,1)S(1)} async-done(((bf16[4,64,512]{2,1,0:T(8,128)(2,1)}), bf16[4,64,512]{2,1,0:T(8,128)(2,1)S(1)}, u32[]{:S(2)}, u32[]{:S(2)}) %all-to-all-start.2) | async-done | bytes 262176 | tf_op jit(solution)/shard_map/first/all_to_all | solution.py:280
  75.3 0.9 hidden.1
  76.2 8.6 %all-to-all-start.3 = ((bf16[4,128,512]{2,1,0:T(8,128)(2,1)}), bf16[4,128,512]{2,1,0:T(8,128)(2,1)S(1)}, u32[]{:S(2)}, u32[]{:S(2)}) async-start(bf16[4,128,512]{2,1,0:T(8,128)(2,1)} %hidden.1), calls=%async_computation.3 | async-start | bytes 1048576 | tf_op jit(solution)/shard_map/hidden/all_to_all | solution.py:280
  85.6 10.4 %all-to-all-done.3.got_ref = bf16[4,128,512]{2,1,0:T(8,128)(2,1)S(1)} async-done(((bf16[4,128,512]{2,1,0:T(8,128)(2,1)}), bf16[4,128,512]{2,1,0:T(8,128)(2,1)S(1)}, u32[]{:S(2)}, u32[]{:S(2)}) %all-to-all-start.3) | async-done | bytes 524320 | tf_op jit(solution)/shard_map/hidden/all_to_all | solution.py:280
  96.0 1.9 %grads.1 = (bf16[256,512]{1,0:T(8,128)(2,1)S(1)}, bf16[32,32,128]{2,1,0:T(8,128)(2,1)}) custom-call(s32[4,2]{1,0:T(4,128)S(1)} %copy.17.index_ref, bf16[4,128,512]{2,1,0:T(8,128)(2,1)S(1)} %all-to-all-done.3.got_ref, bf16[4,128,128]{2,1,0:T(8,128)(2,1)S(1)} %copy-done, f32[1,512]{1,0:T(1,128)S(1)} %bitcast.22, bf16[256,512]{1,0:T(8,128)(2,1)S(1)} %all_gather.3.late_ref.cot_ref), custom_call_target="tpu_custom_call" | custom-call | flops 134217728 | bytes 4194304 | tf_op jit(solution)/shard_map/grads/pallas_call | solution.py:346
  97.9 15.1 %all-to-all-start.4 = ((bf16[128,8,128]{2,1,0:T(8,128)(2,1)}), bf16[128,8,128]{2,1,0:T(8,128)(2,1)S(1)}, u32[]{:S(2)}, u32[]{:S(2)}) async-start(bf16[128,8,128]{2,1,0:T(8,128)(2,1)} %bitcast.13), calls=%async_computation.4 | async-start | bytes 524288 | tf_op jit(solution)/shard_map/grads/all_to_all | solution.py:280
  113.4 4.8 %collective-permute-start.2 = (bf16[64,512]{1,0:T(8,128)(2,1)S(1)}, bf16[64,512]{1,0:T(8,128)(2,1)S(1)}, u32[]{:S(2)}, u32[]{:S(2)}) collective-permute-start(bf16[64,512]{1,0:T(8,128)(2,1)S(1)} %get-tuple-element.15), channel_id=1, source_target_pairs={{0,15},{5,10},{10,5},{15,0},{1,12},{6,11},{11,6},{12,1},{2,13},{7,... | collective-permute-start | bytes 196616 | tf_op jit(solution)/shard_map/second/ppermute | solution.py:286
  118.2 1.9 %collective-permute-done.2.p3_ref.late2_ref = bf16[64,512]{1,0:T(8,128)(2,1)S(1)} collective-permute-done((bf16[64,512]{1,0:T(8,128)(2,1)S(1)}, bf16[64,512]{1,0:T(8,128)(2,1)S(1)}, u32[]{:S(2)}, u32[]{:S(2)}) %collective-permute-start.2) | collective-permute-done | bytes 65568 | tf_op jit(solution)/shard_map/second/ppermute | solution.py:286
  120.1 6.3 %all-to-all-done.4 = bf16[128,8,128]{2,1,0:T(8,128)(2,1)S(1)} async-done(((bf16[128,8,128]{2,1,0:T(8,128)(2,1)}), bf16[128,8,128]{2,1,0:T(8,128)(2,1)S(1)}, u32[]{:S(2)}, u32[]{:S(2)}) %all-to-all-start.4) | async-done | bytes 262176 | tf_op jit(solution)/shard_map/grads/all_to_all | solution.py:280
  126.4 0.9 place.2
  127.3 3.9 %all-to-all-start.5 = ((f32[32,32,128]{2,1,0:T(8,128)}), f32[32,32,128]{2,1,0:T(8,128)S(1)}, u32[]{:S(2)}, u32[]{:S(2)}) async-start(f32[32,32,128]{2,1,0:T(8,128)} %place.2), calls=%async_computation.5 | async-start | bytes 1048576 | tf_op jit(solution)/shard_map/place/all_to_all | solution.py:280
  131.2 8.6 %collective-permute-start = (bf16[64,512]{1,0:T(8,128)(2,1)S(1)}, bf16[64,512]{1,0:T(8,128)(2,1)S(1)}, u32[]{:S(2)}, u32[]{:S(2)}) collective-permute-start(bf16[64,512]{1,0:T(8,128)(2,1)S(1)} %get-tuple-element.17), channel_id=1, source_target_pairs={{0,5},{5,0},{10,15},{15,10},{1,6},{6,1},{11,12},{12,11},{2,7},{7,2... | collective-permute-start | bytes 196616 | tf_op jit(solution)/shard_map/second/ppermute | solution.py:286
  139.9 6.4 %collective-permute-start.1 = (bf16[64,512]{1,0:T(8,128)(2,1)S(1)}, bf16[64,512]{1,0:T(8,128)(2,1)S(1)}, u32[]{:S(2)}, u32[]{:S(2)}) collective-permute-start(bf16[64,512]{1,0:T(8,128)(2,1)S(1)} %get-tuple-element.16), channel_id=1, source_target_pairs={{0,10},{5,15},{10,0},{15,5},{1,11},{6,12},{11,1},{12,6},{2,8},{7,1... | collective-permute-start | bytes 196616 | tf_op jit(solution)/shard_map/second/ppermute | solution.py:286
  146.3 9.1 %collective-permute-done.1.p2_ref = bf16[64,512]{1,0:T(8,128)(2,1)S(1)} collective-permute-done((bf16[64,512]{1,0:T(8,128)(2,1)S(1)}, bf16[64,512]{1,0:T(8,128)(2,1)S(1)}, u32[]{:S(2)}, u32[]{:S(2)}) %collective-permute-start.1) | collective-permute-done | bytes 65568 | tf_op jit(solution)/shard_map/second/ppermute | solution.py:286
  155.5 0.7 second.3
  156.2 0.9 place.3
  (36 shorter events, 3.0 us)
Async XLA Ops:
  0.6 0.9 copy-start.7
  1.6 0.7 copy-start.8
  5.6 10.6 %copy-start.3 = (bf16[48,1024]{1,0:T(8,128)(2,1)S(1)}, bf16[48,1024]{1,0:T(8,128)(2,1)}, u32[]{:S(2)}) copy-start(bf16[48,1024]{1,0:T(8,128)(2,1)} %neigh_ref.2) | copy-start | bytes 294916
  5.6 10.6 %copy-start.4 = (bf16[48,1024]{1,0:T(8,128)(2,1)S(1)}, bf16[48,1024]{1,0:T(8,128)(2,1)}, u32[]{:S(2)}) copy-start(bf16[48,1024]{1,0:T(8,128)(2,1)} %own_ref.2) | copy-start | bytes 294916
  5.6 10.6 %copy-start.5 = (bf16[512,64]{0,1:T(8,128)(2,1)S(1)}, bf16[512,64]{0,1:T(8,128)(2,1)}, u32[]{:S(2)}) copy-start(bf16[512,64]{0,1:T(8,128)(2,1)} %param.25) | copy-start | bytes 196612
  5.6 10.6 %copy-start.6 = (bf16[512,48]{0,1:T(8,128)(2,1)S(1)}, bf16[512,48]{0,1:T(8,128)(2,1)}, u32[]{:S(2)}) copy-start(bf16[512,48]{0,1:T(8,128)(2,1)} %param.15) | copy-start | bytes 147460
  5.6 35.2 %all-to-all-start = ((bf16[32,64,128]{2,1,0:T(8,128)(2,1)}), bf16[32,64,128]{2,1,0:T(8,128)(2,1)S(1)}, u32[]{:S(2)}, u32[]{:S(2)}) async-start(bf16[32,64,128]{2,1,0:T(8,128)(2,1)} %edges.1.late_ref), calls=%async_computation | async-start | bytes 1048576 | tf_op jit(solution)/shard_map/edges/all_to_all | solution.py:280
  57.7 6.5 %copy-start.1 = (bf16[64,1024]{1,0:T(8,128)(2,1)S(1)}, bf16[64,1024]{1,0:T(8,128)(2,1)}, u32[]{:S(2)}) copy-start(bf16[64,1024]{1,0:T(8,128)(2,1)} %neigh_ref.3) | copy-start | bytes 393220
  57.7 6.5 %copy-start.2 = (bf16[64,1024]{1,0:T(8,128)(2,1)S(1)}, bf16[64,1024]{1,0:T(8,128)(2,1)}, u32[]{:S(2)}) copy-start(bf16[64,1024]{1,0:T(8,128)(2,1)} %own_ref.3) | copy-start | bytes 393220
  57.8 17.6 %all-to-all-start.2 = ((bf16[4,64,512]{2,1,0:T(8,128)(2,1)}), bf16[4,64,512]{2,1,0:T(8,128)(2,1)S(1)}, u32[]{:S(2)}, u32[]{:S(2)}) async-start(bf16[4,64,512]{2,1,0:T(8,128)(2,1)} %first.1.late_ref), calls=%async_computation.2 | async-start | bytes 524288 | tf_op jit(solution)/shard_map/first/all_to_all | solution.py:280
  63.5 0.7 copy-start.11
  76.2 8.6 %copy-start.9 = (s32[512]{0:T(512)S(1)}, s32[512]{0:T(512)}, u32[]{:S(2)}) copy-start(s32[512]{0:T(512)} %param.21) | copy-start | bytes 6148
  76.2 19.8 %copy-start = (bf16[4,128,128]{2,1,0:T(8,128)(2,1)S(1)}, bf16[4,128,128]{2,1,0:T(8,128)(2,1)}, u32[]{:S(2)}) copy-start(bf16[4,128,128]{2,1,0:T(8,128)(2,1)} %values_ref.1) | copy-start | bytes 393220
  76.2 19.8 %all-to-all-start.3 = ((bf16[4,128,512]{2,1,0:T(8,128)(2,1)}), bf16[4,128,512]{2,1,0:T(8,128)(2,1)S(1)}, u32[]{:S(2)}, u32[]{:S(2)}) async-start(bf16[4,128,512]{2,1,0:T(8,128)(2,1)} %hidden.1), calls=%async_computation.3 | async-start | bytes 1048576 | tf_op jit(solution)/shard_map/hidden/all_to_all | solution.py:280
  84.9 0.7 copy-start.10
  97.9 28.5 %all-to-all-start.4 = ((bf16[128,8,128]{2,1,0:T(8,128)(2,1)}), bf16[128,8,128]{2,1,0:T(8,128)(2,1)S(1)}, u32[]{:S(2)}, u32[]{:S(2)}) async-start(bf16[128,8,128]{2,1,0:T(8,128)(2,1)} %bitcast.13), calls=%async_computation.4 | async-start | bytes 524288 | tf_op jit(solution)/shard_map/grads/all_to_all | solution.py:280
  113.4 6.8 %collective-permute-start.2 = (bf16[64,512]{1,0:T(8,128)(2,1)S(1)}, bf16[64,512]{1,0:T(8,128)(2,1)S(1)}, u32[]{:S(2)}, u32[]{:S(2)}) collective-permute-start(bf16[64,512]{1,0:T(8,128)(2,1)S(1)} %get-tuple-element.15), channel_id=1, source_target_pairs={{0,15},{5,10},{10,5},{15,0},{1,12},{6,11},{11,6},{12,1},{2,13},{7,... | collective-permute-start | bytes 196616 | tf_op jit(solution)/shard_map/second/ppermute | solution.py:286
  127.3 28.9 %all-to-all-start.5 = ((f32[32,32,128]{2,1,0:T(8,128)}), f32[32,32,128]{2,1,0:T(8,128)S(1)}, u32[]{:S(2)}, u32[]{:S(2)}) async-start(f32[32,32,128]{2,1,0:T(8,128)} %place.2), calls=%async_computation.5 | async-start | bytes 1048576 | tf_op jit(solution)/shard_map/place/all_to_all | solution.py:280
  131.2 15.1 %collective-permute-start = (bf16[64,512]{1,0:T(8,128)(2,1)S(1)}, bf16[64,512]{1,0:T(8,128)(2,1)S(1)}, u32[]{:S(2)}, u32[]{:S(2)}) collective-permute-start(bf16[64,512]{1,0:T(8,128)(2,1)S(1)} %get-tuple-element.17), channel_id=1, source_target_pairs={{0,5},{5,0},{10,15},{15,10},{1,6},{6,1},{11,12},{12,11},{2,7},{7,2... | collective-permute-start | bytes 196616 | tf_op jit(solution)/shard_map/second/ppermute | solution.py:286
  139.8 6.4 %copy-start.12 = (f32[64]{0:T(128)S(1)}, f32[64]{0:T(128)}, u32[]{:S(2)}) copy-start(f32[64]{0:T(128)} %param.24) | copy-start | bytes 772
  139.9 15.6 %collective-permute-start.1 = (bf16[64,512]{1,0:T(8,128)(2,1)S(1)}, bf16[64,512]{1,0:T(8,128)(2,1)S(1)}, u32[]{:S(2)}, u32[]{:S(2)}) collective-permute-start(bf16[64,512]{1,0:T(8,128)(2,1)S(1)} %get-tuple-element.16), channel_id=1, source_target_pairs={{0,10},{5,15},{10,0},{15,5},{1,11},{6,12},{11,1},{12,6},{2,8},{7,1... | collective-permute-start | bytes 196616 | tf_op jit(solution)/shard_map/second/ppermute | solution.py:286
